TPU v7x, 32 devices: a whole 2x2x4 slice. The times are simulated.
32 devices in a mesh: section: 2 (over x), dp: 16 (over z, y, core).
Axes of the slice: x: 2, y: 2, z: 4, core: 2. Of those that a mesh axis runs over, the one named last changes fastest.
Arguments:
- tokens: bfloat16 [8192, 1024], P('dp'), may hold values from -6 to 6
- qkv_weight: bfloat16 [2, 1024, 3072], P('section', 'dp'), may hold values from -0.1875 to 0.1875
- qkv_bias: bfloat16 [2, 3072], P('section', 'dp'), may hold values from -1.1953125 to 1.1953125
- out_weight: bfloat16 [2, 1024, 1024], P('section', 'dp'), may hold values from -0.5 to 0.5
- out_bias: bfloat16 [2, 1024], P('section', 'dp'), may hold values from -1.1953125 to 1.1953125
- norm1_gain: bfloat16 [2, 1024], P('section', 'dp'), may hold values from 0.5 to 1.5
- norm1_bias: bfloat16 [2, 1024], P('section', 'dp'), may hold values from -1.1953125 to 1.1953125
- up_weight: bfloat16 [2, 1024, 4096], P('section', 'dp'), may hold values from -0.1875 to 0.1875
- up_bias: bfloat16 [2, 4096], P('section', 'dp'), may hold values from -1.1953125 to 1.1953125
- down_weight: bfloat16 [2, 4096, 1024], P('section', 'dp'), may hold values from -0.09375 to 0.09375
- down_bias: bfloat16 [2, 1024], P('section', 'dp'), may hold values from -1.1953125 to 1.1953125
- norm2_gain: bfloat16 [2, 1024], P('section', 'dp'), may hold values from 0.5 to 1.5
- norm2_bias: bfloat16 [2, 1024], P('section', 'dp'), may hold values from -1.1953125 to 1.1953125
- proj_weight: bfloat16 [1024, 128], P('dp'), may hold values from -0.1875 to 0.1875
- doc_lengths: int32 [32, 3], P('dp'), may hold values from 1 to 96, 192 in all within a row
- pair_docs: int32 [64, 8], replicated, may hold values from 0 to 47
Outputs:
- query_losses: float32 [64], P('dp')
- activations: bfloat16 [2, 8192, 1024], P('section', 'dp')
- grad_inputs: float32 [2, 8192, 1024], P('section', 'dp')
- grad_qkv_weight: float32 [2, 1024, 3072], P('section', 'dp')
- grad_qkv_bias: float32 [2, 3072], P('section', 'dp')
- grad_out_weight: float32 [2, 1024, 1024], P('section', 'dp')
- grad_out_bias: float32 [2, 1024], P('section', 'dp')
- grad_norm1_gain: float32 [2, 1024], P('section', 'dp')
- grad_norm1_bias: float32 [2, 1024], P('section', 'dp')
- grad_up_weight: float32 [2, 1024, 4096], P('section', 'dp')
- grad_up_bias: float32 [2, 4096], P('section', 'dp')
- grad_down_weight: float32 [2, 4096, 1024], P('section', 'dp')
- grad_down_bias: float32 [2, 1024], P('section', 'dp')
- grad_norm2_gain: float32 [2, 1024], P('section', 'dp')
- grad_norm2_bias: float32 [2, 1024], P('section', 'dp')
- grad_proj_weight: float32 [1024, 128], P(('section', 'dp'))
Inputs may be any that keep to these rules, and one draw needn't show every extreme that they name: `doc_lengths`: each row fills the 192 document rows of a block; its longest document has exactly 96 tokens.
All inputs are finite; a program needn't handle non-finite values.
Results may differ from a plain program's by a relative error of at most 0.019.
Values may be sent and summed in bfloat16 or wider, within the bound.
No kernel may reach another device: no remote copies, remote signals or barrier semaphores. Data moves between devices by JAX's collectives and lax.ppermute only.
A program may use at most 320 MiB of HBM per device.

v0:
```python
from functools import partial
import math

import jax
import jax.numpy as jnp
from jax import lax
from jax.sharding import PartitionSpec as P

HEAD = 64
PROJ = 128
QLEN = 32
DOC_ROWS = 192
QRY_DEV = 2
DOCS_DEV = 3
MICRO = 2
CANDS = 8
ROWS = 256


norm_eps = 1e-05
unit_eps = 1e-06
sharpness = 20.0
score_scale = 0.125
masked_score = -1000000000.0


def from_behind(value, axis, steps):
    count = lax.axis_size(axis)
    first, last = (max(0, -steps), min(count, count - steps))
    return lax.ppermute(value, axis, [(source, source + steps) for source in range(first, last)])


def as_sent(shard):

    def short(part):
        return part.astype(jnp.bfloat16) if part.dtype == jnp.float32 else part

    return jax.tree.map(short, shard)


def product(left_side, right_side):
    return jnp.dot(left_side, right_side, preferred_element_type=jnp.float32)


def product_tn(left_side, right_side):
    return lax.dot_general(
        left_side, right_side, (((0,), (0,)), ((), ())), preferred_element_type=jnp.float32
    )


def product_nt(left_side, right_side):
    return lax.dot_general(
        left_side, right_side, (((1,), (1,)), ((), ())), preferred_element_type=jnp.float32
    )


def layer_norm(values, scales, offset):
    center = values - jnp.mean(values, axis=-1, keepdims=True)
    spread = jnp.mean(center * center, axis=-1, keepdims=True)
    return center * lax.rsqrt(spread + norm_eps) * scales + offset


def doc_layout(doc_lens):
    row_ids = jnp.arange(ROWS, dtype=jnp.int32)
    ends_at = jnp.cumsum(doc_lens)
    starts_at = ends_at - doc_lens
    doc_of = jnp.sum((row_ids[:, None] >= ends_at[None, :]).astype(jnp.int32), axis=1)
    doc_index = jnp.arange(DOCS_DEV, dtype=jnp.int32)
    begins = jnp.sum(
        jnp.where(doc_of[:, None] == doc_index[None, :], starts_at[None, :], 0), axis=1
    )
    in_docs = row_ids < DOC_ROWS
    query_rows = jnp.maximum(row_ids - DOC_ROWS, 0)
    segment = jnp.where(in_docs, doc_of, DOCS_DEV + query_rows // QLEN)
    position = jnp.where(in_docs, row_ids - begins, query_rows % QLEN)
    return (segment, position)


def rotary(position):
    step_ids = jnp.arange(HEAD // 2, dtype=jnp.int32).astype(jnp.float32)
    frequency = jnp.exp(step_ids * (-2.0 * math.log(10000.0) / HEAD))
    angles = position.astype(jnp.float32)[:, None] * frequency[None, :]
    return (jnp.cos(angles), jnp.sin(angles))


def rotate(tensor, cosine, sine_tab):
    halfway = tensor.shape[-1] // 2
    first_half = tensor[..., :halfway]
    second_half = tensor[..., halfway:]
    cos_wide = cosine[:, None, :]
    sin_wide = sine_tab[:, None, :]
    return jnp.concatenate(
        [
            first_half * cos_wide - second_half * sin_wide,
            second_half * cos_wide + first_half * sin_wide,
        ],
        axis=-1,
    )


def score_block(queries, documents, member):
    results = []
    for prefix in (PROJ // 2, 3 * PROJ // 4, PROJ):
        query_part = queries[..., :prefix]
        doc_part = documents[:, :prefix]
        query_unit = query_part * lax.rsqrt(
            jnp.sum(query_part * query_part, axis=-1, keepdims=True) + unit_eps
        )
        doc_unit = doc_part * lax.rsqrt(
            jnp.sum(doc_part * doc_part, axis=-1, keepdims=True) + unit_eps
        )
        similar = jnp.einsum("qtp,rp->qtr", query_unit, doc_unit, precision=lax.Precision.HIGHEST)
        masses = jnp.einsum(
            "qtr,rj->qtj", jnp.exp(sharpness * similar), member, precision=lax.Precision.HIGHEST
        )
        results.append(jnp.sum(jnp.log(masses), axis=1) / sharpness)
    return jnp.stack(results)


def cross_entropy(scores, pair_ids):
    total_docs = scores.shape[2]
    chosen = (
        pair_ids[:, :, None] == jnp.arange(total_docs, dtype=jnp.int32)[None, None, :]
    ).astype(jnp.float32)
    logits = jnp.einsum("kqa,qca->kqc", scores, chosen, precision=lax.Precision.HIGHEST)
    return jnp.sum(jax.nn.logsumexp(logits, axis=-1) - logits[:, :, 0], axis=0)


def layer_forward(source, weights, segment, position):
    (
        qkv_w,
        qkv_b,
        out_w,
        out_b,
        gain_one,
        bias_one,
        up_w,
        up_b,
        down_w,
        down_b,
        gain_two,
        bias_two,
    ) = weights
    row_count = source.shape[0]
    model_width = out_w.shape[0]
    mixed = product(source, qkv_w) + qkv_b.astype(jnp.float32)
    cosine, sine_tab = rotary(position)
    queries = rotate(mixed[:, :model_width].reshape(row_count, -1, HEAD), cosine, sine_tab).astype(
        jnp.bfloat16
    )
    keys_rot = rotate(
        mixed[:, model_width : 2 * model_width].reshape(row_count, -1, HEAD), cosine, sine_tab
    ).astype(jnp.bfloat16)
    values = mixed[:, 2 * model_width :].reshape(row_count, -1, HEAD).astype(jnp.bfloat16)
    scores = (
        jnp.einsum("qhd,khd->hqk", queries, keys_rot, preferred_element_type=jnp.float32)
        * score_scale
    )
    allowed = segment[:, None] == segment[None, :]
    scores = jnp.where(allowed[None], scores, masked_score)
    attention = jax.nn.softmax(scores, axis=-1)
    attention_low = attention.astype(jnp.bfloat16)
    mixture = jnp.einsum("hqk,khd->qhd", attention_low, values, preferred_element_type=jnp.float32)
    mixture = mixture.reshape(row_count, model_width).astype(jnp.bfloat16)
    first_sum = source.astype(jnp.float32) + (product(mixture, out_w) + out_b.astype(jnp.float32))
    first_norm = layer_norm(
        first_sum, gain_one.astype(jnp.float32), bias_one.astype(jnp.float32)
    ).astype(jnp.bfloat16)
    gate_in = product(first_norm, up_w) + up_b.astype(jnp.float32)
    activated = jax.nn.gelu(gate_in, approximate=False).astype(jnp.bfloat16)
    second_sum = first_norm.astype(jnp.float32) + (
        product(activated, down_w) + down_b.astype(jnp.float32)
    )
    result = layer_norm(
        second_sum, gain_two.astype(jnp.float32), bias_two.astype(jnp.float32)
    ).astype(jnp.bfloat16)
    return (
        source,
        cosine,
        sine_tab,
        queries,
        keys_rot,
        values,
        attention,
        attention_low,
        mixture,
        first_sum,
        first_norm,
        gate_in,
        activated,
        second_sum,
        result,
    )


def layer_backward(saved_state, upstream, weights):
    (
        qkv_w,
        qkv_b,
        out_w,
        out_b,
        gain_one,
        bias_one,
        up_w,
        up_b,
        down_w,
        down_b,
        gain_two,
        bias_two,
    ) = weights
    (
        source,
        cosine,
        sine_tab,
        queries,
        keys_rot,
        values,
        attention,
        attention_low,
        mixture,
        first_sum,
        first_norm,
        gate_in,
        activated,
        second_sum,
        result,
    ) = saved_state
    row_count = source.shape[0]
    unused, second_back = jax.vjp(
        layer_norm, second_sum, gain_two.astype(jnp.float32), bias_two.astype(jnp.float32)
    )
    grad_sum_two, grad_gain_two, grad_bias_two = second_back(upstream)
    grad_branch = grad_sum_two.astype(jnp.bfloat16)
    grad_down_w = product_tn(activated, grad_branch)
    grad_down_b = jnp.sum(grad_branch.astype(jnp.float32), axis=0)
    unused, gelu_back = jax.vjp(partial(jax.nn.gelu, approximate=False), gate_in)
    (grad_gate,) = gelu_back(product_nt(grad_branch, down_w))
    grad_gate_low = grad_gate.astype(jnp.bfloat16)
    grad_up_w = product_tn(first_norm, grad_gate_low)
    grad_up_b = jnp.sum(grad_gate_low.astype(jnp.float32), axis=0)
    grad_first = grad_sum_two + product_nt(grad_gate_low, up_w)
    unused, first_back = jax.vjp(
        layer_norm, first_sum, gain_one.astype(jnp.float32), bias_one.astype(jnp.float32)
    )
    grad_sum_one, grad_gain_one, grad_bias_one = first_back(grad_first)
    grad_attended = grad_sum_one.astype(jnp.bfloat16)
    grad_out_w = product_tn(mixture, grad_attended)
    grad_out_b = jnp.sum(grad_attended.astype(jnp.float32), axis=0)
    grad_mixture = (
        product_nt(grad_attended, out_w).astype(jnp.bfloat16).reshape(row_count, -1, HEAD)
    )
    grad_attention = jnp.einsum(
        "qhd,khd->hqk", grad_mixture, values, preferred_element_type=jnp.float32
    )
    grad_values = jnp.einsum(
        "hqk,qhd->khd", attention_low, grad_mixture, preferred_element_type=jnp.float32
    )
    grad_scores = attention * (
        grad_attention - jnp.sum(grad_attention * attention, axis=-1, keepdims=True)
    )
    grad_scores = grad_scores.astype(jnp.bfloat16)
    grad_queries = (
        jnp.einsum("hqk,khd->qhd", grad_scores, keys_rot, preferred_element_type=jnp.float32)
        * score_scale
    )
    grad_keys = (
        jnp.einsum("hqk,qhd->khd", grad_scores, queries, preferred_element_type=jnp.float32)
        * score_scale
    )
    grad_queries = rotate(grad_queries, cosine, -sine_tab)
    grad_keys = rotate(grad_keys, cosine, -sine_tab)
    grad_mixed = jnp.concatenate(
        [
            grad_queries.reshape(row_count, -1),
            grad_keys.reshape(row_count, -1),
            grad_values.reshape(row_count, -1),
        ],
        axis=1,
    ).astype(jnp.bfloat16)
    grad_qkv_w = product_tn(source, grad_mixed)
    grad_qkv_b = jnp.sum(grad_mixed.astype(jnp.float32), axis=0)
    grad_source = grad_sum_one + product_nt(grad_mixed, qkv_w)
    grad_terms = (
        grad_qkv_w,
        grad_qkv_b,
        grad_out_w,
        grad_out_b,
        grad_gain_one,
        grad_bias_one,
        grad_up_w,
        grad_up_b,
        grad_down_w,
        grad_down_b,
        grad_gain_two,
        grad_bias_two,
    )
    return (grad_terms, grad_source)


def loss_part(hidden, projection, segment, pair_rows, dp_index):
    embedded = product(hidden, projection).astype(jnp.bfloat16)
    own_queries = embedded[DOC_ROWS:].reshape(QRY_DEV, QLEN, -1)
    all_queries = lax.all_gather(own_queries, "dp", axis=0, tiled=True)
    doc_index = jnp.arange(DOCS_DEV, dtype=jnp.int32)
    member = (segment[:DOC_ROWS, None] == doc_index[None, :]).astype(jnp.float32)
    local_scores, score_back = jax.vjp(
        lambda query_vals, doc_vals: score_block(query_vals, doc_vals, member),
        all_queries.astype(jnp.float32),
        embedded[:DOC_ROWS].astype(jnp.float32),
    )
    all_scores = lax.all_gather(local_scores, "dp", axis=2, tiled=True)
    losses_all, cross_back = jax.vjp(
        lambda table_vals: cross_entropy(table_vals, pair_rows), all_scores
    )
    (grad_all,) = cross_back(jnp.ones_like(losses_all))
    grad_local = lax.dynamic_slice_in_dim(grad_all, dp_index * DOCS_DEV, DOCS_DEV, 2)
    grad_queries, grad_docs = score_back(grad_local)
    grad_own = lax.psum_scatter(grad_queries, "dp", scatter_dimension=0, tiled=True)
    grad_embedded = jnp.concatenate(
        [grad_docs, grad_own.reshape(QRY_DEV * QLEN, -1)], axis=0
    ).astype(jnp.bfloat16)
    grad_projection = product_tn(hidden, grad_embedded)
    grad_hidden = product_nt(grad_embedded, projection)
    own_losses = lax.dynamic_slice_in_dim(losses_all, dp_index * QRY_DEV, QRY_DEV, 0)
    return (grad_hidden, own_losses, grad_projection)


def shards(
    tokens,
    qkv_weight,
    qkv_bias,
    out_weight,
    out_bias,
    norm1_gain,
    norm1_bias,
    up_weight,
    up_bias,
    down_weight,
    down_bias,
    norm2_gain,
    norm2_bias,
    proj_weight,
    doc_lengths,
    pair_docs,
):
    section_index = lax.axis_index("section")
    dp_index = lax.axis_index("dp")
    is_first = section_index == 0
    last_scale = section_index.astype(jnp.float32)
    gathered = (
        lax.all_gather(qkv_weight, "dp", axis=1, tiled=True),
        lax.all_gather(qkv_bias, "dp", axis=1, tiled=True),
        lax.all_gather(out_weight, "dp", axis=1, tiled=True),
        lax.all_gather(out_bias, "dp", axis=1, tiled=True),
        lax.all_gather(norm1_gain, "dp", axis=1, tiled=True),
        lax.all_gather(norm1_bias, "dp", axis=1, tiled=True),
        lax.all_gather(up_weight, "dp", axis=1, tiled=True),
        lax.all_gather(up_bias, "dp", axis=1, tiled=True),
        lax.all_gather(down_weight, "dp", axis=1, tiled=True),
        lax.all_gather(down_bias, "dp", axis=1, tiled=True),
        lax.all_gather(norm2_gain, "dp", axis=1, tiled=True),
        lax.all_gather(norm2_bias, "dp", axis=1, tiled=True),
        lax.all_gather(proj_weight[None], "dp", axis=1, tiled=True),
    )
    weights = tuple((gathered[number][0] for number in range(12)))
    projection = gathered[12][0]
    model_width = projection.shape[0]
    layouts = [doc_layout(doc_lengths[micro_step]) for micro_step in range(MICRO)]
    pair_grid = pair_docs.reshape(-1, MICRO, QRY_DEV, CANDS)
    blank_rows = jnp.zeros((ROWS, model_width), jnp.bfloat16)
    arrived = blank_rows
    results = []
    received = []
    for tick_step in range(MICRO + 1):
        first_micro = min(tick_step, MICRO - 1)
        second_micro = max(tick_step - 1, 0)
        own_rows = (
            tokens[tick_step * ROWS : (tick_step + 1) * ROWS] if tick_step < MICRO else blank_rows
        )
        source = jnp.where(is_first, own_rows, arrived)
        segment = jnp.where(is_first, layouts[first_micro][0], layouts[second_micro][0])
        position = jnp.where(is_first, layouts[first_micro][1], layouts[second_micro][1])
        saved_state = layer_forward(source, weights, segment, position)
        results.append(saved_state[-1])
        if tick_step < MICRO:
            arrived = from_behind(saved_state[-1], "section", 1)
            received.append(arrived)
    activations = jnp.concatenate(
        [
            jnp.where(is_first, results[micro_step], results[micro_step + 1])
            for micro_step in range(MICRO)
        ],
        axis=0,
    )[None]
    layer_totals = None
    proj_total = jnp.zeros((model_width, projection.shape[1]), jnp.float32)
    back_grad = jnp.zeros((ROWS, model_width), jnp.float32)
    input_grads = []
    loss_slots = [None] * MICRO
    for tick_step in range(MICRO + 1):
        first_micro = MICRO - tick_step
        second_micro = MICRO - 1 - tick_step
        first_valid = first_micro < MICRO
        second_valid = second_micro >= 0
        first_clamp = min(first_micro, MICRO - 1)
        second_clamp = max(second_micro, 0)
        own_rows = tokens[first_clamp * ROWS : (first_clamp + 1) * ROWS]
        source = jnp.where(is_first, own_rows, received[second_clamp])
        segment = jnp.where(is_first, layouts[first_clamp][0], layouts[second_clamp][0])
        position = jnp.where(is_first, layouts[first_clamp][1], layouts[second_clamp][1])
        valid_scale = jnp.where(is_first, float(first_valid), float(second_valid))
        saved_state = layer_forward(source, weights, segment, position)
        if second_valid:
            pair_rows = pair_grid[:, second_clamp].reshape(-1, CANDS)
            loss_grad, own_losses, grad_projection = loss_part(
                saved_state[-1], projection, layouts[second_clamp][0], pair_rows, dp_index
            )
            proj_total = proj_total + grad_projection * last_scale
            upstream = jnp.where(is_first, back_grad, loss_grad)
        else:
            upstream = back_grad
        grad_terms, grad_source = layer_backward(saved_state, upstream * valid_scale, weights)
        input_grads.append(grad_source)
        layer_totals = (
            grad_terms
            if layer_totals is None
            else tuple((total + extra for total, extra in zip(layer_totals, grad_terms)))
        )
        if second_valid:
            sent_grad = grad_source.astype(jnp.bfloat16).astype(jnp.float32)
            back_grad, arrived_losses = (
                from_behind(sent_grad.astype(jnp.bfloat16), "section", -1).astype(sent_grad.dtype),
                from_behind(as_sent(own_losses), "section", -1).astype(own_losses.dtype),
            )
            loss_slots[second_micro] = jnp.where(is_first, arrived_losses, own_losses)
    reduced_grads = (
        lax.psum_scatter(layer_totals[0][None], "dp", scatter_dimension=1, tiled=True),
        lax.psum_scatter(layer_totals[1][None], "dp", scatter_dimension=1, tiled=True),
        lax.psum_scatter(layer_totals[2][None], "dp", scatter_dimension=1, tiled=True),
        lax.psum_scatter(layer_totals[3][None], "dp", scatter_dimension=1, tiled=True),
        lax.psum_scatter(layer_totals[4][None], "dp", scatter_dimension=1, tiled=True),
        lax.psum_scatter(layer_totals[5][None], "dp", scatter_dimension=1, tiled=True),
        lax.psum_scatter(layer_totals[6][None], "dp", scatter_dimension=1, tiled=True),
        lax.psum_scatter(layer_totals[7][None], "dp", scatter_dimension=1, tiled=True),
        lax.psum_scatter(layer_totals[8][None], "dp", scatter_dimension=1, tiled=True),
        lax.psum_scatter(layer_totals[9][None], "dp", scatter_dimension=1, tiled=True),
        lax.psum_scatter(layer_totals[10][None], "dp", scatter_dimension=1, tiled=True),
        lax.psum_scatter(layer_totals[11][None], "dp", scatter_dimension=1, tiled=True),
    )
    proj_grad = lax.psum_scatter(proj_total, ("section", "dp"), scatter_dimension=0, tiled=True)
    grad_inputs = jnp.concatenate(
        [
            jnp.where(
                is_first, input_grads[MICRO - micro_step], input_grads[MICRO - 1 - micro_step]
            )
            for micro_step in range(MICRO)
        ],
        axis=0,
    )[None]
    query_losses = jnp.concatenate(loss_slots, axis=0)
    return (
        query_losses,
        activations,
        grad_inputs,
        reduced_grads[0],
        reduced_grads[1],
        reduced_grads[2],
        reduced_grads[3],
        reduced_grads[4],
        reduced_grads[5],
        reduced_grads[6],
        reduced_grads[7],
        reduced_grads[8],
        reduced_grads[9],
        reduced_grads[10],
        reduced_grads[11],
        proj_grad,
    )


def solution(mesh):
    in_specs = (
        P("dp", None),
        P("section", "dp", None),
        P("section", "dp"),
        P("section", "dp", None),
        P("section", "dp"),
        P("section", "dp"),
        P("section", "dp"),
        P("section", "dp", None),
        P("section", "dp"),
        P("section", "dp", None),
        P("section", "dp"),
        P("section", "dp"),
        P("section", "dp"),
        P("dp", None),
        P("dp", None),
        P(),
    )
    out_specs = (
        P("dp"),
        P("section", "dp", None),
        P("section", "dp", None),
        P("section", "dp", None),
        P("section", "dp"),
        P("section", "dp", None),
        P("section", "dp"),
        P("section", "dp"),
        P("section", "dp"),
        P("section", "dp", None),
        P("section", "dp"),
        P("section", "dp", None),
        P("section", "dp"),
        P("section", "dp"),
        P("section", "dp"),
        P(("section", "dp"), None),
    )
    return jax.shard_map(shards, mesh=mesh, in_specs=in_specs, out_specs=out_specs, check_vma=False)
```

profile of v0, /device:TPU:0, one launch (start us, length us, event | category | flops | bytes accessed | tf_op | source)
XLA Modules:
  0.0 2074.0 jit_solution(11613920787607442758)
XLA Ops:
  19.7 64.1 %all-reduce.15 = (bf16[3072]{0:T(1024)(128)(2,1)S(1)}, bf16[1024]{0:T(1024)(128)(2,1)S(1)}, bf16[1024]{0:T(1024)(128)(2,1)S(1)}, bf16[1024]{0:T(1024)(128)(2,1)S...) all-reduce(bf16[3072]{0:T(1024)(128)(2,1)S(1)} %dynamic-update-slic, ...), channel_id=1, replica_groups=mesh['section'=2,'dp'=16] {'dp'}, use_global_device_ids=true, to_apply=%add.8 | all-reduce | flops 9216 | bytes 36864
  84.4 17.4 all_gather.58
  106.2 4.8 fusion.112
  121.4 72.3 %all-gather.10.cloned.1.call-done = bf16[1,1024,4096]{2,1,0:T(8,128)(2,1)} async-done(((bf16[1,64,4096]{2,1,0:T(8,128)(2,1)}), bf16[1,1024,4096]{2,1,0:T(8,128)(2,1)}) %all-gather.10.cloned.1.call-update) | async-done | bytes 8388624 | tf_op jit(solution)/shard_map/all_gather | solution.py:357
  193.7 75.2 %all-gather.12.cloned.1.call-done = bf16[1,4096,1024]{2,1,0:T(8,128)(2,1)} async-done(((bf16[1,256,1024]{2,1,0:T(8,128)(2,1)}), bf16[1,4096,1024]{2,1,0:T(8,128)(2,1)}) %all-gather.12.cloned.1.call-update) | async-done | bytes 8388624 | tf_op jit(solution)/shard_map/all_gather | solution.py:359
  268.9 28.7 %fusion.689 = (f32[256]{0:T(256)S(1)}, f32[256,1024]{1,0:T(8,128)S(1)}) fusion(f32[1024]{0:T(1024)S(1)} %add.1099, bf16[1,4096,1024]{2,1,0:T(8,128)(2,1)} %all-gather.12.cloned.1.call-done, f32[4096]{0:T(1024)S(1)} %bitcast.674, bf16[1,1024,4096]{2,1,0:T(8,128)(2,1)} %all-gather.10.cloned.1.call-done, f32[256,1024]{1,0:T(8,128)S(1)} %get-tuple-element.179, ...), kind=kOutput, calls=%fused_computation.958 | convolution fusion | flops 4367843328 | bytes 18906112 | tf_op jit(solution)/shard_map/dot_general | solution.py:42
  298.8 3.4 collective-permute-start
  302.2 19.6 all-gather
  324.9 5.0 fusion.124
  343.0 4.5 fusion.694
  353.4 4.7 fusion.692
  358.1 3.0 convolution_convert_fusion.1
  364.2 13.2 multiply_convert_fusion.5
  385.2 18.3 all_gather.64
  432.2 20.4 all_gather.65
  470.8 3.1 multiply_reduce_fusion.45
  473.9 3.1 multiply_reduce_fusion.25
  480.5 3.1 multiply_reduce_fusion.41
  483.6 3.1 multiply_reduce_fusion.26
  490.4 3.4 multiply_reduce_fusion.37
  498.9 16.0 multiply_convert_fusion.1
  514.9 3.4 fusion.706
  531.6 4.6 fusion.121
  544.4 4.2 subtract_convert_fusion.8
  548.6 5.4 fusion.697
  558.1 16.4 multiply_convert_fusion.4
  582.6 18.5 all_gather.66
  625.6 20.5 all_gather.67
  692.6 34.2 %reduce-scatter.32.cloned.1.call-done = f32[2,32,128]{2,1,0:T(8,128)} async-done(((f32[32,32,128]{2,1,0:T(8,128)}), f32[2,32,128]{2,1,0:T(8,128)}) %reduce-scatter.32.cloned.1.call-update) | async-done | bytes 32784 | tf_op jit(solution)/shard_map/reduce_scatter | solution.py:318
  734.9 12.2 convert_reduce_fusion.2
  747.1 7.5 multiply_reduce_fusion.8
  761.1 3.2 convolution_convert_fusion.3
  770.8 3.0 fusion.705
  776.2 9.3 reduce-scatter.34.cloned.1.call-done
  793.4 11.3 convert_reduce_fusion.1
  804.7 6.9 multiply_reduce_fusion.7
  817.7 3.3 convolution_convert_fusion.2
  827.6 3.3 fusion.685
  834.5 9.6 collective-permute-done.5
  846.6 11.5 convert_reduce_fusion
  858.2 6.9 multiply_reduce_fusion.6
  871.1 4.0 convolution_convert_fusion
  903.1 8.1 fusion.670
  911.2 6.5 fusion.669
  917.7 13.6 add_bitcast_fusion.2
  932.0 10.0 fusion.707
  942.1 8.2 fusion.710
  950.2 18.9 add_bitcast_fusion.1
  970.2 9.9 fusion.711
  980.2 8.2 fusion.712
  988.4 18.8 add_bitcast_fusion
  1009.2 4.1 collective-permute-done.1
  1023.0 19.4 fusion.702
  1045.7 4.8 fusion.309
  1056.1 55.5 %reduce-scatter.50.cloned.1.call-done = f32[64,1]{1,0:T(8,128)} async-done(((f32[1024,1]{1,0:T(8,128)}), f32[64,1]{1,0:T(8,128)}) %reduce-scatter.50.cloned.1.call-update) | async-done | bytes 272
  1113.0 57.0 %reduce-scatter.52.cloned.1.call-done = f32[64,1]{1,0:T(8,128)} async-done(((f32[1024,1]{1,0:T(8,128)}), f32[64,1]{1,0:T(8,128)}) %reduce-scatter.52.cloned.1.call-update) | async-done | bytes 272
  1171.4 57.2 %reduce-scatter.48.cloned.1.call-done = f32[64,1]{1,0:T(8,128)} async-done(((f32[1024,1]{1,0:T(8,128)}), f32[64,1]{1,0:T(8,128)}) %reduce-scatter.48.cloned.1.call-update) | async-done | bytes 272
  1229.9 60.8 %reduce-scatter.46.cloned.1.call-done = f32[192,1]{1,0:T(8,128)} async-done(((f32[3072,1]{1,0:T(8,128)}), f32[192,1]{1,0:T(8,128)}) %reduce-scatter.46.cloned.1.call-update) | async-done | bytes 784
  1292.3 63.2 %reduce-scatter.54.cloned.1.call-done = f32[256,1]{1,0:T(8,128)} async-done(((f32[4096,1]{1,0:T(8,128)}), f32[256,1]{1,0:T(8,128)}) %reduce-scatter.54.cloned.1.call-update) | async-done | bytes 1040
  1357.0 133.9 %reduce-scatter.44.cloned.1.call-done = f32[32,128]{1,0:T(8,128)} async-done(((f32[1024,128]{1,0:T(8,128)}), f32[32,128]{1,0:T(8,128)}) %reduce-scatter.44.cloned.1.call-update) | async-done | bytes 16400 | tf_op jit(solution)/shard_map/reduce_scatter | solution.py:450
  1491.0 73.7 %reduce-scatter.38.cloned.1.call-done = f32[1,64,1024]{2,1,0:T(8,128)} async-done(((f32[1,1024,1024]{2,1,0:T(8,128)}), f32[1,64,1024]{2,1,0:T(8,128)}) %reduce-scatter.38.cloned.1.call-update) | async-done | bytes 262160 | tf_op jit(solution)/shard_map/reduce_scatter | solution.py:439
  1564.7 138.1 %reduce-scatter.36.cloned.1.call-done = f32[1,64,3072]{2,1,0:T(8,128)} async-done(((f32[1,1024,3072]{2,1,0:T(8,128)}), f32[1,64,3072]{2,1,0:T(8,128)}) %reduce-scatter.36.cloned.1.call-update) | async-done | bytes 786448 | tf_op jit(solution)/shard_map/reduce_scatter | solution.py:437
  1702.7 182.3 %reduce-scatter.40.cloned.1.call-done = f32[1,64,4096]{2,1,0:T(8,128)} async-done(((f32[1,1024,4096]{2,1,0:T(8,128)}), f32[1,64,4096]{2,1,0:T(8,128)}) %reduce-scatter.40.cloned.1.call-update) | async-done | bytes 1048592 | tf_op jit(solution)/shard_map/reduce_scatter | solution.py:443
  1885.0 182.3 %reduce-scatter.42.cloned.1.call-done = f32[1,256,1024]{2,1,0:T(8,128)} async-done(((f32[1,4096,1024]{2,1,0:T(8,128)}), f32[1,256,1024]{2,1,0:T(8,128)}) %reduce-scatter.42.cloned.1.call-update) | async-done | bytes 1048592 | tf_op jit(solution)/shard_map/reduce_scatter | solution.py:445
  (1002 shorter events, 334.5 us)
Async XLA Ops:
  7.2 99.0 %all-gather.6.cloned.1.call-start = ((), (), s32[]{:S(2)}) async-start(), calls=%async_computation.15 | async-start | bytes 6684672 | tf_op jit(solution)/shard_map/all_gather | solution.py:351
  7.9 110.1 %all-gather.8.cloned.1.call-start = ((), (), s32[]{:S(2)}) async-start(), calls=%async_computation.16 | async-start | bytes 2228224 | tf_op jit(solution)/shard_map/all_gather | solution.py:353
  8.7 185.0 %all-gather.10.cloned.1.call-start = ((), (), s32[]{:S(2)}) async-start(), calls=%async_computation.17 | async-start | bytes 8912896 | tf_op jit(solution)/shard_map/all_gather | solution.py:357
  9.4 259.5 %all-gather.12.cloned.1.call-start = ((), (), s32[]{:S(2)}) async-start(), calls=%async_computation.18 | async-start | bytes 8912896 | tf_op jit(solution)/shard_map/all_gather | solution.py:359
  10.0 716.8 %reduce-scatter.32.cloned.1.call-start = ((), (), s32[]{:S(2)}) async-start(), calls=%async_computation.19 | async-start | bytes 557056 | tf_op jit(solution)/shard_map/reduce_scatter | solution.py:318
  84.4 490.2 %copy-start.163 = (f32[1024]{0:T(1024)}, f32[1024]{0:T(1024)S(1)}, u32[]{:S(2)}) copy-start(f32[1024]{0:T(1024)S(1)} %add.1098) | copy-start | bytes 12292
  84.4 472.6 %copy-start.146 = (f32[1024]{0:T(1024)}, f32[1024]{0:T(1024)S(1)}, u32[]{:S(2)}) copy-start(f32[1024]{0:T(1024)S(1)} %add.1097) | copy-start | bytes 12292
  84.4 184.5 %copy-start.261 = (f32[1024]{0:T(1024)}, f32[1024]{0:T(1024)S(1)}, u32[]{:S(2)}) copy-start(f32[1024]{0:T(1024)S(1)} %add.1099) | copy-start | bytes 12292
  84.4 493.7 %copy-start.183 = (f32[1024]{0:T(1024)}, f32[1024]{0:T(1024)S(1)}, u32[]{:S(2)}) copy-start(f32[1024]{0:T(1024)S(1)} %add.1100) | copy-start | bytes 12292
  84.4 26.6 %copy-start.234 = (f32[3072]{0:T(1024)}, f32[3072]{0:T(1024)S(1)}, u32[]{:S(2)}) copy-start(f32[3072]{0:T(1024)S(1)} %add.1096) | copy-start | bytes 36868
  101.9 167.0 %copy-start.211 = (f32[1,4096]{1,0:T(1,128)}, f32[1,4096]{1,0:T(1,128)S(1)}, u32[]{:S(2)}) copy-start(f32[1,4096]{1,0:T(1,128)S(1)} %add.1079) | copy-start | bytes 49156
  106.2 236.4 %copy-start.149 = (f32[256,32]{0,1:T(8,128)}, f32[256,32]{0,1:T(8,128)S(1)}, u32[]{:S(2)}) copy-start(f32[256,32]{0,1:T(8,128)S(1)} %get-tuple-element.174) | copy-start | bytes 98308
  106.2 245.4 %copy-start.134 = (f32[256,32]{0,1:T(8,128)}, f32[256,32]{0,1:T(8,128)S(1)}, u32[]{:S(2)}) copy-start(f32[256,32]{0,1:T(8,128)S(1)} %get-tuple-element.153) | copy-start | bytes 98308
  297.5 32.4 %copy-start.23 = (f32[256,1024]{1,0:T(8,128)}, f32[256,1024]{1,0:T(8,128)S(1)}, u32[]{:S(2)}) copy-start(f32[256,1024]{1,0:T(8,128)S(1)} %get-tuple-element.181) | copy-start | bytes 3145732
  297.6 27.4 %copy-start.235 = (f32[3072]{0:T(1024)S(1)}, f32[3072]{0:T(1024)}, u32[]{:S(2)}) copy-start(f32[3072]{0:T(1024)} %copy-done.234) | copy-start | bytes 36868
  298.8 26.0 %collective-permute-start = (bf16[256,1024]{1,0:T(8,128)(2,1)S(1)}, bf16[256,1024]{1,0:T(8,128)(2,1)S(1)}, u32[]{:S(2)}, u32[]{:S(2)}) collective-permute-start(bf16[256,1024]{1,0:T(8,128)(2,1)S(1)} %add_convert_fusion.10), channel_id=1, source_target_pairs={{0,16},{1,17},{2,18},{3,19},{4,20},{5,21},{6,22},{7,23},{8,24},{9,... | collective-permute-start | bytes 1572872 | tf_op jit(solution)/shard_map/ppermute | solution.py:30
  321.8 61.1 %copy-start.69 = (bf16[1024,128]{1,0:T(8,128)(2,1)}, bf16[1024,128]{1,0:T(8,128)(2,1)S(1)}, u32[]{:S(2)}) copy-start(bf16[1024,128]{1,0:T(8,128)(2,1)S(1)} %all-gather) | copy-start | bytes 786436
  362.0 15.5 slice-start.2
  382.9 35.9 %copy-start.27 = (bf16[256,1024]{1,0:T(8,128)(2,1)}, bf16[256,1024]{1,0:T(8,128)(2,1)S(1)}, u32[]{:S(2)}) copy-start(bf16[256,1024]{1,0:T(8,128)(2,1)S(1)} %get-tuple-element.68) | copy-start | bytes 1572868
  404.2 116.0 %collective-permute-start.2 = (bf16[256,1024]{1,0:T(8,128)(2,1)S(1)}, bf16[256,1024]{1,0:T(8,128)(2,1)}, u32[]{:S(2)}, u32[]{:S(2)}) collective-permute-start(bf16[256,1024]{1,0:T(8,128)(2,1)S(1)} %get-tuple-element.68), channel_id=1, source_target_pairs={{0,16},{1,17},{2,18},{3,19},{4,20},{5,21},{6,22},{7,23},{8,24},{9,... | collective-permute-start | bytes 1572872 | tf_op jit(solution)/shard_map/ppermute | solution.py:30
  488.1 26.8 %slice-start.4 = ((s8[8388608]{0:T(1024)(128)(4,1)}), s8[4194304]{0:T(1024)(128)(4,1)S(1)}, s32[]{:S(2)}) async-start(s8[8388608]{0:T(1024)(128)(4,1)} %bitcast.697), calls=%async_computation.38 | async-start | bytes 8388608
  488.1 32.1 %slice-start.10 = ((s8[6291456]{0:T(1024)(128)(4,1)}), s8[4194304]{0:T(1024)(128)(4,1)S(1)}, s32[]{:S(2)}) async-start(s8[6291456]{0:T(1024)(128)(4,1)} %bitcast.703), calls=%async_computation.44 | async-start | bytes 8388608
  498.8 16.0 copy-start.263
  498.8 16.0 slice-start.5
  498.9 21.4 %slice-start.11 = ((s8[6291456]{0:T(1024)(128)(4,1)}), s8[2097152]{0:T(1024)(128)(4,1)S(1)}, s32[]{:S(2)}) async-start(s8[6291456]{0:T(1024)(128)(4,1)} %bitcast.703), calls=%async_computation.45 | async-start | bytes 4194304
  520.3 36.7 %copy-start.32 = (bf16[256,1024]{1,0:T(8,128)(2,1)}, bf16[256,1024]{1,0:T(8,128)(2,1)S(1)}, u32[]{:S(2)}) copy-start(bf16[256,1024]{1,0:T(8,128)(2,1)S(1)} %broadcast_select_fusion.4) | copy-start | bytes 1572868
  554.0 20.6 slice-start.6
  557.8 16.7 copy-start.1
  557.8 16.7 copy-start.193
  558.1 16.4 copy-start.253
  558.1 16.4 copy-start.197
  558.1 16.4 copy-start.264
  558.1 16.4 slice-start.7
  577.2 30.6 %copy-start.185 = (s32[256]{0:T(256)S(1)}, s32[256]{0:T(256)}, u32[]{:S(2)}) copy-start(s32[256]{0:T(256)} %get-tuple-element.163) | copy-start | bytes 3076
  577.2 24.8 %copy-start.224 = (f32[256]{0:T(256)}, f32[256]{0:T(256)S(1)}, u32[]{:S(2)}) copy-start(f32[256]{0:T(256)S(1)} %broadcast_multiply_fusion.10) | copy-start | bytes 3076
  579.9 22.4 %copy-start.244 = (f32[192]{0:T(256)}, f32[192]{0:T(256)S(1)}, u32[]{:S(2)}) copy-start(f32[192]{0:T(256)S(1)} %multiply_reduce_fusion.39) | copy-start | bytes 2308
  580.6 20.5 copy-start.29
  602.3 22.6 %copy-start.200 = (f32[192]{0:T(256)}, f32[192]{0:T(256)S(1)}, u32[]{:S(2)}) copy-start(f32[192]{0:T(256)S(1)} %add_rsqrt_fusion.10) | copy-start | bytes 2308
  603.0 21.9 %copy-start.226 = (f32[192]{0:T(256)}, f32[192]{0:T(256)S(1)}, u32[]{:S(2)}) copy-start(f32[192]{0:T(256)S(1)} %add_rsqrt_fusion.11) | copy-start | bytes 2308
  674.6 111.0 %reduce-scatter.34.cloned.1.call-start = ((), (), s32[]{:S(2)}) async-start(), calls=%async_computation.20 | async-start | bytes 557056 | tf_op jit(solution)/shard_map/reduce_scatter | solution.py:318
  677.4 52.1 %copy-start.225 = (f32[256]{0:T(256)S(1)}, f32[256]{0:T(256)}, u32[]{:S(2)}) copy-start(f32[256]{0:T(256)} %copy-done.224) | copy-start | bytes 3076
  679.7 49.9 %copy-start.71 = (bf16[1024,128]{1,0:T(8,128)(2,1)S(1)}, bf16[1024,128]{1,0:T(8,128)(2,1)}, u32[]{:S(2)}) copy-start(bf16[1024,128]{1,0:T(8,128)(2,1)} %copy-done.69) | copy-start | bytes 786436
  679.7 372.4 %reduce-scatter.58.cloned.1.call-start = ((), (), s32[]{:S(2)}) async-start(), calls=%async_computation.32 | async-start | bytes 557056
  684.7 48.3 %copy-start.11 = (f32[256,1024]{1,0:T(8,128)S(1)}, f32[256,1024]{1,0:T(8,128)}, u32[]{:S(2)}) copy-start(f32[256,1024]{1,0:T(8,128)} %copy-done.10) | copy-start | bytes 3145732
  770.8 17.2 copy-start.196
  773.8 14.2 collective-permute-start.4
  830.8 13.3 collective-permute-start.5
  881.4 172.0 %reduce-scatter.60.cloned.1.call-start = ((), (), s32[]{:S(2)}) async-start(), calls=%async_computation.33 | async-start | bytes 557056
  882.6 172.2 %reduce-scatter.56.cloned.1.call-start = ((), (), s32[]{:S(2)}) async-start(), calls=%async_computation.31 | async-start | bytes 557056
  883.7 228.0 %reduce-scatter.50.cloned.1.call-start = ((), (), s32[]{:S(2)}) async-start(), calls=%async_computation.28 | async-start | bytes 557056
  884.8 285.2 %reduce-scatter.52.cloned.1.call-start = ((), (), s32[]{:S(2)}) async-start(), calls=%async_computation.29 | async-start | bytes 557056
  886.0 342.6 %reduce-scatter.48.cloned.1.call-start = ((), (), s32[]{:S(2)}) async-start(), calls=%async_computation.27 | async-start | bytes 557056
  887.1 403.7 %reduce-scatter.46.cloned.1.call-start = ((), (), s32[]{:S(2)}) async-start(), calls=%async_computation.26 | async-start | bytes 1671168
  892.2 463.3 %reduce-scatter.54.cloned.1.call-start = ((), (), s32[]{:S(2)}) async-start(), calls=%async_computation.30 | async-start | bytes 2228224
  894.5 596.5 %reduce-scatter.44.cloned.1.call-start = ((), (), s32[]{:S(2)}) async-start(), calls=%async_computation.25 | async-start | bytes 540672 | tf_op jit(solution)/shard_map/reduce_scatter | solution.py:450
  897.0 667.7 %reduce-scatter.38.cloned.1.call-start = ((), (), s32[]{:S(2)}) async-start(), calls=%async_computation.22 | async-start | bytes 4456448 | tf_op jit(solution)/shard_map/reduce_scatter | solution.py:439
  903.0 799.8 %reduce-scatter.36.cloned.1.call-start = ((), (), s32[]{:S(2)}) async-start(), calls=%async_computation.21 | async-start | bytes 13369344 | tf_op jit(solution)/shard_map/reduce_scatter | solution.py:437
  931.4 953.7 %reduce-scatter.40.cloned.1.call-start = ((), (), s32[]{:S(2)}) async-start(), calls=%async_computation.23 | async-start | bytes 17825792 | tf_op jit(solution)/shard_map/reduce_scatter | solution.py:443
  969.2 1098.1 %reduce-scatter.42.cloned.1.call-start = ((), (), s32[]{:S(2)}) async-start(), calls=%async_computation.24 | async-start | bytes 17825792 | tf_op jit(solution)/shard_map/reduce_scatter | solution.py:445
  1007.9 5.4 collective-permute-start.1
  1015.8 29.2 %collective-permute-start.3 = (bf16[2]{0:T(256)(128)(2,1)S(1)}, bf16[2]{0:T(256)(128)(2,1)S(1)}, u32[]{:S(2)}, u32[]{:S(2)}) collective-permute-start(bf16[2]{0:T(256)(128)(2,1)S(1)} %dynamic_slice.20), channel_id=1, source_target_pairs={{16,0},{17,1},{18,2},{19,3},{20,4},{21,5},{22,6},{23,7},{24,8},{25... | collective-permute-start | bytes 20 | tf_op jit(solution)/shard_map/ppermute | solution.py:30
  1023.0 19.8 copy-start.28
  1023.0 19.8 copy-start.184
  1023.0 20.9 %copy-start.106 = (bf16[256,1024]{1,0:T(8,128)(2,1)S(1)}, bf16[256,1024]{1,0:T(8,128)(2,1)}, u32[]{:S(2)}) copy-start(bf16[256,1024]{1,0:T(8,128)(2,1)} %get-tuple-element.67) | copy-start | bytes 1572868
  (258 other events, 1333.4 us)
Sparse Core Ops, SparseCore 0:
  10.3 65.1 all-gather.5
  77.7 40.0 all-gather.7
  120.0 73.6 all-gather.9
  195.7 73.1 all-gather.11
  674.7 52.0 reduce-scatter.31
  730.6 54.8 reduce-scatter.33
  881.5 54.2 reduce-scatter.57
  939.8 54.7 reduce-scatter.59
  998.2 54.8 reduce-scatter.55
  1056.8 54.7 reduce-scatter.49
  1115.2 54.7 reduce-scatter.51
  1173.9 54.6 reduce-scatter.47
  1232.3 58.4 reduce-scatter.45
  1294.8 60.6 reduce-scatter.53
  1358.2 132.7 reduce-scatter.43
  1495.8 68.8 reduce-scatter.37
  1569.1 133.5 reduce-scatter.35
  1707.3 177.7 reduce-scatter.39
  1889.7 177.5 reduce-scatter.41
where the time goes:
time: 2080 us; the launch traced here: 2070 us
  waiting for transfers between devices  1210 us (58%)
  matrix products  431 us (21%)
  blocking collectives  179 us (9%)
  local copies, waits for them, and re-layouts  129 us (6%)
  other arithmetic  90.4 us (4%)
    unnamed x27, waiting for transfers between devices  297 us
    reduce_scatter x1, waiting for transfers between devices, shards(): lax.psum_scatter(layer_totals[6][None], 'dp', scatter_dimension=1, tiled=...  182 us
    reduce_scatter x1, waiting for transfers between devices, shards(): lax.psum_scatter(layer_totals[8][None], 'dp', scatter_dimension=1, tiled=...  182 us
    reduce_scatter x1, waiting for transfers between devices, shards(): lax.psum_scatter(layer_totals[0][None], 'dp', scatter_dimension=1, tiled=...  138 us
    reduce_scatter x1, waiting for transfers between devices, shards(): lax.psum_scatter(proj_total, ('section', 'dp'), scatter_dimension=0, tile...  134 us
    dot_general x20, matrix products, product(): return jnp.dot(left_side, right_side, preferred_element_type=jnp.float32)  127 us
    dot_general x14, matrix products, product_tn(): lax.dot_general(left_side, right_side, (((0,), (0,)), ((), ())), preferre...  111 us
    dot_general x14, matrix products, product_nt(): lax.dot_general(left_side, right_side, (((1,), (1,)), ((), ())), preferre...  77.4 us
  transfers between devices with their start and end apart: 25, of which 17 were waited for; matrix products, arithmetic and copies ran while one was open for 17% of the time, Pallas kernels for 0%

commit v1 on v0

v1 whole, which is shorter than its diff:
```python
from functools import partial
import math

import jax
import jax.numpy as jnp
from jax import lax
from jax.experimental import pallas as pl
from jax.experimental.pallas import tpu as pltpu
from jax.sharding import PartitionSpec as P

HEAD = 64
PROJ = 128
QLEN = 32
DOC_ROWS = 192
QRY_DEV = 2
DOCS_DEV = 3
MICRO = 2
CANDS = 8
ROWS = 256
PREFIXES = (PROJ // 2, 3 * PROJ // 4, PROJ)


norm_eps = 1e-05
unit_eps = 1e-06
sharpness = 20.0
score_scale = 0.125
masked_score = -1000000000.0


def from_behind(value, axis, steps):
    count = lax.axis_size(axis)
    first, last = (max(0, -steps), min(count, count - steps))
    return lax.ppermute(value, axis, [(source, source + steps) for source in range(first, last)])


def product(left_side, right_side):
    return jnp.dot(left_side, right_side, preferred_element_type=jnp.float32)


def product_tn(left_side, right_side):
    return lax.dot_general(
        left_side, right_side, (((0,), (0,)), ((), ())), preferred_element_type=jnp.float32
    )


def product_nt(left_side, right_side):
    return lax.dot_general(
        left_side, right_side, (((1,), (1,)), ((), ())), preferred_element_type=jnp.float32
    )


def layer_norm(values, scales, offset):
    center = values - jnp.mean(values, axis=-1, keepdims=True)
    spread = jnp.mean(center * center, axis=-1, keepdims=True)
    return center * lax.rsqrt(spread + norm_eps) * scales + offset


def doc_layout(doc_lens):
    row_ids = jnp.arange(ROWS, dtype=jnp.int32)
    ends_at = jnp.cumsum(doc_lens)
    starts_at = ends_at - doc_lens
    doc_of = jnp.sum((row_ids[:, None] >= ends_at[None, :]).astype(jnp.int32), axis=1)
    doc_index = jnp.arange(DOCS_DEV, dtype=jnp.int32)
    begins = jnp.sum(
        jnp.where(doc_of[:, None] == doc_index[None, :], starts_at[None, :], 0), axis=1
    )
    in_docs = row_ids < DOC_ROWS
    query_rows = jnp.maximum(row_ids - DOC_ROWS, 0)
    segment = jnp.where(in_docs, doc_of, DOCS_DEV + query_rows // QLEN)
    position = jnp.where(in_docs, row_ids - begins, query_rows % QLEN)
    return (segment, position)


def rotary(position):
    step_ids = jnp.arange(HEAD // 2, dtype=jnp.int32).astype(jnp.float32)
    frequency = jnp.exp(step_ids * (-2.0 * math.log(10000.0) / HEAD))
    angles = position.astype(jnp.float32)[:, None] * frequency[None, :]
    return (jnp.cos(angles), jnp.sin(angles))


def rotate(tensor, cosine, sine_tab):
    halfway = tensor.shape[-1] // 2
    first_half = tensor[..., :halfway]
    second_half = tensor[..., halfway:]
    cos_wide = cosine[:, None, :]
    sin_wide = sine_tab[:, None, :]
    return jnp.concatenate(
        [
            first_half * cos_wide - second_half * sin_wide,
            second_half * cos_wide + first_half * sin_wide,
        ],
        axis=-1,
    )


def layer_forward(source, weights, segment, position):
    (
        qkv_w,
        qkv_b,
        out_w,
        out_b,
        gain_one,
        bias_one,
        up_w,
        up_b,
        down_w,
        down_b,
        gain_two,
        bias_two,
    ) = weights
    row_count = source.shape[0]
    model_width = out_w.shape[0]
    mixed = product(source, qkv_w) + qkv_b.astype(jnp.float32)
    cosine, sine_tab = rotary(position)
    queries = rotate(mixed[:, :model_width].reshape(row_count, -1, HEAD), cosine, sine_tab).astype(
        jnp.bfloat16
    )
    keys_rot = rotate(
        mixed[:, model_width : 2 * model_width].reshape(row_count, -1, HEAD), cosine, sine_tab
    ).astype(jnp.bfloat16)
    values = mixed[:, 2 * model_width :].reshape(row_count, -1, HEAD).astype(jnp.bfloat16)
    scores = (
        jnp.einsum("qhd,khd->hqk", queries, keys_rot, preferred_element_type=jnp.float32)
        * score_scale
    )
    allowed = segment[:, None] == segment[None, :]
    scores = jnp.where(allowed[None], scores, masked_score)
    attention = jax.nn.softmax(scores, axis=-1)
    attention_low = attention.astype(jnp.bfloat16)
    mixture = jnp.einsum("hqk,khd->qhd", attention_low, values, preferred_element_type=jnp.float32)
    mixture = mixture.reshape(row_count, model_width).astype(jnp.bfloat16)
    first_sum = source.astype(jnp.float32) + (product(mixture, out_w) + out_b.astype(jnp.float32))
    first_norm = layer_norm(
        first_sum, gain_one.astype(jnp.float32), bias_one.astype(jnp.float32)
    ).astype(jnp.bfloat16)
    gate_in = product(first_norm, up_w) + up_b.astype(jnp.float32)
    activated = jax.nn.gelu(gate_in, approximate=False).astype(jnp.bfloat16)
    second_sum = first_norm.astype(jnp.float32) + (
        product(activated, down_w) + down_b.astype(jnp.float32)
    )
    result = layer_norm(
        second_sum, gain_two.astype(jnp.float32), bias_two.astype(jnp.float32)
    ).astype(jnp.bfloat16)
    return (
        source,
        cosine,
        sine_tab,
        queries,
        keys_rot,
        values,
        attention,
        attention_low,
        mixture,
        first_sum,
        first_norm,
        gate_in,
        activated,
        second_sum,
        result,
    )


def layer_backward(saved_state, upstream, weights):
    (
        qkv_w,
        qkv_b,
        out_w,
        out_b,
        gain_one,
        bias_one,
        up_w,
        up_b,
        down_w,
        down_b,
        gain_two,
        bias_two,
    ) = weights
    (
        source,
        cosine,
        sine_tab,
        queries,
        keys_rot,
        values,
        attention,
        attention_low,
        mixture,
        first_sum,
        first_norm,
        gate_in,
        activated,
        second_sum,
        result,
    ) = saved_state
    row_count = source.shape[0]
    unused, second_back = jax.vjp(
        layer_norm, second_sum, gain_two.astype(jnp.float32), bias_two.astype(jnp.float32)
    )
    grad_sum_two, grad_gain_two, grad_bias_two = second_back(upstream)
    grad_branch = grad_sum_two.astype(jnp.bfloat16)
    grad_down_b = jnp.sum(grad_branch.astype(jnp.float32), axis=0)
    unused, gelu_back = jax.vjp(partial(jax.nn.gelu, approximate=False), gate_in)
    (grad_gate,) = gelu_back(product_nt(grad_branch, down_w))
    grad_gate_low = grad_gate.astype(jnp.bfloat16)
    grad_up_b = jnp.sum(grad_gate_low.astype(jnp.float32), axis=0)
    grad_first = grad_sum_two + product_nt(grad_gate_low, up_w)
    unused, first_back = jax.vjp(
        layer_norm, first_sum, gain_one.astype(jnp.float32), bias_one.astype(jnp.float32)
    )
    grad_sum_one, grad_gain_one, grad_bias_one = first_back(grad_first)
    grad_attended = grad_sum_one.astype(jnp.bfloat16)
    grad_out_b = jnp.sum(grad_attended.astype(jnp.float32), axis=0)
    grad_mixture = (
        product_nt(grad_attended, out_w).astype(jnp.bfloat16).reshape(row_count, -1, HEAD)
    )
    grad_attention = jnp.einsum(
        "qhd,khd->hqk", grad_mixture, values, preferred_element_type=jnp.float32
    )
    grad_values = jnp.einsum(
        "hqk,qhd->khd", attention_low, grad_mixture, preferred_element_type=jnp.float32
    )
    grad_scores = attention * (
        grad_attention - jnp.sum(grad_attention * attention, axis=-1, keepdims=True)
    )
    grad_scores = grad_scores.astype(jnp.bfloat16)
    grad_queries = (
        jnp.einsum("hqk,khd->qhd", grad_scores, keys_rot, preferred_element_type=jnp.float32)
        * score_scale
    )
    grad_keys = (
        jnp.einsum("hqk,qhd->khd", grad_scores, queries, preferred_element_type=jnp.float32)
        * score_scale
    )
    grad_queries = rotate(grad_queries, cosine, -sine_tab)
    grad_keys = rotate(grad_keys, cosine, -sine_tab)
    grad_mixed = jnp.concatenate(
        [
            grad_queries.reshape(row_count, -1),
            grad_keys.reshape(row_count, -1),
            grad_values.reshape(row_count, -1),
        ],
        axis=1,
    ).astype(jnp.bfloat16)
    grad_qkv_b = jnp.sum(grad_mixed.astype(jnp.float32), axis=0)
    grad_source = grad_sum_one + product_nt(grad_mixed, qkv_w)
    pairs = (
        (activated, grad_branch),
        (first_norm, grad_gate_low),
        (mixture, grad_attended),
        (source, grad_mixed),
    )
    vectors = (
        grad_qkv_b,
        grad_out_b,
        grad_gain_one,
        grad_bias_one,
        grad_up_b,
        grad_down_b,
        grad_gain_two,
        grad_bias_two,
    )
    return (pairs, vectors, grad_source)


def grid_of(count):
    dims, rest = [], count // 2
    while rest % 4 == 0:
        dims.append(4)
        rest //= 4
    if rest > 1:
        dims.append(rest)
    return dims + [2]


def coordinates(dims, number):
    at = []
    for size in reversed(dims):
        at.append(number % size)
        number = number // size
    return at[::-1]


def shifted(value, dims, dim, steps):
    count = math.prod(dims)
    stride = math.prod(dims[dim + 1 :])
    pairs = []
    for source in range(count):
        place = (source // stride) % dims[dim]
        pairs.append((source, source + ((place + steps) % dims[dim] - place) * stride))
    return lax.ppermute(value, "dp", pairs)


def after(value, *earlier):
    return lax.optimization_barrier((value, *earlier))[0]


def place_kernel(count, rows, places, *refs):
    pieces, out, sems = refs[:-2], refs[-2], refs[-1]
    copies = []
    for number in range(count):
        group, inner = divmod(number, pieces[0].shape[0])
        copies.append(
            pltpu.make_async_copy(
                pieces[group].at[inner], out.at[places[number]], sems.at[number]
            )
        )
    for copy in copies:
        copy.start()
    for copy in copies:
        copy.wait()


def placed(pieces, places):
    count = sum(piece.shape[0] for piece in pieces)
    rows, columns = pieces[0].shape[1:]
    if rows % 16:
        stacked = jnp.concatenate(pieces, axis=0)
        order = jnp.zeros((count,), jnp.int32).at[places].set(jnp.arange(count, dtype=jnp.int32))
        return jnp.take(stacked, order, axis=0).reshape(count * rows, columns)
    return pl.pallas_call(
        partial(place_kernel, count, rows),
        out_shape=jax.ShapeDtypeStruct((count, rows, columns), pieces[0].dtype),
        in_specs=[pl.BlockSpec(memory_space=pltpu.SMEM)]
        + [pl.BlockSpec(memory_space=pl.ANY)] * len(pieces),
        out_specs=pl.BlockSpec(memory_space=pltpu.VMEM),
        scratch_shapes=[pltpu.SemaphoreType.DMA((count,))],
        compiler_params=pltpu.CompilerParams(vmem_limit_bytes=24 << 20),
        name="place",
    )(places, *pieces).reshape(count * rows, columns)


def gather_rows(shards_in_order, dims, dp_index):
    at = [
        (dp_index // math.prod(dims[dim + 1 :])) % dims[dim] for dim in range(len(dims))
    ]
    owners = jnp.zeros((1,), jnp.int32)
    for dim in range(len(dims)):
        steps = jnp.arange(dims[dim], dtype=jnp.int32)
        own = ((at[dim] - steps) % dims[dim]) * math.prod(dims[dim + 1 :])
        owners = (own[:, None] + owners[None, :]).reshape(-1)
    first_done = []
    whole = []
    for number, shard in enumerate(shards_in_order):
        if number >= 2:
            shard = after(shard, first_done[number - 2])
        stack = jnp.stack(
            [shard] + [shifted(shard, dims, 0, steps) for steps in range(1, dims[0])]
        )
        first_done.append(stack)
        groups = [stack]
        for dim in range(1, len(dims)):
            groups = groups + [
                shifted(group, dims, dim, steps)
                for steps in range(1, dims[dim])
                for group in groups
            ]
        whole.append(placed(groups, owners))
    return whole


def scatter_rows(left, right, dims, dp_index):
    count = math.prod(dims)
    at = [
        (dp_index // math.prod(dims[dim + 1 :])) % dims[dim] for dim in range(len(dims))
    ]
    samples, height = left.shape
    rows, columns = height // count, right.shape[1]
    split = left.reshape(samples, count // 2, 2, rows)
    for_other = lax.dynamic_index_in_dim(split, 1 - at[-1], 2, False).reshape(samples, -1)
    for_self = lax.dynamic_index_in_dim(split, at[-1], 2, False).reshape(samples, -1)
    sent = product_tn(for_other, right).astype(jnp.bfloat16)
    total = product_tn(for_self, right) + shifted(sent, dims, len(dims) - 1, 1).astype(jnp.float32)
    for dim in reversed(range(len(dims) - 1)):
        low = total.astype(jnp.bfloat16).reshape(-1, dims[dim], rows, columns)
        total = lax.dynamic_index_in_dim(low, at[dim], 1, False).astype(jnp.float32)
        for steps in range(1, dims[dim]):
            part = lax.dynamic_index_in_dim(low, (at[dim] + steps) % dims[dim], 1, False)
            total = total + shifted(part, dims, dim, steps).astype(jnp.float32)
    return total.reshape(rows, columns)


def spread(value, count):
    return lax.all_to_all(
        jnp.broadcast_to(value[None], (count, *value.shape)), "dp", 0, 0, tiled=True
    )


def summed(parts):
    return jnp.sum(lax.all_to_all(parts, "dp", 0, 0, tiled=True).astype(jnp.float32), axis=0)


def halves(value):
    high = value.astype(jnp.bfloat16)
    return high, (value - high.astype(jnp.float32)).astype(jnp.bfloat16)


def exact_product(left_side, right_side):
    high, low = halves(right_side)
    return product(left_side, high) + product(left_side, low)


def product_by_ones(left_side, right_side):
    high, low = halves(left_side)
    return product(high, right_side) + product(low, right_side)


def prefix_masks(length):
    places = lax.broadcasted_iota(jnp.int32, (1, length), 1)
    return [places < width for width in PREFIXES]


def similar_parts(documents, queries_t):
    docs_f32 = documents.astype(jnp.float32)
    squares = docs_f32 * docs_f32
    query_squares = queries_t * queries_t
    queries_low = queries_t.astype(jnp.bfloat16)
    parts = []
    for width, mask in zip(PREFIXES, prefix_masks(PROJ)):
        cut = jnp.where(mask, docs_f32, 0.0)
        doc_scale = lax.rsqrt(
            jnp.sum(jnp.where(mask, squares, 0.0), axis=1, keepdims=True) + unit_eps
        )
        query_scale = lax.rsqrt(
            jnp.sum(query_squares[:width], axis=0, keepdims=True) + unit_eps
        )
        cut = cut.astype(jnp.bfloat16)
        similar = product(cut, queries_low) * doc_scale * query_scale
        parts.append((cut, doc_scale, query_scale, similar))
    return parts


def members_of(ends_ref, micro_step, by_row):
    shape = (DOC_ROWS, 8) if by_row else (8, DOC_ROWS)
    rows = lax.broadcasted_iota(jnp.int32, shape, 0 if by_row else 1)
    docs = lax.broadcasted_iota(jnp.int32, shape, 1 if by_row else 0)
    inside = jnp.zeros(shape, jnp.float32)
    for number in range(DOCS_DEV):
        begin = ends_ref[micro_step, number - 1] if number else 0
        held = (docs == number) & (rows >= begin) & (rows < ends_ref[micro_step, number])
        inside = jnp.where(held, 1.0, inside)
    return inside.astype(jnp.bfloat16)


def query_of_token(tokens, by_token):
    shape = (tokens, 128) if by_token else (128, tokens)
    token = lax.broadcasted_iota(jnp.int32, shape, 0 if by_token else 1)
    query = lax.broadcasted_iota(jnp.int32, shape, 1 if by_token else 0)
    held = (token >= query * QLEN) & (token < query * QLEN + QLEN)
    return jnp.where(held, 1.0, 0.0).astype(jnp.bfloat16)


def score_kernel(ends_ref, queries_ref, docs_ref, out_ref):
    micro_step = pl.program_id(0)
    tokens = queries_ref.shape[0] * queries_ref.shape[2]
    queries_t = queries_ref[:, 0].astype(jnp.float32).reshape(tokens, PROJ).T
    members = members_of(ends_ref, micro_step, False)
    by_query = query_of_token(tokens, True)
    for number, (_, _, _, similar) in enumerate(similar_parts(docs_ref[0], queries_t)):
        masses = exact_product(members, jnp.exp(sharpness * similar))
        held = lax.broadcasted_iota(jnp.int32, masses.shape, 0) < DOCS_DEV
        logs = jnp.log(jnp.where(held, masses, 1.0))
        out_ref[0, 0, number] = product_by_ones(logs, by_query) / sharpness


def loss_kernel(
    ends_ref, queries_ref, docs_ref, table_ref, own_ref, times_ref, first_ref, own_times_ref,
    own_first_ref, loss_ref, grad_queries_ref, grad_docs_ref
):
    micro_step = pl.program_id(0)
    step = pl.program_id(1)
    devices, width = queries_ref.shape[0], queries_ref.shape[2]
    tokens = devices * width
    queries_t = queries_ref[:, 0].astype(jnp.float32).reshape(tokens, PROJ).T
    queries_low = queries_t.astype(jnp.bfloat16)
    members = members_of(ends_ref, micro_step, False)
    members_by_row = members_of(ends_ref, micro_step, True)
    spread_out = query_of_token(tokens, False)
    places = lax.broadcasted_iota(jnp.int32, (PROJ, 1), 0)
    grad_queries = jnp.zeros((PROJ, tokens), jnp.float32)
    grad_docs = jnp.zeros((DOC_ROWS, PROJ), jnp.float32)
    losses = jnp.zeros((1, 128), jnp.float32)
    docs_f32 = docs_ref[0].astype(jnp.float32)
    times, first = times_ref[0, 0], first_ref[0, 0]
    for number, (cut, doc_scale, query_scale, similar) in enumerate(
        similar_parts(docs_ref[0], queries_t)
    ):
        table = table_ref[0, 0, number]
        top = jnp.max(jnp.where(times > 0, table, -1e30), axis=0, keepdims=True)
        top = jnp.where(top > -1e29, top, 0.0)
        normal = top + jnp.log(
            jnp.maximum(
                jnp.sum(times * jnp.exp(jnp.minimum(table - top, 0.0)), axis=0, keepdims=True),
                1e-30,
            )
        )
        losses = losses + normal - jnp.sum(first * table, axis=0, keepdims=True)
        own = own_ref[0, 0, number]
        own_times = own_times_ref[0, 0]
        grad_score = (
            own_times * jnp.exp(jnp.where(own_times > 0, own - normal, 0.0)) - own_first_ref[0, 0]
        )
        weights = jnp.exp(sharpness * similar)
        masses = exact_product(members, weights)
        by_token = product_by_ones(grad_score, spread_out)
        held = lax.broadcasted_iota(jnp.int32, masses.shape, 0) < DOCS_DEV
        by_token = jnp.where(held, by_token / jnp.where(held, masses, 1.0), 0.0)
        grad_similar = weights * exact_product(members_by_row, by_token)
        along = grad_similar * similar
        pulled = (grad_similar * doc_scale * query_scale).astype(jnp.bfloat16)
        mask = lax.broadcasted_iota(jnp.int32, (1, PROJ), 1) < PREFIXES[number]
        grad_docs = (
            grad_docs
            + jnp.where(mask, product_nt(pulled, queries_low), 0.0)
            - cut.astype(jnp.float32)
            * (doc_scale * doc_scale * jnp.sum(along, axis=1, keepdims=True))
        )
        toward = product_tn(cut, pulled)
        back = queries_t * (
            query_scale * query_scale * jnp.sum(along, axis=0, keepdims=True)
        )
        grad_queries = grad_queries + toward - jnp.where(places < PREFIXES[number], back, 0.0)
    loss_ref[0, 0] = losses
    grad_queries_ref[:, 0] = grad_queries.T.reshape(devices, width, PROJ).astype(jnp.bfloat16)

    @pl.when(step == 0)
    def _():
        grad_docs_ref[0] = grad_docs

    @pl.when(step > 0)
    def _():
        grad_docs_ref[0] += grad_docs


def loss_parts(hidden, projection, ends, pair_rows, dp_index, count):
    group = math.gcd(count, 16)
    steps = count // group
    queries_in_step = group * QRY_DEV
    total_docs = count * DOCS_DEV
    doc_rows = -(-total_docs // 8) * 8
    doc_ids = jnp.arange(doc_rows, dtype=jnp.int32)
    chosen = (pair_rows[:, None, :, :] == doc_ids[None, :, None, None]).astype(jnp.float32)
    by_doc = [jnp.sum(chosen, axis=3), chosen[..., 0]]

    def steps_of(value):
        value = value.reshape(*value.shape[:-1], steps, queries_in_step)
        value = jnp.pad(value, [(0, 0)] * (value.ndim - 1) + [(0, 128 - queries_in_step)])
        return jnp.moveaxis(value, -2, 1)

    times, first = [steps_of(value) for value in by_doc]
    own_times, own_first = [
        jnp.pad(
            lax.dynamic_slice_in_dim(value, dp_index * DOCS_DEV, DOCS_DEV, 2),
            [(0, 0), (0, 0), (0, 8 - DOCS_DEV), (0, 0)],
        )
        for value in (times, first)
    ]
    embedded = product(hidden.reshape(MICRO * ROWS, -1), projection).astype(jnp.bfloat16)
    embedded = embedded.reshape(MICRO, ROWS, -1)
    documents = embedded[:, :DOC_ROWS]
    all_queries = spread(embedded[:, DOC_ROWS:], count)
    in_smem = pl.BlockSpec(memory_space=pltpu.SMEM)
    queries_spec = pl.BlockSpec((group, 1, QRY_DEV * QLEN, PROJ), lambda m, b: (b, m, 0, 0))
    docs_spec = pl.BlockSpec((1, DOC_ROWS, PROJ), lambda m, b: (m, 0, 0))
    own_spec = pl.BlockSpec((1, 1, 3, 8, 128), lambda m, b: (m, b, 0, 0, 0))
    params = pltpu.CompilerParams(vmem_limit_bytes=48 << 20)
    own_scores = pl.pallas_call(
        score_kernel,
        grid=(MICRO, steps),
        out_shape=jax.ShapeDtypeStruct((MICRO, steps, 3, 8, 128), jnp.float32),
        in_specs=[in_smem, queries_spec, docs_spec],
        out_specs=own_spec,
        compiler_params=params,
        name="scores",
    )(ends, all_queries, documents)
    tables = spread(own_scores[:, :, :, :DOCS_DEV], count)
    table = jnp.transpose(tables, (1, 2, 3, 0, 4, 5)).reshape(MICRO, steps, 3, total_docs, 128)
    table = jnp.pad(table, [(0, 0)] * 3 + [(0, doc_rows - total_docs), (0, 0)])
    counts_spec = pl.BlockSpec((1, 1, doc_rows, 128), lambda m, b: (m, b, 0, 0))
    own_counts_spec = pl.BlockSpec((1, 1, 8, 128), lambda m, b: (m, b, 0, 0))
    losses, grad_queries, grad_docs = pl.pallas_call(
        loss_kernel,
        grid=(MICRO, steps),
        out_shape=(
            jax.ShapeDtypeStruct((MICRO, steps, 1, 128), jnp.float32),
            jax.ShapeDtypeStruct((count, MICRO, QRY_DEV * QLEN, PROJ), jnp.bfloat16),
            jax.ShapeDtypeStruct((MICRO, DOC_ROWS, PROJ), jnp.float32),
        ),
        in_specs=[
            in_smem,
            queries_spec,
            docs_spec,
            pl.BlockSpec((1, 1, 3, doc_rows, 128), lambda m, b: (m, b, 0, 0, 0)),
            own_spec,
            counts_spec,
            counts_spec,
            own_counts_spec,
            own_counts_spec,
        ],
        out_specs=(
            pl.BlockSpec((1, 1, 1, 128), lambda m, b: (m, b, 0, 0)),
            queries_spec,
            docs_spec,
        ),
        compiler_params=params,
        name="losses",
    )(ends, all_queries, documents, table, own_scores, times, first, own_times, own_first)
    losses = losses[:, :, 0, :queries_in_step].reshape(MICRO, count * QRY_DEV)
    own_losses = lax.dynamic_slice_in_dim(losses, dp_index * QRY_DEV, QRY_DEV, 1)
    grad_own = summed(grad_queries)
    grad_embedded = jnp.concatenate([grad_docs, grad_own], axis=1).astype(jnp.bfloat16)
    grad_projection = product_tn(
        hidden.reshape(MICRO * ROWS, -1), grad_embedded.reshape(MICRO * ROWS, -1)
    )
    grad_hidden = product_nt(grad_embedded.reshape(MICRO * ROWS, -1), projection)
    return (grad_hidden.reshape(MICRO, ROWS, -1), own_losses.reshape(-1), grad_projection)


def shards(
    tokens,
    qkv_weight,
    qkv_bias,
    out_weight,
    out_bias,
    norm1_gain,
    norm1_bias,
    up_weight,
    up_bias,
    down_weight,
    down_bias,
    norm2_gain,
    norm2_bias,
    proj_weight,
    doc_lengths,
    pair_docs,
):
    section_index = lax.axis_index("section")
    dp_index = lax.axis_index("dp")
    count = lax.axis_size("dp")
    dims = grid_of(count)
    is_first = section_index == 0
    last_scale = section_index.astype(jnp.float32)
    model_width = tokens.shape[1]
    small = (
        qkv_bias,
        out_bias,
        norm1_gain,
        norm1_bias,
        up_bias,
        down_bias,
        norm2_gain,
        norm2_bias,
        proj_weight.reshape(1, -1),
    )
    widths = [value.shape[1] for value in small]
    together = spread(jnp.concatenate(small, axis=1)[0], count)
    cuts, start = [], 0
    for width in widths:
        cuts.append(together[:, start : start + width].reshape(-1))
        start += width
    qkv_b, out_b, gain_one, bias_one, up_b, down_b, gain_two, bias_two, projection = cuts
    projection = projection.reshape(model_width, -1)
    qkv_w, out_w, up_w, down_w = gather_rows(
        [qkv_weight[0], out_weight[0], up_weight[0], down_weight[0]], dims, dp_index
    )
    weights = (
        qkv_w,
        qkv_b,
        out_w,
        out_b,
        gain_one,
        bias_one,
        up_w,
        up_b,
        down_w,
        down_b,
        gain_two,
        bias_two,
    )
    layouts = [doc_layout(doc_lengths[micro_step]) for micro_step in range(MICRO)]
    blank_rows = jnp.zeros((ROWS, model_width), jnp.bfloat16)
    arrived = blank_rows
    states = []
    for tick_step in range(MICRO + 1):
        first_micro = min(tick_step, MICRO - 1)
        second_micro = max(tick_step - 1, 0)
        own_rows = (
            tokens[tick_step * ROWS : (tick_step + 1) * ROWS] if tick_step < MICRO else blank_rows
        )
        source = jnp.where(is_first, own_rows, arrived)
        segment = jnp.where(is_first, layouts[first_micro][0], layouts[second_micro][0])
        position = jnp.where(is_first, layouts[first_micro][1], layouts[second_micro][1])
        states.append(layer_forward(source, weights, segment, position))
        if tick_step < MICRO:
            arrived = from_behind(states[-1][-1], "section", 1)
    results = [state[-1] for state in states]
    activations = jnp.concatenate(
        [
            jnp.where(is_first, results[micro_step], results[micro_step + 1])
            for micro_step in range(MICRO)
        ],
        axis=0,
    )[None]
    loss_grads, own_losses, proj_total = loss_parts(
        jnp.stack(results[1:]),
        projection,
        jnp.cumsum(doc_lengths, axis=1),
        jnp.moveaxis(pair_docs.reshape(count, MICRO, QRY_DEV, CANDS), 1, 0).reshape(
            MICRO, count * QRY_DEV, CANDS
        ),
        dp_index,
        count,
    )
    query_losses = jnp.where(is_first, from_behind(own_losses, "section", -1), own_losses)
    proj_total = proj_total * last_scale
    back_grad = jnp.zeros((ROWS, model_width), jnp.float32)
    input_grads, pairs, vectors = [], [], None
    for tick_step in range(MICRO + 1):
        second_micro = MICRO - 1 - tick_step
        upstream = jnp.where(
            is_first,
            back_grad,
            loss_grads[second_micro] if second_micro >= 0 else jnp.zeros_like(back_grad),
        )
        tick_pairs, tick_vectors, grad_source = layer_backward(
            states[MICRO - tick_step], upstream, weights
        )
        pairs.append(tick_pairs)
        vectors = (
            tick_vectors
            if vectors is None
            else tuple(total + extra for total, extra in zip(vectors, tick_vectors))
        )
        input_grads.append(grad_source)
        if second_micro >= 0:
            back_grad = from_behind(grad_source.astype(jnp.bfloat16), "section", -1).astype(
                jnp.float32
            )
    weight_grads = []
    for number in range(4):
        left, right = (
            jnp.concatenate(
                [pairs[1][number][side]]
                + [jnp.where(is_first, pairs[2][number][side], pairs[0][number][side])]
            )
            for side in range(2)
        )
        weight_grads.append(scatter_rows(left, right, dims, dp_index)[None])
    grad_down, grad_up, grad_out, grad_qkv = weight_grads
    own = summed(jnp.concatenate([value.reshape(count, -1) for value in vectors], axis=1))
    small_grads, start = [], 0
    for width in widths[:-1]:
        small_grads.append(own[None, start : start + width])
        start += width
    proj_parts = proj_total.reshape(2, count, -1, proj_total.shape[1])
    proj_own = summed(jnp.swapaxes(proj_parts, 0, 1))
    proj_grad = jnp.where(is_first, from_behind(proj_own[0], "section", -1), proj_own[1])
    grad_inputs = jnp.concatenate(
        [
            jnp.where(
                is_first, input_grads[MICRO - micro_step], input_grads[MICRO - 1 - micro_step]
            )
            for micro_step in range(MICRO)
        ],
        axis=0,
    )[None]
    return (
        query_losses,
        activations,
        grad_inputs,
        grad_qkv,
        small_grads[0],
        grad_out,
        small_grads[1],
        small_grads[2],
        small_grads[3],
        grad_up,
        small_grads[4],
        grad_down,
        small_grads[5],
        small_grads[6],
        small_grads[7],
        proj_grad,
    )


def solution(mesh):
    in_specs = (
        P("dp", None),
        P("section", "dp", None),
        P("section", "dp"),
        P("section", "dp", None),
        P("section", "dp"),
        P("section", "dp"),
        P("section", "dp"),
        P("section", "dp", None),
        P("section", "dp"),
        P("section", "dp", None),
        P("section", "dp"),
        P("section", "dp"),
        P("section", "dp"),
        P("dp", None),
        P("dp", None),
        P(),
    )
    out_specs = (
        P("dp"),
        P("section", "dp", None),
        P("section", "dp", None),
        P("section", "dp", None),
        P("section", "dp"),
        P("section", "dp", None),
        P("section", "dp"),
        P("section", "dp"),
        P("section", "dp"),
        P("section", "dp", None),
        P("section", "dp"),
        P("section", "dp", None),
        P("section", "dp"),
        P("section", "dp"),
        P("section", "dp"),
        P(("section", "dp"), None),
    )
    return jax.shard_map(shards, mesh=mesh, in_specs=in_specs, out_specs=out_specs, check_vma=False)
```

time: 2080 us -> 923 us (0.44)
  waiting for transfers between devices: 1210 us -> 347 us
  matrix products: 431 us -> 211 us
  blocking collectives: 179 us -> 0 us
  starting transfers between devices: 12.1 us -> 129 us
  Pallas kernels: 0 us -> 29.1 us
    reduce_scatter x7 -> x0, waiting for transfers between devices: 754 us -> none  [the longest x1 182 us: shards(): lax.psum_scatter(layer_totals[6][None], 'dp', scatter_dimension=1, tiled=...]
    ppermute x0 -> x44, waiting for transfers between devices: none -> 301 us  [shifted(): return lax.ppermute(value, 'dp', pairs)]
    unnamed x27 -> x0, waiting for transfers between devices: 297 us -> none
    all_gather x4 -> x0, waiting for transfers between devices: 148 us -> none  [the longest x1 75.2 us: shards(): lax.all_gather(down_weight, 'dp', axis=1, tiled=True)]
    all_gather x6 -> x0, blocking collectives: 115 us -> none  [the longest x2 40.9 us: loss_part(): all_scores = lax.all_gather(local_scores, 'dp', axis=2, tiled=True)]
    ppermute x0 -> x44, starting transfers between devices: none -> 87.1 us  [shifted(): return lax.ppermute(value, 'dp', pairs)]
    dot_general x36 -> x0, matrix products: 72.9 us -> none  [the longest x18 41.2 us: score_block(): jnp.einsum('qtp,rp->qtr', query_unit, doc_unit, precision=lax.Precision.H...]
    dot_general x14 -> x9, matrix products: 111 us -> 38.4 us  [product_tn(): lax.dot_general(left_side, right_side, (((0,), (0,)), ((), ())), preferre...]
  transfers between devices with their start and end apart: 25 -> 56, of which waited for: 17 -> 20; matrix products, arithmetic and copies ran while one was open for 17% -> 21% of each run, Pallas kernels for 0% -> 1%
where the time goes in v1:
time: 923 us; the launch traced here: 916 us
  waiting for transfers between devices  347 us (38%)
  matrix products  211 us (23%)
  starting transfers between devices  129 us (14%)
  local copies, waits for them, and re-layouts  110 us (12%)
  other arithmetic  86.6 us (9%)
  Pallas kernels  29.1 us (3%)
    ppermute x44, waiting for transfers between devices, shifted(): return lax.ppermute(value, 'dp', pairs)  301 us
    ppermute x44, starting transfers between devices, shifted(): return lax.ppermute(value, 'dp', pairs)  87.1 us
    dot_general x13, matrix products, product(): return jnp.dot(left_side, right_side, preferred_element_type=jnp.float32)  68.7 us
    dot_general x13, matrix products, product_nt(): lax.dot_general(left_side, right_side, (((1,), (1,)), ((), ())), preferre...  63.8 us
    unnamed x370, local copies, waits for them, and re-layouts  43.1 us
    dot_general x9, matrix products, product_tn(): lax.dot_general(left_side, right_side, (((0,), (0,)), ((), ())), preferre...  38.4 us
    ppermute x6, waiting for transfers between devices, from_behind(): lax.ppermute(value, axis, [(source, source + steps) for source in range(f...  31.6 us
  transfers between devices with their start and end apart: 56, of which 20 were waited for; matrix products, arithmetic and copies ran while one was open for 21% of the time, Pallas kernels for 1%

profile of v1, /device:TPU:0, one launch (start us, length us, event | category | flops | bytes accessed | tf_op | source)
XLA Modules:
  0.0 915.7 jit_solution(4298618812481589140)
XLA Ops:
  0.7 5.1 collective-permute-start.2
  16.9 4.1 all-to-all-start
  21.1 14.3 %collective-permute-done.8 = bf16[64,1024]{1,0:T(8,128)(2,1)S(1)} collective-permute-done((bf16[64,1024]{1,0:T(8,128)(2,1)}, bf16[64,1024]{1,0:T(8,128)(2,1)S(1)}, u32[]{:S(2)}, u32[]{:S(2)}) %collective-permute-start.8) | collective-permute-done | bytes 131104 | tf_op jit(solution)/shard_map/ppermute | solution.py:290
  35.4 17.5 %collective-permute-start.6 = (bf16[64,1024]{1,0:T(8,128)(2,1)}, bf16[64,1024]{1,0:T(8,128)(2,1)S(1)}, u32[]{:S(2)}, u32[]{:S(2)}) collective-permute-start(bf16[64,1024]{1,0:T(8,128)(2,1)} %bitcast.435), channel_id=1, source_target_pairs={{0,4},{1,5},{2,6},{3,7},{4,8},{5,9},{6,10},{7,11},{8,12},{9,13},{1... | collective-permute-start | bytes 393224 | tf_op jit(solution)/shard_map/ppermute | solution.py:290
  56.8 3.2 collective-permute-start.20
  67.8 5.2 collective-permute-done.20
  73.0 22.8 %collective-permute-start.12 = (bf16[64,4096]{1,0:T(8,128)(2,1)S(1)}, bf16[64,4096]{1,0:T(8,128)(2,1)}, u32[]{:S(2)}, u32[]{:S(2)}) collective-permute-start(bf16[64,4096]{1,0:T(8,128)(2,1)S(1)} %bitcast.422), channel_id=1, source_target_pairs={{0,4},{1,5},{2,6},{3,7},{4,8},{5,9},{6,10},{7,11},{8,12},{9,13},{1... | collective-permute-start | bytes 1572872 | tf_op jit(solution)/shard_map/ppermute | solution.py:290
  95.8 34.5 %collective-permute-done.19 = bf16[256,1024]{1,0:T(8,128)(2,1)S(1)} collective-permute-done((bf16[256,1024]{1,0:T(8,128)(2,1)}, bf16[256,1024]{1,0:T(8,128)(2,1)S(1)}, u32[]{:S(2)}, u32[]{:S(2)}) %collective-permute-start.19) | collective-permute-done | bytes 524320 | tf_op jit(solution)/shard_map/ppermute | solution.py:290
  135.4 16.0 %collective-permute-done.13 = bf16[64,4096]{1,0:T(8,128)(2,1)} collective-permute-done((bf16[64,4096]{1,0:T(8,128)(2,1)S(1)}, bf16[64,4096]{1,0:T(8,128)(2,1)}, u32[]{:S(2)}, u32[]{:S(2)}) %collective-permute-start.13) | collective-permute-done | bytes 524320 | tf_op jit(solution)/shard_map/ppermute | solution.py:290
  157.0 10.9 %collective-permute-done.3.refs_1_ = bf16[4,64,3072]{2,1,0:T(8,128)(2,1)} collective-permute-done((bf16[4,64,3072]{2,1,0:T(8,128)(2,1)}, bf16[4,64,3072]{2,1,0:T(8,128)(2,1)}, u32[]{:S(2)}, u32[]{:S(2)}) %collective-permute-start.3) | collective-permute-done | bytes 1572896 | tf_op jit(solution)/shard_map/ppermute | solution.py:290
  168.1 74.5 %collective-permute-done.9.refs_1_ = bf16[4,64,1024]{2,1,0:T(8,128)(2,1)S(1)} collective-permute-done((bf16[4,64,1024]{2,1,0:T(8,128)(2,1)S(1)}, bf16[4,64,1024]{2,1,0:T(8,128)(2,1)S(1)}, u32[]{:S(2)}, u32[]{:S(2)}) %collective-permute-start.9) | collective-permute-done | bytes 524320 | tf_op jit(solution)/shard_map/ppermute | solution.py:290
  251.5 3.6 place.5
  256.2 3.5 place.4
  271.6 4.7 fusion.162
  280.9 4.1 place.7
  285.0 6.5 place.6
  291.5 16.6 %multiply_convert_fusion.5 = (bf16[256,4096]{1,0:T(8,128)(2,1)S(1)}, f32[256,4096]{1,0:T(8,128)}, f32[256,4096]{1,0:T(8,128)}) fusion(f32[4096]{0:T(1024)S(1)} %bitcast.440, bf16[1024,4096]{1,0:T(8,128)(2,1)S(1)} %bitcast.310, f32[256,1024]{1,0:T(8,128)S(1)} %get-tuple-element.189, f32[1024]{0:T(1024)S(1)} %reshape.1127, f32[1024]{0:T(1024)S(1)} %reshape.1126, ...), kind=kOutput, calls=%fused_computation.65 | convolution fusion | flops 2218000384 | bytes 19949568 | tf_op jit(solution)/shard_map/dot_general | solution.py:37
  312.1 4.2 collective-permute-start.24
  320.4 6.8 collective-permute-done.24
  328.4 4.8 convolution_add_fusion.4
  345.4 4.6 fusion.165
  355.2 16.7 %multiply_convert_fusion.4 = (bf16[256,4096]{1,0:T(8,128)(2,1)S(1)}, f32[256,4096]{1,0:T(8,128)}, f32[256,4096]{1,0:T(8,128)}) fusion(f32[4096]{0:T(1024)S(1)} %bitcast.441, bf16[256,1024]{1,0:T(8,128)(2,1)S(1)} %add_convert_fusion.10, bf16[1024,4096]{1,0:T(8,128)(2,1)} %bitcast.311), kind=kOutput, calls=%fused_computation.50 | convolution fusion | flops 2216689664 | bytes 19415040 | tf_op jit(solution)/shard_map/dot_general | solution.py:37
  376.2 4.8 collective-permute-start.25
  382.9 8.7 collective-permute-done.25
  391.6 4.8 convolution_add_fusion.3
  405.5 5.4 fusion.168
  410.9 3.7 broadcast_select_fusion.3
  417.5 13.6 %broadcast_select_fusion = (bf16[256,4096]{1,0:T(8,128)(2,1)}, bf16[256,4096]{1,0:T(8,128)(2,1)S(1)}, f32[256,4096]{1,0:T(8,128)}, f32[256,4096]{1,0:T(8,128)}) fusion(bf16[256,4096]{1,0:T(8,128)(2,1)S(1)} %copy-done.162, pred[]{:T(512)S(6)} %eq.135, f32[4096]{0:T(1024)S(1)} %bitcast.442, bf16[256,1024]{1,0:T(8,128)(2,1)S(1)} %get-tuple-element.52, ...), kind=kOutput, calls=%fused_computation.112 | convolution fusion | flops 2217738240 | bytes 23609344 | tf_op jit(solution)/shard_map/dot_general | solution.py:37
  437.0 3.6 all-to-all-start.1
  447.3 4.7 pad_maximum_fusion.1
  455.0 3.9 scores.1.own_ref
  459.6 4.0 all-to-all-start.2
  466.1 5.7 all-to-all-done.2
  471.9 7.6 losses.1
  479.5 4.7 all-to-all-start.3
  488.8 7.8 reshape.1119
  501.1 9.9 %constant_dynamic-slice_fusion.4 = (bf16[512,8,1,256]{3,2,1,0:T(2,128)(2,1)}, bf16[512,8,1,256]{3,2,1,0:T(2,128)(2,1)}) fusion(bf16[512,8,2,256]{3,2,1,0:T(2,128)(2,1)S(1)} %copy-done.7, s32[]{:T(128)S(6)} %select_n.492, s32[]{:T(128)S(6)} %select_n.495), kind=kLoop, calls=%fused_computation.343 | loop fusion | bytes 8388616 | tf_op jit(solution)/shard_map/jit(dynamic_index_in_dim)/dynamic_slice | solution.py:370
  517.0 12.7 %convert_reduce_fusion.2 = (f32[4096]{0:T(1024)S(1)}, bf16[256,4096]{1,0:T(8,128)(2,1)}) fusion(f32[256,4096]{1,0:T(8,128)} %get-tuple-element.48, f32[256,4096]{1,0:T(8,128)} %get-tuple-element.204, bf16[256,1024]{1,0:T(8,128)(2,1)S(1)} %get-tuple-element.58, bf16[4096,1024]{1,0:T(8,128)(2,1)} %bitcast.301), kind=kOutput, calls=%fused_computation.25 | convolution fusion | flops 2164256768 | bytes 19415040 | tf_op jit(solution)/shard_map/dot_general | solution.py:47
  529.7 4.4 multiply_reduce_fusion.8
  539.1 3.3 convolution_convert_fusion.8
  553.6 10.5 %copy.210 = bf16[512,8,1,256]{0,3,1,2:T(8,128)(2,1)} copy(bf16[512,8,1,256]{3,2,1,0:T(2,128)(2,1)} %get-tuple-element.86) | data formatting | bytes 4194304
  564.1 10.5 %copy.209 = bf16[512,8,1,256]{0,3,1,2:T(8,128)(2,1)} copy(bf16[512,8,1,256]{3,2,1,0:T(2,128)(2,1)} %get-tuple-element.85) | data formatting | bytes 4194304
  576.2 4.9 collective-permute-done.26
  584.1 6.3 all-to-all-start.5
  596.6 11.7 %convert_reduce_fusion.1 = (f32[4096]{0:T(1024)S(1)}, bf16[256,4096]{1,0:T(8,128)(2,1)S(1)}) fusion(f32[256,4096]{1,0:T(8,128)} %get-tuple-element.82, f32[256,4096]{1,0:T(8,128)} %get-tuple-element.197, bf16[256,1024]{1,0:T(8,128)(2,1)S(1)} %get-tuple-element.56, bf16[4096,1024]{1,0:T(8,128)(2,1)} %bitcast.302), kind=kOutput, calls=%fused_computation.24 | convolution fusion | flops 2164256768 | bytes 19415040 | tf_op jit(solution)/shard_map/dot_general | solution.py:47
  624.0 3.4 fusion.161
  633.0 11.1 %collective-permute-done.49 = f32[32,128]{1,0:T(8,128)S(1)} collective-permute-done((f32[32,128]{1,0:T(8,128)S(1)}, f32[32,128]{1,0:T(8,128)S(1)}, u32[]{:S(2)}, u32[]{:S(2)}) %collective-permute-start.49) | collective-permute-done | bytes 16416 | tf_op jit(solution)/shard_map/ppermute | solution.py:33
  649.9 13.7 %broadcast_select_fusion.1 = (bf16[256,4096]{1,0:T(8,128)(2,1)}, bf16[256,4096]{1,0:T(8,128)(2,1)}) fusion(bf16[256,4096]{1,0:T(8,128)(2,1)} %get-tuple-element.62, pred[]{:T(512)S(6)} %eq.135, f32[256,4096]{1,0:T(8,128)} %get-tuple-element.84, f32[256,4096]{1,0:T(8,128)} %get-tuple-element.190, bf16[256,1024]{1,0:T(8,128)(2,1)S(1)} %get-tuple-element.45, ...), kind=kOutput, calls=%fused_computation.113 | convolution fusion | flops 2163212288 | bytes 23592960 | tf_op jit(solution)/shard_map/dot_general | solution.py:47
  663.7 5.0 multiply_reduce_fusion.6
  673.8 3.1 convolution_convert_fusion.4
  683.3 10.5 %convolution_convert_fusion.1 = bf16[512,3072]{1,0:T(8,128)(2,1)} fusion(bf16[512,512]{0,1:T(8,128)(2,1)S(1)} %bitcast.411, bf16[256,3072]{0,1:T(8,128)(2,1)S(1)} %broadcast_select_fusion.2, bf16[256,1024]{0,1:T(8,128)(2,1)S(1)} %bitcast.393, bf16[256,1024]{0,1:T(8,128)(2,1)S(1)} %bitcast.374, bf16[256,1024]{0,1:T(8,128)(2,1)S(1)} %bitcast.378), kind=kOutput, calls=%fused_computation.13 | convolution fusion | flops 1624768512 | bytes 6815744 | tf_op jit(solution)/shard_map/dot_general | solution.py:41
  696.2 4.4 convolution_convert_fusion
  700.6 4.4 convolution_convert_fusion.2
  715.0 4.7 all-to-all-start.4
  722.4 4.8 all-to-all-done.4
  730.3 3.5 collective-permute-start.38
  734.9 4.7 add_convert_fusion.2
  741.3 4.5 add_convert_fusion.1
  747.6 4.6 add_convert_fusion
  753.7 23.4 %collective-permute-done.30 = bf16[4,64,3072]{2,1,0:T(8,128)(2,1)S(1)} collective-permute-done((bf16[4,64,3072]{2,1,0:T(8,128)(2,1)S(1)}, bf16[4,64,3072]{2,1,0:T(8,128)(2,1)S(1)}, u32[]{:S(2)}, u32[]{:S(2)}) %collective-permute-start.30) | collective-permute-done | bytes 1572896 | tf_op jit(solution)/shard_map/ppermute | solution.py:290
  781.7 40.3 %collective-permute-done.40 = bf16[4,64,4096]{2,1,0:T(8,128)(2,1)S(1)} collective-permute-done((bf16[4,64,4096]{2,1,0:T(8,128)(2,1)S(1)}, bf16[4,64,4096]{2,1,0:T(8,128)(2,1)S(1)}, u32[]{:S(2)}, u32[]{:S(2)}) %collective-permute-start.40) | collective-permute-done | bytes 2097184 | tf_op jit(solution)/shard_map/ppermute | solution.py:290
  828.0 37.3 %collective-permute-done.45 = bf16[4,256,1024]{2,1,0:T(8,128)(2,1)S(1)} collective-permute-done((bf16[4,256,1024]{2,1,0:T(8,128)(2,1)S(1)}, bf16[4,256,1024]{2,1,0:T(8,128)(2,1)S(1)}, u32[]{:S(2)}, u32[]{:S(2)}) %collective-permute-start.45) | collective-permute-done | bytes 2097184 | tf_op jit(solution)/shard_map/ppermute | solution.py:290
  871.8 10.0 %collective-permute-done.48 = bf16[1,256,1024]{2,1,0:T(8,128)(2,1)S(1)} collective-permute-done((bf16[1,256,1024]{2,1,0:T(8,128)(2,1)S(1)}, bf16[1,256,1024]{2,1,0:T(8,128)(2,1)S(1)}, u32[]{:S(2)}, u32[]{:S(2)}) %collective-permute-start.48) | collective-permute-done | bytes 524320 | tf_op jit(solution)/shard_map/ppermute | solution.py:290
  881.9 32.3 %collective-permute-done.47 = bf16[1,256,1024]{2,1,0:T(8,128)(2,1)S(1)} collective-permute-done((bf16[1,256,1024]{2,1,0:T(8,128)(2,1)S(1)}, bf16[1,256,1024]{2,1,0:T(8,128)(2,1)S(1)}, u32[]{:S(2)}, u32[]{:S(2)}) %collective-permute-start.47) | collective-permute-done | bytes 524320 | tf_op jit(solution)/shard_map/ppermute | solution.py:290
  (698 shorter events, 245.1 us)
Async XLA Ops:
  0.6 62.6 %copy-start.108 = (bf16[1,64,3072]{2,1,0:T(8,128)(2,1)S(1)}, bf16[1,64,3072]{2,1,0:T(8,128)(2,1)}, u32[]{:S(2)}) copy-start(bf16[1,64,3072]{2,1,0:T(8,128)(2,1)} %param.17) | copy-start | bytes 1179652
  0.7 131.6 %copy-start.106 = (bf16[1,256,1024]{2,1,0:T(8,128)(2,1)S(1)}, bf16[1,256,1024]{2,1,0:T(8,128)(2,1)}, u32[]{:S(2)}) copy-start(bf16[1,256,1024]{2,1,0:T(8,128)(2,1)} %param.25) | copy-start | bytes 1572868
  0.7 65.3 %copy-start.107 = (bf16[1,64,4096]{2,1,0:T(8,128)(2,1)S(1)}, bf16[1,64,4096]{2,1,0:T(8,128)(2,1)}, u32[]{:S(2)}) copy-start(bf16[1,64,4096]{2,1,0:T(8,128)(2,1)} %param.23) | copy-start | bytes 1572868
  0.7 131.2 %copy-start.140 = (s32[2,3]{1,0:T(2,128)S(1)}, s32[2,3]{1,0:T(2,128)}, u32[]{:S(2)}) copy-start(s32[2,3]{1,0:T(2,128)} %param.30) | copy-start | bytes 76
  0.7 60.6 %collective-permute-start.2 = (bf16[64,3072]{1,0:T(8,128)(2,1)}, bf16[64,3072]{1,0:T(8,128)(2,1)}, u32[]{:S(2)}, u32[]{:S(2)}) collective-permute-start(bf16[64,3072]{1,0:T(8,128)(2,1)} %bitcast.427), channel_id=1, source_target_pairs={{0,12},{1,13},{2,14},{3,15},{4,0},{5,1},{6,2},{7,3},{8,4},{9,5},{1... | collective-permute-start | bytes 1179656 | tf_op jit(solution)/shard_map/ppermute | solution.py:290
  5.8 57.5 %collective-permute-start.1 = (bf16[64,3072]{1,0:T(8,128)(2,1)}, bf16[64,3072]{1,0:T(8,128)(2,1)}, u32[]{:S(2)}, u32[]{:S(2)}) collective-permute-start(bf16[64,3072]{1,0:T(8,128)(2,1)} %bitcast.428), channel_id=1, source_target_pairs={{0,8},{1,9},{2,10},{3,11},{4,12},{5,13},{6,14},{7,15},{8,0},{9,1},... | collective-permute-start | bytes 1179656 | tf_op jit(solution)/shard_map/ppermute | solution.py:290
  5.8 57.5 %collective-permute-start = (bf16[64,3072]{1,0:T(8,128)(2,1)}, bf16[64,3072]{1,0:T(8,128)(2,1)}, u32[]{:S(2)}, u32[]{:S(2)}) collective-permute-start(bf16[64,3072]{1,0:T(8,128)(2,1)} %bitcast.429), channel_id=1, source_target_pairs={{0,4},{1,5},{2,6},{3,7},{4,8},{5,9},{6,10},{7,11},{8,12},{9,13},{1... | collective-permute-start | bytes 1179656 | tf_op jit(solution)/shard_map/ppermute | solution.py:290
  6.8 28.6 %collective-permute-start.8 = (bf16[64,1024]{1,0:T(8,128)(2,1)}, bf16[64,1024]{1,0:T(8,128)(2,1)S(1)}, u32[]{:S(2)}, u32[]{:S(2)}) collective-permute-start(bf16[64,1024]{1,0:T(8,128)(2,1)} %bitcast.433), channel_id=1, source_target_pairs={{0,12},{1,13},{2,14},{3,15},{4,0},{5,1},{6,2},{7,3},{8,4},{9,5},{1... | collective-permute-start | bytes 393224 | tf_op jit(solution)/shard_map/ppermute | solution.py:290
  9.6 45.5 %collective-permute-start.7 = (bf16[64,1024]{1,0:T(8,128)(2,1)}, bf16[64,1024]{1,0:T(8,128)(2,1)S(1)}, u32[]{:S(2)}, u32[]{:S(2)}) collective-permute-start(bf16[64,1024]{1,0:T(8,128)(2,1)} %bitcast.434), channel_id=1, source_target_pairs={{0,8},{1,9},{2,10},{3,11},{4,12},{5,13},{6,14},{7,15},{8,0},{9,1},... | collective-permute-start | bytes 393224 | tf_op jit(solution)/shard_map/ppermute | solution.py:290
  16.9 227.5 %all-to-all-start = ((bf16[16,2,4512]{2,1,0:T(2,128)(2,1)}), bf16[16,2,4512]{2,1,0:T(2,128)(2,1)S(1)}, u32[]{:S(2)}, u32[]{:S(2)}) async-start(bf16[16,2,4512]{2,1,0:T(2,128)(2,1)} %reshape.1148), calls=%async_computation | async-start | bytes 589824 | tf_op jit(solution)/shard_map/all_to_all | solution.py:383
  35.4 20.4 %collective-permute-start.6 = (bf16[64,1024]{1,0:T(8,128)(2,1)}, bf16[64,1024]{1,0:T(8,128)(2,1)S(1)}, u32[]{:S(2)}, u32[]{:S(2)}) collective-permute-start(bf16[64,1024]{1,0:T(8,128)(2,1)} %bitcast.435), channel_id=1, source_target_pairs={{0,4},{1,5},{2,6},{3,7},{4,8},{5,9},{6,10},{7,11},{8,12},{9,13},{1... | collective-permute-start | bytes 393224 | tf_op jit(solution)/shard_map/ppermute | solution.py:290
  56.8 16.2 %collective-permute-start.20 = (bf16[256,1024]{1,0:T(8,128)(2,1)}, bf16[256,1024]{1,0:T(8,128)(2,1)S(1)}, u32[]{:S(2)}, u32[]{:S(2)}) collective-permute-start(bf16[256,1024]{1,0:T(8,128)(2,1)} %bitcast.417), channel_id=1, source_target_pairs={{0,12},{1,13},{2,14},{3,15},{4,0},{5,1},{6,2},{7,3},{8,4},{9,5},{1... | collective-permute-start | bytes 1572872 | tf_op jit(solution)/shard_map/ppermute | solution.py:290
  60.0 70.3 %collective-permute-start.19 = (bf16[256,1024]{1,0:T(8,128)(2,1)}, bf16[256,1024]{1,0:T(8,128)(2,1)S(1)}, u32[]{:S(2)}, u32[]{:S(2)}) collective-permute-start(bf16[256,1024]{1,0:T(8,128)(2,1)} %bitcast.418), channel_id=1, source_target_pairs={{0,8},{1,9},{2,10},{3,11},{4,12},{5,13},{6,14},{7,15},{8,0},{9,1},... | collective-permute-start | bytes 1572872 | tf_op jit(solution)/shard_map/ppermute | solution.py:290
  61.3 71.0 %collective-permute-start.18 = (bf16[256,1024]{1,0:T(8,128)(2,1)}, bf16[256,1024]{1,0:T(8,128)(2,1)}, u32[]{:S(2)}, u32[]{:S(2)}) collective-permute-start(bf16[256,1024]{1,0:T(8,128)(2,1)} %bitcast.419), channel_id=1, source_target_pairs={{0,4},{1,5},{2,6},{3,7},{4,8},{5,9},{6,10},{7,11},{8,12},{9,13},{1... | collective-permute-start | bytes 1572872 | tf_op jit(solution)/shard_map/ppermute | solution.py:290
  66.0 69.4 %collective-permute-start.14 = (bf16[64,4096]{1,0:T(8,128)(2,1)S(1)}, bf16[64,4096]{1,0:T(8,128)(2,1)}, u32[]{:S(2)}, u32[]{:S(2)}) collective-permute-start(bf16[64,4096]{1,0:T(8,128)(2,1)S(1)} %bitcast.420), channel_id=1, source_target_pairs={{0,12},{1,13},{2,14},{3,15},{4,0},{5,1},{6,2},{7,3},{8,4},{9,5},{1... | collective-permute-start | bytes 1572872 | tf_op jit(solution)/shard_map/ppermute | solution.py:290
  67.8 83.5 %collective-permute-start.13 = (bf16[64,4096]{1,0:T(8,128)(2,1)S(1)}, bf16[64,4096]{1,0:T(8,128)(2,1)}, u32[]{:S(2)}, u32[]{:S(2)}) collective-permute-start(bf16[64,4096]{1,0:T(8,128)(2,1)S(1)} %bitcast.421), channel_id=1, source_target_pairs={{0,8},{1,9},{2,10},{3,11},{4,12},{5,13},{6,14},{7,15},{8,0},{9,1},... | collective-permute-start | bytes 1572872 | tf_op jit(solution)/shard_map/ppermute | solution.py:290
  73.0 78.4 %collective-permute-start.12 = (bf16[64,4096]{1,0:T(8,128)(2,1)S(1)}, bf16[64,4096]{1,0:T(8,128)(2,1)}, u32[]{:S(2)}, u32[]{:S(2)}) collective-permute-start(bf16[64,4096]{1,0:T(8,128)(2,1)S(1)} %bitcast.422), channel_id=1, source_target_pairs={{0,4},{1,5},{2,6},{3,7},{4,8},{5,9},{6,10},{7,11},{8,12},{9,13},{1... | collective-permute-start | bytes 1572872 | tf_op jit(solution)/shard_map/ppermute | solution.py:290
  130.3 37.6 %collective-permute-start.3 = (bf16[4,64,3072]{2,1,0:T(8,128)(2,1)}, bf16[4,64,3072]{2,1,0:T(8,128)(2,1)}, u32[]{:S(2)}, u32[]{:S(2)}) collective-permute-start(bf16[4,64,3072]{2,1,0:T(8,128)(2,1)} %pad_maximum_fusion.9.refs_0_), channel_id=1, source_target_pairs={{0,2},{1,3},{2,0},{3,1},{4,6},{5,7},{6,4},{7,5},{8,10},{9,11},{10,... | collective-permute-start | bytes 4718600 | tf_op jit(solution)/shard_map/ppermute | solution.py:290
  134.9 120.8 %collective-permute-start.21 = (bf16[4,256,1024]{2,1,0:T(8,128)(2,1)}, bf16[4,256,1024]{2,1,0:T(8,128)(2,1)}, u32[]{:S(2)}, u32[]{:S(2)}) collective-permute-start(bf16[4,256,1024]{2,1,0:T(8,128)(2,1)} %pad_maximum_fusion.8.refs_0_), channel_id=1, source_target_pairs={{0,2},{1,3},{2,0},{3,1},{4,6},{5,7},{6,4},{7,5},{8,10},{9,11},{10,... | collective-permute-start | bytes 6291464 | tf_op jit(solution)/shard_map/ppermute | solution.py:290
  154.3 101.5 %collective-permute-start.15 = (bf16[4,64,4096]{2,1,0:T(8,128)(2,1)}, bf16[4,64,4096]{2,1,0:T(8,128)(2,1)}, u32[]{:S(2)}, u32[]{:S(2)}) collective-permute-start(bf16[4,64,4096]{2,1,0:T(8,128)(2,1)} %pad_maximum_fusion.7.refs_0_), channel_id=1, source_target_pairs={{0,2},{1,3},{2,0},{3,1},{4,6},{5,7},{6,4},{7,5},{8,10},{9,11},{10,... | collective-permute-start | bytes 6291464 | tf_op jit(solution)/shard_map/ppermute | solution.py:290
  156.5 86.1 %collective-permute-start.9 = (bf16[4,64,1024]{2,1,0:T(8,128)(2,1)S(1)}, bf16[4,64,1024]{2,1,0:T(8,128)(2,1)S(1)}, u32[]{:S(2)}, u32[]{:S(2)}) collective-permute-start(bf16[4,64,1024]{2,1,0:T(8,128)(2,1)S(1)} %pad_maximum_fusion.33.refs_0_), channel_id=1, source_target_pairs={{0,2},{1,3},{2,0},{3,1},{4,6},{5,7},{6,4},{7,5},{8,10},{9,11},{10,... | collective-permute-start | bytes 1572872 | tf_op jit(solution)/shard_map/ppermute | solution.py:290
  157.0 98.1 %collective-permute-start.4 = (bf16[4,64,3072]{2,1,0:T(8,128)(2,1)}, bf16[4,64,3072]{2,1,0:T(8,128)(2,1)}, u32[]{:S(2)}, u32[]{:S(2)}) collective-permute-start(bf16[4,64,3072]{2,1,0:T(8,128)(2,1)} %pad_maximum_fusion.9.refs_0_), channel_id=1, source_target_pairs={{0,1},{1,0},{2,3},{3,2},{4,5},{5,4},{6,7},{7,6},{8,9},{9,8},{10,11... | collective-permute-start | bytes 4718600 | tf_op jit(solution)/shard_map/ppermute | solution.py:290
  168.0 88.3 %collective-permute-start.5 = (bf16[4,64,3072]{2,1,0:T(8,128)(2,1)}, bf16[4,64,3072]{2,1,0:T(8,128)(2,1)}, u32[]{:S(2)}, u32[]{:S(2)}) collective-permute-start(bf16[4,64,3072]{2,1,0:T(8,128)(2,1)} %collective-permute-done.3.refs_1_), channel_id=1, source_target_pairs={{0,1},{1,0},{2,3},{3,2},{4,5},{5,4},{6,7},{7,6},{8,9},{9,8},{10,11... | collective-permute-start | bytes 4718600 | tf_op jit(solution)/shard_map/ppermute | solution.py:290
  242.6 2.4 collective-permute-start.10
  244.4 98.2 %copy-start.111 = (f32[256,32]{0,1:T(8,128)}, f32[256,32]{0,1:T(8,128)S(1)}, u32[]{:S(2)}) copy-start(f32[256,32]{0,1:T(8,128)S(1)} %get-tuple-element.184) | copy-start | bytes 98308
  245.8 2.9 collective-permute-start.11
  249.4 30.8 %collective-permute-start.22 = (bf16[4,256,1024]{2,1,0:T(8,128)(2,1)}, bf16[4,256,1024]{2,1,0:T(8,128)(2,1)}, u32[]{:S(2)}, u32[]{:S(2)}) collective-permute-start(bf16[4,256,1024]{2,1,0:T(8,128)(2,1)} %pad_maximum_fusion.8.refs_0_), channel_id=1, source_target_pairs={{0,1},{1,0},{2,3},{3,2},{4,5},{5,4},{6,7},{7,6},{8,9},{9,8},{10,11... | collective-permute-start | bytes 6291464 | tf_op jit(solution)/shard_map/ppermute | solution.py:290
  255.1 29.9 %collective-permute-start.16 = (bf16[4,64,4096]{2,1,0:T(8,128)(2,1)}, bf16[4,64,4096]{2,1,0:T(8,128)(2,1)}, u32[]{:S(2)}, u32[]{:S(2)}) collective-permute-start(bf16[4,64,4096]{2,1,0:T(8,128)(2,1)} %pad_maximum_fusion.7.refs_0_), channel_id=1, source_target_pairs={{0,1},{1,0},{2,3},{3,2},{4,5},{5,4},{6,7},{7,6},{8,9},{9,8},{10,11... | collective-permute-start | bytes 6291464 | tf_op jit(solution)/shard_map/ppermute | solution.py:290
  255.7 24.6 %collective-permute-start.23 = (bf16[4,256,1024]{2,1,0:T(8,128)(2,1)}, bf16[4,256,1024]{2,1,0:T(8,128)(2,1)}, u32[]{:S(2)}, u32[]{:S(2)}) collective-permute-start(bf16[4,256,1024]{2,1,0:T(8,128)(2,1)} %collective-permute-done.21.refs_1_), channel_id=1, source_target_pairs={{0,1},{1,0},{2,3},{3,2},{4,5},{5,4},{6,7},{7,6},{8,9},{9,8},{10,11... | collective-permute-start | bytes 6291464 | tf_op jit(solution)/shard_map/ppermute | solution.py:290
  255.8 29.2 %collective-permute-start.17 = (bf16[4,64,4096]{2,1,0:T(8,128)(2,1)}, bf16[4,64,4096]{2,1,0:T(8,128)(2,1)}, u32[]{:S(2)}, u32[]{:S(2)}) collective-permute-start(bf16[4,64,4096]{2,1,0:T(8,128)(2,1)} %collective-permute-done.15.refs_1_), channel_id=1, source_target_pairs={{0,1},{1,0},{2,3},{3,2},{4,5},{5,4},{6,7},{7,6},{8,9},{9,8},{10,11... | collective-permute-start | bytes 6291464 | tf_op jit(solution)/shard_map/ppermute | solution.py:290
  310.8 64.0 %copy-start.9 = (f32[256,1024]{1,0:T(8,128)}, f32[256,1024]{1,0:T(8,128)S(1)}, u32[]{:S(2)}) copy-start(f32[256,1024]{1,0:T(8,128)S(1)} %get-tuple-element.192) | copy-start | bytes 3145732
  310.8 64.0 %copy-start.119 = (f32[256]{0:T(256)}, f32[256]{0:T(256)S(1)}, u32[]{:S(2)}) copy-start(f32[256]{0:T(256)S(1)} %broadcast_multiply_fusion.4) | copy-start | bytes 3076
  311.1 63.7 %copy-start.121 = (f32[256]{0:T(256)}, f32[256]{0:T(256)S(1)}, u32[]{:S(2)}) copy-start(f32[256]{0:T(256)S(1)} %fusion.98) | copy-start | bytes 3076
  312.1 15.1 %collective-permute-start.24 = (bf16[256,1024]{1,0:T(8,128)(2,1)}, bf16[256,1024]{1,0:T(8,128)(2,1)}, u32[]{:S(2)}, u32[]{:S(2)}) collective-permute-start(bf16[256,1024]{1,0:T(8,128)(2,1)} %add_convert_fusion.11), channel_id=1, source_target_pairs={{0,16},{1,17},{2,18},{3,19},{4,20},{5,21},{6,22},{7,23},{8,24},{9,... | collective-permute-start | bytes 1572872 | tf_op jit(solution)/shard_map/ppermute | solution.py:33
  376.2 15.4 %collective-permute-start.25 = (bf16[256,1024]{1,0:T(8,128)(2,1)}, bf16[256,1024]{1,0:T(8,128)(2,1)S(1)}, u32[]{:S(2)}, u32[]{:S(2)}) collective-permute-start(bf16[256,1024]{1,0:T(8,128)(2,1)} %get-tuple-element.80), channel_id=1, source_target_pairs={{0,16},{1,17},{2,18},{3,19},{4,20},{5,21},{6,22},{7,23},{8,24},{9,... | collective-permute-start | bytes 1572872 | tf_op jit(solution)/shard_map/ppermute | solution.py:33
  437.0 18.0 %all-to-all-start.1 = ((bf16[16,2,64,128]{3,2,1,0:T(8,128)(2,1)}), bf16[16,2,64,128]{3,2,1,0:T(8,128)(2,1)S(1)}, u32[]{:S(2)}, u32[]{:S(2)}) async-start(bf16[16,2,64,128]{3,2,1,0:T(8,128)(2,1)} %broadcast_in_dim.111), calls=%async_computation.1 | async-start | bytes 1048576 | tf_op jit(solution)/shard_map/all_to_all | solution.py:383
  459.6 12.2 %all-to-all-start.2 = ((f32[16,2,1,3,3,128]{5,1,4,3,2,0:T(2,128)}), f32[16,2,1,3,3,128]{5,1,4,3,2,0:T(2,128)S(1)}, u32[]{:S(2)}, u32[]{:S(2)}) async-start(f32[16,2,1,3,3,128]{5,1,4,3,2,0:T(2,128)} %broadcast_in_dim.113), calls=%async_computation.2 | async-start | bytes 294912 | tf_op jit(solution)/shard_map/all_to_all | solution.py:383
  479.5 31.5 %all-to-all-start.3 = ((bf16[16,2,64,128]{3,2,1,0:T(8,128)(2,1)}), bf16[16,2,64,128]{3,2,1,0:T(8,128)(2,1)}, u32[]{:S(2)}, u32[]{:S(2)}) async-start(bf16[16,2,64,128]{3,2,1,0:T(8,128)(2,1)} %get-tuple-element.25), calls=%async_computation.3 | async-start | bytes 1048576 | tf_op jit(solution)/shard_map/all_to_all | solution.py:389
  551.2 41.2 %collective-permute-start.27 = (bf16[256,1024]{1,0:T(8,128)(2,1)}, bf16[256,1024]{1,0:T(8,128)(2,1)}, u32[]{:S(2)}, u32[]{:S(2)}) collective-permute-start(bf16[256,1024]{1,0:T(8,128)(2,1)} %get-tuple-element.210), channel_id=1, source_target_pairs={{16,0},{17,1},{18,2},{19,3},{20,4},{21,5},{22,6},{23,7},{24,8},{25... | collective-permute-start | bytes 1572872 | tf_op jit(solution)/shard_map/ppermute | solution.py:33
  574.7 6.3 collective-permute-start.26
  584.1 44.5 %all-to-all-start.5 = ((f32[16,2,32,128]{3,2,1,0:T(8,128)}), f32[16,2,32,128]{3,2,1,0:T(8,128)}, u32[]{:S(2)}, u32[]{:S(2)}) async-start(f32[16,2,32,128]{3,2,1,0:T(8,128)} %bitcast.381), calls=%async_computation.5 | async-start | bytes 1048576 | tf_op jit(solution)/shard_map/all_to_all | solution.py:389
  627.4 17.4 %collective-permute-start.28 = (bf16[256,1024]{1,0:T(8,128)(2,1)}, bf16[256,1024]{1,0:T(8,128)(2,1)}, u32[]{:S(2)}, u32[]{:S(2)}) collective-permute-start(bf16[256,1024]{1,0:T(8,128)(2,1)} %get-tuple-element.132), channel_id=1, source_target_pairs={{16,0},{17,1},{18,2},{19,3},{20,4},{21,5},{22,6},{23,7},{24,8},{25... | collective-permute-start | bytes 1572872 | tf_op jit(solution)/shard_map/ppermute | solution.py:33
  629.8 14.4 %collective-permute-start.49 = (f32[32,128]{1,0:T(8,128)S(1)}, f32[32,128]{1,0:T(8,128)S(1)}, u32[]{:S(2)}, u32[]{:S(2)}) collective-permute-start(f32[32,128]{1,0:T(8,128)S(1)} %slice_bitcast_fusion.2), channel_id=1, source_target_pairs={{16,0},{17,1},{18,2},{19,3},{20,4},{21,5},{22,6},{23,7},{24,8},{25... | collective-permute-start | bytes 49160 | tf_op jit(solution)/shard_map/ppermute | solution.py:33
  693.8 40.0 %collective-permute-start.29 = (bf16[512,3072]{1,0:T(8,128)(2,1)}, bf16[512,3072]{1,0:T(8,128)(2,1)}, u32[]{:S(2)}, u32[]{:S(2)}) collective-permute-start(bf16[512,3072]{1,0:T(8,128)(2,1)} %convolution_convert_fusion.1), channel_id=1, source_target_pairs={{0,1},{1,0},{2,3},{3,2},{4,5},{5,4},{6,7},{7,6},{8,9},{9,8},{10,11... | collective-permute-start | bytes 9437192 | tf_op jit(solution)/shard_map/ppermute | solution.py:290
  695.6 13.9 %collective-permute-start.34 = (bf16[512,1024]{1,0:T(8,128)(2,1)}, bf16[512,1024]{1,0:T(8,128)(2,1)}, u32[]{:S(2)}, u32[]{:S(2)}) collective-permute-start(bf16[512,1024]{1,0:T(8,128)(2,1)} %convolution_convert_fusion.3), channel_id=1, source_target_pairs={{0,1},{1,0},{2,3},{3,2},{4,5},{5,4},{6,7},{7,6},{8,9},{9,8},{10,11... | collective-permute-start | bytes 3145736 | tf_op jit(solution)/shard_map/ppermute | solution.py:290
  700.5 39.2 %collective-permute-start.39 = (bf16[512,4096]{1,0:T(8,128)(2,1)}, bf16[512,4096]{1,0:T(8,128)(2,1)}, u32[]{:S(2)}, u32[]{:S(2)}) collective-permute-start(bf16[512,4096]{1,0:T(8,128)(2,1)} %convolution_convert_fusion), channel_id=1, source_target_pairs={{0,1},{1,0},{2,3},{3,2},{4,5},{5,4},{6,7},{7,6},{8,9},{9,8},{10,11... | collective-permute-start | bytes 12582920 | tf_op jit(solution)/shard_map/ppermute | solution.py:290
  705.0 42.4 %collective-permute-start.44 = (bf16[2048,1024]{1,0:T(8,128)(2,1)}, bf16[2048,1024]{1,0:T(8,128)(2,1)}, u32[]{:S(2)}, u32[]{:S(2)}) collective-permute-start(bf16[2048,1024]{1,0:T(8,128)(2,1)} %convolution_convert_fusion.2), channel_id=1, source_target_pairs={{0,1},{1,0},{2,3},{3,2},{4,5},{5,4},{6,7},{7,6},{8,9},{9,8},{10,11... | collective-permute-start | bytes 12582920 | tf_op jit(solution)/shard_map/ppermute | solution.py:290
  712.5 16.5 %collective-permute-start.35 = (bf16[4,64,1024]{2,1,0:T(8,128)(2,1)}, bf16[4,64,1024]{2,1,0:T(8,128)(2,1)}, u32[]{:S(2)}, u32[]{:S(2)}) collective-permute-start(bf16[4,64,1024]{2,1,0:T(8,128)(2,1)} %dynamic-slice_bitcast_fusion.3), channel_id=1, source_target_pairs={{0,2},{1,3},{2,0},{3,1},{4,6},{5,7},{6,4},{7,5},{8,10},{9,11},{10,... | collective-permute-start | bytes 1572872 | tf_op jit(solution)/shard_map/ppermute | solution.py:290
  715.0 12.2 %all-to-all-start.4 = ((f32[16,1,832]{2,1,0:T(1,128)}), f32[16,1,832]{2,1,0:T(1,128)S(1)}, u32[]{:S(2)}, u32[]{:S(2)}) async-start(f32[16,1,832]{2,1,0:T(1,128)} %all_to_all.29), calls=%async_computation.4 | async-start | bytes 114688 | tf_op jit(solution)/shard_map/all_to_all | solution.py:389
  730.3 15.8 %collective-permute-start.38 = (bf16[1,64,1024]{2,1,0:T(8,128)(2,1)S(1)}, bf16[1,64,1024]{2,1,0:T(8,128)(2,1)S(1)}, u32[]{:S(2)}, u32[]{:S(2)}) collective-permute-start(bf16[1,64,1024]{2,1,0:T(8,128)(2,1)S(1)} %get-tuple-element.135), channel_id=1, source_target_pairs={{0,12},{1,13},{2,14},{3,15},{4,0},{5,1},{6,2},{7,3},{8,4},{9,5},{1... | collective-permute-start | bytes 393224 | tf_op jit(solution)/shard_map/ppermute | solution.py:290
  733.8 12.9 %collective-permute-start.37 = (bf16[1,64,1024]{2,1,0:T(8,128)(2,1)S(1)}, bf16[1,64,1024]{2,1,0:T(8,128)(2,1)S(1)}, u32[]{:S(2)}, u32[]{:S(2)}) collective-permute-start(bf16[1,64,1024]{2,1,0:T(8,128)(2,1)S(1)} %get-tuple-element.136), channel_id=1, source_target_pairs={{0,8},{1,9},{2,10},{3,11},{4,12},{5,13},{6,14},{7,15},{8,0},{9,1},... | collective-permute-start | bytes 393224 | tf_op jit(solution)/shard_map/ppermute | solution.py:290
  733.8 12.9 %collective-permute-start.36 = (bf16[1,64,1024]{2,1,0:T(8,128)(2,1)S(1)}, bf16[1,64,1024]{2,1,0:T(8,128)(2,1)S(1)}, u32[]{:S(2)}, u32[]{:S(2)}) collective-permute-start(bf16[1,64,1024]{2,1,0:T(8,128)(2,1)S(1)} %get-tuple-element.134), channel_id=1, source_target_pairs={{0,4},{1,5},{2,6},{3,7},{4,8},{5,9},{6,10},{7,11},{8,12},{9,13},{1... | collective-permute-start | bytes 393224 | tf_op jit(solution)/shard_map/ppermute | solution.py:290
  739.7 37.4 %collective-permute-start.30 = (bf16[4,64,3072]{2,1,0:T(8,128)(2,1)S(1)}, bf16[4,64,3072]{2,1,0:T(8,128)(2,1)S(1)}, u32[]{:S(2)}, u32[]{:S(2)}) collective-permute-start(bf16[4,64,3072]{2,1,0:T(8,128)(2,1)S(1)} %dynamic-slice_bitcast_fusion.2), channel_id=1, source_target_pairs={{0,2},{1,3},{2,0},{3,1},{4,6},{5,7},{6,4},{7,5},{8,10},{9,11},{10,... | collective-permute-start | bytes 4718600 | tf_op jit(solution)/shard_map/ppermute | solution.py:290
  746.0 76.0 %collective-permute-start.40 = (bf16[4,64,4096]{2,1,0:T(8,128)(2,1)S(1)}, bf16[4,64,4096]{2,1,0:T(8,128)(2,1)S(1)}, u32[]{:S(2)}, u32[]{:S(2)}) collective-permute-start(bf16[4,64,4096]{2,1,0:T(8,128)(2,1)S(1)} %dynamic-slice_bitcast_fusion.1), channel_id=1, source_target_pairs={{0,2},{1,3},{2,0},{3,1},{4,6},{5,7},{6,4},{7,5},{8,10},{9,11},{10,... | collective-permute-start | bytes 6291464 | tf_op jit(solution)/shard_map/ppermute | solution.py:290
  752.3 112.9 %collective-permute-start.45 = (bf16[4,256,1024]{2,1,0:T(8,128)(2,1)S(1)}, bf16[4,256,1024]{2,1,0:T(8,128)(2,1)S(1)}, u32[]{:S(2)}, u32[]{:S(2)}) collective-permute-start(bf16[4,256,1024]{2,1,0:T(8,128)(2,1)S(1)} %dynamic-slice_bitcast_fusion), channel_id=1, source_target_pairs={{0,2},{1,3},{2,0},{3,1},{4,6},{5,7},{6,4},{7,5},{8,10},{9,11},{10,... | collective-permute-start | bytes 6291464 | tf_op jit(solution)/shard_map/ppermute | solution.py:290
  777.8 47.9 %collective-permute-start.33 = (bf16[1,64,3072]{2,1,0:T(8,128)(2,1)S(1)}, bf16[1,64,3072]{2,1,0:T(8,128)(2,1)S(1)}, u32[]{:S(2)}, u32[]{:S(2)}) collective-permute-start(bf16[1,64,3072]{2,1,0:T(8,128)(2,1)S(1)} %get-tuple-element.100), channel_id=1, source_target_pairs={{0,12},{1,13},{2,14},{3,15},{4,0},{5,1},{6,2},{7,3},{8,4},{9,5},{1... | collective-permute-start | bytes 1179656 | tf_op jit(solution)/shard_map/ppermute | solution.py:290
  780.6 46.3 %collective-permute-start.32 = (bf16[1,64,3072]{2,1,0:T(8,128)(2,1)S(1)}, bf16[1,64,3072]{2,1,0:T(8,128)(2,1)S(1)}, u32[]{:S(2)}, u32[]{:S(2)}) collective-permute-start(bf16[1,64,3072]{2,1,0:T(8,128)(2,1)S(1)} %get-tuple-element.101), channel_id=1, source_target_pairs={{0,8},{1,9},{2,10},{3,11},{4,12},{5,13},{6,14},{7,15},{8,0},{9,1},... | collective-permute-start | bytes 1179656 | tf_op jit(solution)/shard_map/ppermute | solution.py:290
  781.7 45.2 %collective-permute-start.31 = (bf16[1,64,3072]{2,1,0:T(8,128)(2,1)S(1)}, bf16[1,64,3072]{2,1,0:T(8,128)(2,1)S(1)}, u32[]{:S(2)}, u32[]{:S(2)}) collective-permute-start(bf16[1,64,3072]{2,1,0:T(8,128)(2,1)S(1)} %get-tuple-element.99), channel_id=1, source_target_pairs={{0,4},{1,5},{2,6},{3,7},{4,8},{5,9},{6,10},{7,11},{8,12},{9,13},{1... | collective-permute-start | bytes 1179656 | tf_op jit(solution)/shard_map/ppermute | solution.py:290
  823.0 47.3 %collective-permute-start.43 = (bf16[1,64,4096]{2,1,0:T(8,128)(2,1)S(1)}, bf16[1,64,4096]{2,1,0:T(8,128)(2,1)S(1)}, u32[]{:S(2)}, u32[]{:S(2)}) collective-permute-start(bf16[1,64,4096]{2,1,0:T(8,128)(2,1)S(1)} %get-tuple-element.97), channel_id=1, source_target_pairs={{0,12},{1,13},{2,14},{3,15},{4,0},{5,1},{6,2},{7,3},{8,4},{9,5},{1... | collective-permute-start | bytes 1572872 | tf_op jit(solution)/shard_map/ppermute | solution.py:290
  825.8 44.9 %collective-permute-start.42 = (bf16[1,64,4096]{2,1,0:T(8,128)(2,1)S(1)}, bf16[1,64,4096]{2,1,0:T(8,128)(2,1)S(1)}, u32[]{:S(2)}, u32[]{:S(2)}) collective-permute-start(bf16[1,64,4096]{2,1,0:T(8,128)(2,1)S(1)} %get-tuple-element.98), channel_id=1, source_target_pairs={{0,8},{1,9},{2,10},{3,11},{4,12},{5,13},{6,14},{7,15},{8,0},{9,1},... | collective-permute-start | bytes 1572872 | tf_op jit(solution)/shard_map/ppermute | solution.py:290
  826.9 43.7 %collective-permute-start.41 = (bf16[1,64,4096]{2,1,0:T(8,128)(2,1)S(1)}, bf16[1,64,4096]{2,1,0:T(8,128)(2,1)S(1)}, u32[]{:S(2)}, u32[]{:S(2)}) collective-permute-start(bf16[1,64,4096]{2,1,0:T(8,128)(2,1)S(1)} %get-tuple-element.96), channel_id=1, source_target_pairs={{0,4},{1,5},{2,6},{3,7},{4,8},{5,9},{6,10},{7,11},{8,12},{9,13},{1... | collective-permute-start | bytes 1572872 | tf_op jit(solution)/shard_map/ppermute | solution.py:290
  866.4 15.5 %collective-permute-start.48 = (bf16[1,256,1024]{2,1,0:T(8,128)(2,1)S(1)}, bf16[1,256,1024]{2,1,0:T(8,128)(2,1)S(1)}, u32[]{:S(2)}, u32[]{:S(2)}) collective-permute-start(bf16[1,256,1024]{2,1,0:T(8,128)(2,1)S(1)} %get-tuple-element.94), channel_id=1, source_target_pairs={{0,12},{1,13},{2,14},{3,15},{4,0},{5,1},{6,2},{7,3},{8,4},{9,5},{1... | collective-permute-start | bytes 1572872 | tf_op jit(solution)/shard_map/ppermute | solution.py:290
  869.5 44.7 %collective-permute-start.47 = (bf16[1,256,1024]{2,1,0:T(8,128)(2,1)S(1)}, bf16[1,256,1024]{2,1,0:T(8,128)(2,1)S(1)}, u32[]{:S(2)}, u32[]{:S(2)}) collective-permute-start(bf16[1,256,1024]{2,1,0:T(8,128)(2,1)S(1)} %get-tuple-element.95), channel_id=1, source_target_pairs={{0,8},{1,9},{2,10},{3,11},{4,12},{5,13},{6,14},{7,15},{8,0},{9,1},... | collective-permute-start | bytes 1572872 | tf_op jit(solution)/shard_map/ppermute | solution.py:290
  870.3 43.9 %collective-permute-start.46 = (bf16[1,256,1024]{2,1,0:T(8,128)(2,1)S(1)}, bf16[1,256,1024]{2,1,0:T(8,128)(2,1)S(1)}, u32[]{:S(2)}, u32[]{:S(2)}) collective-permute-start(bf16[1,256,1024]{2,1,0:T(8,128)(2,1)S(1)} %get-tuple-element.93), channel_id=1, source_target_pairs={{0,4},{1,5},{2,6},{3,7},{4,8},{5,9},{6,10},{7,11},{8,12},{9,13},{1... | collective-permute-start | bytes 1572872 | tf_op jit(solution)/shard_map/ppermute | solution.py:290
  (173 other events, 1224.6 us)

commit v2 on v1

v2 whole, which is shorter than its diff:
```python
from functools import partial
import math

import jax
import jax.numpy as jnp
from jax import lax
from jax.experimental import pallas as pl
from jax.experimental.pallas import tpu as pltpu
from jax.sharding import PartitionSpec as P

HEAD = 64
PROJ = 128
QLEN = 32
DOC_ROWS = 192
QRY_DEV = 2
DOCS_DEV = 3
MICRO = 2
CANDS = 8
ROWS = 256
PREFIXES = (PROJ // 2, 3 * PROJ // 4, PROJ)


norm_eps = 1e-05
unit_eps = 1e-06
sharpness = 20.0
score_scale = 0.125
masked_score = -1000000000.0


def from_behind(value, axis, steps):
    count = lax.axis_size(axis)
    first, last = (max(0, -steps), min(count, count - steps))
    return lax.ppermute(value, axis, [(source, source + steps) for source in range(first, last)])


def product(left_side, right_side):
    return jnp.dot(left_side, right_side, preferred_element_type=jnp.float32)


def product_tn(left_side, right_side):
    return lax.dot_general(
        left_side, right_side, (((0,), (0,)), ((), ())), preferred_element_type=jnp.float32
    )


def product_nt(left_side, right_side):
    return lax.dot_general(
        left_side, right_side, (((1,), (1,)), ((), ())), preferred_element_type=jnp.float32
    )


def doc_layout(doc_lens):
    row_ids = jnp.arange(ROWS, dtype=jnp.int32)
    ends_at = jnp.cumsum(doc_lens)
    starts_at = ends_at - doc_lens
    doc_of = jnp.sum((row_ids[:, None] >= ends_at[None, :]).astype(jnp.int32), axis=1)
    doc_index = jnp.arange(DOCS_DEV, dtype=jnp.int32)
    begins = jnp.sum(
        jnp.where(doc_of[:, None] == doc_index[None, :], starts_at[None, :], 0), axis=1
    )
    in_docs = row_ids < DOC_ROWS
    query_rows = jnp.maximum(row_ids - DOC_ROWS, 0)
    segment = jnp.where(in_docs, doc_of, DOCS_DEV + query_rows // QLEN)
    position = jnp.where(in_docs, row_ids - begins, query_rows % QLEN)
    return (segment, position)


def rotary(position):
    step_ids = jnp.arange(HEAD // 2, dtype=jnp.int32).astype(jnp.float32)
    frequency = jnp.exp(step_ids * (-2.0 * math.log(10000.0) / HEAD))
    angles = position.astype(jnp.float32)[..., None] * frequency
    cosine, sine = jnp.cos(angles), jnp.sin(angles)
    return (
        jnp.concatenate([cosine] * 4, axis=-1),
        jnp.concatenate([-sine, sine] * 2, axis=-1),
    )


def lane_ids():
    return lax.broadcasted_iota(jnp.int32, (1, 2 * HEAD), 1)


def turned(value, cosine, sine):
    in_first = lane_ids() % HEAD < HEAD // 2
    ahead = pltpu.roll(value, 2 * HEAD - HEAD // 2, 1)
    behind = pltpu.roll(value, HEAD // 2, 1)
    return value * cosine + jnp.where(in_first, ahead, behind) * sine


def statistics(values):
    center = values - jnp.mean(values, axis=1, keepdims=True)
    spread = jnp.mean(center * center, axis=1, keepdims=True)
    scale = lax.rsqrt(spread + norm_eps)
    return center * scale, scale


def norm_back(grad, unit, scale, gain):
    inner = grad * gain
    along = jnp.mean(inner * unit, axis=1, keepdims=True)
    grad_in = scale * (inner - jnp.mean(inner, axis=1, keepdims=True) - unit * along)
    return grad_in, jnp.sum(grad * unit, axis=0, keepdims=True), jnp.sum(grad, axis=0, keepdims=True)


def gelu_parts(value):
    bell = jnp.exp(-0.5 * value * value)
    part = 1.0 / (1.0 + (0.3275911 * math.sqrt(0.5)) * jnp.abs(value))
    tail = 0.5 * 1.061405429 * part - 0.5 * 1.453152027
    tail = tail * part + 0.5 * 1.421413741
    tail = tail * part - 0.5 * 0.284496736
    tail = tail * part + 0.5 * 0.254829592
    tail = tail * part * bell
    below = jnp.where(value >= 0, 1.0 - tail, tail)
    return value * below, below + value * bell * (1.0 / math.sqrt(2.0 * math.pi))


def probabilities(queries, keys, allowed, held):
    scores = product_nt(jnp.where(held, queries, jnp.zeros_like(queries)), keys)
    scores = jnp.where(allowed, scores, masked_score)
    scores = jnp.exp(scores - jnp.max(scores, axis=1, keepdims=True))
    return scores * (1.0 / jnp.sum(scores, axis=1, keepdims=True))


LOW, WIDE = jnp.bfloat16, jnp.float32
VMEM_LIMIT = 52 << 20
BLOCK = 512
NO_COST = pl.CostEstimate(flops=1, bytes_accessed=1, transcendentals=0)
FULL_COST = pl.CostEstimate(flops=40 * 10**9, bytes_accessed=10**8, transcendentals=0)


class Weight:
    def __init__(self, places, rows, columns, width, parts):
        self.places, self.rows, self.columns, self.width = places, rows, columns, width
        self.count = places.shape[0]
        self.height = self.count * rows
        self.arrays = [group for _, _, groups in parts for group in groups]
        self.plan = [
            (start, width, [group.shape[0] for group in groups]) for start, width, groups in parts
        ]

    def scratch(self):
        return [
            pltpu.VMEM((self.height, self.columns), LOW),
            pltpu.SemaphoreType.DMA((self.columns // self.width, self.count)),
        ]


class Fetch:
    def __init__(self, weight, places_ref, refs, buffer, sems):
        self.weight, self.places_ref = weight, places_ref
        self.refs, self.buffer, self.sems = refs, buffer, sems
        self.waited = set()

    def copies(self, number):
        weight, begin = self.weight, number * self.weight.width
        passed = 0
        for start, width, lengths in weight.plan:
            if start <= begin < start + width:
                break
            passed += len(lengths)
        columns = pl.ds(begin - start, weight.width)
        block = 0
        for group, length in enumerate(lengths):
            for inner in range(length):
                place = pl.multiple_of(self.places_ref[block] * weight.rows, weight.rows)
                yield pltpu.make_async_copy(
                    self.refs[passed + group].at[inner, pl.ds(0, weight.rows), columns],
                    self.buffer.at[pl.ds(place, weight.rows), pl.ds(begin, weight.width)],
                    self.sems.at[number, block],
                )
                block += 1

    def start(self):
        for number in range(self.weight.columns // self.weight.width):
            for copy in self.copies(number):
                copy.start()

    def ready(self, until=None):
        until = self.weight.columns if until is None else until
        for number in range(-(-until // self.weight.width)):
            if number not in self.waited:
                self.waited.add(number)
                for copy in self.copies(number):
                    copy.wait()
        return self.buffer


class Parts:
    def __init__(self, refs, loads, weights, outs, scratch):
        self.pick, self.places, *refs = refs
        loaded, refs = refs[: len(loads)], refs[len(loads) :]
        fetched = {}
        for name, weight in weights.items():
            fetched[name], refs = refs[: len(weight.arrays)], refs[len(weight.arrays) :]
        stored, refs = refs[: len(outs)], refs[len(outs) :]
        self.buffers, refs = dict(zip(loads, refs)), refs[len(loads) :]
        self.weights = {}
        for name, weight in weights.items():
            buffer, sems, *refs = refs
            self.weights[name] = Fetch(weight, self.places, fetched[name], buffer, sems)
        self.outs, refs = dict(zip(outs, refs)), refs[len(outs) :]
        self.scratch, refs = dict(zip(scratch, refs)), refs[len(scratch) :]
        load_sems, out_sems = refs
        self.loads = {
            name: pltpu.make_async_copy(ref, self.buffers[name], load_sems.at[number])
            for number, (name, ref) in enumerate(zip(loads, loaded))
        }
        self.stores = {
            name: pltpu.make_async_copy(self.outs[name], ref, out_sems.at[number])
            for number, (name, ref) in enumerate(zip(outs, stored))
        }
        self.waited = set()

    def start(self, order):
        for name in order:
            (self.loads[name] if name in self.loads else self.weights[name]).start()

    def ref(self, name):
        if name in self.outs:
            return self.outs[name]
        if name in self.scratch:
            return self.scratch[name]
        if name not in self.waited:
            self.waited.add(name)
            self.loads[name].wait()
        return self.buffers[name]

    def refs(self, *names):
        return [self.ref(name) for name in names]

    def leave(self, *names):
        for name in names:
            self.stores[name].start()

    def finish(self):
        for name in self.stores:
            self.stores[name].wait()


def run_parts(name, bodies, pick, places, loads, weights, outs, scratch, order, cost):
    def kernel(*refs):
        parts = Parts(refs, list(loads), weights, list(outs), list(scratch))
        parts.start(order)
        for body in bodies:
            body(parts)
        parts.finish()

    arrays = [*loads.values(), *(array for weight in weights.values() for array in weight.arrays)]
    results = pl.pallas_call(
        kernel,
        in_specs=[pl.BlockSpec(memory_space=pltpu.SMEM)] * 2
        + [pl.BlockSpec(memory_space=pl.ANY)] * len(arrays),
        out_specs=[pl.BlockSpec(memory_space=pltpu.HBM)] * len(outs),
        out_shape=[pltpu.HBM(*out) for out in outs.values()],
        scratch_shapes=[pltpu.VMEM(array.shape, array.dtype) for array in loads.values()]
        + [entry for weight in weights.values() for entry in weight.scratch()]
        + [pltpu.VMEM(*out) for out in outs.values()]
        + list(scratch.values())
        + [pltpu.SemaphoreType.DMA((len(loads),)), pltpu.SemaphoreType.DMA((len(outs),))],
        compiler_params=pltpu.CompilerParams(vmem_limit_bytes=VMEM_LIMIT),
        cost_estimate=cost,
        name=name,
    )(pick, places, *arrays)
    return dict(zip(outs, results))


def attend_part(parts):
    micro_step = parts.pick[1]
    source = parts.ref("x")
    cos_ref, sin_ref, column_ref, row_ref, bias_ref = parts.refs(
        "cosine", "sine", "column", "row", "qkv_bias"
    )
    cosine, sine = cos_ref[micro_step], sin_ref[micro_step]
    outs = parts.refs("q", "k", "v")
    width = source.shape[1]
    for part, ref in enumerate(outs):
        qkv = parts.weights["qkv"].ready((part + 1) * width)
        for start in range(0, width, BLOCK):
            at = slice(part * width + start, part * width + start + BLOCK)
            value = product(source[...], qkv[:, at])
            value = value + bias_ref[part : part + 1, start : start + BLOCK]
            for pair in range(0, BLOCK, 2 * HEAD):
                two = value[:, pair : pair + 2 * HEAD]
                if part < 2:
                    two = turned(two, cosine, sine)
                ref[:, start + pair : start + pair + 2 * HEAD] = two.astype(LOW)
    parts.leave("q", "k", "v")
    allowed = column_ref[micro_step] == row_ref[micro_step]
    q_ref, k_ref, v_ref = outs
    mixture_ref, sum_ref, norm_ref, small_ref = parts.refs("mixture", "sum_one", "norm", "small")
    for start in range(0, width, 2 * HEAD):
        at = slice(start, start + 2 * HEAD)
        queries = q_ref[:, at] * LOW(score_scale)
        keys, values = k_ref[:, at], v_ref[:, at]
        mixed = []
        for head in range(2):
            held = lane_ids() // HEAD == head
            attention = probabilities(queries, keys, allowed, held)
            mixed.append(product(attention.astype(LOW), values))
        mixture_ref[:, at] = jnp.where(lane_ids() < HEAD, mixed[0], mixed[1]).astype(LOW)
    out = parts.weights["out"].ready()
    for start in range(0, width, BLOCK):
        at = slice(start, start + BLOCK)
        sum_ref[:, at] = (
            source[:, at].astype(WIDE)
            + small_ref[0:1, at]
            + product(mixture_ref[...], out[:, at])
        )
    unit, _ = statistics(sum_ref[...])
    norm_ref[...] = (unit * small_ref[1:2] + small_ref[2:3]).astype(LOW)
    parts.leave("mixture", "sum_one", "norm")


def up_part(parts):
    norm_ref, bias_ref, active_ref, slope_ref = parts.refs("norm", "up_bias", "active", "slope")
    for start in range(0, active_ref.shape[1], BLOCK):
        up = parts.weights["up"].ready(start + BLOCK)
        at = slice(start, start + BLOCK)
        active, slope = gelu_parts(product(norm_ref[...], up[:, at]) + bias_ref[:, at])
        active_ref[:, at] = active.astype(LOW)
        slope_ref[:, at] = slope.astype(LOW)
    parts.leave("active", "slope")


def down_part(parts):
    active_ref, norm_ref, small_ref = parts.refs("active", "norm", "small")
    sum_ref, result_ref = parts.refs("sum_two", "result")
    for start in range(0, sum_ref.shape[1], BLOCK):
        at = slice(start, start + BLOCK)
        down = parts.weights["down"].ready(start + BLOCK)
        sum_ref[:, at] = (
            norm_ref[:, at].astype(WIDE)
            + small_ref[3:4, at]
            + product(active_ref[...], down[:, at])
        )
    unit, _ = statistics(sum_ref[...])
    result = (unit * small_ref[4:5] + small_ref[5:6]).astype(LOW)
    result_ref[...] = result
    parts.leave("result", "sum_two")
    if "embedded" in parts.outs:
        parts.ref("embedded")[...] = product(result, parts.ref("projection")[...]).astype(LOW)
        parts.leave("embedded")
    if "activations" in parts.outs:
        early, late, own, both = parts.refs("early", "late", "own", "activations")

        @pl.when(parts.pick[0] == 1)
        def _():
            both[:ROWS] = early[...]
            both[ROWS:] = late[...]

        @pl.when(parts.pick[0] == 0)
        def _():
            both[:ROWS] = own[...]
            both[ROWS:] = result

        parts.leave("activations")


def feed_back_part(parts):
    if "docs" in parts.loads:
        own = jnp.sum(parts.ref("own_parts")[...].astype(WIDE), axis=0)
        embedded = jnp.concatenate([parts.ref("docs")[...], own], axis=0).astype(LOW)
        parts.ref("grad_embedded")[...] = embedded
        parts.leave("grad_embedded")
        upstream = product_nt(embedded, parts.ref("projection")[...])
        upstream = upstream * (1 - parts.pick[0]).astype(WIDE)
    else:
        upstream = parts.ref("back")[...].astype(WIDE)
    branch_ref, gate_ref, attended_ref = parts.refs("branch", "gate", "attended")
    vector_ref, up_bias_ref, total, small_ref = parts.refs("vectors", "grad_up_bias", "total", "small")
    unit, scale = statistics(parts.ref("sum_two")[...])
    grad, gain, bias = norm_back(upstream, unit, scale, small_ref[4:5])
    low = grad.astype(LOW)
    branch_ref[...] = low
    vector_ref[...] = jnp.zeros_like(vector_ref)
    vector_ref[3:4] = jnp.sum(low.astype(WIDE), axis=0, keepdims=True)
    vector_ref[4:5] = gain
    vector_ref[5:6] = bias
    total[...] = grad
    parts.leave("branch")
    slope_ref = parts.ref("slope")
    down = parts.weights["down"].ready()
    for start in range(0, gate_ref.shape[1], BLOCK):
        at = slice(start, start + BLOCK)
        gate = product_nt(branch_ref[...], down[at]) * slope_ref[:, at].astype(WIDE)
        gate = gate.astype(LOW)
        gate_ref[:, at] = gate
        up_bias_ref[:, at] = jnp.sum(gate.astype(WIDE), axis=0, keepdims=True)
    parts.leave("gate", "grad_up_bias")
    up = parts.weights["up"].ready()
    for start in range(0, total.shape[1], BLOCK):
        at = slice(start, start + BLOCK)
        total[:, at] += product_nt(gate_ref[...], up[at])
    unit, scale = statistics(parts.ref("sum_one")[...])
    grad, gain, bias = norm_back(total[...], unit, scale, small_ref[1:2])
    total[...] = grad
    low = grad.astype(LOW)
    attended_ref[...] = low
    vector_ref[0:1] = jnp.sum(low.astype(WIDE), axis=0, keepdims=True)
    vector_ref[1:2] = gain
    vector_ref[2:3] = bias
    parts.leave("attended", "vectors")
    if "grad_one" in parts.outs:
        parts.ref("grad_one")[...] = grad
        parts.leave("grad_one")


def attend_back_part(parts):
    micro_step = parts.pick[1]
    attended_ref, mixed_ref, vector_ref, mixture, total = parts.refs(
        "attended", "mixed", "qkv_vectors", "mixture", "total"
    )
    cos_ref, sin_ref, column_ref, row_ref = parts.refs("cosine", "sine", "column", "row")
    cosine, sine = cos_ref[micro_step], sin_ref[micro_step]
    allowed = column_ref[micro_step] == row_ref[micro_step]
    width = mixture.shape[1]
    if "grad_one" in parts.loads:
        total[...] = parts.ref("grad_one")[...]
    out = parts.weights["out"].ready()
    for start in range(0, width, BLOCK):
        at = slice(start, start + BLOCK)
        mixture[:, at] = product_nt(attended_ref[...], out[at]).astype(LOW)
    q_ref, k_ref, v_ref = parts.refs("q", "k", "v")
    for start in range(0, width, 2 * HEAD):
        at = slice(start, start + 2 * HEAD)
        queries, keys, values = q_ref[:, at], k_ref[:, at], v_ref[:, at]
        scaled = queries * LOW(score_scale)
        grad_mixture = mixture[:, at]
        grads = []
        for head in range(2):
            held = lane_ids() // HEAD == head
            attention = probabilities(scaled, keys, allowed, held)
            own = jnp.where(held, grad_mixture, jnp.zeros_like(grad_mixture))
            grad_attention = product_nt(own, values)
            grad_values = product_tn(attention.astype(LOW), own)
            along = jnp.sum(grad_attention * attention, axis=1, keepdims=True)
            grad_scores = (attention * (grad_attention - along)).astype(LOW)
            grads.append((product(grad_scores, keys), product_tn(grad_scores, queries), grad_values))
        first_head = lane_ids() < HEAD
        for part in range(2):
            value = jnp.where(first_head, grads[0][part], grads[1][part]) * score_scale
            mixed_ref[part, :, at] = turned(value, cosine, -sine).astype(LOW)
        mixed_ref[2, :, at] = (grads[0][2] + grads[1][2]).astype(LOW)
    parts.leave("mixed")
    vector_ref[...] = jnp.zeros_like(vector_ref)
    for part in range(3):
        vector_ref[part : part + 1] = jnp.sum(
            mixed_ref[part].astype(WIDE), axis=0, keepdims=True
        )
    parts.leave("qkv_vectors")
    qkv = parts.weights["qkv"].ready()
    for start in range(0, width, BLOCK):
        at = slice(start, start + BLOCK)
        value = total[:, at]
        for part in range(3):
            value = value + product_nt(mixed_ref[part], qkv[at, part * width : (part + 1) * width])
        total[:, at] = value
    if "grad_low" in parts.outs:
        parts.ref("grad_low")[...] = total[...].astype(LOW)
        parts.leave("grad_low")
        parts.ref("grad_source")[...] = total[...]
    else:
        late, early, own, source_ref = parts.refs("late", "early", "own", "grad_source")

        @pl.when(parts.pick[0] == 1)
        def _():
            source_ref[:ROWS] = total[...]
            source_ref[ROWS:] = own[...]

        @pl.when(parts.pick[0] == 0)
        def _():
            source_ref[:ROWS] = early[...]
            source_ref[ROWS:] = late[...]

    parts.leave("grad_source")


class Layer:
    def __init__(self, places, layout):
        self.places = places
        self.layout = dict(zip(("cosine", "sine", "column", "row"), layout))

    def attend_set(self, source):
        rows = source.shape
        return (
            {"x": source, **self.layout, "qkv_bias": self.qkv_bias, "small": self.small},
            {"qkv": self.qkv, "out": self.out},
            {
                "q": (rows, LOW),
                "k": (rows, LOW),
                "v": (rows, LOW),
                "mixture": (rows, LOW),
                "sum_one": (rows, WIDE),
                "norm": (rows, LOW),
            },
            {},
        )

    def up_set(self):
        rows = (ROWS, self.up.columns)
        return (
            {"up_bias": self.up_bias},
            {"up": self.up},
            {"active": (rows, LOW), "slope": (rows, LOW)},
            {},
        )

    def down_set(self, projection, earlier):
        rows = (ROWS, self.down.columns)
        loads = {"small": self.small}
        outs = {"sum_two": (rows, WIDE), "result": (rows, LOW)}
        if projection is not None:
            loads["projection"] = projection
            outs["embedded"] = ((ROWS, PROJ), LOW)
        if earlier:
            loads |= dict(zip(("early", "late", "own"), earlier))
            outs["activations"] = ((MICRO * ROWS, self.down.columns), LOW)
        return loads, {"down": self.down}, outs, {}

    def run(self, name, bodies, sets, pick, more=None, cost=NO_COST):
        loads, weights, outs, scratch = dict(more or {}), {}, {}, {}
        order = list(loads)
        for one in sets:
            order += [key for key in (*one[0], *one[1]) if key not in order]
            loads, weights = loads | one[0], weights | one[1]
            outs, scratch = outs | one[2], scratch | one[3]
        return run_parts(
            name, bodies, pick, self.places, loads, weights, outs, scratch, order, cost
        )

    def attend(self, source, pick):
        return self.run("attend", [attend_part], [self.attend_set(source)], pick)

    def rise(self, norm, pick):
        return self.run("up", [up_part], [self.up_set()], pick, {"norm": norm})

    def fall(self, active, norm, pick):
        return self.run(
            "down", [down_part], [self.down_set(None, ())], pick, {"active": active, "norm": norm}
        )

    def forward(self, source, pick, projection, earlier):
        return self.run(
            "forward",
            [attend_part, up_part, down_part],
            [self.attend_set(source), self.up_set(), self.down_set(projection, earlier)],
            pick,
            cost=FULL_COST,
        )

    def feed_back_set(self, state, loss_grads, back_grad):
        rows, hidden = (ROWS, self.down.columns), self.up.columns
        loads, outs = {}, {}
        if loss_grads is not None:
            loads |= dict(zip(("docs", "own_parts", "projection"), loss_grads))
            outs["grad_embedded"] = ((ROWS, PROJ), LOW)
        if back_grad is not None:
            loads["back"] = back_grad
        loads |= {"sum_two": state["sum_two"], "small": self.small, "slope": state["slope"]}
        outs |= {
            "branch": (rows, LOW),
            "gate": ((ROWS, hidden), LOW),
            "attended": (rows, LOW),
            "vectors": ((8, rows[1]), WIDE),
            "grad_up_bias": ((1, hidden), WIDE),
        }
        return (
            loads,
            {"down": self.down, "up": self.up},
            outs,
            {"total": pltpu.VMEM(rows, WIDE)},
        )

    def attend_back_set(self, state, earlier):
        rows = (ROWS, self.out.columns)
        outs = {"mixed": ((3, *rows), LOW), "qkv_vectors": ((8, rows[1]), WIDE)}
        loads = {"q": state["q"], "k": state["k"], "v": state["v"], **self.layout}
        if earlier:
            loads |= dict(zip(("late", "early", "own"), earlier))
            outs["grad_source"] = ((MICRO * ROWS, rows[1]), WIDE)
        else:
            outs |= {"grad_source": (rows, WIDE), "grad_low": (rows, LOW)}
        return (
            loads,
            {"out": self.out, "qkv": self.qkv},
            outs,
            {"mixture": pltpu.VMEM(rows, LOW), "total": pltpu.VMEM(rows, WIDE)},
        )

    def backward(self, state, loss_grads, back_grad, pick):
        return self.run(
            "backward",
            [feed_back_part, attend_back_part],
            [
                self.feed_back_set(state, loss_grads, back_grad),
                ({"sum_one": state["sum_one"]}, {}, {}, {}),
                self.attend_back_set(state, ()),
            ],
            pick,
            cost=FULL_COST,
        )

    def feed_back(self, state, back_grad, pick):
        rows = (ROWS, self.down.columns)
        return self.run(
            "feed_back",
            [feed_back_part],
            [
                self.feed_back_set(state, None, back_grad),
                ({"sum_one": state["sum_one"]}, {}, {"grad_one": (rows, WIDE)}, {}),
            ],
            pick,
        )

    def attend_back(self, state, attended, grad_one, earlier, pick):
        return self.run(
            "attend_back",
            [attend_back_part],
            [self.attend_back_set(state, earlier)],
            pick,
            {"attended": attended, "grad_one": grad_one},
        )


def grid_of(count):
    dims = []
    while count % 2 == 0:
        dims.append(2)
        count //= 2
    return ([count] if count > 1 else []) + dims


def coordinates(dims, number):
    at = []
    for size in reversed(dims):
        at.append(number % size)
        number = number // size
    return at[::-1]


def shifted(value, dims, dim, steps):
    count = math.prod(dims)
    stride = math.prod(dims[dim + 1 :])
    pairs = []
    for source in range(count):
        place = (source // stride) % dims[dim]
        pairs.append((source, source + ((place + steps) % dims[dim] - place) * stride))
    return lax.ppermute(value, "dp", pairs)


def after(value, *earlier):
    return lax.optimization_barrier((value, *earlier))[0]


def stage(sends, dims, earlier):
    values = lax.optimization_barrier((*(value for value, _, _ in sends), *earlier))
    arrived = [
        shifted(value, dims, dim, steps) for value, (_, dim, steps) in zip(values, sends)
    ]
    return list(lax.optimization_barrier(tuple(arrived)))


def rows_kernel(top, places, *refs):
    pieces, out, sems = refs[:-2], refs[-2], refs[-1]
    copies = []
    for group in pieces:
        for inner in range(group.shape[0]):
            number = len(copies)
            copies.append(
                pltpu.make_async_copy(
                    group.at[inner, pl.ds(top, out.shape[1])],
                    out.at[places[number]],
                    sems.at[number],
                )
            )
    for copy in copies:
        copy.start()
    for copy in copies:
        copy.wait()


def placed_rows(groups, places, top, rows):
    count, columns = places.shape[0], groups[0].shape[2]
    return pl.pallas_call(
        partial(rows_kernel, top),
        out_shape=jax.ShapeDtypeStruct((count, rows, columns), groups[0].dtype),
        in_specs=[pl.BlockSpec(memory_space=pltpu.SMEM)]
        + [pl.BlockSpec(memory_space=pl.ANY)] * len(groups),
        out_specs=pl.BlockSpec(memory_space=pltpu.VMEM),
        scratch_shapes=[pltpu.SemaphoreType.DMA((count,))],
        name="place",
    )(places, *groups)


class Gather:
    def __init__(self, chunks, dims, at):
        self.dims, self.chunks = dims, chunks
        self.held = [[value[None]] for value in chunks]
        self.arrived, self.step = [], 0
        owners = jnp.zeros((1,), jnp.int32)
        for dim in range(len(dims)):
            steps = jnp.arange(dims[dim], dtype=jnp.int32)
            own = ((at[dim] - steps) % dims[dim]) * math.prod(dims[dim + 1 :])
            owners = (own[:, None] + owners[None, :]).reshape(-1)
        self.owners = owners

    def until(self, number):
        while self.step < number + len(self.dims):
            self.advance()
        return self.held[number]

    def advance(self, *earlier):
        sends, takers = [], []
        for dim in range(len(self.dims)):
            number = self.step - dim
            if 0 <= number < len(self.chunks):
                for steps in range(1, self.dims[dim]):
                    for group in self.held[number]:
                        sends.append((group, dim, steps))
                        takers.append(number)
        self.arrived = stage(sends, self.dims, [*self.arrived, *earlier])
        for number in sorted(set(takers)):
            got = [value for value, taker in zip(self.arrived, takers) if taker == number]
            if self.step - number < len(self.dims) - 2:
                self.held[number] = [jnp.concatenate(self.held[number] + got)]
            else:
                self.held[number] = self.held[number] + got
        self.step += 1


def scatter_rows_plain(left, right, dims, dp_index):
    count = math.prod(dims)
    at = [
        (dp_index // math.prod(dims[dim + 1 :])) % dims[dim] for dim in range(len(dims))
    ]
    samples, height = left.shape
    rows, columns = height // count, right.shape[1]
    split = left.reshape(samples, count // 2, 2, rows)
    for_other = lax.dynamic_index_in_dim(split, 1 - at[-1], 2, False).reshape(samples, -1)
    for_self = lax.dynamic_index_in_dim(split, at[-1], 2, False).reshape(samples, -1)
    sent = product_tn(for_other, right).astype(jnp.bfloat16)
    total = product_tn(for_self, right) + shifted(sent, dims, len(dims) - 1, 1).astype(jnp.float32)
    for dim in reversed(range(len(dims) - 1)):
        low = total.astype(jnp.bfloat16).reshape(-1, dims[dim], rows, columns)
        total = lax.dynamic_index_in_dim(low, at[dim], 1, False).astype(jnp.float32)
        for steps in range(1, dims[dim]):
            part = lax.dynamic_index_in_dim(low, (at[dim] + steps) % dims[dim], 1, False)
            total = total + shifted(part, dims, dim, steps).astype(jnp.float32)
    return total.reshape(rows, columns)


def fetch_chosen(pick_ref, pair, place, target, sem):
    for wanted, ref in ((1, pair[0]), (0, pair[1])):

        @pl.when(pick_ref[0] == wanted)
        def _(ref=ref):
            pltpu.make_async_copy(ref.at[place], target, sem).start()

    return pltpu.make_async_copy(pair[0].at[place], target, sem)


def grad_kernel(pick_ref, *refs, rows, slots, outer, start, sends):
    lefts, rights, refs = (refs[0:2], refs[2:4]), (refs[4:6], refs[6:8]), refs[8:]
    if not sends:
        other_ref, *refs = refs
    out_refs, refs = refs[: 1 if sends else slots], refs[1 if sends else slots :]
    if sends:
        left, right, out, left_sems, right_sems, out_sems = refs
    else:
        left, right, other, out, left_sems, right_sems, other_sems, out_sems = refs
    chips, width = outer * slots, right.shape[1]
    samples = lefts[0][0].shape[0]
    side = 1 - pick_ref[1] if sends else pick_ref[1]
    thin = rows % 128 != 0
    block = min(BLOCK, width) if thin else width
    blocks = width // block
    wide_part = rights[0][0].shape[-1]

    def left_copies(number):
        if thin:
            place, target = (slice(None), slice(None)), slice(None)
        else:
            chip = number if sends else chip_of(number)
            place = (slice(None), pl.ds(pl.multiple_of((2 * chip + side) * rows, rows), rows))
            target = slice(number * rows, (number + 1) * rows)
        return [
            fetch_chosen(
                pick_ref,
                lefts[half],
                place,
                left.at[half * samples : (half + 1) * samples, target],
                left_sems.at[number, half],
            )
            for half in range(2)
        ]

    def right_copies(number):
        begin = start + number * block
        columns = pl.ds(begin % wide_part, block)
        place = (slice(None), columns)
        if len(rights[0][0].shape) == 3:
            place = (begin // wide_part, *place)
        at = slice(number * block, (number + 1) * block)
        return [
            fetch_chosen(
                pick_ref,
                rights[half],
                place,
                right.at[half * samples : (half + 1) * samples, at],
                right_sems.at[number, half],
            )
            for half in range(2)
        ]

    def chip_of(number):
        return (number % outer) * slots + lax.rem(pick_ref[2] + number // outer, slots)

    def other_copy(number):
        if thin:
            return pltpu.make_async_copy(
                other_ref.at[pl.ds(0, chips * rows), pl.ds(start + number * block, block)],
                other.at[:, number * block : (number + 1) * block],
                other_sems.at[number],
            )
        return pltpu.make_async_copy(
            other_ref.at[
                pl.ds(pl.multiple_of(chip_of(number) * rows, rows), rows), pl.ds(start, width)
            ],
            other.at[number * rows : (number + 1) * rows],
            other_sems.at[number],
        )

    def wait(copies):
        for copy in copies:
            copy.wait()

    leaving = []
    if thin:
        halves_of_left = left_copies(0)
        arriving = [right_copies(number) for number in range(blocks)]
        if not sends:
            others = [other_copy(number) for number in range(blocks)]
            for copy in others:
                copy.start()
        wait(halves_of_left)
        flipped = left[...].T
        turned = jnp.concatenate(
            [
                jnp.where(
                    side == 0,
                    flipped[2 * rows * chip : 2 * rows * chip + rows],
                    flipped[2 * rows * chip + rows : 2 * rows * (chip + 1)],
                )
                for chip in range(chips)
            ]
        )
        for number in range(blocks):
            at = slice(number * block, (number + 1) * block)
            wait(arriving[number])
            result = product(turned, right[:, at])
            if sends:
                out[:, at] = result.astype(LOW)
                leaving.append(
                    pltpu.make_async_copy(out.at[:, at], out_refs[0].at[:, at], out_sems.at[number])
                )
                leaving[-1].start()
                continue
            others[number].wait()
            out[:, at] = (result + other[:, at].astype(WIDE)).astype(LOW)
            for place in range(chips):
                leaving.append(
                    pltpu.make_async_copy(
                        out.at[pl.ds(pl.multiple_of(chip_of(place) * rows, rows), rows), at],
                        out_refs[place // outer].at[place % outer, :, at],
                        out_sems.at[number * chips + place],
                    )
                )
                leaving[-1].start()
    else:
        arriving = right_copies(0)
        pieces = [left_copies(number) for number in range(chips)]
        if not sends:
            others = [other_copy(number) for number in range(chips)]
            for copy in others:
                copy.start()
        wait(arriving)
        for number in range(chips):
            at = slice(number * rows, (number + 1) * rows)
            wait(pieces[number])
            result = product_tn(left[:, at], right[...])
            if sends:
                out[at] = result.astype(LOW)
                target = out_refs[0].at[at]
            else:
                others[number].wait()
                out[at] = (result + other[at].astype(WIDE)).astype(LOW)
                target = out_refs[number // outer].at[number % outer]
            leaving.append(pltpu.make_async_copy(out.at[at], target, out_sems.at[number]))
            leaving[-1].start()
    wait(leaving)


def fold_kernel(pick_ref, held_ref, other_ref, out_ref, *send_refs, slots, thin_rows):
    for slot in range(slots):
        place = lax.rem(pick_ref[0] + slot, slots)
        for number in range(out_ref.shape[0]):
            index = number * slots + place
            value = held_ref[index].astype(WIDE) + other_ref[index].astype(WIDE)
            if slot == 0:
                out_ref[number] = value
                continue
            send_refs[slot - 1][number] = value.astype(LOW)
            if thin_rows:
                pair = value[thin_rows : thin_rows + 1] + value[thin_rows + 1 : thin_rows + 2]
                high, low = halves(pair)
                ids = lax.broadcasted_iota(jnp.int32, (16, value.shape[1]), 0)
                send_refs[slot - 1][number, thin_rows:] = jnp.where(
                    ids == 0, high.astype(WIDE), jnp.where(ids == 1, low.astype(WIDE), 0.0)
                ).astype(LOW)


def terms(value):
    high = lax.reduce_precision(value, 8, 7)
    return high.astype(LOW), (value - high).astype(LOW)


class Scatter:
    def __init__(self, name, lefts, rights, dims, at, first):
        self.name, self.lefts, self.rights, self.dims, self.at = name, lefts, rights, dims, at
        self.count = math.prod(dims)
        self.height = lefts[0][0].shape[1]
        self.rows = self.height // self.count
        sample = rights[0][0]
        self.columns = sample.shape[-1] * (3 if sample.ndim == 3 else 1)
        self.pick = jnp.stack([first, at[-1], at[-2]])

    def product(self, start, width, other, quick=False):
        samples = self.lefts[0][0].shape[0]
        half, rows, slots = self.height // 2, self.rows, self.dims[-2]
        chips = self.count // 2
        outer = chips // slots
        sends = other is None
        thin = rows % 128 != 0
        blocks = width // min(BLOCK, width) if thin else 1
        pieces = 1 if thin else chips
        anywhere = pl.BlockSpec(memory_space=pl.ANY)
        args = [*self.lefts[0], *self.lefts[1], *self.rights[0], *self.rights[1]]
        args += [] if sends else [other]
        out_sems = blocks * (1 if sends else chips) if thin else chips
        other_scratch = [] if sends else [pltpu.VMEM((half, width), LOW)]
        other_sems = [] if sends else [pltpu.SemaphoreType.DMA((blocks if thin else chips,))]
        outs = [(half, width)] if sends else [(outer, rows, width)] * slots
        return pl.pallas_call(
            partial(
                grad_kernel, rows=rows, slots=slots, outer=outer, start=start, sends=sends
            ),
            in_specs=[pl.BlockSpec(memory_space=pltpu.SMEM)] + [anywhere] * len(args),
            out_specs=[anywhere] * len(outs),
            out_shape=[jax.ShapeDtypeStruct(out, LOW) for out in outs],
            scratch_shapes=[
                pltpu.VMEM((2 * samples, self.height if thin else half), LOW),
                pltpu.VMEM((2 * samples, width), LOW),
                *other_scratch,
                pltpu.VMEM((half, width), LOW),
                pltpu.SemaphoreType.DMA((pieces, 2)),
                pltpu.SemaphoreType.DMA((blocks, 2)),
                *other_sems,
                pltpu.SemaphoreType.DMA((out_sems,)),
            ],
            compiler_params=pltpu.CompilerParams(vmem_limit_bytes=VMEM_LIMIT),
            cost_estimate=NO_COST if sends or quick else FULL_COST,
            name=self.name + ("_send" if sends else "_keep"),
        )(self.pick, *args)

    def send(self, extra=None):
        sent = self.product(0, self.columns, None)[0]
        self.extra = None
        if extra is not None:
            split = extra.reshape(-1, 2, extra.shape[1])
            sent = jnp.concatenate(
                [sent, *terms(lax.dynamic_index_in_dim(split, 1 - self.at[-1], 1, False))]
            )
        self.other = shifted(sent, self.dims, len(self.dims) - 1, 1)
        if extra is not None:
            held = lax.dynamic_index_in_dim(split, self.at[-1], 1, False)
            arrived = self.other[self.height // 2 :].astype(WIDE)
            held = held + arrived[: held.shape[0]] + arrived[held.shape[0] :]
            rows = jnp.stack(terms(held), axis=1)
            rows = jnp.pad(rows, [(0, 0), (0, 14), (0, 0)])
            self.extra = rows.reshape(-1, self.dims[-2], 16, extra.shape[1])

    def keep(self, start, width, quick=False):
        pieces = self.product(start, width, self.other, quick)
        if self.extra is not None:
            pieces = [
                jnp.concatenate(
                    [
                        piece,
                        lax.dynamic_index_in_dim(
                            self.extra, (self.at[-2] + slot) % self.dims[-2], 1, False
                        ),
                    ],
                    axis=1,
                )
                for slot, piece in enumerate(pieces)
            ]
        return pieces


def folded(held, moved, dims, dim, at, thin_rows):
    outer, rows, columns = held.shape
    slots = dims[dim]
    if rows % 16 == 0 and len(moved) == 1:
        whole = pl.BlockSpec(memory_space=pltpu.VMEM)
        shape = (outer // slots, rows, columns)
        total, *sends = pl.pallas_call(
            partial(fold_kernel, slots=slots, thin_rows=thin_rows),
            out_shape=[jax.ShapeDtypeStruct(shape, WIDE)]
            + [jax.ShapeDtypeStruct(shape, LOW)] * (slots - 1),
            in_specs=[pl.BlockSpec(memory_space=pltpu.SMEM), whole, whole],
            out_specs=[whole] * slots,
            compiler_params=pltpu.CompilerParams(vmem_limit_bytes=24 << 20),
            cost_estimate=NO_COST,
            name="fold",
        )(at[dim][None], held, moved[0])
        return total, sends
    total = held.astype(WIDE)
    for piece in moved:
        total = total + piece.astype(WIDE)
    split = total.reshape(outer // slots, slots, rows, columns)
    blocks = [
        lax.dynamic_index_in_dim(split, (at[dim] + steps) % slots, 1, False)
        for steps in range(slots)
    ]
    return blocks[0], [block.astype(LOW) for block in blocks[1:]]


def travels(makers, dims, at, own_rows, before):
    chip_dims = list(reversed(range(len(dims) - 1)))
    held, sends, sums = {}, {}, {}
    arrived = []
    for step in range(len(makers) + len(chip_dims) - 1):
        if step < len(makers):
            held[step], *sends[step] = makers[step](arrived)
        outgoing, takers = [], []
        for phase, dim in enumerate(chip_dims):
            number = step - phase
            if 0 <= number < len(makers):
                outgoing += [(value, dim, k) for k, value in enumerate(sends[number], start=1)]
                takers += [number] * len(sends[number])
        arrived = stage(outgoing, dims, [*arrived, *before.get(step, lambda _: ())(arrived)])
        for phase, dim in enumerate(chip_dims):
            number = step - phase
            if 0 <= number < len(makers):
                moved = [value for value, taker in zip(arrived, takers) if taker == number]
                if dim:
                    rows = held[number].shape[1]
                    held[number], sends[number] = folded(
                        held[number], moved, dims, dim - 1, at, own_rows if rows == own_rows + 16 else 0
                    )
                else:
                    total = held[number].astype(WIDE)
                    for piece in moved:
                        total = total + piece.astype(WIDE)
                    sums[number] = total.reshape(total.shape[-2:])
    return [sums[number] for number in range(len(makers))]


def spread(value, count):
    return lax.all_to_all(
        jnp.broadcast_to(value[None], (count, *value.shape)), "dp", 0, 0, tiled=True
    )


def summed(parts):
    return jnp.sum(lax.all_to_all(parts, "dp", 0, 0, tiled=True).astype(jnp.float32), axis=0)


def halves(value):
    high = value.astype(jnp.bfloat16)
    return high, (value - high.astype(jnp.float32)).astype(jnp.bfloat16)


def exact_product(left_side, right_side):
    high, low = halves(right_side)
    return product(left_side, high) + product(left_side, low)


def product_by_ones(left_side, right_side):
    high, low = halves(left_side)
    return product(high, right_side) + product(low, right_side)


def prefix_masks(length):
    places = lax.broadcasted_iota(jnp.int32, (1, length), 1)
    return [places < width for width in PREFIXES]


def similar_parts(documents, queries_t):
    docs_f32 = documents.astype(jnp.float32)
    squares = docs_f32 * docs_f32
    query_squares = queries_t * queries_t
    queries_low = queries_t.astype(jnp.bfloat16)
    parts = []
    for width, mask in zip(PREFIXES, prefix_masks(PROJ)):
        cut = jnp.where(mask, docs_f32, 0.0)
        doc_scale = lax.rsqrt(
            jnp.sum(jnp.where(mask, squares, 0.0), axis=1, keepdims=True) + unit_eps
        )
        query_scale = lax.rsqrt(
            jnp.sum(query_squares[:width], axis=0, keepdims=True) + unit_eps
        )
        cut = cut.astype(jnp.bfloat16)
        similar = product(cut, queries_low) * doc_scale * query_scale
        parts.append((cut, doc_scale, query_scale, similar))
    return parts


def members_of(ends_ref, micro_step, by_row):
    shape = (DOC_ROWS, 8) if by_row else (8, DOC_ROWS)
    rows = lax.broadcasted_iota(jnp.int32, shape, 0 if by_row else 1)
    docs = lax.broadcasted_iota(jnp.int32, shape, 1 if by_row else 0)
    inside = jnp.zeros(shape, jnp.float32)
    for number in range(DOCS_DEV):
        begin = ends_ref[micro_step, number - 1] if number else 0
        held = (docs == number) & (rows >= begin) & (rows < ends_ref[micro_step, number])
        inside = jnp.where(held, 1.0, inside)
    return inside.astype(jnp.bfloat16)


def query_of_token(tokens, by_token):
    shape = (tokens, 128) if by_token else (128, tokens)
    token = lax.broadcasted_iota(jnp.int32, shape, 0 if by_token else 1)
    query = lax.broadcasted_iota(jnp.int32, shape, 1 if by_token else 0)
    held = (token >= query * QLEN) & (token < query * QLEN + QLEN)
    return jnp.where(held, 1.0, 0.0).astype(jnp.bfloat16)


def score_kernel(ends_ref, queries_ref, docs_ref, out_ref, *, micro_step):
    tokens = queries_ref.shape[0] * queries_ref.shape[1]
    queries_t = queries_ref[...].astype(WIDE).reshape(tokens, PROJ).T
    members = members_of(ends_ref, micro_step, False)
    by_query = query_of_token(tokens, True)
    for number, (_, _, _, similar) in enumerate(similar_parts(docs_ref[:DOC_ROWS], queries_t)):
        masses = exact_product(members, jnp.exp(sharpness * similar))
        held = lax.broadcasted_iota(jnp.int32, masses.shape, 0) < DOCS_DEV
        logs = jnp.log(jnp.where(held, masses, 1.0))
        out_ref[0, number] = product_by_ones(logs, by_query) / sharpness


def loss_kernel(
    ends_ref, where_ref, queries_ref, docs_ref, tables_ref, times_ref, first_ref,
    loss_ref, grad_queries_ref, grad_docs_ref, table, *, micro_step
):
    step = pl.program_id(0)
    devices, width = queries_ref.shape[:2]
    tokens = devices * width
    queries_t = queries_ref[...].astype(WIDE).reshape(tokens, PROJ).T
    queries_low = queries_t.astype(LOW)
    members = members_of(ends_ref, micro_step, False)
    members_by_row = members_of(ends_ref, micro_step, True)
    spread_out = query_of_token(tokens, False)
    places = lax.broadcasted_iota(jnp.int32, (PROJ, 1), 0)
    grad_queries = jnp.zeros((PROJ, tokens), WIDE)
    grad_docs = jnp.zeros((DOC_ROWS, PROJ), WIDE)
    losses = jnp.zeros((1, 128), WIDE)
    times, first = times_ref[0], first_ref[0]
    own_rows = pl.ds(pl.multiple_of(where_ref[0] * 8, 8), 8)
    own_times, own_first = times_ref[0, own_rows], first_ref[0, own_rows]
    table[...] = jnp.zeros_like(table)
    for number, (cut, doc_scale, query_scale, similar) in enumerate(
        similar_parts(docs_ref[:DOC_ROWS], queries_t)
    ):
        for device in range(table.shape[0] // 8):
            table[8 * device : 8 * device + DOCS_DEV] = tables_ref[device, 0, number]
        scores = table[...]
        top = jnp.max(jnp.where(times > 0, scores, -1e30), axis=0, keepdims=True)
        top = jnp.where(top > -1e29, top, 0.0)
        normal = top + jnp.log(
            jnp.maximum(
                jnp.sum(times * jnp.exp(jnp.minimum(scores - top, 0.0)), axis=0, keepdims=True),
                1e-30,
            )
        )
        losses = losses + normal - jnp.sum(first * scores, axis=0, keepdims=True)
        own = table[own_rows]
        grad_score = own_times * jnp.exp(jnp.where(own_times > 0, own - normal, 0.0)) - own_first
        weights = jnp.exp(sharpness * similar)
        masses = exact_product(members, weights)
        by_token = product_by_ones(grad_score, spread_out)
        held = lax.broadcasted_iota(jnp.int32, masses.shape, 0) < DOCS_DEV
        by_token = jnp.where(held, by_token / jnp.where(held, masses, 1.0), 0.0)
        grad_similar = weights * exact_product(members_by_row, by_token)
        along = grad_similar * similar
        pulled = (grad_similar * doc_scale * query_scale).astype(LOW)
        mask = lax.broadcasted_iota(jnp.int32, (1, PROJ), 1) < PREFIXES[number]
        grad_docs = (
            grad_docs
            + jnp.where(mask, product_nt(pulled, queries_low), 0.0)
            - cut.astype(WIDE) * (doc_scale * doc_scale * jnp.sum(along, axis=1, keepdims=True))
        )
        toward = product_tn(cut, pulled)
        back = queries_t * (query_scale * query_scale * jnp.sum(along, axis=0, keepdims=True))
        grad_queries = grad_queries + toward - jnp.where(places < PREFIXES[number], back, 0.0)
    loss_ref[0] = losses
    grad_queries_ref[...] = grad_queries.T.reshape(devices, width, PROJ).astype(LOW)

    @pl.when(step == 0)
    def _():
        grad_docs_ref[...] = grad_docs

    @pl.when(step > 0)
    def _():
        grad_docs_ref[...] += grad_docs


class Loss:
    def __init__(self, micro_step, ends, pair_rows, dp_index, count):
        self.micro_step, self.ends, self.dp_index, self.count = micro_step, ends, dp_index, count
        self.group = math.gcd(count, 16)
        self.steps = count // self.group
        place = jnp.arange(8 * count, dtype=jnp.int32)
        doc_ids = jnp.where(place % 8 < DOCS_DEV, place // 8 * DOCS_DEV + place % 8, -1)
        picked = (pair_rows[None, :, :] == doc_ids[:, None, None]).astype(WIDE)
        self.times, self.first = [
            jnp.pad(
                jnp.swapaxes(value.reshape(8 * count, self.steps, -1), 0, 1),
                [(0, 0), (0, 0), (0, 128 - self.group * QRY_DEV)],
            )
            for value in (jnp.sum(picked, axis=2), picked[..., 0])
        ]
        self.params = dict(
            grid=(self.steps,), compiler_params=pltpu.CompilerParams(vmem_limit_bytes=VMEM_LIMIT)
        )
        self.queries_spec = pl.BlockSpec((self.group, QRY_DEV * QLEN, PROJ), lambda i: (i, 0, 0))
        self.smem = pl.BlockSpec(memory_space=pltpu.SMEM)

    def scores(self, embedded):
        self.embedded = embedded
        self.queries = spread(embedded[DOC_ROWS:], self.count)
        return pl.pallas_call(
            partial(score_kernel, micro_step=self.micro_step),
            out_shape=jax.ShapeDtypeStruct((self.steps, 3, 8, 128), WIDE),
            in_specs=[
                self.smem,
                self.queries_spec,
                pl.BlockSpec((ROWS, PROJ), lambda i: (0, 0)),
            ],
            out_specs=pl.BlockSpec((1, 3, 8, 128), lambda i: (i, 0, 0, 0)),
            name="scores",
            cost_estimate=NO_COST,
            **self.params,
        )(self.ends, self.queries, embedded)[:, :, :DOCS_DEV]

    def grads(self, tables, *earlier):
        losses, grad_queries, grad_docs = pl.pallas_call(
            partial(loss_kernel, micro_step=self.micro_step),
            out_shape=(
                jax.ShapeDtypeStruct((self.steps, 1, 128), WIDE),
                jax.ShapeDtypeStruct(self.queries.shape, LOW),
                jax.ShapeDtypeStruct((DOC_ROWS, PROJ), WIDE),
            ),
            in_specs=[
                self.smem,
                self.smem,
                self.queries_spec,
                pl.BlockSpec((ROWS, PROJ), lambda i: (0, 0)),
                pl.BlockSpec((self.count, 1, 3, DOCS_DEV, 128), lambda i: (0, i, 0, 0, 0)),
                pl.BlockSpec((1, 8 * self.count, 128), lambda i: (i, 0, 0)),
                pl.BlockSpec((1, 8 * self.count, 128), lambda i: (i, 0, 0)),
            ],
            out_specs=(
                pl.BlockSpec((1, 1, 128), lambda i: (i, 0, 0)),
                self.queries_spec,
                pl.BlockSpec((DOC_ROWS, PROJ), lambda i: (0, 0)),
            ),
            scratch_shapes=[pltpu.VMEM((8 * self.count, 128), WIDE)],
            name="losses",
            cost_estimate=NO_COST,
            **self.params,
        )(
            self.ends,
            self.dp_index[None],
            self.queries,
            after(self.embedded, *earlier),
            tables,
            self.times,
            self.first,
        )
        losses = losses[:, 0, : self.group * QRY_DEV].reshape(self.count * QRY_DEV)
        own = lax.dynamic_slice_in_dim(losses, self.dp_index * QRY_DEV, QRY_DEV, 0)
        return own, grad_queries, grad_docs


def shards(
    tokens,
    qkv_weight,
    qkv_bias,
    out_weight,
    out_bias,
    norm1_gain,
    norm1_bias,
    up_weight,
    up_bias,
    down_weight,
    down_bias,
    norm2_gain,
    norm2_bias,
    proj_weight,
    doc_lengths,
    pair_docs,
):
    section_index = lax.axis_index("section")
    dp_index = lax.axis_index("dp")
    count = lax.axis_size("dp")
    dims = grid_of(count)
    at = coordinates(dims, dp_index)
    is_first = section_index == 0
    first = is_first.astype(jnp.int32)
    width, hidden = tokens.shape[1], up_weight.shape[2]
    own_height = width // count
    by_hand = own_height % 16 == 0

    segments, positions = [
        jnp.stack(value)
        for value in zip(*(doc_layout(doc_lengths[micro_step]) for micro_step in range(MICRO)))
    ]
    layout = (*rotary(positions), segments[:, :, None], segments[:, None, :])
    picks = [jnp.stack([first, jnp.int32(micro_step)]) for micro_step in range(MICRO)]
    own_rows = [tokens[micro_step * ROWS : (micro_step + 1) * ROWS] for micro_step in range(MICRO)]
    ends = jnp.cumsum(doc_lengths, axis=1)
    pair_rows = pair_docs.reshape(count, MICRO, QRY_DEV, CANDS)
    losses_of = [
        Loss(
            micro_step,
            ends,
            pair_rows[:, micro_step].reshape(count * QRY_DEV, CANDS),
            dp_index,
            count,
        )
        for micro_step in range(MICRO)
    ]

    vectors = (
        qkv_bias,
        out_bias,
        norm1_gain,
        norm1_bias,
        up_bias,
        down_bias,
        norm2_gain,
        norm2_bias,
    )
    lengths = [value.shape[1] for value in vectors]
    short = sum(lengths)
    shards_of = [out_weight[0], qkv_weight[0], up_weight[0], down_weight[0]]

    fetched = (width, width, hidden // 4, width // 2)

    def small_parameters(layer, rows, projection):
        cuts, start = [], 0
        for length in lengths:
            cuts.append(rows[:, start : start + length].astype(WIDE).reshape(-1))
            start += length
        qkv_b, out_b, gain_one, bias_one, up_b, down_b, gain_two, bias_two = cuts
        layer.qkv_bias = qkv_b.reshape(3, width)
        layer.up_bias = up_b[None]
        layer.small = jnp.concatenate(
            [
                jnp.stack([out_b, gain_one, bias_one, down_b, gain_two, bias_two]),
                jnp.zeros((2, width), WIDE),
            ]
        )
        return projection.reshape(width, -1)

    if by_hand:
        line = jnp.concatenate([*vectors, jnp.zeros((1, width - short), LOW)], axis=1)
        proj_lines = proj_weight.reshape(-1, width)
        filler = jnp.zeros((15 - proj_lines.shape[0], width), LOW)
        chunks = [jnp.concatenate([shards_of[0], line, proj_lines, filler])]
        cuts_of = ([1], [1, 2], [2, 2], [2, 2])
        for number in (1, 2, 3):
            parts, shard = cuts_of[number], shards_of[number]
            unit, start = shard.shape[1] // sum(parts), 0
            for part in parts:
                chunks.append(lax.slice_in_dim(shard, start, start + part * unit, axis=1))
                start += part * unit
        gather = Gather(chunks, dims, at)
        layer = Layer(gather.owners, layout)

        def whole(number, first_chunk):
            parts, start = [], 0
            unit = shards_of[number].shape[1] // sum(cuts_of[number])
            for offset, part in enumerate(cuts_of[number]):
                parts.append((start, part * unit, gather.until(first_chunk + offset)))
                start += part * unit
            return Weight(gather.owners, shards_of[number].shape[0], start, fetched[number], parts)

        layer.out = whole(0, 0)
        block = placed_rows(layer.out.arrays, gather.owners, own_height, 16)
        projection = small_parameters(
            layer, block[:, 0], block[:, 1 : 1 + proj_lines.shape[0]]
        )
        layer.qkv = whole(1, 1)
        states = [layer.attend(rows, pick) for rows, pick in zip(own_rows, picks)]
        gather.advance()
        gather.advance(states[0]["norm"])
        layer.up = whole(2, 3)
        for state, pick in zip(states, picks):
            state |= layer.rise(state["norm"], pick)
        gather.advance(states[1]["norm"])
        gather.advance(*(state["active"] for state in states))
        layer.down = whole(3, 5)
    else:
        layer = Layer(jnp.zeros((1,), jnp.int32), layout)
        wholes = [
            lax.all_gather(value, "dp", axis=0, tiled=True)[None] for value in shards_of
        ]
        layer.out, layer.qkv, layer.up, layer.down = [
            Weight(layer.places, *value.shape[1:], columns, [(0, value.shape[2], [value])])
            for value, columns in zip(wholes, fetched)
        ]
        together = spread(jnp.concatenate([*vectors, proj_weight.reshape(1, -1)], axis=1)[0], count)
        projection = small_parameters(layer, together[:, :short], together[:, short:])
        states = [layer.attend(rows, pick) for rows, pick in zip(own_rows, picks)]
        for state, pick in zip(states, picks):
            state |= layer.rise(state["norm"], pick)

    arrived = []
    for state, pick in zip(states, picks):
        active = after(state["active"], *(one["result"] for one in states if "result" in one))
        state |= layer.fall(active, state["norm"], pick)
        arrived.append(from_behind(state["result"], "section", 1))
    own_scores = []
    for micro_step in range(MICRO):
        last = micro_step == MICRO - 1
        states.append(
            layer.forward(
                arrived[micro_step],
                picks[micro_step],
                projection,
                [state["result"] for state in states] if last else (),
            )
        )
        own_scores.append(losses_of[micro_step].scores(states[-1]["embedded"]))
    activations = states[-1]["activations"][None]

    tables = spread(jnp.stack(own_scores), count)
    own_losses, loss_grads = [None] * MICRO, [None] * MICRO
    earlier = []
    for micro_step in reversed(range(MICRO)):
        own_losses[micro_step], grad_queries, grad_docs = losses_of[micro_step].grads(
            tables[:, micro_step], *earlier
        )
        earlier = [grad_queries]
        loss_grads[micro_step] = (
            grad_docs,
            lax.all_to_all(grad_queries, "dp", 0, 0, tiled=True),
            projection,
        )
    own_losses = jnp.concatenate(own_losses)

    back, back_grads = [], []
    for micro_step in reversed(range(MICRO)):
        back.append(
            layer.backward(states[MICRO + micro_step], loss_grads[micro_step], None, picks[micro_step])
        )
        back_grads.append(from_behind(back[-1]["grad_low"], "section", -1))
    def exchanged(earlier):
        proj_total = product_tn(
            jnp.concatenate([state["result"] for state in states[:1:-1]]),
            after(jnp.concatenate([grads["grad_embedded"] for grads in back[:MICRO]]), *earlier),
        ) * section_index.astype(WIDE)
        proj_parts = proj_total.reshape(2, count, -1, proj_total.shape[1])
        proj_own = summed(jnp.swapaxes(proj_parts, 0, 1))
        proj_other, loss_other = [
            from_behind(value, "section", -1) for value in (proj_own[0], after(own_losses, *earlier))
        ]
        return (
            jnp.where(is_first, proj_other, proj_own[1]),
            jnp.where(is_first, loss_other, own_losses),
        )

    back.append(layer.backward(states[1], None, back_grads[0], picks[1]))
    back_grad = after(back_grads[1], back[-1]["mixed"])
    grads = layer.feed_back(states[0], back_grad, picks[0])

    def pairs(values):
        return [values[1], values[3]], [values[0], values[2]]

    lefts = [
        pairs([state[name] for state in states]) for name in ("active", "norm", "mixture")
    ] + [pairs([*own_rows, *arrived])]

    def rights_of(name):
        return pairs([grads[name], *(back[number][name] for number in (2, 1, 0))])

    def scatter(name, number, right):
        return Scatter(name, lefts[number], rights_of(right), dims, at, first)

    attended = grads["attended"]
    if by_hand:
        of_down, of_up = scatter("down", 0, "branch"), scatter("up", 1, "gate")
        of_down.send()
        of_up.send()
        down_first = of_down.keep(0, width // 2)
        attended = after(attended, *down_first)
    grads |= layer.attend_back(
        states[0], attended, grads["grad_one"], [one["grad_source"] for one in back], picks[0]
    )
    grad_inputs = grads["grad_source"]
    grad_vectors = [
        (
            one["qkv_vectors"][:3].reshape(-1),
            *(one["vectors"][number] for number in range(3)),
            one["grad_up_bias"][0],
            *(one["vectors"][number] for number in range(3, 6)),
        )
        for one in (*back, grads)
    ]
    totals = [sum(values) for values in zip(*grad_vectors)]
    packed = jnp.concatenate([value.reshape(count, -1) for value in totals], axis=1)
    if by_hand:
        of_out, of_qkv = scatter("out", 2, "attended"), scatter("qkv", 3, "mixed")
        of_qkv.send()
        of_out.send(jnp.pad(packed, [(0, 0), (0, width - packed.shape[1])]))

        def maker(weight, start, columns, quick=False):
            return lambda arrived: weight.keep(start, columns, quick)

        shared = []

        def exchange(arrived):
            shared.extend(exchanged(arrived))
            return ()

        sums = travels(
            [
                lambda arrived: down_first,
                maker(of_down, width // 2, width // 2, True),
                maker(of_up, 0, hidden // 2, True),
                maker(of_up, hidden // 2, hidden // 2),
                maker(of_qkv, 0, 2 * width),
                maker(of_qkv, 2 * width, width),
                maker(of_out, 0, width),
            ],
            dims,
            at,
            own_height,
            {1: lambda _: [grads["mixed"]], 5: exchange, 7: lambda _: shared},
        )
        proj_grad, query_losses = shared
        grad_down, grad_up, grad_qkv = (
            jnp.concatenate(group, axis=1)[None] for group in (sums[0:2], sums[2:4], sums[4:6])
        )
        grad_out, own = sums[6][None, :own_height], sums[6][own_height] + sums[6][own_height + 1]
    else:
        weight_grads = []
        for number, name in enumerate(("branch", "gate", "attended", "mixed")):
            left = jnp.concatenate([jnp.where(is_first, *pair) for pair in lefts[number]])
            right = [jnp.where(is_first, *pair) for pair in rights_of(name)]
            if number == 3:
                right = [jnp.swapaxes(value, 0, 1).reshape(ROWS, -1) for value in right]
            weight_grads.append(
                scatter_rows_plain(left, jnp.concatenate(right), dims, dp_index)[None]
            )
        grad_down, grad_up, grad_out, grad_qkv = weight_grads
        own = summed(packed)
        proj_grad, query_losses = exchanged(())
    small_grads, start = [], 0
    for length in lengths:
        small_grads.append(own[None, start : start + length])
        start += length
    grad_qkv_b, grad_out_b, grad_gain1, grad_bias1, grad_up_b, grad_down_b, grad_gain2, grad_bias2 = (
        small_grads
    )
    return (
        query_losses,
        activations,
        grad_inputs[None],
        grad_qkv,
        grad_qkv_b,
        grad_out,
        grad_out_b,
        grad_gain1,
        grad_bias1,
        grad_up,
        grad_up_b,
        grad_down,
        grad_down_b,
        grad_gain2,
        grad_bias2,
        proj_grad,
    )


def solution(mesh):
    in_specs = (
        P("dp", None),
        P("section", "dp", None),
        P("section", "dp"),
        P("section", "dp", None),
        P("section", "dp"),
        P("section", "dp"),
        P("section", "dp"),
        P("section", "dp", None),
        P("section", "dp"),
        P("section", "dp", None),
        P("section", "dp"),
        P("section", "dp"),
        P("section", "dp"),
        P("dp", None),
        P("dp", None),
        P(),
    )
    out_specs = (
        P("dp"),
        P("section", "dp", None),
        P("section", "dp", None),
        P("section", "dp", None),
        P("section", "dp"),
        P("section", "dp", None),
        P("section", "dp"),
        P("section", "dp"),
        P("section", "dp"),
        P("section", "dp", None),
        P("section", "dp"),
        P("section", "dp", None),
        P("section", "dp"),
        P("section", "dp"),
        P("section", "dp"),
        P(("section", "dp"), None),
    )
    return jax.shard_map(shards, mesh=mesh, in_specs=in_specs, out_specs=out_specs, check_vma=False)
```

time: 923 us -> 698 us (0.76)
  Pallas kernels: 29.1 us -> 306 us
  matrix products: 211 us -> 0.47 us
  waiting for transfers between devices: 347 us -> 197 us
  local copies, waits for them, and re-layouts: 110 us -> 31.4 us
  other arithmetic: 86.6 us -> 39.3 us
  starting transfers between devices: 129 us -> 113 us
    pallas_call x6 -> x43, Pallas kernels: 29.1 us -> 306 us  [the longest x13 222 us: run_parts(): pl.pallas_call(kernel, in_specs=[pl.BlockSpec(memory_space=pltpu.SMEM)] *...]
    dot_general x41 -> x0, matrix products: 157 us -> none  [the longest x13 68.7 us: product(): return jnp.dot(left_side, right_side, preferred_element_type=jnp.float32)]
    ppermute x44 -> x60, waiting for transfers between devices: 301 us -> 155 us  [shifted(): return lax.ppermute(value, 'dp', pairs)]
    dot_general x9 -> x1, matrix products: 38.4 us -> 0.47 us  [product_tn(): lax.dot_general(left_side, right_side, (((0,), (0,)), ((), ())), preferre...]
    unnamed x370 -> x219, local copies, waits for them, and re-layouts: 43.1 us -> 11.7 us
    slice x20 -> x8, local copies, waits for them, and re-layouts: 24 us -> 3.78 us  [the longest x1 1.11 us: shards(): tables[:, micro_step]]
    another operation x16 -> x10, other arithmetic: 20.2 us -> 0.8 us  [the longest x4 9.24 us: gather_rows(): jnp.stack([shard] + [shifted(shard, dims, 0, steps) for steps in range(1,...]
    reduce_sum x26 -> x1, other arithmetic: 19.2 us -> 0.2 us  [__init__(): jnp.sum(picked, axis=2)]
  transfers between devices with their start and end apart: 56 -> 72, of which waited for: 20 -> 40; matrix products, arithmetic and copies ran while one was open for 21% -> 5% of each run, Pallas kernels for 1% -> 36%
where the time goes in v2:
time: 698 us; the launch traced here: 689 us
  Pallas kernels  306 us (44%)
  waiting for transfers between devices  197 us (28%)
  starting transfers between devices  113 us (16%)
  other arithmetic  39.3 us (6%)
  local copies, waits for them, and re-layouts  31.4 us (4%)
    pallas_call x13, Pallas kernels, run_parts(): pl.pallas_call(kernel, in_specs=[pl.BlockSpec(memory_space=pltpu.SMEM)] *...  222 us
    ppermute x60, waiting for transfers between devices, shifted(): return lax.ppermute(value, 'dp', pairs)  155 us
    ppermute x60, starting transfers between devices, shifted(): return lax.ppermute(value, 'dp', pairs)  78.9 us
    pallas_call x11, Pallas kernels, product(): pl.pallas_call(partial(grad_kernel, rows=rows, slots=slots, outer=outer,...  58.7 us
    all_to_all x3, waiting for transfers between devices, spread(): lax.all_to_all(jnp.broadcast_to(value[None], (count, *value.shape)), 'dp'...  24.4 us
    concatenate x14, other arithmetic, advance(): self.held[number] = [jnp.concatenate(self.held[number] + got)]  14.9 us
  transfers between devices with their start and end apart: 72, of which 40 were waited for; matrix products, arithmetic and copies ran while one was open for 5% of the time, Pallas kernels for 36%

profile of v2, /device:TPU:0, one launch (start us, length us, event | category | flops | bytes accessed | tf_op | source)
XLA Modules:
  0.0 689.2 jit_solution(12630233612775879703)
XLA Ops:
  3.4 4.1 collective-permute-start
  8.4 6.8 collective-permute-done
  15.3 4.1 collective-permute-start.2
  20.4 3.7 collective-permute-done.1
  24.0 4.4 collective-permute-done.2
  34.5 9.5 %collective-permute-done.3 = bf16[1,64,2048]{2,1,0:T(8,128)(2,1)S(1)} collective-permute-done((bf16[1,64,2048]{2,1,0:T(8,128)(2,1)S(1)}, bf16[1,64,2048]{2,1,0:T(8,128)(2,1)S(1)}, u32[]{:S(2)}, u32[]{:S(2)}) %collective-permute-start.3) | collective-permute-done | bytes 262176 | tf_op jit(solution)/shard_map/ppermute | solution.py:647
  47.8 3.4 collective-permute-start.6
  51.3 12.7 %collective-permute-done.6 = bf16[1,64,2048]{2,1,0:T(8,128)(2,1)} collective-permute-done((bf16[1,64,2048]{2,1,0:T(8,128)(2,1)}, bf16[1,64,2048]{2,1,0:T(8,128)(2,1)}, u32[]{:S(2)}, u32[]{:S(2)}) %collective-permute-start.6) | collective-permute-done | bytes 262176 | tf_op jit(solution)/shard_map/ppermute | solution.py:647
  78.6 12.2 %collective-permute-done.11 = bf16[1,64,2048]{2,1,0:T(8,128)(2,1)S(1)} collective-permute-done((bf16[1,64,2048]{2,1,0:T(8,128)(2,1)}, bf16[1,64,2048]{2,1,0:T(8,128)(2,1)S(1)}, u32[]{:S(2)}, u32[]{:S(2)}) %collective-permute-start.11) | collective-permute-done | bytes 262176 | tf_op jit(solution)/shard_map/ppermute | solution.py:647
  91.5 3.6 collective-permute-done.13.refs_14_.refs_16_.refs_19_.refs_41_.refs_39_.refs_23_
  105.7 13.8 %collective-permute-done.16 = bf16[1,256,512]{2,1,0:T(8,128)(2,1)S(1)} collective-permute-done((bf16[1,256,512]{2,1,0:T(8,128)(2,1)S(1)}, bf16[1,256,512]{2,1,0:T(8,128)(2,1)S(1)}, u32[]{:S(2)}, u32[]{:S(2)}) %collective-permute-start.16) | collective-permute-done | bytes 262176 | tf_op jit(solution)/shard_map/ppermute | solution.py:647
  129.5 2.6 place.1
  135.5 10.6 %attend.2 = (bf16[256,1024]{1,0:T(8,128)(2,1)}, bf16[256,1024]{1,0:T(8,128)(2,1)}, bf16[256,1024]{1,0:T(8,128)(2,1)}, bf16[256,1024]{1,0:T(8,128)(2,1)}, f32[256,1024]{1,0:T(8,128)}, /*index=5*/bf16[256,1024]{1,0:T(8,128)(2,1)}) custom-call(s32[2]{0:T(128)S(1)} %get-tuple-element.555.refs_0_, s32[16]{0:T(128)S(1)} %copy-done.53, ...), custom_call_target="tpu_custom_call" | custom-call | flops 1 | bytes 1 | tf_op jit(solution)/shard_map/attend/pallas_call | solution.py:248
  153.7 10.8 %attend.3 = (bf16[256,1024]{1,0:T(8,128)(2,1)}, bf16[256,1024]{1,0:T(8,128)(2,1)}, bf16[256,1024]{1,0:T(8,128)(2,1)}, bf16[256,1024]{1,0:T(8,128)(2,1)}, f32[256,1024]{1,0:T(8,128)}, /*index=5*/bf16[256,1024]{1,0:T(8,128)(2,1)}) custom-call(s32[2]{0:T(128)S(1)} %get-tuple-element.556.refs_0_, s32[16]{0:T(128)S(1)} %copy-done.53, ...), custom_call_target="tpu_custom_call" | custom-call | flops 1 | bytes 1 | tf_op jit(solution)/shard_map/attend/pallas_call | solution.py:248
  165.8 8.4 %collective-permute-done.27.refs_6_.refs_32_.refs_35_.refs_17_.refs_15_.refs_8_ = bf16[4,256,512]{2,1,0:T(8,128)(2,1)S(1)} collective-permute-done((bf16[4,256,512]{2,1,0:T(8,128)(2,1)S(1)}, bf16[4,256,512]{2,1,0:T(8,128)(2,1)S(1)}, u32[]{:S(2)}, u32[]{:S(2)}) %collective-permute-start.27) | collective-permute-done | bytes 1048608 | tf_op jit(solution)/shard_map/ppermute | solution.py:647
  176.7 11.0 %up.3 = (bf16[256,4096]{1,0:T(8,128)(2,1)}, bf16[256,4096]{1,0:T(8,128)(2,1)}) custom-call(s32[2]{0:T(128)S(1)} %get-tuple-element.556.refs_0_, s32[16]{0:T(128)S(1)} %copy-done.53, bf16[256,1024]{1,0:T(8,128)(2,1)S(1)} %copy-done.5, f32[1,4096]{1,0:T(1,128)S(1)} %bitcast.152, ...), custom_call_target="tpu_custom_call" | custom-call | flops 1 | bytes 1 | tf_op jit(solution)/shard_map/up/pallas_call | solution.py:248
  187.7 11.3 %up.2 = (bf16[256,4096]{1,0:T(8,128)(2,1)}, bf16[256,4096]{1,0:T(8,128)(2,1)}) custom-call(s32[2]{0:T(128)S(1)} %get-tuple-element.555.refs_0_, s32[16]{0:T(128)S(1)} %copy-done.53, bf16[256,1024]{1,0:T(8,128)(2,1)S(1)} %copy-done.3, f32[1,4096]{1,0:T(1,128)S(1)} %bitcast.153, ...), custom_call_target="tpu_custom_call" | custom-call | flops 1 | bytes 1 | tf_op jit(solution)/shard_map/up/pallas_call | solution.py:248
  204.3 7.3 %down.2 = (f32[256,1024]{1,0:T(8,128)}, bf16[256,1024]{1,0:T(8,128)(2,1)}) custom-call(s32[2]{0:T(128)S(1)} %get-tuple-element.555.refs_0_, s32[16]{0:T(128)S(1)} %copy-done.53, bf16[256,4096]{1,0:T(8,128)(2,1)} %get-tuple-element.314.refs_2_, bf16[256,1024]{1,0:T(8,128)(2,1)S(1)} %copy-done.3, f32[8,1024]{1,0:T(8,128)S(1)} %concatenate.107.refs_8_.refs_4_.refs_6_, ...), custom_call_target="tpu_custom_call" | custom-call | flops 1 | bytes 1 | tf_op jit(solution)/shard_map/down/pallas_call | solution.py:248
  211.7 3.4 collective-permute-start.35
  216.0 7.3 %down.3 = (f32[256,1024]{1,0:T(8,128)}, bf16[256,1024]{1,0:T(8,128)(2,1)}) custom-call(s32[2]{0:T(128)S(1)} %get-tuple-element.556.refs_0_, s32[16]{0:T(128)S(1)} %copy-done.53, bf16[256,4096]{1,0:T(8,128)(2,1)} %get-tuple-element.331.refs_2_.refs_0_, bf16[256,1024]{1,0:T(8,128)(2,1)S(1)} %copy-done.5, f32[8,1024]{1,0:T(8,128)S(1)} %concatenate.107.refs_8_.refs_4_.refs_6_, ...), custom_call_target="tpu_custom_call" | custom-call | flops 1 | bytes 1 | tf_op jit(solution)/shard_map/down/pallas_call | solution.py:248
  224.6 3.0 collective-permute-done.35.refs_2_.refs_3_
  227.7 20.9 %forward.2 = (bf16[256,1024]{1,0:T(8,128)(2,1)}, bf16[256,1024]{1,0:T(8,128)(2,1)}, bf16[256,1024]{1,0:T(8,128)(2,1)}, bf16[256,1024]{1,0:T(8,128)(2,1)}, f32[25...) custom-call(s32[2]{0:T(128)S(1)} %get-tuple-element.555.refs_0_, ...), custom_call_target="tpu_custom_call" | custom-call | flops 40000000000 | bytes 100000000 | tf_op jit(solution)/shard_map/forward/pallas_call | solution.py:248
  248.6 21.4 %forward.3 = (bf16[256,1024]{1,0:T(8,128)(2,1)}, bf16[256,1024]{1,0:T(8,128)(2,1)}, bf16[256,1024]{1,0:T(8,128)(2,1)}, bf16[256,1024]{1,0:T(8,128)(2,1)}, f32[25...) custom-call(s32[2]{0:T(128)S(1)} %get-tuple-element.556.refs_0_, ...), custom_call_target="tpu_custom_call" | custom-call | flops 40000000000 | bytes 100000000 | tf_op jit(solution)/shard_map/forward/pallas_call | solution.py:248
  271.6 4.7 all-to-all-start.1
  276.4 9.9 %all-to-all-done.1.queries_ref = bf16[16,64,128]{2,1,0:T(8,128)(2,1)S(1)} async-done(((bf16[16,64,128]{2,1,0:T(8,128)(2,1)}), bf16[16,64,128]{2,1,0:T(8,128)(2,1)S(1)}, u32[]{:S(2)}, u32[]{:S(2)}) %all-to-all-start.1) | async-done | bytes 262176 | tf_op jit(solution)/shard_map/all_to_all | solution.py:1069
  287.1 3.5 all-to-all-start
  294.1 6.5 all-to-all-done.queries_ref
  303.5 4.2 all-to-all-start.2
  308.0 8.0 %all-to-all-done.2 = f32[16,2,1,3,3,128]{5,1,4,3,2,0:T(2,128)} async-done(((f32[16,2,1,3,3,128]{5,1,4,3,2,0:T(2,128)}), f32[16,2,1,3,3,128]{5,1,4,3,2,0:T(2,128)}, u32[]{:S(2)}, u32[]{:S(2)}) %all-to-all-start.2) | async-done | bytes 147488 | tf_op jit(solution)/shard_map/all_to_all | solution.py:1069
  317.1 4.4 losses.2
  321.5 3.5 all-to-all-start.3
  326.0 4.5 losses.3
  330.5 4.6 all-to-all-done.3.refs_3_
  335.0 3.7 all-to-all-start.4
  339.8 29.0 %backward.3 = (bf16[256,128]{1,0:T(8,128)(2,1)}, bf16[256,1024]{1,0:T(8,128)(2,1)}, bf16[256,4096]{1,0:T(8,128)(2,1)}, bf16[256,1024]{1,0:T(8,128)(2,1)}, f32[8,...) custom-call(s32[2]{0:T(128)S(1)} %get-tuple-element.556.refs_0_, ...), custom_call_target="tpu_custom_call" | custom-call | flops 40000000000 | bytes 100000000 | tf_op jit(solution)/shard_map/backward/pallas_call | solution.py:248
  371.2 28.9 %backward.5 = (bf16[256,128]{1,0:T(8,128)(2,1)}, bf16[256,1024]{1,0:T(8,128)(2,1)}, bf16[256,4096]{1,0:T(8,128)(2,1)}, bf16[256,1024]{1,0:T(8,128)(2,1)}, f32[8,...) custom-call(s32[2]{0:T(128)S(1)} %get-tuple-element.555.refs_0_, ...), custom_call_target="tpu_custom_call" | custom-call | flops 40000000000 | bytes 100000000 | tf_op jit(solution)/shard_map/backward/pallas_call | solution.py:248
  401.4 29.1 %backward.4 = (bf16[256,1024]{1,0:T(8,128)(2,1)}, bf16[256,4096]{1,0:T(8,128)(2,1)}, bf16[256,1024]{1,0:T(8,128)(2,1)}, f32[8,1024]{1,0:T(8,128)}, f32[1,4096]{1...) custom-call(s32[2]{0:T(128)S(1)} %get-tuple-element.556.refs_0_, ...), custom_call_target="tpu_custom_call" | custom-call | flops 40000000000 | bytes 100000000 | tf_op jit(solution)/shard_map/backward/pallas_call | solution.py:248
  430.5 15.6 %feed_back.1 = (bf16[256,1024]{1,0:T(8,128)(2,1)}, bf16[256,4096]{1,0:T(8,128)(2,1)}, bf16[256,1024]{1,0:T(8,128)(2,1)}, f32[8,1024]{1,0:T(8,128)}, f32[1,4096]{1,0:T(1,128)}, /*index=5*/f32[256,1024]{1,0:T(8,128)}) custom-call(s32[2]{0:T(128)S(1)} %get-tuple-element.555.refs_0_, s32[16]{0:T(128)S(1)} %copy-done.53, ...), custom_call_target="tpu_custom_call" | custom-call | flops 1 | bytes 1 | tf_op jit(solution)/shard_map/feed_back/pallas_call | solution.py:248
  447.2 6.6 down_send.1
  456.4 6.3 up_send.1
  463.0 3.5 out_send.1
  466.6 6.3 down_keep.2
  480.0 19.4 %attend_back.1 = (bf16[3,256,1024]{2,1,0:T(8,128)(2,1)}, f32[8,1024]{1,0:T(8,128)}, f32[512,1024]{1,0:T(8,128)}) custom-call(s32[2]{0:T(128)S(1)} %get-tuple-element.555.refs_0_, s32[16]{0:T(128)S(1)} %copy-done.53, bf16[256,1024]{1,0:T(8,128)(2,1)S(1)} %copy-done.25, f32[256,1024]{1,0:T(8,128)} %get-tuple-element.378.refs_3_, ...), custom_call_target="tpu_custom_call" | custom-call | flops 1 | bytes 1 | tf_op jit(solution)/shard_map/attend_back/pallas_call | solution.py:248
  499.5 5.8 qkv_send.1
  507.7 6.3 down_keep.3
  517.6 5.3 up_keep.2
  523.0 5.3 up_keep.3
  529.5 11.2 %collective-permute-done.43.other_ref = bf16[4,256,512]{2,1,0:T(8,128)(2,1)S(1)} collective-permute-done((bf16[4,256,512]{2,1,0:T(8,128)(2,1)S(1)}, bf16[4,256,512]{2,1,0:T(8,128)(2,1)S(1)}, u32[]{:S(2)}, u32[]{:S(2)}) %collective-permute-start.43) | collective-permute-done | bytes 1048608 | tf_op jit(solution)/shard_map/ppermute | solution.py:647
  543.1 3.9 out_keep.1
  554.9 11.5 %collective-permute-done.47 = bf16[1,256,512]{2,1,0:T(8,128)(2,1)S(1)} collective-permute-done((bf16[1,256,512]{2,1,0:T(8,128)(2,1)S(1)}, bf16[1,256,512]{2,1,0:T(8,128)(2,1)S(1)}, u32[]{:S(2)}, u32[]{:S(2)}) %collective-permute-start.47) | collective-permute-done | bytes 262176 | tf_op jit(solution)/shard_map/ppermute | solution.py:647
  575.6 5.3 qkv_keep.2
  581.0 7.7 %collective-permute-done.50 = bf16[1,256,512]{2,1,0:T(8,128)(2,1)S(1)} collective-permute-done((bf16[1,256,512]{2,1,0:T(8,128)(2,1)S(1)}, bf16[1,256,512]{2,1,0:T(8,128)(2,1)S(1)}, u32[]{:S(2)}, u32[]{:S(2)}) %collective-permute-start.50) | collective-permute-done | bytes 262176 | tf_op jit(solution)/shard_map/ppermute | solution.py:647
  589.4 3.9 collective-permute-done.48.other_ref
  595.2 4.3 qkv_keep.3
  605.6 10.1 %collective-permute-done.53 = bf16[1,64,2048]{2,1,0:T(8,128)(2,1)S(1)} collective-permute-done((bf16[1,64,2048]{2,1,0:T(8,128)(2,1)S(1)}, bf16[1,64,2048]{2,1,0:T(8,128)(2,1)S(1)}, u32[]{:S(2)}, u32[]{:S(2)}) %collective-permute-start.53) | collective-permute-done | bytes 262176 | tf_op jit(solution)/shard_map/ppermute | solution.py:647
  619.8 2.8 collective-permute-start.56
  622.6 2.7 collective-permute-start.57
  626.6 4.2 all-to-all-start.5
  633.3 7.1 %collective-permute-done.57 = bf16[1,64,2048]{2,1,0:T(8,128)(2,1)} collective-permute-done((bf16[1,64,2048]{2,1,0:T(8,128)(2,1)S(1)}, bf16[1,64,2048]{2,1,0:T(8,128)(2,1)}, u32[]{:S(2)}, u32[]{:S(2)}) %collective-permute-start.57) | collective-permute-done | bytes 262176 | tf_op jit(solution)/shard_map/ppermute | solution.py:647
  646.5 3.0 collective-permute-start.60
  649.5 3.1 collective-permute-start.61
  659.0 9.9 %collective-permute-done.62 = f32[32,128]{1,0:T(8,128)S(1)} collective-permute-done((f32[32,128]{1,0:T(8,128)S(1)}, f32[32,128]{1,0:T(8,128)S(1)}, u32[]{:S(2)}, u32[]{:S(2)}) %collective-permute-start.62) | collective-permute-done | bytes 16416 | tf_op jit(solution)/shard_map/ppermute | solution.py:33
  670.9 6.3 collective-permute-done.64
  681.7 4.8 collective-permute-done.65
  (483 shorter events, 164.0 us)
Async XLA Ops:
  15.3 13.1 %collective-permute-start.2 = (bf16[2,80,1024]{2,1,0:T(8,128)(2,1)S(1)}, bf16[2,80,1024]{2,1,0:T(8,128)(2,1)S(1)}, u32[]{:S(2)}, u32[]{:S(2)}) collective-permute-start(bf16[2,80,1024]{2,1,0:T(8,128)(2,1)S(1)} %pad_maximum_fusion.15), channel_id=1, source_target_pairs={{0,4},{1,5},{2,6},{3,7},{4,0},{5,1},{6,2},{7,3},{8,12},{9,13},{10,... | collective-permute-start | bytes 983048 | tf_op jit(solution)/shard_map/ppermute | solution.py:647
  28.5 16.0 %collective-permute-start.5 = (bf16[4,80,1024]{2,1,0:T(8,128)(2,1)S(1)}, bf16[4,80,1024]{2,1,0:T(8,128)(2,1)S(1)}, u32[]{:S(2)}, u32[]{:S(2)}) collective-permute-start(bf16[4,80,1024]{2,1,0:T(8,128)(2,1)S(1)} %pad_maximum_fusion.6.refs_0_.refs_17_.refs_19_.refs_22_.refs_32_.refs_30_.refs_14_), channel_id=1, source_target_pairs={{0,2},{1,3},{2,0},{3,1},{4,6},{5,7},{6,4},{7,5},{8,10},{9,11},{10,... | collective-permute-start | bytes 1966088 | tf_op jit(solution)/shard_map/ppermute | solution.py:647
  30.1 13.8 %collective-permute-start.3 = (bf16[1,64,2048]{2,1,0:T(8,128)(2,1)S(1)}, bf16[1,64,2048]{2,1,0:T(8,128)(2,1)S(1)}, u32[]{:S(2)}, u32[]{:S(2)}) collective-permute-start(bf16[1,64,2048]{2,1,0:T(8,128)(2,1)S(1)} %slice_bitcast_fusion.4), channel_id=1, source_target_pairs={{0,8},{1,9},{2,10},{3,11},{4,12},{5,13},{6,14},{7,15},{8,0},{9,1},... | collective-permute-start | bytes 786440 | tf_op jit(solution)/shard_map/ppermute | solution.py:647
  31.9 12.4 %collective-permute-start.4 = (bf16[2,64,1024]{2,1,0:T(8,128)(2,1)S(1)}, bf16[2,64,1024]{2,1,0:T(8,128)(2,1)S(1)}, u32[]{:S(2)}, u32[]{:S(2)}) collective-permute-start(bf16[2,64,1024]{2,1,0:T(8,128)(2,1)S(1)} %pad_maximum_fusion.18), channel_id=1, source_target_pairs={{0,4},{1,5},{2,6},{3,7},{4,0},{5,1},{6,2},{7,3},{8,12},{9,13},{10,... | collective-permute-start | bytes 786440 | tf_op jit(solution)/shard_map/ppermute | solution.py:647
  45.5 20.5 %collective-permute-start.9 = (bf16[4,80,1024]{2,1,0:T(8,128)(2,1)S(1)}, bf16[4,80,1024]{2,1,0:T(8,128)(2,1)S(1)}, u32[]{:S(2)}, u32[]{:S(2)}) collective-permute-start(bf16[4,80,1024]{2,1,0:T(8,128)(2,1)S(1)} %pad_maximum_fusion.6.refs_0_.refs_17_.refs_19_.refs_22_.refs_32_.refs_30_.refs_14_), channel_id=1, source_target_pairs={{0,1},{1,0},{2,3},{3,2},{4,5},{5,4},{6,7},{7,6},{8,9},{9,8},{10,11... | collective-permute-start | bytes 1966088 | tf_op jit(solution)/shard_map/ppermute | solution.py:647
  45.6 20.4 %collective-permute-start.10 = (bf16[4,80,1024]{2,1,0:T(8,128)(2,1)S(1)}, bf16[4,80,1024]{2,1,0:T(8,128)(2,1)S(1)}, u32[]{:S(2)}, u32[]{:S(2)}) collective-permute-start(bf16[4,80,1024]{2,1,0:T(8,128)(2,1)S(1)} %collective-permute-done.5.refs_1_.refs_18_.refs_20_.refs_23_.refs_33_.refs_31_.refs_15_), channel_id=1, source_target_pairs={{0,1},{1,0},{2,3},{3,2},{4,5},{5,4},{6,7},{7,6},{8,9},{9,8},{10,11... | collective-permute-start | bytes 1966088 | tf_op jit(solution)/shard_map/ppermute | solution.py:647
  46.1 19.9 %collective-permute-start.7 = (bf16[2,64,2048]{2,1,0:T(8,128)(2,1)}, bf16[2,64,2048]{2,1,0:T(8,128)(2,1)}, u32[]{:S(2)}, u32[]{:S(2)}) collective-permute-start(bf16[2,64,2048]{2,1,0:T(8,128)(2,1)} %pad_maximum_fusion.9), channel_id=1, source_target_pairs={{0,4},{1,5},{2,6},{3,7},{4,0},{5,1},{6,2},{7,3},{8,12},{9,13},{10,... | collective-permute-start | bytes 1572872 | tf_op jit(solution)/shard_map/ppermute | solution.py:647
  46.6 19.4 %collective-permute-start.8 = (bf16[4,64,1024]{2,1,0:T(8,128)(2,1)S(1)}, bf16[4,64,1024]{2,1,0:T(8,128)(2,1)}, u32[]{:S(2)}, u32[]{:S(2)}) collective-permute-start(bf16[4,64,1024]{2,1,0:T(8,128)(2,1)S(1)} %pad_maximum_fusion.10.refs_9_.refs_11_.refs_14_.refs_36_.refs_34_.refs_18_), channel_id=1, source_target_pairs={{0,2},{1,3},{2,0},{3,1},{4,6},{5,7},{6,4},{7,5},{8,10},{9,11},{10,... | collective-permute-start | bytes 1572872 | tf_op jit(solution)/shard_map/ppermute | solution.py:647
  47.8 16.1 %collective-permute-start.6 = (bf16[1,64,2048]{2,1,0:T(8,128)(2,1)}, bf16[1,64,2048]{2,1,0:T(8,128)(2,1)}, u32[]{:S(2)}, u32[]{:S(2)}) collective-permute-start(bf16[1,64,2048]{2,1,0:T(8,128)(2,1)} %get-tuple-element.267), channel_id=1, source_target_pairs={{0,8},{1,9},{2,10},{3,11},{4,12},{5,13},{6,14},{7,15},{8,0},{9,1},... | collective-permute-start | bytes 786440 | tf_op jit(solution)/shard_map/ppermute | solution.py:647
  70.5 24.6 %collective-permute-start.13 = (bf16[4,64,2048]{2,1,0:T(8,128)(2,1)}, bf16[4,64,2048]{2,1,0:T(8,128)(2,1)}, u32[]{:S(2)}, u32[]{:S(2)}) collective-permute-start(bf16[4,64,2048]{2,1,0:T(8,128)(2,1)} %pad_maximum_fusion.1.refs_13_.refs_15_.refs_18_.refs_40_.refs_38_.refs_22_), channel_id=1, source_target_pairs={{0,2},{1,3},{2,0},{3,1},{4,6},{5,7},{6,4},{7,5},{8,10},{9,11},{10,... | collective-permute-start | bytes 3145736 | tf_op jit(solution)/shard_map/ppermute | solution.py:647
  72.6 18.9 %collective-permute-start.12 = (bf16[2,64,2048]{2,1,0:T(8,128)(2,1)}, bf16[2,64,2048]{2,1,0:T(8,128)(2,1)S(1)}, u32[]{:S(2)}, u32[]{:S(2)}) collective-permute-start(bf16[2,64,2048]{2,1,0:T(8,128)(2,1)} %pad_maximum_fusion.11), channel_id=1, source_target_pairs={{0,4},{1,5},{2,6},{3,7},{4,0},{5,1},{6,2},{7,3},{8,12},{9,13},{10,... | collective-permute-start | bytes 1572872 | tf_op jit(solution)/shard_map/ppermute | solution.py:647
  74.6 16.9 %collective-permute-start.14 = (bf16[4,64,1024]{2,1,0:T(8,128)(2,1)S(1)}, bf16[4,64,1024]{2,1,0:T(8,128)(2,1)S(1)}, u32[]{:S(2)}, u32[]{:S(2)}) collective-permute-start(bf16[4,64,1024]{2,1,0:T(8,128)(2,1)S(1)} %pad_maximum_fusion.10.refs_9_.refs_11_.refs_14_.refs_36_.refs_34_.refs_18_), channel_id=1, source_target_pairs={{0,1},{1,0},{2,3},{3,2},{4,5},{5,4},{6,7},{7,6},{8,9},{9,8},{10,11... | collective-permute-start | bytes 1572872 | tf_op jit(solution)/shard_map/ppermute | solution.py:647
  74.6 16.9 %collective-permute-start.15 = (bf16[4,64,1024]{2,1,0:T(8,128)(2,1)}, bf16[4,64,1024]{2,1,0:T(8,128)(2,1)S(1)}, u32[]{:S(2)}, u32[]{:S(2)}) collective-permute-start(bf16[4,64,1024]{2,1,0:T(8,128)(2,1)} %collective-permute-done.8.refs_10_.refs_12_.refs_15_.refs_37_.refs_35_.refs_19_), channel_id=1, source_target_pairs={{0,1},{1,0},{2,3},{3,2},{4,5},{5,4},{6,7},{7,6},{8,9},{9,8},{10,11... | collective-permute-start | bytes 1572872 | tf_op jit(solution)/shard_map/ppermute | solution.py:647
  75.2 15.6 %collective-permute-start.11 = (bf16[1,64,2048]{2,1,0:T(8,128)(2,1)}, bf16[1,64,2048]{2,1,0:T(8,128)(2,1)S(1)}, u32[]{:S(2)}, u32[]{:S(2)}) collective-permute-start(bf16[1,64,2048]{2,1,0:T(8,128)(2,1)} %get-tuple-element.277), channel_id=1, source_target_pairs={{0,8},{1,9},{2,10},{3,11},{4,12},{5,13},{6,14},{7,15},{8,0},{9,1},... | collective-permute-start | bytes 786440 | tf_op jit(solution)/shard_map/ppermute | solution.py:647
  98.1 23.6 %collective-permute-start.18 = (bf16[4,64,2048]{2,1,0:T(8,128)(2,1)S(1)}, bf16[4,64,2048]{2,1,0:T(8,128)(2,1)}, u32[]{:S(2)}, u32[]{:S(2)}) collective-permute-start(bf16[4,64,2048]{2,1,0:T(8,128)(2,1)S(1)} %pad_maximum_fusion.2.refs_4_.refs_23_.refs_26_.refs_24_.refs_22_.refs_15_), channel_id=1, source_target_pairs={{0,2},{1,3},{2,0},{3,1},{4,6},{5,7},{6,4},{7,5},{8,10},{9,11},{10,... | collective-permute-start | bytes 3145736 | tf_op jit(solution)/shard_map/ppermute | solution.py:647
  99.7 22.0 %collective-permute-start.19 = (bf16[4,64,2048]{2,1,0:T(8,128)(2,1)}, bf16[4,64,2048]{2,1,0:T(8,128)(2,1)}, u32[]{:S(2)}, u32[]{:S(2)}) collective-permute-start(bf16[4,64,2048]{2,1,0:T(8,128)(2,1)} %pad_maximum_fusion.1.refs_13_.refs_15_.refs_18_.refs_40_.refs_38_.refs_22_), channel_id=1, source_target_pairs={{0,1},{1,0},{2,3},{3,2},{4,5},{5,4},{6,7},{7,6},{8,9},{9,8},{10,11... | collective-permute-start | bytes 3145736 | tf_op jit(solution)/shard_map/ppermute | solution.py:647
  99.7 22.0 %collective-permute-start.20 = (bf16[4,64,2048]{2,1,0:T(8,128)(2,1)}, bf16[4,64,2048]{2,1,0:T(8,128)(2,1)}, u32[]{:S(2)}, u32[]{:S(2)}) collective-permute-start(bf16[4,64,2048]{2,1,0:T(8,128)(2,1)} %collective-permute-done.13.refs_14_.refs_16_.refs_19_.refs_41_.refs_39_.refs_23_), channel_id=1, source_target_pairs={{0,1},{1,0},{2,3},{3,2},{4,5},{5,4},{6,7},{7,6},{8,9},{9,8},{10,11... | collective-permute-start | bytes 3145736 | tf_op jit(solution)/shard_map/ppermute | solution.py:647
  100.3 20.1 %collective-permute-start.17 = (bf16[2,64,2048]{2,1,0:T(8,128)(2,1)}, bf16[2,64,2048]{2,1,0:T(8,128)(2,1)}, u32[]{:S(2)}, u32[]{:S(2)}) collective-permute-start(bf16[2,64,2048]{2,1,0:T(8,128)(2,1)} %pad_maximum_fusion.12), channel_id=1, source_target_pairs={{0,4},{1,5},{2,6},{3,7},{4,0},{5,1},{6,2},{7,3},{8,12},{9,13},{10,... | collective-permute-start | bytes 1572872 | tf_op jit(solution)/shard_map/ppermute | solution.py:647
  102.4 17.2 %collective-permute-start.16 = (bf16[1,256,512]{2,1,0:T(8,128)(2,1)S(1)}, bf16[1,256,512]{2,1,0:T(8,128)(2,1)S(1)}, u32[]{:S(2)}, u32[]{:S(2)}) collective-permute-start(bf16[1,256,512]{2,1,0:T(8,128)(2,1)S(1)} %get-tuple-element.287), channel_id=1, source_target_pairs={{0,8},{1,9},{2,10},{3,11},{4,12},{5,13},{6,14},{7,15},{8,0},{9,1},... | collective-permute-start | bytes 786440 | tf_op jit(solution)/shard_map/ppermute | solution.py:647
  124.7 23.6 %collective-permute-start.23 = (bf16[4,64,2048]{2,1,0:T(8,128)(2,1)}, bf16[4,64,2048]{2,1,0:T(8,128)(2,1)}, u32[]{:S(2)}, u32[]{:S(2)}) collective-permute-start(bf16[4,64,2048]{2,1,0:T(8,128)(2,1)} %pad_maximum_fusion.3.refs_8_.refs_27_.refs_30_.refs_28_.refs_26_.refs_19_), channel_id=1, source_target_pairs={{0,2},{1,3},{2,0},{3,1},{4,6},{5,7},{6,4},{7,5},{8,10},{9,11},{10,... | collective-permute-start | bytes 3145736 | tf_op jit(solution)/shard_map/ppermute | solution.py:647
  126.2 22.0 %collective-permute-start.24 = (bf16[4,64,2048]{2,1,0:T(8,128)(2,1)S(1)}, bf16[4,64,2048]{2,1,0:T(8,128)(2,1)}, u32[]{:S(2)}, u32[]{:S(2)}) collective-permute-start(bf16[4,64,2048]{2,1,0:T(8,128)(2,1)S(1)} %pad_maximum_fusion.2.refs_4_.refs_23_.refs_26_.refs_24_.refs_22_.refs_15_), channel_id=1, source_target_pairs={{0,1},{1,0},{2,3},{3,2},{4,5},{5,4},{6,7},{7,6},{8,9},{9,8},{10,11... | collective-permute-start | bytes 3145736 | tf_op jit(solution)/shard_map/ppermute | solution.py:647
  126.2 22.0 %collective-permute-start.25 = (bf16[4,64,2048]{2,1,0:T(8,128)(2,1)}, bf16[4,64,2048]{2,1,0:T(8,128)(2,1)}, u32[]{:S(2)}, u32[]{:S(2)}) collective-permute-start(bf16[4,64,2048]{2,1,0:T(8,128)(2,1)} %collective-permute-done.18.refs_5_.refs_24_.refs_27_.refs_25_.refs_23_.refs_16_), channel_id=1, source_target_pairs={{0,1},{1,0},{2,3},{3,2},{4,5},{5,4},{6,7},{7,6},{8,9},{9,8},{10,11... | collective-permute-start | bytes 3145736 | tf_op jit(solution)/shard_map/ppermute | solution.py:647
  127.4 20.1 %collective-permute-start.22 = (bf16[2,256,512]{2,1,0:T(8,128)(2,1)}, bf16[2,256,512]{2,1,0:T(8,128)(2,1)}, u32[]{:S(2)}, u32[]{:S(2)}) collective-permute-start(bf16[2,256,512]{2,1,0:T(8,128)(2,1)} %pad_maximum_fusion.13), channel_id=1, source_target_pairs={{0,4},{1,5},{2,6},{3,7},{4,0},{5,1},{6,2},{7,3},{8,12},{9,13},{10,... | collective-permute-start | bytes 1572872 | tf_op jit(solution)/shard_map/ppermute | solution.py:647
  133.1 13.6 %collective-permute-start.21 = (bf16[1,256,512]{2,1,0:T(8,128)(2,1)}, bf16[1,256,512]{2,1,0:T(8,128)(2,1)}, u32[]{:S(2)}, u32[]{:S(2)}) collective-permute-start(bf16[1,256,512]{2,1,0:T(8,128)(2,1)} %get-tuple-element.298), channel_id=1, source_target_pairs={{0,8},{1,9},{2,10},{3,11},{4,12},{5,13},{6,14},{7,15},{8,0},{9,1},... | collective-permute-start | bytes 786440 | tf_op jit(solution)/shard_map/ppermute | solution.py:647
  150.4 23.8 %collective-permute-start.27 = (bf16[4,256,512]{2,1,0:T(8,128)(2,1)S(1)}, bf16[4,256,512]{2,1,0:T(8,128)(2,1)S(1)}, u32[]{:S(2)}, u32[]{:S(2)}) collective-permute-start(bf16[4,256,512]{2,1,0:T(8,128)(2,1)S(1)} %pad_maximum_fusion.4.refs_5_.refs_31_.refs_34_.refs_16_.refs_14_.refs_7_), channel_id=1, source_target_pairs={{0,2},{1,3},{2,0},{3,1},{4,6},{5,7},{6,4},{7,5},{8,10},{9,11},{10,... | collective-permute-start | bytes 3145736 | tf_op jit(solution)/shard_map/ppermute | solution.py:647
  151.2 23.0 %collective-permute-start.28 = (bf16[4,64,2048]{2,1,0:T(8,128)(2,1)}, bf16[4,64,2048]{2,1,0:T(8,128)(2,1)S(1)}, u32[]{:S(2)}, u32[]{:S(2)}) collective-permute-start(bf16[4,64,2048]{2,1,0:T(8,128)(2,1)} %pad_maximum_fusion.3.refs_8_.refs_27_.refs_30_.refs_28_.refs_26_.refs_19_), channel_id=1, source_target_pairs={{0,1},{1,0},{2,3},{3,2},{4,5},{5,4},{6,7},{7,6},{8,9},{9,8},{10,11... | collective-permute-start | bytes 3145736 | tf_op jit(solution)/shard_map/ppermute | solution.py:647
  151.2 23.0 %collective-permute-start.29 = (bf16[4,64,2048]{2,1,0:T(8,128)(2,1)}, bf16[4,64,2048]{2,1,0:T(8,128)(2,1)S(1)}, u32[]{:S(2)}, u32[]{:S(2)}) collective-permute-start(bf16[4,64,2048]{2,1,0:T(8,128)(2,1)} %collective-permute-done.23.refs_9_.refs_28_.refs_31_.refs_29_.refs_27_.refs_20_), channel_id=1, source_target_pairs={{0,1},{1,0},{2,3},{3,2},{4,5},{5,4},{6,7},{7,6},{8,9},{9,8},{10,11... | collective-permute-start | bytes 3145736 | tf_op jit(solution)/shard_map/ppermute | solution.py:647
  151.7 14.1 %collective-permute-start.26 = (bf16[2,256,512]{2,1,0:T(8,128)(2,1)S(1)}, bf16[2,256,512]{2,1,0:T(8,128)(2,1)S(1)}, u32[]{:S(2)}, u32[]{:S(2)}) collective-permute-start(bf16[2,256,512]{2,1,0:T(8,128)(2,1)S(1)} %pad_maximum_fusion.14), channel_id=1, source_target_pairs={{0,4},{1,5},{2,6},{3,7},{4,0},{5,1},{6,2},{7,3},{8,12},{9,13},{10,... | collective-permute-start | bytes 1572872 | tf_op jit(solution)/shard_map/ppermute | solution.py:647
  175.5 23.5 %collective-permute-start.30 = (bf16[4,256,512]{2,1,0:T(8,128)(2,1)S(1)}, bf16[4,256,512]{2,1,0:T(8,128)(2,1)S(1)}, u32[]{:S(2)}, u32[]{:S(2)}) collective-permute-start(bf16[4,256,512]{2,1,0:T(8,128)(2,1)S(1)} %pad_maximum_fusion.5.refs_9_.refs_35_.refs_38_.refs_20_.refs_18_.refs_11_), channel_id=1, source_target_pairs={{0,2},{1,3},{2,0},{3,1},{4,6},{5,7},{6,4},{7,5},{8,10},{9,11},{10,... | collective-permute-start | bytes 3145736 | tf_op jit(solution)/shard_map/ppermute | solution.py:647
  176.1 22.9 %collective-permute-start.31 = (bf16[4,256,512]{2,1,0:T(8,128)(2,1)S(1)}, bf16[4,256,512]{2,1,0:T(8,128)(2,1)S(1)}, u32[]{:S(2)}, u32[]{:S(2)}) collective-permute-start(bf16[4,256,512]{2,1,0:T(8,128)(2,1)S(1)} %pad_maximum_fusion.4.refs_5_.refs_31_.refs_34_.refs_16_.refs_14_.refs_7_), channel_id=1, source_target_pairs={{0,1},{1,0},{2,3},{3,2},{4,5},{5,4},{6,7},{7,6},{8,9},{9,8},{10,11... | collective-permute-start | bytes 3145736 | tf_op jit(solution)/shard_map/ppermute | solution.py:647
  176.1 22.9 %collective-permute-start.32 = (bf16[4,256,512]{2,1,0:T(8,128)(2,1)S(1)}, bf16[4,256,512]{2,1,0:T(8,128)(2,1)S(1)}, u32[]{:S(2)}, u32[]{:S(2)}) collective-permute-start(bf16[4,256,512]{2,1,0:T(8,128)(2,1)S(1)} %collective-permute-done.27.refs_6_.refs_32_.refs_35_.refs_17_.refs_15_.refs_8_), channel_id=1, source_target_pairs={{0,1},{1,0},{2,3},{3,2},{4,5},{5,4},{6,7},{7,6},{8,9},{9,8},{10,11... | collective-permute-start | bytes 3145736 | tf_op jit(solution)/shard_map/ppermute | solution.py:647
  211.7 16.0 %collective-permute-start.35 = (bf16[256,1024]{1,0:T(8,128)(2,1)}, bf16[256,1024]{1,0:T(8,128)(2,1)S(1)}, u32[]{:S(2)}, u32[]{:S(2)}) collective-permute-start(bf16[256,1024]{1,0:T(8,128)(2,1)} %get-tuple-element.329.refs_11_), channel_id=1, source_target_pairs={{0,16},{1,17},{2,18},{3,19},{4,20},{5,21},{6,22},{7,23},{8,24},{9,... | collective-permute-start | bytes 1572872 | tf_op jit(solution)/shard_map/ppermute | solution.py:33
  223.3 25.3 %collective-permute-start.36 = (bf16[256,1024]{1,0:T(8,128)(2,1)}, bf16[256,1024]{1,0:T(8,128)(2,1)S(1)}, u32[]{:S(2)}, u32[]{:S(2)}) collective-permute-start(bf16[256,1024]{1,0:T(8,128)(2,1)} %get-tuple-element.332.refs_12_), channel_id=1, source_target_pairs={{0,16},{1,17},{2,18},{3,19},{4,20},{5,21},{6,22},{7,23},{8,24},{9,... | collective-permute-start | bytes 1572872 | tf_op jit(solution)/shard_map/ppermute | solution.py:33
  271.6 14.8 %all-to-all-start.1 = ((bf16[16,64,128]{2,1,0:T(8,128)(2,1)}), bf16[16,64,128]{2,1,0:T(8,128)(2,1)S(1)}, u32[]{:S(2)}, u32[]{:S(2)}) async-start(bf16[16,64,128]{2,1,0:T(8,128)(2,1)} %broadcast_in_dim.179), calls=%async_computation.1 | async-start | bytes 524288 | tf_op jit(solution)/shard_map/all_to_all | solution.py:1069
  287.1 13.5 %all-to-all-start = ((bf16[16,64,128]{2,1,0:T(8,128)(2,1)}), bf16[16,64,128]{2,1,0:T(8,128)(2,1)S(1)}, u32[]{:S(2)}, u32[]{:S(2)}) async-start(bf16[16,64,128]{2,1,0:T(8,128)(2,1)} %broadcast_in_dim.178), calls=%async_computation | async-start | bytes 524288 | tf_op jit(solution)/shard_map/all_to_all | solution.py:1069
  321.5 13.5 %all-to-all-start.3 = ((bf16[16,64,128]{2,1,0:T(8,128)(2,1)}), bf16[16,64,128]{2,1,0:T(8,128)(2,1)S(1)}, u32[]{:S(2)}, u32[]{:S(2)}) async-start(bf16[16,64,128]{2,1,0:T(8,128)(2,1)} %get-tuple-element.335), calls=%async_computation.3 | async-start | bytes 524288 | tf_op jit(solution)/shard_map/all_to_all | solution.py:1457
  335.0 35.1 %all-to-all-start.4 = ((bf16[16,64,128]{2,1,0:T(8,128)(2,1)}), bf16[16,64,128]{2,1,0:T(8,128)(2,1)S(1)}, u32[]{:S(2)}, u32[]{:S(2)}) async-start(bf16[16,64,128]{2,1,0:T(8,128)(2,1)} %get-tuple-element.356), calls=%async_computation.4 | async-start | bytes 524288 | tf_op jit(solution)/shard_map/all_to_all | solution.py:1457
  368.9 32.5 %collective-permute-start.37 = (bf16[256,1024]{1,0:T(8,128)(2,1)}, bf16[256,1024]{1,0:T(8,128)(2,1)}, u32[]{:S(2)}, u32[]{:S(2)}) collective-permute-start(bf16[256,1024]{1,0:T(8,128)(2,1)} %get-tuple-element.346), channel_id=1, source_target_pairs={{16,0},{17,1},{18,2},{19,3},{20,4},{21,5},{22,6},{23,7},{24,8},{25... | collective-permute-start | bytes 1572872 | tf_op jit(solution)/shard_map/ppermute | solution.py:33
  400.1 30.4 %collective-permute-start.38 = (bf16[256,1024]{1,0:T(8,128)(2,1)}, bf16[256,1024]{1,0:T(8,128)(2,1)S(1)}, u32[]{:S(2)}, u32[]{:S(2)}) collective-permute-start(bf16[256,1024]{1,0:T(8,128)(2,1)} %get-tuple-element.363), channel_id=1, source_target_pairs={{16,0},{17,1},{18,2},{19,3},{20,4},{21,5},{22,6},{23,7},{24,8},{25... | collective-permute-start | bytes 1572872 | tf_op jit(solution)/shard_map/ppermute | solution.py:33
  453.8 12.8 %collective-permute-start.39 = (bf16[2048,1024]{1,0:T(8,128)(2,1)}, bf16[2048,1024]{1,0:T(8,128)(2,1)}, u32[]{:S(2)}, u32[]{:S(2)}) collective-permute-start(bf16[2048,1024]{1,0:T(8,128)(2,1)} %down_send.1), channel_id=1, source_target_pairs={{0,1},{1,0},{2,3},{3,2},{4,5},{5,4},{6,7},{7,6},{8,9},{9,8},{10,11... | collective-permute-start | bytes 12582920 | tf_op jit(solution)/shard_map/ppermute | solution.py:647
  462.7 54.9 %collective-permute-start.41 = (bf16[512,4096]{1,0:T(8,128)(2,1)}, bf16[512,4096]{1,0:T(8,128)(2,1)}, u32[]{:S(2)}, u32[]{:S(2)}) collective-permute-start(bf16[512,4096]{1,0:T(8,128)(2,1)} %up_send.1), channel_id=1, source_target_pairs={{0,1},{1,0},{2,3},{3,2},{4,5},{5,4},{6,7},{7,6},{8,9},{9,8},{10,11... | collective-permute-start | bytes 12582920 | tf_op jit(solution)/shard_map/ppermute | solution.py:647
  472.9 41.1 %collective-permute-start.42 = (bf16[4,256,512]{2,1,0:T(8,128)(2,1)}, bf16[4,256,512]{2,1,0:T(8,128)(2,1)}, u32[]{:S(2)}, u32[]{:S(2)}) collective-permute-start(bf16[4,256,512]{2,1,0:T(8,128)(2,1)} %get-tuple-element.376), channel_id=1, source_target_pairs={{0,2},{1,3},{2,0},{3,1},{4,6},{5,7},{6,4},{7,5},{8,10},{9,11},{10,... | collective-permute-start | bytes 3145736 | tf_op jit(solution)/shard_map/ppermute | solution.py:647
  505.3 70.4 %collective-permute-start.40 = (bf16[512,3072]{1,0:T(8,128)(2,1)}, bf16[512,3072]{1,0:T(8,128)(2,1)}, u32[]{:S(2)}, u32[]{:S(2)}) collective-permute-start(bf16[512,3072]{1,0:T(8,128)(2,1)} %qkv_send.1), channel_id=1, source_target_pairs={{0,1},{1,0},{2,3},{3,2},{4,5},{5,4},{6,7},{7,6},{8,9},{9,8},{10,11... | collective-permute-start | bytes 9437192 | tf_op jit(solution)/shard_map/ppermute | solution.py:647
  507.1 35.0 %collective-permute-start.58 = (bf16[528,1024]{1,0:T(8,128)(2,1)S(1)}, bf16[528,1024]{1,0:T(8,128)(2,1)S(1)}, u32[]{:S(2)}, u32[]{:S(2)}) collective-permute-start(bf16[528,1024]{1,0:T(8,128)(2,1)S(1)} %pad_maximum_fusion), channel_id=1, source_target_pairs={{0,1},{1,0},{2,3},{3,2},{4,5},{5,4},{6,7},{7,6},{8,9},{9,8},{10,11... | collective-permute-start | bytes 3244040 | tf_op jit(solution)/shard_map/ppermute | solution.py:647
  515.5 25.2 %collective-permute-start.43 = (bf16[4,256,512]{2,1,0:T(8,128)(2,1)S(1)}, bf16[4,256,512]{2,1,0:T(8,128)(2,1)S(1)}, u32[]{:S(2)}, u32[]{:S(2)}) collective-permute-start(bf16[4,256,512]{2,1,0:T(8,128)(2,1)S(1)} %copy-done.102), channel_id=1, source_target_pairs={{0,2},{1,3},{2,0},{3,1},{4,6},{5,7},{6,4},{7,5},{8,10},{9,11},{10,... | collective-permute-start | bytes 3145736 | tf_op jit(solution)/shard_map/ppermute | solution.py:647
  515.8 13.7 %collective-permute-start.44 = (bf16[2,256,512]{2,1,0:T(8,128)(2,1)S(1)}, bf16[2,256,512]{2,1,0:T(8,128)(2,1)S(1)}, u32[]{:S(2)}, u32[]{:S(2)}) collective-permute-start(bf16[2,256,512]{2,1,0:T(8,128)(2,1)S(1)} %get-tuple-element.402), channel_id=1, source_target_pairs={{0,4},{1,5},{2,6},{3,7},{4,0},{5,1},{6,2},{7,3},{8,12},{9,13},{10,... | collective-permute-start | bytes 1572872 | tf_op jit(solution)/shard_map/ppermute | solution.py:647
  541.8 25.6 %collective-permute-start.45 = (bf16[4,64,2048]{2,1,0:T(8,128)(2,1)}, bf16[4,64,2048]{2,1,0:T(8,128)(2,1)}, u32[]{:S(2)}, u32[]{:S(2)}) collective-permute-start(bf16[4,64,2048]{2,1,0:T(8,128)(2,1)} %get-tuple-element.408), channel_id=1, source_target_pairs={{0,2},{1,3},{2,0},{3,1},{4,6},{5,7},{6,4},{7,5},{8,10},{9,11},{10,... | collective-permute-start | bytes 3145736 | tf_op jit(solution)/shard_map/ppermute | solution.py:647
  548.6 18.8 %collective-permute-start.46 = (bf16[2,256,512]{2,1,0:T(8,128)(2,1)}, bf16[2,256,512]{2,1,0:T(8,128)(2,1)}, u32[]{:S(2)}, u32[]{:S(2)}) collective-permute-start(bf16[2,256,512]{2,1,0:T(8,128)(2,1)} %get-tuple-element.409), channel_id=1, source_target_pairs={{0,4},{1,5},{2,6},{3,7},{4,0},{5,1},{6,2},{7,3},{8,12},{9,13},{10,... | collective-permute-start | bytes 1572872 | tf_op jit(solution)/shard_map/ppermute | solution.py:647
  550.5 15.9 %collective-permute-start.47 = (bf16[1,256,512]{2,1,0:T(8,128)(2,1)S(1)}, bf16[1,256,512]{2,1,0:T(8,128)(2,1)S(1)}, u32[]{:S(2)}, u32[]{:S(2)}) collective-permute-start(bf16[1,256,512]{2,1,0:T(8,128)(2,1)S(1)} %get-tuple-element.410), channel_id=1, source_target_pairs={{0,8},{1,9},{2,10},{3,11},{4,12},{5,13},{6,14},{7,15},{8,0},{9,1},... | collective-permute-start | bytes 786440 | tf_op jit(solution)/shard_map/ppermute | solution.py:647
  570.1 23.3 %collective-permute-start.48 = (bf16[4,64,2048]{2,1,0:T(8,128)(2,1)S(1)}, bf16[4,64,2048]{2,1,0:T(8,128)(2,1)S(1)}, u32[]{:S(2)}, u32[]{:S(2)}) collective-permute-start(bf16[4,64,2048]{2,1,0:T(8,128)(2,1)S(1)} %copy-done.100), channel_id=1, source_target_pairs={{0,2},{1,3},{2,0},{3,1},{4,6},{5,7},{6,4},{7,5},{8,10},{9,11},{10,... | collective-permute-start | bytes 3145736 | tf_op jit(solution)/shard_map/ppermute | solution.py:647
  571.7 17.7 %collective-permute-start.49 = (bf16[2,64,2048]{2,1,0:T(8,128)(2,1)S(1)}, bf16[2,64,2048]{2,1,0:T(8,128)(2,1)S(1)}, u32[]{:S(2)}, u32[]{:S(2)}) collective-permute-start(bf16[2,64,2048]{2,1,0:T(8,128)(2,1)S(1)} %get-tuple-element.418), channel_id=1, source_target_pairs={{0,4},{1,5},{2,6},{3,7},{4,0},{5,1},{6,2},{7,3},{8,12},{9,13},{10,... | collective-permute-start | bytes 1572872 | tf_op jit(solution)/shard_map/ppermute | solution.py:647
  574.0 14.7 %collective-permute-start.50 = (bf16[1,256,512]{2,1,0:T(8,128)(2,1)S(1)}, bf16[1,256,512]{2,1,0:T(8,128)(2,1)S(1)}, u32[]{:S(2)}, u32[]{:S(2)}) collective-permute-start(bf16[1,256,512]{2,1,0:T(8,128)(2,1)S(1)} %get-tuple-element.419), channel_id=1, source_target_pairs={{0,8},{1,9},{2,10},{3,11},{4,12},{5,13},{6,14},{7,15},{8,0},{9,1},... | collective-permute-start | bytes 786440 | tf_op jit(solution)/shard_map/ppermute | solution.py:647
  593.7 22.7 %collective-permute-start.51 = (bf16[4,64,2048]{2,1,0:T(8,128)(2,1)S(1)}, bf16[4,64,2048]{2,1,0:T(8,128)(2,1)S(1)}, u32[]{:S(2)}, u32[]{:S(2)}) collective-permute-start(bf16[4,64,2048]{2,1,0:T(8,128)(2,1)S(1)} %copy-done.101), channel_id=1, source_target_pairs={{0,2},{1,3},{2,0},{3,1},{4,6},{5,7},{6,4},{7,5},{8,10},{9,11},{10,... | collective-permute-start | bytes 3145736 | tf_op jit(solution)/shard_map/ppermute | solution.py:647
  599.5 16.9 %collective-permute-start.52 = (bf16[2,64,2048]{2,1,0:T(8,128)(2,1)S(1)}, bf16[2,64,2048]{2,1,0:T(8,128)(2,1)S(1)}, u32[]{:S(2)}, u32[]{:S(2)}) collective-permute-start(bf16[2,64,2048]{2,1,0:T(8,128)(2,1)S(1)} %get-tuple-element.427), channel_id=1, source_target_pairs={{0,4},{1,5},{2,6},{3,7},{4,0},{5,1},{6,2},{7,3},{8,12},{9,13},{10,... | collective-permute-start | bytes 1572872 | tf_op jit(solution)/shard_map/ppermute | solution.py:647
  602.0 13.7 %collective-permute-start.53 = (bf16[1,64,2048]{2,1,0:T(8,128)(2,1)S(1)}, bf16[1,64,2048]{2,1,0:T(8,128)(2,1)S(1)}, u32[]{:S(2)}, u32[]{:S(2)}) collective-permute-start(bf16[1,64,2048]{2,1,0:T(8,128)(2,1)S(1)} %get-tuple-element.428), channel_id=1, source_target_pairs={{0,8},{1,9},{2,10},{3,11},{4,12},{5,13},{6,14},{7,15},{8,0},{9,1},... | collective-permute-start | bytes 786440 | tf_op jit(solution)/shard_map/ppermute | solution.py:647
  616.4 16.3 %collective-permute-start.54 = (f32[4]{0:T(128)S(1)}, f32[4]{0:T(128)S(1)}, u32[]{:S(2)}, u32[]{:S(2)}) collective-permute-start(f32[4]{0:T(128)S(1)} %copy-done.103), channel_id=1, source_target_pairs={{16,0},{17,1},{18,2},{19,3},{20,4},{21,5},{22,6},{23,7},{24,8},{25... | collective-permute-start | bytes 56 | tf_op jit(solution)/shard_map/ppermute | solution.py:33
  618.8 21.6 %collective-permute-start.55 = (bf16[4,64,1024]{2,1,0:T(8,128)(2,1)}, bf16[4,64,1024]{2,1,0:T(8,128)(2,1)}, u32[]{:S(2)}, u32[]{:S(2)}) collective-permute-start(bf16[4,64,1024]{2,1,0:T(8,128)(2,1)} %get-tuple-element.441), channel_id=1, source_target_pairs={{0,2},{1,3},{2,0},{3,1},{4,6},{5,7},{6,4},{7,5},{8,10},{9,11},{10,... | collective-permute-start | bytes 1572872 | tf_op jit(solution)/shard_map/ppermute | solution.py:647
  619.8 20.6 %collective-permute-start.56 = (bf16[2,64,2048]{2,1,0:T(8,128)(2,1)}, bf16[2,64,2048]{2,1,0:T(8,128)(2,1)S(1)}, u32[]{:S(2)}, u32[]{:S(2)}) collective-permute-start(bf16[2,64,2048]{2,1,0:T(8,128)(2,1)} %get-tuple-element.442), channel_id=1, source_target_pairs={{0,4},{1,5},{2,6},{3,7},{4,0},{5,1},{6,2},{7,3},{8,12},{9,13},{10,... | collective-permute-start | bytes 1572872 | tf_op jit(solution)/shard_map/ppermute | solution.py:647
  622.6 17.8 %collective-permute-start.57 = (bf16[1,64,2048]{2,1,0:T(8,128)(2,1)S(1)}, bf16[1,64,2048]{2,1,0:T(8,128)(2,1)}, u32[]{:S(2)}, u32[]{:S(2)}) collective-permute-start(bf16[1,64,2048]{2,1,0:T(8,128)(2,1)S(1)} %get-tuple-element.443), channel_id=1, source_target_pairs={{0,8},{1,9},{2,10},{3,11},{4,12},{5,13},{6,14},{7,15},{8,0},{9,1},... | collective-permute-start | bytes 786440 | tf_op jit(solution)/shard_map/ppermute | solution.py:647
  626.6 27.7 %all-to-all-start.5 = ((f32[16,2,32,128]{3,2,1,0:T(8,128)}), f32[16,2,32,128]{3,2,1,0:T(8,128)}, u32[]{:S(2)}, u32[]{:S(2)}) async-start(f32[16,2,32,128]{3,2,1,0:T(8,128)} %bitcast.158), calls=%async_computation.5 | async-start | bytes 1048576 | tf_op jit(solution)/shard_map/all_to_all | solution.py:1075
  645.2 24.3 %collective-permute-start.59 = (bf16[4,80,1024]{2,1,0:T(8,128)(2,1)}, bf16[4,80,1024]{2,1,0:T(8,128)(2,1)S(1)}, u32[]{:S(2)}, u32[]{:S(2)}) collective-permute-start(bf16[4,80,1024]{2,1,0:T(8,128)(2,1)} %pad_maximum_fusion.7), channel_id=1, source_target_pairs={{0,2},{1,3},{2,0},{3,1},{4,6},{5,7},{6,4},{7,5},{8,10},{9,11},{10,... | collective-permute-start | bytes 1966088 | tf_op jit(solution)/shard_map/ppermute | solution.py:647
  646.5 22.9 %collective-permute-start.60 = (bf16[2,64,1024]{2,1,0:T(8,128)(2,1)S(1)}, bf16[2,64,1024]{2,1,0:T(8,128)(2,1)S(1)}, u32[]{:S(2)}, u32[]{:S(2)}) collective-permute-start(bf16[2,64,1024]{2,1,0:T(8,128)(2,1)S(1)} %get-tuple-element.472), channel_id=1, source_target_pairs={{0,4},{1,5},{2,6},{3,7},{4,0},{5,1},{6,2},{7,3},{8,12},{9,13},{10,... | collective-permute-start | bytes 786440 | tf_op jit(solution)/shard_map/ppermute | solution.py:647
  649.5 20.0 %collective-permute-start.61 = (bf16[1,64,2048]{2,1,0:T(8,128)(2,1)}, bf16[1,64,2048]{2,1,0:T(8,128)(2,1)}, u32[]{:S(2)}, u32[]{:S(2)}) collective-permute-start(bf16[1,64,2048]{2,1,0:T(8,128)(2,1)} %get-tuple-element.473), channel_id=1, source_target_pairs={{0,8},{1,9},{2,10},{3,11},{4,12},{5,13},{6,14},{7,15},{8,0},{9,1},... | collective-permute-start | bytes 786440 | tf_op jit(solution)/shard_map/ppermute | solution.py:647
  655.4 13.4 %collective-permute-start.62 = (f32[32,128]{1,0:T(8,128)S(1)}, f32[32,128]{1,0:T(8,128)S(1)}, u32[]{:S(2)}, u32[]{:S(2)}) collective-permute-start(f32[32,128]{1,0:T(8,128)S(1)} %slice_bitcast_fusion.9), channel_id=1, source_target_pairs={{16,0},{17,1},{18,2},{19,3},{20,4},{21,5},{22,6},{23,7},{24,8},{25... | collective-permute-start | bytes 49160 | tf_op jit(solution)/shard_map/ppermute | solution.py:33
  (114 other events, 1574.1 us)

commit v3 on v2

--- a/solution.py
+++ b/solution.py
@@ -121,16 +121,24 @@
 
 
 LOW, WIDE = jnp.bfloat16, jnp.float32
-VMEM_LIMIT = 52 << 20
+VMEM_LIMIT = 46 << 20
+
+
+def in_hbm(array):
+    if array.size < 1 << 17:
+        return array
+    return pltpu.with_memory_space_constraint(array, pltpu.HBM)
+
+
 BLOCK = 512
 NO_COST = pl.CostEstimate(flops=1, bytes_accessed=1, transcendentals=0)
+SOME_COST = pl.CostEstimate(flops=10**8, bytes_accessed=2 * 10**6, transcendentals=0)
 FULL_COST = pl.CostEstimate(flops=40 * 10**9, bytes_accessed=10**8, transcendentals=0)
 
 
 class Weight:
-    def __init__(self, places, rows, columns, width, parts):
-        self.places, self.rows, self.columns, self.width = places, rows, columns, width
-        self.count = places.shape[0]
+    def __init__(self, count, rows, columns, width, parts):
+        self.count, self.rows, self.columns, self.width = count, rows, columns, width
         self.height = self.count * rows
         self.arrays = [group for _, _, groups in parts for group in groups]
         self.plan = [
@@ -208,7 +216,7 @@
             name: pltpu.make_async_copy(self.outs[name], ref, out_sems.at[number])
             for number, (name, ref) in enumerate(zip(outs, stored))
         }
-        self.waited = set()
+        self.waited, self.begun = set(), set()
 
     def start(self, order):
         for name in order:
@@ -242,24 +250,26 @@
         parts.start(order)
         for body in bodies:
             body(parts)
+        if "vectors" in outs:
+            parts.leave("vectors")
         parts.finish()
 
     arrays = [*loads.values(), *(array for weight in weights.values() for array in weight.arrays)]
+    scratch_shapes = [pltpu.VMEM(array.shape, array.dtype) for array in loads.values()]
+    scratch_shapes += [entry for weight in weights.values() for entry in weight.scratch()]
+    scratch_shapes += [pltpu.VMEM(*out) for out in outs.values()] + list(scratch.values())
     results = pl.pallas_call(
         kernel,
         in_specs=[pl.BlockSpec(memory_space=pltpu.SMEM)] * 2
         + [pl.BlockSpec(memory_space=pl.ANY)] * len(arrays),
         out_specs=[pl.BlockSpec(memory_space=pltpu.HBM)] * len(outs),
         out_shape=[pltpu.HBM(*out) for out in outs.values()],
-        scratch_shapes=[pltpu.VMEM(array.shape, array.dtype) for array in loads.values()]
-        + [entry for weight in weights.values() for entry in weight.scratch()]
-        + [pltpu.VMEM(*out) for out in outs.values()]
-        + list(scratch.values())
+        scratch_shapes=scratch_shapes
         + [pltpu.SemaphoreType.DMA((len(loads),)), pltpu.SemaphoreType.DMA((len(outs),))],
         compiler_params=pltpu.CompilerParams(vmem_limit_bytes=VMEM_LIMIT),
         cost_estimate=cost,
         name=name,
-    )(pick, places, *arrays)
+    )(pick, places, *(in_hbm(array) for array in arrays))
     return dict(zip(outs, results))
 
 
@@ -284,7 +294,7 @@
                     two = turned(two, cosine, sine)
                 ref[:, start + pair : start + pair + 2 * HEAD] = two.astype(LOW)
     parts.leave("q", "k", "v")
-    allowed = column_ref[micro_step] == row_ref[micro_step]
+    allowed = jnp.concatenate([column_ref[micro_step]] * 2, axis=1) == row_ref[micro_step]
     q_ref, k_ref, v_ref = outs
     mixture_ref, sum_ref, norm_ref, small_ref = parts.refs("mixture", "sum_one", "norm", "small")
     for start in range(0, width, 2 * HEAD):
@@ -355,7 +365,15 @@
         parts.leave("activations")
 
 
-def feed_back_part(parts):
+def vector_rows(parts):
+    vector_ref = parts.ref("vectors")
+    if "vectors" not in parts.begun:
+        parts.begun.add("vectors")
+        vector_ref[...] = jnp.zeros_like(vector_ref)
+    return vector_ref
+
+
+def norm_back_part(parts):
     if "docs" in parts.loads:
         own = jnp.sum(parts.ref("own_parts")[...].astype(WIDE), axis=0)
         embedded = jnp.concatenate([parts.ref("docs")[...], own], axis=0).astype(LOW)
@@ -365,28 +383,39 @@
         upstream = upstream * (1 - parts.pick[0]).astype(WIDE)
     else:
         upstream = parts.ref("back")[...].astype(WIDE)
-    branch_ref, gate_ref, attended_ref = parts.refs("branch", "gate", "attended")
-    vector_ref, up_bias_ref, total, small_ref = parts.refs("vectors", "grad_up_bias", "total", "small")
+    branch_ref, total, small_ref = parts.refs("branch", "total", "small")
+    vector_ref = vector_rows(parts)
     unit, scale = statistics(parts.ref("sum_two")[...])
     grad, gain, bias = norm_back(upstream, unit, scale, small_ref[4:5])
     low = grad.astype(LOW)
     branch_ref[...] = low
-    vector_ref[...] = jnp.zeros_like(vector_ref)
-    vector_ref[3:4] = jnp.sum(low.astype(WIDE), axis=0, keepdims=True)
-    vector_ref[4:5] = gain
-    vector_ref[5:6] = bias
     total[...] = grad
+    vector_ref[10:11] = jnp.sum(low.astype(WIDE), axis=0, keepdims=True)
+    vector_ref[11:12] = gain
+    vector_ref[12:13] = bias
     parts.leave("branch")
-    slope_ref = parts.ref("slope")
+    if "total" in parts.outs:
+        parts.leave("total")
+
+
+def feed_back_part(parts):
+    branch_ref, gate_ref, attended_ref = parts.refs("branch", "gate", "attended")
+    small_ref, slope_ref = parts.refs("small", "slope")
+    vector_ref = vector_rows(parts)
+    width = attended_ref.shape[1]
     down = parts.weights["down"].ready()
     for start in range(0, gate_ref.shape[1], BLOCK):
         at = slice(start, start + BLOCK)
         gate = product_nt(branch_ref[...], down[at]) * slope_ref[:, at].astype(WIDE)
         gate = gate.astype(LOW)
         gate_ref[:, at] = gate
-        up_bias_ref[:, at] = jnp.sum(gate.astype(WIDE), axis=0, keepdims=True)
-    parts.leave("gate", "grad_up_bias")
+        row, column = 6 + start // width, start % width
+        vector_ref[row : row + 1, column : column + BLOCK] = jnp.sum(
+            gate.astype(WIDE), axis=0, keepdims=True
+        )
+    parts.leave("gate")
     up = parts.weights["up"].ready()
+    total = parts.ref("total")
     for start in range(0, total.shape[1], BLOCK):
         at = slice(start, start + BLOCK)
         total[:, at] += product_nt(gate_ref[...], up[at])
@@ -395,10 +424,10 @@
     total[...] = grad
     low = grad.astype(LOW)
     attended_ref[...] = low
-    vector_ref[0:1] = jnp.sum(low.astype(WIDE), axis=0, keepdims=True)
-    vector_ref[1:2] = gain
-    vector_ref[2:3] = bias
-    parts.leave("attended", "vectors")
+    vector_ref[3:4] = jnp.sum(low.astype(WIDE), axis=0, keepdims=True)
+    vector_ref[4:5] = gain
+    vector_ref[5:6] = bias
+    parts.leave("attended")
     if "grad_one" in parts.outs:
         parts.ref("grad_one")[...] = grad
         parts.leave("grad_one")
@@ -406,12 +435,11 @@
 
 def attend_back_part(parts):
     micro_step = parts.pick[1]
-    attended_ref, mixed_ref, vector_ref, mixture, total = parts.refs(
-        "attended", "mixed", "qkv_vectors", "mixture", "total"
-    )
+    attended_ref, mixed_ref, mixture, total = parts.refs("attended", "mixed", "mixture", "total")
+    vector_ref = vector_rows(parts)
     cos_ref, sin_ref, column_ref, row_ref = parts.refs("cosine", "sine", "column", "row")
     cosine, sine = cos_ref[micro_step], sin_ref[micro_step]
-    allowed = column_ref[micro_step] == row_ref[micro_step]
+    allowed = jnp.concatenate([column_ref[micro_step]] * 2, axis=1) == row_ref[micro_step]
     width = mixture.shape[1]
     if "grad_one" in parts.loads:
         total[...] = parts.ref("grad_one")[...]
@@ -441,12 +469,10 @@
             mixed_ref[part, :, at] = turned(value, cosine, -sine).astype(LOW)
         mixed_ref[2, :, at] = (grads[0][2] + grads[1][2]).astype(LOW)
     parts.leave("mixed")
-    vector_ref[...] = jnp.zeros_like(vector_ref)
     for part in range(3):
         vector_ref[part : part + 1] = jnp.sum(
             mixed_ref[part].astype(WIDE), axis=0, keepdims=True
         )
-    parts.leave("qkv_vectors")
     qkv = parts.weights["qkv"].ready()
     for start in range(0, width, BLOCK):
         at = slice(start, start + BLOCK)
@@ -547,32 +573,33 @@
             cost=FULL_COST,
         )
 
-    def feed_back_set(self, state, loss_grads, back_grad):
+    def norm_back_set(self, state, loss_grads, back_grad):
+        rows = (ROWS, self.down.columns)
+        outs = {"branch": (rows, LOW), "vectors": ((16, rows[1]), WIDE)}
+        if loss_grads is not None:
+            loads = dict(zip(("docs", "own_parts", "projection"), loss_grads))
+            outs["grad_embedded"] = ((ROWS, PROJ), LOW)
+        else:
+            loads = {"back": back_grad}
+        loads |= {"sum_two": state["sum_two"], "small": self.small}
+        return loads, {}, outs, {"total": pltpu.VMEM(rows, WIDE)}
+
+    def feed_back_set(self, state):
         rows, hidden = (ROWS, self.down.columns), self.up.columns
-        loads, outs = {}, {}
-        if loss_grads is not None:
-            loads |= dict(zip(("docs", "own_parts", "projection"), loss_grads))
-            outs["grad_embedded"] = ((ROWS, PROJ), LOW)
-        if back_grad is not None:
-            loads["back"] = back_grad
-        loads |= {"sum_two": state["sum_two"], "small": self.small, "slope": state["slope"]}
-        outs |= {
-            "branch": (rows, LOW),
-            "gate": ((ROWS, hidden), LOW),
-            "attended": (rows, LOW),
-            "vectors": ((8, rows[1]), WIDE),
-            "grad_up_bias": ((1, hidden), WIDE),
-        }
         return (
-            loads,
+            {"slope": state["slope"], "small": self.small},
             {"down": self.down, "up": self.up},
-            outs,
+            {
+                "gate": ((ROWS, hidden), LOW),
+                "attended": (rows, LOW),
+                "vectors": ((16, rows[1]), WIDE),
+            },
             {"total": pltpu.VMEM(rows, WIDE)},
         )
 
     def attend_back_set(self, state, earlier):
         rows = (ROWS, self.out.columns)
-        outs = {"mixed": ((3, *rows), LOW), "qkv_vectors": ((8, rows[1]), WIDE)}
+        outs = {"mixed": ((3, *rows), LOW), "vectors": ((16, rows[1]), WIDE)}
         loads = {"q": state["q"], "k": state["k"], "v": state["v"], **self.layout}
         if earlier:
             loads |= dict(zip(("late", "early", "own"), earlier))
@@ -589,9 +616,10 @@
     def backward(self, state, loss_grads, back_grad, pick):
         return self.run(
             "backward",
-            [feed_back_part, attend_back_part],
+            [norm_back_part, feed_back_part, attend_back_part],
             [
-                self.feed_back_set(state, loss_grads, back_grad),
+                self.norm_back_set(state, loss_grads, back_grad),
+                self.feed_back_set(state),
                 ({"sum_one": state["sum_one"]}, {}, {}, {}),
                 self.attend_back_set(state, ()),
             ],
@@ -599,16 +627,21 @@
             cost=FULL_COST,
         )
 
-    def feed_back(self, state, back_grad, pick):
-        rows = (ROWS, self.down.columns)
+    def norm_back(self, state, back_grad, pick):
+        loads, weights, outs, scratch = self.norm_back_set(state, None, back_grad)
+        outs |= {"total": (state["sum_two"].shape, WIDE)}
+        return self.run("norm_back", [norm_back_part], [(loads, weights, outs, {})], pick)
+
+    def feed_back(self, state, branch, total, pick):
+        loads, weights, outs, scratch = self.feed_back_set(state)
+        outs |= {"grad_one": (total.shape, WIDE)}
+        loads = {"branch": branch} | loads
         return self.run(
             "feed_back",
             [feed_back_part],
-            [
-                self.feed_back_set(state, None, back_grad),
-                ({"sum_one": state["sum_one"]}, {}, {"grad_one": (rows, WIDE)}, {}),
-            ],
+            [(loads, weights, outs, {}), ({"total": total, "sum_one": state["sum_one"]}, {}, {}, {})],
             pick,
+            cost=FULL_COST,
         )
 
     def attend_back(self, state, attended, grad_one, earlier, pick):
@@ -618,6 +651,7 @@
             [self.attend_back_set(state, earlier)],
             pick,
             {"attended": attended, "grad_one": grad_one},
+            cost=FULL_COST,
         )
 
 
@@ -651,12 +685,16 @@
     return lax.optimization_barrier((value, *earlier))[0]
 
 
-def stage(sends, dims, earlier):
-    values = lax.optimization_barrier((*(value for value, _, _ in sends), *earlier))
-    arrived = [
-        shifted(value, dims, dim, steps) for value, (_, dim, steps) in zip(values, sends)
-    ]
-    return list(lax.optimization_barrier(tuple(arrived)))
+def stage(sends, earlier, beside=None):
+    values = [after(value, *earlier) for value, _ in sends]
+    backwards = list(zip(values, sends))[::-1]
+    arrived = [permuted(value) for value, (_, permuted) in backwards][::-1]
+    made = beside(earlier, arrived) if beside else []
+    return list(lax.optimization_barrier((*arrived, *made)))[: len(sends)]
+
+
+def step_along(dims, dim, steps):
+    return lambda value: shifted(value, dims, dim, steps)
 
 
 def rows_kernel(top, places, *refs):
@@ -691,39 +729,46 @@
     )(places, *groups)
 
 
+def block_owners(order, dims, at):
+    owners = jnp.zeros((1,), jnp.int32)
+    for dim in order:
+        steps = jnp.arange(dims[dim], dtype=jnp.int32)
+        own = ((at[dim] - steps) % dims[dim]) * math.prod(dims[dim + 1 :])
+        owners = (own[:, None] + owners[None, :]).reshape(-1)
+    return owners
+
+
 class Gather:
-    def __init__(self, chunks, dims, at):
+    def __init__(self, chunks, dims):
         self.dims, self.chunks = dims, chunks
-        self.held = [[value[None]] for value in chunks]
+        self.held = [[value[None]] for value, _, _ in chunks]
         self.arrived, self.step = [], 0
-        owners = jnp.zeros((1,), jnp.int32)
-        for dim in range(len(dims)):
-            steps = jnp.arange(dims[dim], dtype=jnp.int32)
-            own = ((at[dim] - steps) % dims[dim]) * math.prod(dims[dim + 1 :])
-            owners = (own[:, None] + owners[None, :]).reshape(-1)
-        self.owners = owners
-
-    def until(self, number):
-        while self.step < number + len(self.dims):
+
+    def groups(self, number):
+        _, order, start = self.chunks[number]
+        while self.step < start + len(order):
             self.advance()
         return self.held[number]
 
-    def advance(self, *earlier):
+    def advance(self, *needed):
         sends, takers = [], []
-        for dim in range(len(self.dims)):
-            number = self.step - dim
-            if 0 <= number < len(self.chunks):
+        for number, (value, order, start) in enumerate(self.chunks):
+            if start <= self.step < start + len(order):
+                dim = order[self.step - start]
                 for steps in range(1, self.dims[dim]):
                     for group in self.held[number]:
-                        sends.append((group, dim, steps))
+                        sends.append((group, step_along(self.dims, dim, steps)))
                         takers.append(number)
-        self.arrived = stage(sends, self.dims, [*self.arrived, *earlier])
+        self.arrived = stage(sends, [*self.arrived, *needed])
         for number in sorted(set(takers)):
-            got = [value for value, taker in zip(self.arrived, takers) if taker == number]
-            if self.step - number < len(self.dims) - 2:
-                self.held[number] = [jnp.concatenate(self.held[number] + got)]
-            else:
-                self.held[number] = self.held[number] + got
+            value, order, start = self.chunks[number]
+            got = [one for one, taker in zip(self.arrived, takers) if taker == number]
+            held = self.held[number] + got
+            blocks = sum(group.shape[0] for group in held)
+            last = self.step - start >= len(order) - 2
+            if not last or (blocks * value.size < 1 << 20 and self.step - start < len(order) - 1):
+                held = [jnp.concatenate(held)]
+            self.held[number] = held
         self.step += 1
 
 
@@ -758,7 +803,7 @@
     return pltpu.make_async_copy(pair[0].at[place], target, sem)
 
 
-def grad_kernel(pick_ref, *refs, rows, slots, outer, start, sends):
+def grad_kernel(pick_ref, *refs, rows, slots, outer, stride, start, other_start, sends):
     lefts, rights, refs = (refs[0:2], refs[2:4]), (refs[4:6], refs[6:8]), refs[8:]
     if not sends:
         other_ref, *refs = refs
@@ -771,7 +816,7 @@
     samples = lefts[0][0].shape[0]
     side = 1 - pick_ref[1] if sends else pick_ref[1]
     thin = rows % 128 != 0
-    block = min(BLOCK, width) if thin else width
+    block = min(2 * BLOCK, width) if thin else width
     blocks = width // block
     wide_part = rights[0][0].shape[-1]
 
@@ -812,18 +857,20 @@
         ]
 
     def chip_of(number):
-        return (number % outer) * slots + lax.rem(pick_ref[2] + number // outer, slots)
+        inner = number % outer
+        first_chip = inner // stride * stride * slots + inner % stride
+        return first_chip + stride * lax.rem(pick_ref[2] + number // outer, slots)
 
     def other_copy(number):
         if thin:
             return pltpu.make_async_copy(
-                other_ref.at[pl.ds(0, chips * rows), pl.ds(start + number * block, block)],
+                other_ref.at[pl.ds(0, chips * rows), pl.ds(other_start + number * block, block)],
                 other.at[:, number * block : (number + 1) * block],
                 other_sems.at[number],
             )
         return pltpu.make_async_copy(
             other_ref.at[
-                pl.ds(pl.multiple_of(chip_of(number) * rows, rows), rows), pl.ds(start, width)
+                pl.ds(pl.multiple_of(chip_of(number) * rows, rows), rows), pl.ds(other_start, width)
             ],
             other.at[number * rows : (number + 1) * rows],
             other_sems.at[number],
@@ -899,48 +946,42 @@
     wait(leaving)
 
 
-def fold_kernel(pick_ref, held_ref, other_ref, out_ref, *send_refs, slots, thin_rows):
+def fold_kernel(pick_ref, held_ref, other_ref, out_ref, *send_refs, slots, stride):
     for slot in range(slots):
         place = lax.rem(pick_ref[0] + slot, slots)
         for number in range(out_ref.shape[0]):
-            index = number * slots + place
+            index = number // stride * stride * slots + number % stride + place * stride
             value = held_ref[index].astype(WIDE) + other_ref[index].astype(WIDE)
             if slot == 0:
                 out_ref[number] = value
                 continue
             send_refs[slot - 1][number] = value.astype(LOW)
-            if thin_rows:
-                pair = value[thin_rows : thin_rows + 1] + value[thin_rows + 1 : thin_rows + 2]
-                high, low = halves(pair)
-                ids = lax.broadcasted_iota(jnp.int32, (16, value.shape[1]), 0)
-                send_refs[slot - 1][number, thin_rows:] = jnp.where(
-                    ids == 0, high.astype(WIDE), jnp.where(ids == 1, low.astype(WIDE), 0.0)
-                ).astype(LOW)
-
-
-def terms(value):
-    high = lax.reduce_precision(value, 8, 7)
-    return high.astype(LOW), (value - high).astype(LOW)
+
+
+def slots_of(value, slots, stride):
+    return value.reshape(-1, slots, stride, *value.shape[1:])
 
 
 class Scatter:
-    def __init__(self, name, lefts, rights, dims, at, first):
+    def __init__(self, name, lefts, rights, dims, at, dim, first):
         self.name, self.lefts, self.rights, self.dims, self.at = name, lefts, rights, dims, at
         self.count = math.prod(dims)
         self.height = lefts[0][0].shape[1]
         self.rows = self.height // self.count
         sample = rights[0][0]
         self.columns = sample.shape[-1] * (3 if sample.ndim == 3 else 1)
-        self.pick = jnp.stack([first, at[-1], at[-2]])
-
-    def product(self, start, width, other, quick=False):
+        self.slots, self.stride = dims[dim], math.prod(dims[dim + 1 : -1])
+        self.place = at[dim]
+        self.pick = jnp.stack([first, at[-1], self.place])
+
+    def product(self, start, width, other, other_start, cost, earlier=()):
         samples = self.lefts[0][0].shape[0]
-        half, rows, slots = self.height // 2, self.rows, self.dims[-2]
+        half, rows, slots = self.height // 2, self.rows, self.slots
         chips = self.count // 2
         outer = chips // slots
         sends = other is None
         thin = rows % 128 != 0
-        blocks = width // min(BLOCK, width) if thin else 1
+        blocks = width // min(2 * BLOCK, width) if thin else 1
         pieces = 1 if thin else chips
         anywhere = pl.BlockSpec(memory_space=pl.ANY)
         args = [*self.lefts[0], *self.lefts[1], *self.rights[0], *self.rights[1]]
@@ -949,71 +990,106 @@
         other_scratch = [] if sends else [pltpu.VMEM((half, width), LOW)]
         other_sems = [] if sends else [pltpu.SemaphoreType.DMA((blocks if thin else chips,))]
         outs = [(half, width)] if sends else [(outer, rows, width)] * slots
+        scratch = [
+            pltpu.VMEM((2 * samples, self.height if thin else half), LOW),
+            pltpu.VMEM((2 * samples, width), LOW),
+            *other_scratch,
+            pltpu.VMEM((half, width), LOW),
+        ]
         return pl.pallas_call(
             partial(
-                grad_kernel, rows=rows, slots=slots, outer=outer, start=start, sends=sends
+                grad_kernel,
+                rows=rows,
+                slots=slots,
+                outer=outer,
+                stride=self.stride,
+                start=start,
+                other_start=other_start,
+                sends=sends,
             ),
             in_specs=[pl.BlockSpec(memory_space=pltpu.SMEM)] + [anywhere] * len(args),
             out_specs=[anywhere] * len(outs),
             out_shape=[jax.ShapeDtypeStruct(out, LOW) for out in outs],
             scratch_shapes=[
-                pltpu.VMEM((2 * samples, self.height if thin else half), LOW),
-                pltpu.VMEM((2 * samples, width), LOW),
-                *other_scratch,
-                pltpu.VMEM((half, width), LOW),
+                *scratch,
                 pltpu.SemaphoreType.DMA((pieces, 2)),
                 pltpu.SemaphoreType.DMA((blocks, 2)),
                 *other_sems,
                 pltpu.SemaphoreType.DMA((out_sems,)),
             ],
             compiler_params=pltpu.CompilerParams(vmem_limit_bytes=VMEM_LIMIT),
-            cost_estimate=NO_COST if sends or quick else FULL_COST,
+            cost_estimate=cost,
             name=self.name + ("_send" if sends else "_keep"),
-        )(self.pick, *args)
-
-    def send(self, extra=None):
-        sent = self.product(0, self.columns, None)[0]
-        self.extra = None
-        if extra is not None:
-            split = extra.reshape(-1, 2, extra.shape[1])
-            sent = jnp.concatenate(
-                [sent, *terms(lax.dynamic_index_in_dim(split, 1 - self.at[-1], 1, False))]
+        )(after(self.pick, *earlier), *(in_hbm(array) for array in args))
+
+    def make(self, cost, earlier=(), start=0, width=None):
+        self.sent = self.product(start, width or self.columns, None, 0, cost, earlier)[0]
+        self.other_from = start
+        return self.sent
+
+    def keep(self, start, width, cost, earlier=()):
+        return self.product(start, width, self.other, start - self.other_from, cost, earlier)
+
+
+def own_kernel(where_ref, vectors_ref, *out_refs, spans):
+    width = vectors_ref.shape[1]
+    for (first_row, rows, length), out_ref in zip(spans, out_refs):
+        start = where_ref[0] * length
+        if rows > 1 and width % length == 0:
+            line = vectors_ref[pl.ds(first_row + start // width, 1)]
+        else:
+            line = jnp.concatenate(
+                [vectors_ref[first_row + row : first_row + row + 1] for row in range(rows)], axis=1
             )
-        self.other = shifted(sent, self.dims, len(self.dims) - 1, 1)
-        if extra is not None:
-            held = lax.dynamic_index_in_dim(split, self.at[-1], 1, False)
-            arrived = self.other[self.height // 2 :].astype(WIDE)
-            held = held + arrived[: held.shape[0]] + arrived[held.shape[0] :]
-            rows = jnp.stack(terms(held), axis=1)
-            rows = jnp.pad(rows, [(0, 0), (0, 14), (0, 0)])
-            self.extra = rows.reshape(-1, self.dims[-2], 16, extra.shape[1])
-
-    def keep(self, start, width, quick=False):
-        pieces = self.product(start, width, self.other, quick)
-        if self.extra is not None:
-            pieces = [
-                jnp.concatenate(
-                    [
-                        piece,
-                        lax.dynamic_index_in_dim(
-                            self.extra, (self.at[-2] + slot) % self.dims[-2], 1, False
-                        ),
-                    ],
-                    axis=1,
-                )
-                for slot, piece in enumerate(pieces)
-            ]
-        return pieces
-
-
-def folded(held, moved, dims, dim, at, thin_rows):
+        turns = lax.rem(line.shape[1] - lax.rem(start, line.shape[1]), line.shape[1])
+        line = pltpu.roll(jnp.broadcast_to(line, (8, line.shape[1])), turns, 1)
+        out_ref[...] = line[0:1, :length]
+
+
+def own_parts(vectors, spans, dp_index):
+    return pl.pallas_call(
+        partial(own_kernel, spans=spans),
+        in_specs=[
+            pl.BlockSpec(memory_space=pltpu.SMEM),
+            pl.BlockSpec(memory_space=pltpu.VMEM),
+        ],
+        out_specs=[pl.BlockSpec(memory_space=pltpu.VMEM)] * len(spans),
+        out_shape=[jax.ShapeDtypeStruct((1, length), WIDE) for _, _, length in spans],
+        name="own_parts",
+    )(dp_index[None], vectors)
+
+
+class Whole:
+    def __init__(self, value):
+        self.value = value
+
+    def outgoing(self, dim):
+        return self.value
+
+    def take(self, arrived):
+        self.value = self.value + arrived
+
+
+class Halved:
+    def __init__(self, value, dims, at):
+        self.value, self.dims, self.at = value, dims, at
+
+    def outgoing(self, dim):
+        split = self.value.reshape(-1, self.dims[dim], *self.value.shape[1:])
+        self.kept = lax.dynamic_index_in_dim(split, self.at[dim], 1, False)
+        return lax.dynamic_index_in_dim(split, 1 - self.at[dim], 1, False)
+
+    def take(self, arrived):
+        self.value = self.kept + arrived
+
+
+def folded(held, moved, slots, stride, place):
     outer, rows, columns = held.shape
-    slots = dims[dim]
     if rows % 16 == 0 and len(moved) == 1:
         whole = pl.BlockSpec(memory_space=pltpu.VMEM)
         shape = (outer // slots, rows, columns)
         total, *sends = pl.pallas_call(
-            partial(fold_kernel, slots=slots, thin_rows=thin_rows),
+            partial(fold_kernel, slots=slots, stride=stride),
             out_shape=[jax.ShapeDtypeStruct(shape, WIDE)]
             + [jax.ShapeDtypeStruct(shape, LOW)] * (slots - 1),
             in_specs=[pl.BlockSpec(memory_space=pltpu.SMEM), whole, whole],
@@ -1021,48 +1097,67 @@
             compiler_params=pltpu.CompilerParams(vmem_limit_bytes=24 << 20),
             cost_estimate=NO_COST,
             name="fold",
-        )(at[dim][None], held, moved[0])
+        )(place[None], held, moved[0])
         return total, sends
     total = held.astype(WIDE)
     for piece in moved:
         total = total + piece.astype(WIDE)
-    split = total.reshape(outer // slots, slots, rows, columns)
+    split = slots_of(total, slots, stride)
     blocks = [
-        lax.dynamic_index_in_dim(split, (at[dim] + steps) % slots, 1, False)
+        lax.dynamic_index_in_dim(split, (place + steps) % slots, 1, False).reshape(-1, rows, columns)
         for steps in range(slots)
     ]
     return blocks[0], [block.astype(LOW) for block in blocks[1:]]
 
 
-def travels(makers, dims, at, own_rows, before):
-    chip_dims = list(reversed(range(len(dims) - 1)))
+def travels(pieces, chunks, order, dims, at, cores, riders, during):
     held, sends, sums = {}, {}, {}
-    arrived = []
-    for step in range(len(makers) + len(chip_dims) - 1):
-        if step < len(makers):
-            held[step], *sends[step] = makers[step](arrived)
+    arrived, riding = [], []
+    ways = list(reversed(range(len(dims))))
+    for step in range(chunks + len(order) - 1):
+        if step < chunks:
+            held[step], *sends[step] = pieces[step]
+        if step in riders:
+            riding += [(rider, step) for rider in riders[step]()]
         outgoing, takers = [], []
-        for phase, dim in enumerate(chip_dims):
+        for phase, dim in enumerate(order):
             number = step - phase
-            if 0 <= number < len(makers):
-                outgoing += [(value, dim, k) for k, value in enumerate(sends[number], start=1)]
+            if 0 <= number < chunks:
+                outgoing += [
+                    (value, step_along(dims, dim, k)) for k, value in enumerate(sends[number], start=1)
+                ]
                 takers += [number] * len(sends[number])
-        arrived = stage(outgoing, dims, [*arrived, *before.get(step, lambda _: ())(arrived)])
-        for phase, dim in enumerate(chip_dims):
+        exchanging = cores.get(step, lambda: [])()
+        outgoing += [(weight.sent, step_along(dims, ways[0], 1)) for weight in exchanging]
+        along = [(rider, ways[step - start]) for rider, start in riding if step - start < len(ways)]
+        outgoing += [(rider.outgoing(dim), step_along(dims, dim, 1)) for rider, dim in along]
+
+        def beside(earlier, arriving):
+            for weight, half in zip(exchanging, arriving[len(takers) :]):
+                weight.other = half
+            return during[step](earlier) if step < len(during) else []
+
+        arrived = stage(outgoing, arrived, beside)
+        for (rider, _), part in zip(along, arrived[len(takers) + len(exchanging) :]):
+            rider.take(part)
+        arrived = arrived[: len(takers)]
+        for phase, dim in enumerate(order):
             number = step - phase
-            if 0 <= number < len(makers):
-                moved = [value for value, taker in zip(arrived, takers) if taker == number]
-                if dim:
-                    rows = held[number].shape[1]
-                    held[number], sends[number] = folded(
-                        held[number], moved, dims, dim - 1, at, own_rows if rows == own_rows + 16 else 0
-                    )
-                else:
-                    total = held[number].astype(WIDE)
-                    for piece in moved:
-                        total = total + piece.astype(WIDE)
-                    sums[number] = total.reshape(total.shape[-2:])
-    return [sums[number] for number in range(len(makers))]
+            if not 0 <= number < chunks:
+                continue
+            moved = [value for value, taker in zip(arrived, takers) if taker == number]
+            left = order[phase + 1 :]
+            if left:
+                stride = math.prod(dims[other] for other in left if other > left[0])
+                held[number], sends[number] = folded(
+                    held[number], moved, dims[left[0]], stride, at[left[0]]
+                )
+            else:
+                total = held[number].astype(WIDE)
+                for piece in moved:
+                    total = total + piece.astype(WIDE)
+                sums[number] = total.reshape(total.shape[-2:])
+    return [sums[number] for number in range(chunks)]
 
 
 def spread(value, count):
@@ -1229,7 +1324,7 @@
             for value in (jnp.sum(picked, axis=2), picked[..., 0])
         ]
         self.params = dict(
-            grid=(self.steps,), compiler_params=pltpu.CompilerParams(vmem_limit_bytes=VMEM_LIMIT)
+            grid=(self.steps,), compiler_params=pltpu.CompilerParams(vmem_limit_bytes=40 << 20)
         )
         self.queries_spec = pl.BlockSpec((self.group, QRY_DEV * QLEN, PROJ), lambda i: (i, 0, 0))
         self.smem = pl.BlockSpec(memory_space=pltpu.SMEM)
@@ -1324,7 +1419,8 @@
         jnp.stack(value)
         for value in zip(*(doc_layout(doc_lengths[micro_step]) for micro_step in range(MICRO)))
     ]
-    layout = (*rotary(positions), segments[:, :, None], segments[:, None, :])
+    by_row = jnp.broadcast_to(segments[:, :, None], (MICRO, ROWS, ROWS // 2))
+    layout = (*rotary(positions), by_row, segments[:, None, :])
     picks = [jnp.stack([first, jnp.int32(micro_step)]) for micro_step in range(MICRO)]
     own_rows = [tokens[micro_step * ROWS : (micro_step + 1) * ROWS] for micro_step in range(MICRO)]
     ends = jnp.cumsum(doc_lengths, axis=1)
@@ -1376,27 +1472,29 @@
         line = jnp.concatenate([*vectors, jnp.zeros((1, width - short), LOW)], axis=1)
         proj_lines = proj_weight.reshape(-1, width)
         filler = jnp.zeros((15 - proj_lines.shape[0], width), LOW)
-        chunks = [jnp.concatenate([shards_of[0], line, proj_lines, filler])]
+        order = list(range(len(dims)))
+        chunks = [(jnp.concatenate([shards_of[0], line, proj_lines, filler]), order, 0)]
         cuts_of = ([1], [1, 2], [2, 2], [2, 2])
         for number in (1, 2, 3):
             parts, shard = cuts_of[number], shards_of[number]
             unit, start = shard.shape[1] // sum(parts), 0
             for part in parts:
-                chunks.append(lax.slice_in_dim(shard, start, start + part * unit, axis=1))
+                value = lax.slice_in_dim(shard, start, start + part * unit, axis=1)
+                chunks.append((value, order, len(chunks)))
                 start += part * unit
-        gather = Gather(chunks, dims, at)
-        layer = Layer(gather.owners, layout)
+        gather = Gather(chunks, dims)
+        layer = Layer(block_owners(order, dims, at), layout)
 
         def whole(number, first_chunk):
             parts, start = [], 0
             unit = shards_of[number].shape[1] // sum(cuts_of[number])
             for offset, part in enumerate(cuts_of[number]):
-                parts.append((start, part * unit, gather.until(first_chunk + offset)))
+                parts.append((start, part * unit, gather.groups(first_chunk + offset)))
                 start += part * unit
-            return Weight(gather.owners, shards_of[number].shape[0], start, fetched[number], parts)
+            return Weight(count, shards_of[number].shape[0], start, fetched[number], parts)
 
         layer.out = whole(0, 0)
-        block = placed_rows(layer.out.arrays, gather.owners, own_height, 16)
+        block = placed_rows(layer.out.arrays, layer.places, own_height, 16)
         projection = small_parameters(
             layer, block[:, 0], block[:, 1 : 1 + proj_lines.shape[0]]
         )
@@ -1416,7 +1514,7 @@
             lax.all_gather(value, "dp", axis=0, tiled=True)[None] for value in shards_of
         ]
         layer.out, layer.qkv, layer.up, layer.down = [
-            Weight(layer.places, *value.shape[1:], columns, [(0, value.shape[2], [value])])
+            Weight(1, *value.shape[1:], columns, [(0, value.shape[2], [value])])
             for value, columns in zip(wholes, fetched)
         ]
         together = spread(jnp.concatenate([*vectors, proj_weight.reshape(1, -1)], axis=1)[0], count)
@@ -1458,6 +1556,8 @@
             projection,
         )
     own_losses = jnp.concatenate(own_losses)
+    query_losses = jnp.where(is_first, from_behind(own_losses, "section", -1), own_losses)
+    loss_grads[0] = (after(loss_grads[0][0], query_losses), *loss_grads[0][1:])
 
     back, back_grads = [], []
     for micro_step in reversed(range(MICRO)):
@@ -1465,24 +1565,10 @@
             layer.backward(states[MICRO + micro_step], loss_grads[micro_step], None, picks[micro_step])
         )
         back_grads.append(from_behind(back[-1]["grad_low"], "section", -1))
-    def exchanged(earlier):
-        proj_total = product_tn(
-            jnp.concatenate([state["result"] for state in states[:1:-1]]),
-            after(jnp.concatenate([grads["grad_embedded"] for grads in back[:MICRO]]), *earlier),
-        ) * section_index.astype(WIDE)
-        proj_parts = proj_total.reshape(2, count, -1, proj_total.shape[1])
-        proj_own = summed(jnp.swapaxes(proj_parts, 0, 1))
-        proj_other, loss_other = [
-            from_behind(value, "section", -1) for value in (proj_own[0], after(own_losses, *earlier))
-        ]
-        return (
-            jnp.where(is_first, proj_other, proj_own[1]),
-            jnp.where(is_first, loss_other, own_losses),
-        )
-
     back.append(layer.backward(states[1], None, back_grads[0], picks[1]))
     back_grad = after(back_grads[1], back[-1]["mixed"])
-    grads = layer.feed_back(states[0], back_grad, picks[0])
+    grads = layer.norm_back(states[0], back_grad, picks[0])
+    vectors_of = [one["vectors"] for one in (*back, grads)]
 
     def pairs(values):
         return [values[1], values[3]], [values[0], values[2]]
@@ -1494,66 +1580,103 @@
     def rights_of(name):
         return pairs([grads[name], *(back[number][name] for number in (2, 1, 0))])
 
-    def scatter(name, number, right):
-        return Scatter(name, lefts[number], rights_of(right), dims, at, first)
-
-    attended = grads["attended"]
+    def feed_back(*earlier):
+        grads.update(
+            layer.feed_back(states[0], after(grads["branch"], *earlier), grads["total"], picks[0])
+        )
+
+    def attend_back(*earlier):
+        grads.update(
+            layer.attend_back(
+                states[0],
+                after(grads["attended"], *earlier),
+                grads["grad_one"],
+                [one["grad_source"] for one in back],
+                picks[0],
+            )
+        )
+
     if by_hand:
-        of_down, of_up = scatter("down", 0, "branch"), scatter("up", 1, "gate")
-        of_down.send()
-        of_up.send()
-        down_first = of_down.keep(0, width // 2)
-        attended = after(attended, *down_first)
-    grads |= layer.attend_back(
-        states[0], attended, grads["grad_one"], [one["grad_source"] for one in back], picks[0]
-    )
-    grad_inputs = grads["grad_source"]
-    grad_vectors = [
-        (
-            one["qkv_vectors"][:3].reshape(-1),
-            *(one["vectors"][number] for number in range(3)),
-            one["grad_up_bias"][0],
-            *(one["vectors"][number] for number in range(3, 6)),
-        )
-        for one in (*back, grads)
-    ]
-    totals = [sum(values) for values in zip(*grad_vectors)]
-    packed = jnp.concatenate([value.reshape(count, -1) for value in totals], axis=1)
-    if by_hand:
-        of_out, of_qkv = scatter("out", 2, "attended"), scatter("qkv", 3, "mixed")
-        of_qkv.send()
-        of_out.send(jnp.pad(packed, [(0, 0), (0, width - packed.shape[1])]))
-
-        def maker(weight, start, columns, quick=False):
-            return lambda arrived: weight.keep(start, columns, quick)
-
-        shared = []
-
-        def exchange(arrived):
-            shared.extend(exchanged(arrived))
-            return ()
-
+        last_dim = len(dims) - 2
+        weights = {}
+
+        def weight_of(name, number, right):
+            weights[name] = Scatter(
+                name, lefts[number], rights_of(right), dims, at, last_dim, first
+            )
+            return weights[name]
+
+        half = width // 2
+        downs = [weight_of("down", 0, "branch") for _ in range(2)]
+        for number, (weight, earlier) in enumerate(zip(downs, ([], [downs[0]]))):
+            weight.make(NO_COST, [one.sent for one in earlier], number * half, half)
+            weight.other = shifted(weight.sent, dims, len(dims) - 1, 1)
+        pieces = {0: downs[0].keep(0, half, NO_COST, [downs[1].sent])}
+
+        def first_stage(earlier):
+            feed_back(*pieces[0])
+            vectors_of.append(grads["vectors"])
+            sent = weight_of("up", 1, "gate").make(SOME_COST)
+            pieces[1] = downs[1].keep(half, half, SOME_COST, [sent])
+            return pieces[1]
+
+        def second_stage(earlier):
+            attend_back(*earlier)
+            vectors_of.append(grads["vectors"])
+            pieces[2] = weights["up"].keep(0, hidden // 2, SOME_COST, [grads["mixed"]])
+            return pieces[2]
+
+        def third_stage(earlier):
+            sent = weight_of("qkv", 3, "mixed").make(FULL_COST, earlier)
+            sent = weight_of("out", 2, "attended").make(FULL_COST, [sent])
+            pieces[3] = weights["up"].keep(hidden // 2, hidden // 2, FULL_COST, [sent])
+            return pieces[3]
+
+        def fourth_stage(earlier):
+            pieces[4] = weights["qkv"].keep(0, 2 * width, FULL_COST, earlier)
+            pieces[5] = weights["qkv"].keep(2 * width, width, FULL_COST, pieces[4])
+            return pieces[5]
+
+        def fifth_stage(earlier):
+            pieces[6] = weights["out"].keep(0, width, FULL_COST, earlier)
+            return pieces[6]
+
+        def projection_grad():
+            total = product_tn(
+                jnp.concatenate([state["result"] for state in states[:1:-1]]),
+                jnp.concatenate([one["grad_embedded"] for one in back[:MICRO]]),
+            ) * section_index.astype(WIDE)
+            parts = jnp.swapaxes(total.reshape(2, count, -1, total.shape[1]), 0, 1)
+            riding.append(Halved(parts, dims, at))
+            return riding[-1]
+
+        def vector_grads():
+            riding.append(Whole(sum(vectors_of)))
+            return riding[-1]
+
+        riding = []
         sums = travels(
-            [
-                lambda arrived: down_first,
-                maker(of_down, width // 2, width // 2, True),
-                maker(of_up, 0, hidden // 2, True),
-                maker(of_up, hidden // 2, hidden // 2),
-                maker(of_qkv, 0, 2 * width),
-                maker(of_qkv, 2 * width, width),
-                maker(of_out, 0, width),
-            ],
+            pieces,
+            7,
+            list(reversed(range(last_dim + 1))),
             dims,
             at,
-            own_height,
-            {1: lambda _: [grads["mixed"]], 5: exchange, 7: lambda _: shared},
-        )
-        proj_grad, query_losses = shared
+            {
+                1: lambda: [weights["up"]],
+                3: lambda: [weights["qkv"], weights["out"]],
+            },
+            {4: lambda: [projection_grad(), vector_grads()]},
+            [first_stage, second_stage, third_stage, fourth_stage, fifth_stage],
+        )
+        proj_own, own_vectors = riding[0].value[0], riding[1].value
         grad_down, grad_up, grad_qkv = (
             jnp.concatenate(group, axis=1)[None] for group in (sums[0:2], sums[2:4], sums[4:6])
         )
-        grad_out, own = sums[6][None, :own_height], sums[6][own_height] + sums[6][own_height + 1]
+        grad_out = sums[6][None]
     else:
+        feed_back()
+        vectors_of.append(grads["vectors"])
+        attend_back()
         weight_grads = []
         for number, name in enumerate(("branch", "gate", "attended", "mixed")):
             left = jnp.concatenate([jnp.where(is_first, *pair) for pair in lefts[number]])
@@ -1564,14 +1687,25 @@
                 scatter_rows_plain(left, jnp.concatenate(right), dims, dp_index)[None]
             )
         grad_down, grad_up, grad_out, grad_qkv = weight_grads
-        own = summed(packed)
-        proj_grad, query_losses = exchanged(())
-    small_grads, start = [], 0
-    for length in lengths:
-        small_grads.append(own[None, start : start + length])
-        start += length
+        own_vectors = lax.psum(sum([*vectors_of, grads["vectors"]]), "dp")
+        proj_total = product_tn(
+            jnp.concatenate([state["result"] for state in states[:1:-1]]),
+            jnp.concatenate([one["grad_embedded"] for one in back[:MICRO]]),
+        ) * section_index.astype(WIDE)
+        proj_own = summed(jnp.swapaxes(proj_total.reshape(2, count, -1, PROJ), 0, 1))
+    grad_inputs = grads["grad_source"]
+    proj_grad = jnp.where(is_first, from_behind(proj_own[0], "section", -1), proj_own[1])
     grad_qkv_b, grad_out_b, grad_gain1, grad_bias1, grad_up_b, grad_down_b, grad_gain2, grad_bias2 = (
-        small_grads
+        own_parts(
+            own_vectors,
+            [
+                (first_row, rows, rows * width // count)
+                for first_row, rows in (
+                    (0, 3), (3, 1), (4, 1), (5, 1), (6, hidden // width), (10, 1), (11, 1), (12, 1)
+                )
+            ],
+            dp_index,
+        )
     )
     return (
         query_losses,

time: 698 us -> 673 us (0.964)
  waiting for transfers between devices: 197 us -> 180 us
  other arithmetic: 39.3 us -> 29.1 us
    all_to_all x3, waiting for transfers between devices: 24.4 us -> 15.7 us  [spread(): lax.all_to_all(jnp.broadcast_to(value[None], (count, *value.shape)), 'dp'...]
    ppermute x6, waiting for transfers between devices: 12.9 us -> 4.8 us  [from_behind(): lax.ppermute(value, axis, [(source, source + steps) for source in range(f...]
    pallas_call x11 -> x12, Pallas kernels: 58.7 us -> 64.1 us  [product(): pl.pallas_call(partial(grad_kernel, rows=rows, slots=slots, outer=outer,...]
    ppermute x60 -> x67, waiting for transfers between devices: 155 us -> 160 us  [shifted(): return lax.ppermute(value, 'dp', pairs)]
    pallas_call x13 -> x14, Pallas kernels: 222 us -> 227 us  [run_parts(): pl.pallas_call(kernel, in_specs=[pl.BlockSpec(memory_space=pltpu.SMEM)] *...]
    ppermute x60 -> x67, starting transfers between devices: 78.9 us -> 74.7 us  [shifted(): return lax.ppermute(value, 'dp', pairs)]
    concatenate x18 -> x16, other arithmetic: 18.7 us -> 18.8 us  [advance(): held = [jnp.concatenate(held)]]
  transfers between devices with their start and end apart: 72 -> 78, of which waited for: 40 -> 41; matrix products, arithmetic and copies ran while one was open for 5% -> 4% of each run, Pallas kernels for 36% -> 43%
where the time goes in v3:
time: 673 us; the launch traced here: 663 us
  Pallas kernels  311 us (46%)
  waiting for transfers between devices  180 us (27%)
  starting transfers between devices  108 us (16%)
  local copies, waits for them, and re-layouts  29.9 us (4%)
  other arithmetic  29.1 us (4%)
    pallas_call x14, Pallas kernels, run_parts(): pl.pallas_call(kernel, in_specs=[pl.BlockSpec(memory_space=pltpu.SMEM)] *...  227 us
    ppermute x67, waiting for transfers between devices, shifted(): return lax.ppermute(value, 'dp', pairs)  160 us
    ppermute x67, starting transfers between devices, shifted(): return lax.ppermute(value, 'dp', pairs)  74.7 us
    pallas_call x12, Pallas kernels, product(): pl.pallas_call(partial(grad_kernel, rows=rows, slots=slots, outer=outer,...  64.1 us
    concatenate x16, other arithmetic, advance(): held = [jnp.concatenate(held)]  18.8 us
    all_to_all x3, waiting for transfers between devices, spread(): lax.all_to_all(jnp.broadcast_to(value[None], (count, *value.shape)), 'dp'...  15.7 us
    unnamed x106, local copies, waits for them, and re-layouts  13.7 us
    all_to_all x3, starting transfers between devices, spread(): lax.all_to_all(jnp.broadcast_to(value[None], (count, *value.shape)), 'dp'...  13.6 us
  transfers between devices with their start and end apart: 78, of which 41 were waited for; matrix products, arithmetic and copies ran while one was open for 4% of the time, Pallas kernels for 43%

profile of v3, /device:TPU:0, one launch (start us, length us, event | category | flops | bytes accessed | tf_op | source)
XLA Modules:
  0.0 662.9 jit_solution(648532904850260981)
XLA Ops:
  3.4 4.1 collective-permute-start
  9.3 5.8 collective-permute-done
  16.9 3.4 collective-permute-start.2
  20.7 5.3 collective-permute-done.2
  28.4 3.4 collective-permute-start.4
  33.7 8.0 %collective-permute-done.4 = bf16[2,64,1024]{2,1,0:T(8,128)(2,1)} collective-permute-done((bf16[2,64,1024]{2,1,0:T(8,128)(2,1)S(1)}, bf16[2,64,1024]{2,1,0:T(8,128)(2,1)}, u32[]{:S(2)}, u32[]{:S(2)}) %collective-permute-start.4) | collective-permute-done | bytes 262176 | tf_op jit(solution)/shard_map/ppermute | solution.py:681
  41.8 3.9 collective-permute-done.5
  56.7 14.3 %collective-permute-done.9 = bf16[1,64,2048]{2,1,0:T(8,128)(2,1)} collective-permute-done((bf16[1,64,2048]{2,1,0:T(8,128)(2,1)}, bf16[1,64,2048]{2,1,0:T(8,128)(2,1)}, u32[]{:S(2)}, u32[]{:S(2)}) %collective-permute-start.9) | collective-permute-done | bytes 262176 | tf_op jit(solution)/shard_map/ppermute | solution.py:681
  72.6 2.7 pad_maximum_fusion.2.refs_11_.refs_13_.refs_16_.refs_36_.refs_34_.refs_18_
  83.8 14.2 %collective-permute-done.13 = bf16[1,64,2048]{2,1,0:T(8,128)(2,1)S(1)} collective-permute-done((bf16[1,64,2048]{2,1,0:T(8,128)(2,1)S(1)}, bf16[1,64,2048]{2,1,0:T(8,128)(2,1)S(1)}, u32[]{:S(2)}, u32[]{:S(2)}) %collective-permute-start.13) | collective-permute-done | bytes 262176 | tf_op jit(solution)/shard_map/ppermute | solution.py:681
  100.0 3.4 collective-permute-done.11.refs_12_.refs_14_.refs_17_.refs_37_.refs_35_.refs_19_
  111.8 13.5 %collective-permute-done.18 = bf16[1,256,512]{2,1,0:T(8,128)(2,1)S(1)} collective-permute-done((bf16[1,256,512]{2,1,0:T(8,128)(2,1)S(1)}, bf16[1,256,512]{2,1,0:T(8,128)(2,1)S(1)}, u32[]{:S(2)}, u32[]{:S(2)}) %collective-permute-start.18) | collective-permute-done | bytes 262176 | tf_op jit(solution)/shard_map/ppermute | solution.py:681
  126.4 3.1 collective-permute-done.16.refs_5_.refs_20_.refs_23_.refs_25_.refs_16_
  129.6 2.6 pad_maximum_fusion.4.refs_8_.refs_23_.refs_26_.refs_28_.refs_19_
  136.9 2.6 place.1
  143.2 10.5 %attend.2 = (bf16[256,1024]{1,0:T(8,128)(2,1)}, bf16[256,1024]{1,0:T(8,128)(2,1)}, bf16[256,1024]{1,0:T(8,128)(2,1)}, bf16[256,1024]{1,0:T(8,128)(2,1)}, f32[256,1024]{1,0:T(8,128)}, /*index=5*/bf16[256,1024]{1,0:T(8,128)(2,1)}) custom-call(s32[2]{0:T(128)S(1)} %get-tuple-element.593.refs_0_, s32[16]{0:T(128)S(1)} %copy-done.9, ...), custom_call_target="tpu_custom_call" | custom-call | flops 1 | bytes 1 | tf_op jit(solution)/shard_map/attend/pallas_call | solution.py:261
  160.2 10.7 %attend.3 = (bf16[256,1024]{1,0:T(8,128)(2,1)}, bf16[256,1024]{1,0:T(8,128)(2,1)}, bf16[256,1024]{1,0:T(8,128)(2,1)}, bf16[256,1024]{1,0:T(8,128)(2,1)}, f32[256,1024]{1,0:T(8,128)}, /*index=5*/bf16[256,1024]{1,0:T(8,128)(2,1)}) custom-call(s32[2]{0:T(128)S(1)} %get-tuple-element.594.refs_0_, s32[16]{0:T(128)S(1)} %copy-done.9, ...), custom_call_target="tpu_custom_call" | custom-call | flops 1 | bytes 1 | tf_op jit(solution)/shard_map/attend/pallas_call | solution.py:261
  172.5 10.8 %collective-permute-done.26.refs_6_.refs_28_.refs_31_.refs_17_.refs_15_.refs_8_ = bf16[4,256,512]{2,1,0:T(8,128)(2,1)S(1)} collective-permute-done((bf16[4,256,512]{2,1,0:T(8,128)(2,1)S(1)}, bf16[4,256,512]{2,1,0:T(8,128)(2,1)S(1)}, u32[]{:S(2)}, u32[]{:S(2)}) %collective-permute-start.26) | collective-permute-done | bytes 1048608 | tf_op jit(solution)/shard_map/ppermute | solution.py:681
  185.6 11.0 %up.3 = (bf16[256,4096]{1,0:T(8,128)(2,1)}, bf16[256,4096]{1,0:T(8,128)(2,1)}) custom-call(s32[2]{0:T(128)S(1)} %get-tuple-element.594.refs_0_, s32[16]{0:T(128)S(1)} %copy-done.9, bf16[256,1024]{1,0:T(8,128)(2,1)} %get-tuple-element.342.refs_2_.refs_3_.refs_0_, f32[1,4096]{1,0:T(1,128)S(1)} %bitcast.130, bf16[4,64,2048]{2,1,0:T(8,128)(2,1)} %copy-done.16, ...), custom_call_target="tpu_custom_call" | custom-call | flops 1 | bytes 1 | tf_op jit(solution)/shard_map/up/pallas_call | solution.py:261
  196.7 11.1 %up.2 = (bf16[256,4096]{1,0:T(8,128)(2,1)}, bf16[256,4096]{1,0:T(8,128)(2,1)}) custom-call(s32[2]{0:T(128)S(1)} %get-tuple-element.593.refs_0_, s32[16]{0:T(128)S(1)} %copy-done.9, bf16[256,1024]{1,0:T(8,128)(2,1)} %get-tuple-element.319.refs_2_.refs_3_, f32[1,4096]{1,0:T(1,128)S(1)} %bitcast.131, bf16[4,64,2048]{2,1,0:T(8,128)(2,1)} %copy-done.16, ...), custom_call_target="tpu_custom_call" | custom-call | flops 1 | bytes 1 | tf_op jit(solution)/shard_map/up/pallas_call | solution.py:261
  213.7 7.7 %down.2 = (f32[256,1024]{1,0:T(8,128)}, bf16[256,1024]{1,0:T(8,128)(2,1)}) custom-call(s32[2]{0:T(128)S(1)} %get-tuple-element.593.refs_0_, s32[16]{0:T(128)S(1)} %copy-done.9, bf16[256,4096]{1,0:T(8,128)(2,1)} %get-tuple-element.339.refs_2_, bf16[256,1024]{1,0:T(8,128)(2,1)} %get-tuple-element.319.refs_2_.refs_3_, ...), custom_call_target="tpu_custom_call" | custom-call | flops 1 | bytes 1 | tf_op jit(solution)/shard_map/down/pallas_call | solution.py:261
  221.4 4.2 collective-permute-start.33
  226.9 7.7 %down.3 = (f32[256,1024]{1,0:T(8,128)}, bf16[256,1024]{1,0:T(8,128)(2,1)}) custom-call(s32[2]{0:T(128)S(1)} %get-tuple-element.594.refs_0_, s32[16]{0:T(128)S(1)} %copy-done.9, bf16[256,4096]{1,0:T(8,128)(2,1)} %get-tuple-element.356.refs_2_.refs_0_, bf16[256,1024]{1,0:T(8,128)(2,1)} %get-tuple-element.342.refs_2_.refs_3_.refs_0_, ...), custom_call_target="tpu_custom_call" | custom-call | flops 1 | bytes 1 | tf_op jit(solution)/shard_map/down/pallas_call | solution.py:261
  236.6 20.7 %forward.2 = (bf16[256,1024]{1,0:T(8,128)(2,1)}, bf16[256,1024]{1,0:T(8,128)(2,1)}, bf16[256,1024]{1,0:T(8,128)(2,1)}, bf16[256,1024]{1,0:T(8,128)(2,1)}, f32[25...) custom-call(s32[2]{0:T(128)S(1)} %get-tuple-element.593.refs_0_, ...), custom_call_target="tpu_custom_call" | custom-call | flops 40000000000 | bytes 100000000 | tf_op jit(solution)/shard_map/forward/pallas_call | solution.py:261
  258.9 4.0 all-to-all-start
  263.8 21.3 %forward.3 = (bf16[256,1024]{1,0:T(8,128)(2,1)}, bf16[256,1024]{1,0:T(8,128)(2,1)}, bf16[256,1024]{1,0:T(8,128)(2,1)}, bf16[256,1024]{1,0:T(8,128)(2,1)}, f32[25...) custom-call(s32[2]{0:T(128)S(1)} %get-tuple-element.594.refs_0_, ...), custom_call_target="tpu_custom_call" | custom-call | flops 40000000000 | bytes 100000000 | tf_op jit(solution)/shard_map/forward/pallas_call | solution.py:261
  286.6 6.0 all-to-all-start.1
  295.0 7.6 %all-to-all-done.1.queries_ref = bf16[16,64,128]{2,1,0:T(8,128)(2,1)S(1)} async-done(((bf16[16,64,128]{2,1,0:T(8,128)(2,1)}), bf16[16,64,128]{2,1,0:T(8,128)(2,1)S(1)}, u32[]{:S(2)}, u32[]{:S(2)}) %all-to-all-start.1) | async-done | bytes 262176 | tf_op jit(solution)/shard_map/all_to_all | solution.py:1164
  306.4 3.5 all-to-all-start.2
  310.1 8.0 %all-to-all-done.2 = f32[16,2,1,3,3,128]{5,1,4,3,2,0:T(2,128)S(1)} async-done(((f32[16,2,1,3,3,128]{5,1,4,3,2,0:T(2,128)}), f32[16,2,1,3,3,128]{5,1,4,3,2,0:T(2,128)S(1)}, u32[]{:S(2)}, u32[]{:S(2)}) %all-to-all-start.2) | async-done | bytes 147488 | tf_op jit(solution)/shard_map/all_to_all | solution.py:1164
  318.3 4.5 losses.2
  322.7 3.5 all-to-all-start.4
  326.4 4.4 losses.3
  332.2 4.1 collective-permute-done.35
  337.0 6.0 all-to-all-start.3
  343.0 29.5 %backward.4 = (bf16[256,1024]{1,0:T(8,128)(2,1)}, f32[16,1024]{1,0:T(8,128)}, bf16[256,128]{1,0:T(8,128)(2,1)}, bf16[256,4096]{1,0:T(8,128)(2,1)}, bf16[256,1024...) custom-call(s32[2]{0:T(128)S(1)} %get-tuple-element.594.refs_0_, ...), custom_call_target="tpu_custom_call" | custom-call | flops 40000000000 | bytes 100000000 | tf_op jit(solution)/shard_map/backward/pallas_call | solution.py:261
  374.5 29.2 %backward.3 = (bf16[256,1024]{1,0:T(8,128)(2,1)}, f32[16,1024]{1,0:T(8,128)}, bf16[256,128]{1,0:T(8,128)(2,1)}, bf16[256,4096]{1,0:T(8,128)(2,1)}, bf16[256,1024...) custom-call(s32[2]{0:T(128)S(1)} %get-tuple-element.593.refs_0_, ...), custom_call_target="tpu_custom_call" | custom-call | flops 40000000000 | bytes 100000000 | tf_op jit(solution)/shard_map/backward/pallas_call | solution.py:261
  405.8 29.2 %backward.5 = (bf16[256,1024]{1,0:T(8,128)(2,1)}, f32[16,1024]{1,0:T(8,128)}, bf16[256,4096]{1,0:T(8,128)(2,1)}, bf16[256,1024]{1,0:T(8,128)(2,1)}, bf16[3,256,1...) custom-call(s32[2]{0:T(128)S(1)} %get-tuple-element.594.refs_0_, s32[16]{0:T(128)S(1)} %copy-done.9, ...), custom_call_target="tpu_custom_call" | custom-call | flops 40000000000 | bytes 100000000 | tf_op jit(solution)/shard_map/backward/pallas_call | solution.py:261
  435.8 3.9 norm_back.1
  439.8 5.3 down_send.2
  445.6 5.3 down_send.3
  452.4 6.4 down_keep.2
  460.8 15.3 %feed_back.1 = (bf16[256,4096]{1,0:T(8,128)(2,1)}, bf16[256,1024]{1,0:T(8,128)(2,1)}, f32[16,1024]{1,0:T(8,128)}, f32[256,1024]{1,0:T(8,128)}) custom-call(s32[2]{0:T(128)S(1)} %get-tuple-element.593.refs_0_, s32[16]{0:T(128)S(1)} %copy-done.9, bf16[256,1024]{1,0:T(8,128)(2,1)} %get-tuple-element.402.refs_6_.refs_2_, ...), custom_call_target="tpu_custom_call" | custom-call | flops 40000000000 | bytes 100000000 | tf_op jit(solution)/shard_map/feed_back/pallas_call | solution.py:261
  476.2 6.8 %up_send.1 = bf16[512,4096]{1,0:T(8,128)(2,1)S(1)} custom-call(s32[3]{0:T(128)S(1)} %pad_add_fusion.3.pick_ref, bf16[256,1024]{1,0:T(8,128)(2,1)} %get-tuple-element.342.refs_2_.refs_3_.refs_0_, bf16[256,1024]{1,0:T(8,128)(2,1)} %get-tuple-element.407.refs_1_, bf16[256,1024]{1,0:T(8,128)(2,1)} %get-tuple-element.319.refs_2_.refs_3_, ...), custom_call_target="tpu_custom_call" | custom-call | flops 100000000 | bytes 2000000 | tf_op jit(solution)/shard_map/up_send/pallas_call | solution.py:999
  484.3 6.4 down_keep.3
  493.1 19.5 %attend_back.1 = (bf16[3,256,1024]{2,1,0:T(8,128)(2,1)}, f32[16,1024]{1,0:T(8,128)}, f32[512,1024]{1,0:T(8,128)}) custom-call(s32[2]{0:T(128)S(1)} %get-tuple-element.593.refs_0_, s32[16]{0:T(128)S(1)} %copy-done.9, bf16[256,1024]{1,0:T(8,128)(2,1)} %get-tuple-element.417.refs_2_.refs_6_, f32[256,1024]{1,0:T(8,128)} %get-tuple-element.418.refs_3_, ...), custom_call_target="tpu_custom_call" | custom-call | flops 40000000000 | bytes 100000000 | tf_op jit(solution)/shard_map/attend_back/pallas_call | solution.py:261
  512.6 5.3 up_keep.2
  524.5 6.1 qkv_send.1
  530.7 3.1 out_send.1
  533.7 4.9 up_keep.3
  542.3 5.2 collective-permute-done.44.other_ref
  554.3 4.9 qkv_keep.2
  559.3 4.6 qkv_keep.3
  566.1 4.7 collective-permute-done.49.other_ref
  570.8 7.0 %collective-permute-done.48.other_ref = bf16[4,64,2048]{2,1,0:T(8,128)(2,1)S(1)} collective-permute-done((bf16[4,64,2048]{2,1,0:T(8,128)(2,1)S(1)}, bf16[4,64,2048]{2,1,0:T(8,128)(2,1)S(1)}, u32[]{:S(2)}, u32[]{:S(2)}) %collective-permute-start.48) | collective-permute-done | bytes 1048608 | tf_op jit(solution)/shard_map/ppermute | solution.py:681
  583.2 4.8 out_keep.1
  589.1 4.3 collective-permute-done.54
  593.5 6.8 %collective-permute-done.53.other_ref = bf16[2,64,2048]{2,1,0:T(8,128)(2,1)S(1)} collective-permute-done((bf16[2,64,2048]{2,1,0:T(8,128)(2,1)S(1)}, bf16[2,64,2048]{2,1,0:T(8,128)(2,1)S(1)}, u32[]{:S(2)}, u32[]{:S(2)}) %collective-permute-start.53) | collective-permute-done | bytes 524320 | tf_op jit(solution)/shard_map/ppermute | solution.py:681
  600.3 6.0 collective-permute-done.52.other_ref
  612.4 12.6 %collective-permute-done.60 = f32[4,2,32,128]{3,2,1,0:T(8,128)S(1)} collective-permute-done((f32[4,2,32,128]{3,2,1,0:T(8,128)S(1)}, f32[4,2,32,128]{3,2,1,0:T(8,128)S(1)}, u32[]{:S(2)}, u32[]{:S(2)}) %collective-permute-start.60) | collective-permute-done | bytes 131104 | tf_op jit(solution)/shard_map/ppermute | solution.py:681
  636.0 4.8 collective-permute-done.63.other_ref
  646.0 3.7 collective-permute-start.67
  650.4 3.8 collective-permute-done.67.other_ref
  655.6 2.6 collective-permute-start.71
  (367 shorter events, 150.4 us)
Async XLA Ops:
  3.4 11.8 %collective-permute-start = (bf16[1,80,1024]{2,1,0:T(8,128)(2,1)S(1)}, bf16[1,80,1024]{2,1,0:T(8,128)(2,1)S(1)}, u32[]{:S(2)}, u32[]{:S(2)}) collective-permute-start(bf16[1,80,1024]{2,1,0:T(8,128)(2,1)S(1)} %maximum_bitcast_fusion.3), channel_id=1, source_target_pairs={{0,8},{1,9},{2,10},{3,11},{4,12},{5,13},{6,14},{7,15},{8,0},{9,1},... | collective-permute-start | bytes 491528 | tf_op jit(solution)/shard_map/ppermute | solution.py:681
  15.2 11.8 %collective-permute-start.1 = (bf16[2,80,1024]{2,1,0:T(8,128)(2,1)S(1)}, bf16[2,80,1024]{2,1,0:T(8,128)(2,1)S(1)}, u32[]{:S(2)}, u32[]{:S(2)}) collective-permute-start(bf16[2,80,1024]{2,1,0:T(8,128)(2,1)S(1)} %pad_maximum_fusion.14), channel_id=1, source_target_pairs={{0,4},{1,5},{2,6},{3,7},{4,0},{5,1},{6,2},{7,3},{8,12},{9,13},{10,... | collective-permute-start | bytes 983048 | tf_op jit(solution)/shard_map/ppermute | solution.py:681
  16.9 9.0 %collective-permute-start.2 = (bf16[1,64,1024]{2,1,0:T(8,128)(2,1)S(1)}, bf16[1,64,1024]{2,1,0:T(8,128)(2,1)S(1)}, u32[]{:S(2)}, u32[]{:S(2)}) collective-permute-start(bf16[1,64,1024]{2,1,0:T(8,128)(2,1)S(1)} %slice_bitcast_fusion.5), channel_id=1, source_target_pairs={{0,8},{1,9},{2,10},{3,11},{4,12},{5,13},{6,14},{7,15},{8,0},{9,1},... | collective-permute-start | bytes 393224 | tf_op jit(solution)/shard_map/ppermute | solution.py:681
  27.0 18.6 %collective-permute-start.3 = (bf16[4,80,1024]{2,1,0:T(8,128)(2,1)S(1)}, bf16[4,80,1024]{2,1,0:T(8,128)(2,1)}, u32[]{:S(2)}, u32[]{:S(2)}) collective-permute-start(bf16[4,80,1024]{2,1,0:T(8,128)(2,1)S(1)} %pad_maximum_fusion.7), channel_id=1, source_target_pairs={{0,2},{1,3},{2,0},{3,1},{4,6},{5,7},{6,4},{7,5},{8,10},{9,11},{10,... | collective-permute-start | bytes 1966088 | tf_op jit(solution)/shard_map/ppermute | solution.py:681
  28.4 13.4 %collective-permute-start.4 = (bf16[2,64,1024]{2,1,0:T(8,128)(2,1)S(1)}, bf16[2,64,1024]{2,1,0:T(8,128)(2,1)}, u32[]{:S(2)}, u32[]{:S(2)}) collective-permute-start(bf16[2,64,1024]{2,1,0:T(8,128)(2,1)S(1)} %pad_maximum_fusion.17), channel_id=1, source_target_pairs={{0,4},{1,5},{2,6},{3,7},{4,0},{5,1},{6,2},{7,3},{8,12},{9,13},{10,... | collective-permute-start | bytes 786440 | tf_op jit(solution)/shard_map/ppermute | solution.py:681
  31.8 13.8 %collective-permute-start.5 = (bf16[1,64,2048]{2,1,0:T(8,128)(2,1)S(1)}, bf16[1,64,2048]{2,1,0:T(8,128)(2,1)}, u32[]{:S(2)}, u32[]{:S(2)}) collective-permute-start(bf16[1,64,2048]{2,1,0:T(8,128)(2,1)S(1)} %slice_bitcast_fusion.4), channel_id=1, source_target_pairs={{0,8},{1,9},{2,10},{3,11},{4,12},{5,13},{6,14},{7,15},{8,0},{9,1},... | collective-permute-start | bytes 786440 | tf_op jit(solution)/shard_map/ppermute | solution.py:681
  46.9 25.7 %collective-permute-start.6 = (bf16[8,80,1024]{2,1,0:T(8,128)(2,1)S(1)}, bf16[8,80,1024]{2,1,0:T(8,128)(2,1)S(1)}, u32[]{:S(2)}, u32[]{:S(2)}) collective-permute-start(bf16[8,80,1024]{2,1,0:T(8,128)(2,1)S(1)} %pad_maximum_fusion.refs_0_.refs_15_.refs_17_.refs_20_.refs_32_.refs_30_.refs_14_), channel_id=1, source_target_pairs={{0,1},{1,0},{2,3},{3,2},{4,5},{5,4},{6,7},{7,6},{8,9},{9,8},{10,11... | collective-permute-start | bytes 3932168 | tf_op jit(solution)/shard_map/ppermute | solution.py:681
  52.7 19.9 %collective-permute-start.8 = (bf16[2,64,2048]{2,1,0:T(8,128)(2,1)}, bf16[2,64,2048]{2,1,0:T(8,128)(2,1)}, u32[]{:S(2)}, u32[]{:S(2)}) collective-permute-start(bf16[2,64,2048]{2,1,0:T(8,128)(2,1)} %pad_maximum_fusion.9), channel_id=1, source_target_pairs={{0,4},{1,5},{2,6},{3,7},{4,0},{5,1},{6,2},{7,3},{8,12},{9,13},{10,... | collective-permute-start | bytes 1572872 | tf_op jit(solution)/shard_map/ppermute | solution.py:681
  53.5 19.1 %collective-permute-start.7 = (bf16[4,64,1024]{2,1,0:T(8,128)(2,1)}, bf16[4,64,1024]{2,1,0:T(8,128)(2,1)}, u32[]{:S(2)}, u32[]{:S(2)}) collective-permute-start(bf16[4,64,1024]{2,1,0:T(8,128)(2,1)} %pad_maximum_fusion.8), channel_id=1, source_target_pairs={{0,2},{1,3},{2,0},{3,1},{4,6},{5,7},{6,4},{7,5},{8,10},{9,11},{10,... | collective-permute-start | bytes 1572872 | tf_op jit(solution)/shard_map/ppermute | solution.py:681
  55.1 15.8 %collective-permute-start.9 = (bf16[1,64,2048]{2,1,0:T(8,128)(2,1)}, bf16[1,64,2048]{2,1,0:T(8,128)(2,1)}, u32[]{:S(2)}, u32[]{:S(2)}) collective-permute-start(bf16[1,64,2048]{2,1,0:T(8,128)(2,1)} %get-tuple-element.299), channel_id=1, source_target_pairs={{0,8},{1,9},{2,10},{3,11},{4,12},{5,13},{6,14},{7,15},{8,0},{9,1},... | collective-permute-start | bytes 786440 | tf_op jit(solution)/shard_map/ppermute | solution.py:681
  77.5 21.5 %collective-permute-start.10 = (bf16[8,64,1024]{2,1,0:T(8,128)(2,1)}, bf16[8,64,1024]{2,1,0:T(8,128)(2,1)S(1)}, u32[]{:S(2)}, u32[]{:S(2)}) collective-permute-start(bf16[8,64,1024]{2,1,0:T(8,128)(2,1)} %pad_maximum_fusion.1.refs_9_.refs_11_.refs_14_.refs_34_.refs_32_.refs_16_), channel_id=1, source_target_pairs={{0,1},{1,0},{2,3},{3,2},{4,5},{5,4},{6,7},{7,6},{8,9},{9,8},{10,11... | collective-permute-start | bytes 3145736 | tf_op jit(solution)/shard_map/ppermute | solution.py:681
  77.6 25.9 %collective-permute-start.11 = (bf16[4,64,2048]{2,1,0:T(8,128)(2,1)}, bf16[4,64,2048]{2,1,0:T(8,128)(2,1)}, u32[]{:S(2)}, u32[]{:S(2)}) collective-permute-start(bf16[4,64,2048]{2,1,0:T(8,128)(2,1)} %pad_maximum_fusion.2.refs_11_.refs_13_.refs_16_.refs_36_.refs_34_.refs_18_), channel_id=1, source_target_pairs={{0,2},{1,3},{2,0},{3,1},{4,6},{5,7},{6,4},{7,5},{8,10},{9,11},{10,... | collective-permute-start | bytes 3145736 | tf_op jit(solution)/shard_map/ppermute | solution.py:681
  79.3 19.7 %collective-permute-start.12 = (bf16[2,64,2048]{2,1,0:T(8,128)(2,1)S(1)}, bf16[2,64,2048]{2,1,0:T(8,128)(2,1)S(1)}, u32[]{:S(2)}, u32[]{:S(2)}) collective-permute-start(bf16[2,64,2048]{2,1,0:T(8,128)(2,1)S(1)} %pad_maximum_fusion.10), channel_id=1, source_target_pairs={{0,4},{1,5},{2,6},{3,7},{4,0},{5,1},{6,2},{7,3},{8,12},{9,13},{10,... | collective-permute-start | bytes 1572872 | tf_op jit(solution)/shard_map/ppermute | solution.py:681
  80.9 17.1 %collective-permute-start.13 = (bf16[1,64,2048]{2,1,0:T(8,128)(2,1)S(1)}, bf16[1,64,2048]{2,1,0:T(8,128)(2,1)S(1)}, u32[]{:S(2)}, u32[]{:S(2)}) collective-permute-start(bf16[1,64,2048]{2,1,0:T(8,128)(2,1)S(1)} %get-tuple-element.307), channel_id=1, source_target_pairs={{0,8},{1,9},{2,10},{3,11},{4,12},{5,13},{6,14},{7,15},{8,0},{9,1},... | collective-permute-start | bytes 786440 | tf_op jit(solution)/shard_map/ppermute | solution.py:681
  104.6 25.0 %collective-permute-start.16 = (bf16[4,64,2048]{2,1,0:T(8,128)(2,1)S(1)}, bf16[4,64,2048]{2,1,0:T(8,128)(2,1)}, u32[]{:S(2)}, u32[]{:S(2)}) collective-permute-start(bf16[4,64,2048]{2,1,0:T(8,128)(2,1)S(1)} %pad_maximum_fusion.3.refs_4_.refs_19_.refs_22_.refs_24_.refs_15_), channel_id=1, source_target_pairs={{0,2},{1,3},{2,0},{3,1},{4,6},{5,7},{6,4},{7,5},{8,10},{9,11},{10,... | collective-permute-start | bytes 3145736 | tf_op jit(solution)/shard_map/ppermute | solution.py:681
  105.2 24.3 %collective-permute-start.14 = (bf16[4,64,2048]{2,1,0:T(8,128)(2,1)}, bf16[4,64,2048]{2,1,0:T(8,128)(2,1)S(1)}, u32[]{:S(2)}, u32[]{:S(2)}) collective-permute-start(bf16[4,64,2048]{2,1,0:T(8,128)(2,1)} %pad_maximum_fusion.2.refs_11_.refs_13_.refs_16_.refs_36_.refs_34_.refs_18_), channel_id=1, source_target_pairs={{0,1},{1,0},{2,3},{3,2},{4,5},{5,4},{6,7},{7,6},{8,9},{9,8},{10,11... | collective-permute-start | bytes 3145736 | tf_op jit(solution)/shard_map/ppermute | solution.py:681
  105.2 24.3 %collective-permute-start.15 = (bf16[4,64,2048]{2,1,0:T(8,128)(2,1)}, bf16[4,64,2048]{2,1,0:T(8,128)(2,1)}, u32[]{:S(2)}, u32[]{:S(2)}) collective-permute-start(bf16[4,64,2048]{2,1,0:T(8,128)(2,1)} %collective-permute-done.11.refs_12_.refs_14_.refs_17_.refs_37_.refs_35_.refs_19_), channel_id=1, source_target_pairs={{0,1},{1,0},{2,3},{3,2},{4,5},{5,4},{6,7},{7,6},{8,9},{9,8},{10,11... | collective-permute-start | bytes 3145736 | tf_op jit(solution)/shard_map/ppermute | solution.py:681
  106.6 19.8 %collective-permute-start.17 = (bf16[2,64,2048]{2,1,0:T(8,128)(2,1)}, bf16[2,64,2048]{2,1,0:T(8,128)(2,1)}, u32[]{:S(2)}, u32[]{:S(2)}) collective-permute-start(bf16[2,64,2048]{2,1,0:T(8,128)(2,1)} %pad_maximum_fusion.11), channel_id=1, source_target_pairs={{0,4},{1,5},{2,6},{3,7},{4,0},{5,1},{6,2},{7,3},{8,12},{9,13},{10,... | collective-permute-start | bytes 1572872 | tf_op jit(solution)/shard_map/ppermute | solution.py:681
  108.7 16.6 %collective-permute-start.18 = (bf16[1,256,512]{2,1,0:T(8,128)(2,1)S(1)}, bf16[1,256,512]{2,1,0:T(8,128)(2,1)S(1)}, u32[]{:S(2)}, u32[]{:S(2)}) collective-permute-start(bf16[1,256,512]{2,1,0:T(8,128)(2,1)S(1)} %get-tuple-element.316), channel_id=1, source_target_pairs={{0,8},{1,9},{2,10},{3,11},{4,12},{5,13},{6,14},{7,15},{8,0},{9,1},... | collective-permute-start | bytes 786440 | tf_op jit(solution)/shard_map/ppermute | solution.py:681
  132.2 24.2 %collective-permute-start.21 = (bf16[4,64,2048]{2,1,0:T(8,128)(2,1)}, bf16[4,64,2048]{2,1,0:T(8,128)(2,1)}, u32[]{:S(2)}, u32[]{:S(2)}) collective-permute-start(bf16[4,64,2048]{2,1,0:T(8,128)(2,1)} %pad_maximum_fusion.4.refs_8_.refs_23_.refs_26_.refs_28_.refs_19_), channel_id=1, source_target_pairs={{0,2},{1,3},{2,0},{3,1},{4,6},{5,7},{6,4},{7,5},{8,10},{9,11},{10,... | collective-permute-start | bytes 3145736 | tf_op jit(solution)/shard_map/ppermute | solution.py:681
  132.7 23.6 %collective-permute-start.19 = (bf16[4,64,2048]{2,1,0:T(8,128)(2,1)S(1)}, bf16[4,64,2048]{2,1,0:T(8,128)(2,1)}, u32[]{:S(2)}, u32[]{:S(2)}) collective-permute-start(bf16[4,64,2048]{2,1,0:T(8,128)(2,1)S(1)} %pad_maximum_fusion.3.refs_4_.refs_19_.refs_22_.refs_24_.refs_15_), channel_id=1, source_target_pairs={{0,1},{1,0},{2,3},{3,2},{4,5},{5,4},{6,7},{7,6},{8,9},{9,8},{10,11... | collective-permute-start | bytes 3145736 | tf_op jit(solution)/shard_map/ppermute | solution.py:681
  132.7 23.6 %collective-permute-start.20 = (bf16[4,64,2048]{2,1,0:T(8,128)(2,1)}, bf16[4,64,2048]{2,1,0:T(8,128)(2,1)}, u32[]{:S(2)}, u32[]{:S(2)}) collective-permute-start(bf16[4,64,2048]{2,1,0:T(8,128)(2,1)} %collective-permute-done.16.refs_5_.refs_20_.refs_23_.refs_25_.refs_16_), channel_id=1, source_target_pairs={{0,1},{1,0},{2,3},{3,2},{4,5},{5,4},{6,7},{7,6},{8,9},{9,8},{10,11... | collective-permute-start | bytes 3145736 | tf_op jit(solution)/shard_map/ppermute | solution.py:681
  135.4 19.8 %collective-permute-start.22 = (bf16[2,256,512]{2,1,0:T(8,128)(2,1)}, bf16[2,256,512]{2,1,0:T(8,128)(2,1)}, u32[]{:S(2)}, u32[]{:S(2)}) collective-permute-start(bf16[2,256,512]{2,1,0:T(8,128)(2,1)} %pad_maximum_fusion.12), channel_id=1, source_target_pairs={{0,4},{1,5},{2,6},{3,7},{4,0},{5,1},{6,2},{7,3},{8,12},{9,13},{10,... | collective-permute-start | bytes 1572872 | tf_op jit(solution)/shard_map/ppermute | solution.py:681
  140.5 13.5 %collective-permute-start.23 = (bf16[1,256,512]{2,1,0:T(8,128)(2,1)S(1)}, bf16[1,256,512]{2,1,0:T(8,128)(2,1)S(1)}, u32[]{:S(2)}, u32[]{:S(2)}) collective-permute-start(bf16[1,256,512]{2,1,0:T(8,128)(2,1)S(1)} %get-tuple-element.327), channel_id=1, source_target_pairs={{0,8},{1,9},{2,10},{3,11},{4,12},{5,13},{6,14},{7,15},{8,0},{9,1},... | collective-permute-start | bytes 786440 | tf_op jit(solution)/shard_map/ppermute | solution.py:681
  157.5 14.9 %collective-permute-start.24 = (bf16[4,64,2048]{2,1,0:T(8,128)(2,1)}, bf16[4,64,2048]{2,1,0:T(8,128)(2,1)S(1)}, u32[]{:S(2)}, u32[]{:S(2)}) collective-permute-start(bf16[4,64,2048]{2,1,0:T(8,128)(2,1)} %pad_maximum_fusion.4.refs_8_.refs_23_.refs_26_.refs_28_.refs_19_), channel_id=1, source_target_pairs={{0,1},{1,0},{2,3},{3,2},{4,5},{5,4},{6,7},{7,6},{8,9},{9,8},{10,11... | collective-permute-start | bytes 3145736 | tf_op jit(solution)/shard_map/ppermute | solution.py:681
  157.6 14.8 %collective-permute-start.25 = (bf16[4,64,2048]{2,1,0:T(8,128)(2,1)}, bf16[4,64,2048]{2,1,0:T(8,128)(2,1)S(1)}, u32[]{:S(2)}, u32[]{:S(2)}) collective-permute-start(bf16[4,64,2048]{2,1,0:T(8,128)(2,1)} %collective-permute-done.21.refs_9_.refs_24_.refs_27_.refs_29_.refs_20_), channel_id=1, source_target_pairs={{0,1},{1,0},{2,3},{3,2},{4,5},{5,4},{6,7},{7,6},{8,9},{9,8},{10,11... | collective-permute-start | bytes 3145736 | tf_op jit(solution)/shard_map/ppermute | solution.py:681
  158.1 25.1 %collective-permute-start.26 = (bf16[4,256,512]{2,1,0:T(8,128)(2,1)S(1)}, bf16[4,256,512]{2,1,0:T(8,128)(2,1)S(1)}, u32[]{:S(2)}, u32[]{:S(2)}) collective-permute-start(bf16[4,256,512]{2,1,0:T(8,128)(2,1)S(1)} %pad_maximum_fusion.5.refs_5_.refs_27_.refs_30_.refs_16_.refs_14_.refs_7_), channel_id=1, source_target_pairs={{0,2},{1,3},{2,0},{3,1},{4,6},{5,7},{6,4},{7,5},{8,10},{9,11},{10,... | collective-permute-start | bytes 3145736 | tf_op jit(solution)/shard_map/ppermute | solution.py:681
  158.8 13.7 %collective-permute-start.27 = (bf16[2,256,512]{2,1,0:T(8,128)(2,1)S(1)}, bf16[2,256,512]{2,1,0:T(8,128)(2,1)S(1)}, u32[]{:S(2)}, u32[]{:S(2)}) collective-permute-start(bf16[2,256,512]{2,1,0:T(8,128)(2,1)S(1)} %pad_maximum_fusion.13), channel_id=1, source_target_pairs={{0,4},{1,5},{2,6},{3,7},{4,0},{5,1},{6,2},{7,3},{8,12},{9,13},{10,... | collective-permute-start | bytes 1572872 | tf_op jit(solution)/shard_map/ppermute | solution.py:681
  184.5 24.6 %collective-permute-start.30 = (bf16[4,256,512]{2,1,0:T(8,128)(2,1)}, bf16[4,256,512]{2,1,0:T(8,128)(2,1)}, u32[]{:S(2)}, u32[]{:S(2)}) collective-permute-start(bf16[4,256,512]{2,1,0:T(8,128)(2,1)} %pad_maximum_fusion.6.refs_9_.refs_31_.refs_34_.refs_20_.refs_18_.refs_11_), channel_id=1, source_target_pairs={{0,2},{1,3},{2,0},{3,1},{4,6},{5,7},{6,4},{7,5},{8,10},{9,11},{10,... | collective-permute-start | bytes 3145736 | tf_op jit(solution)/shard_map/ppermute | solution.py:681
  185.0 24.0 %collective-permute-start.28 = (bf16[4,256,512]{2,1,0:T(8,128)(2,1)S(1)}, bf16[4,256,512]{2,1,0:T(8,128)(2,1)S(1)}, u32[]{:S(2)}, u32[]{:S(2)}) collective-permute-start(bf16[4,256,512]{2,1,0:T(8,128)(2,1)S(1)} %pad_maximum_fusion.5.refs_5_.refs_27_.refs_30_.refs_16_.refs_14_.refs_7_), channel_id=1, source_target_pairs={{0,1},{1,0},{2,3},{3,2},{4,5},{5,4},{6,7},{7,6},{8,9},{9,8},{10,11... | collective-permute-start | bytes 3145736 | tf_op jit(solution)/shard_map/ppermute | solution.py:681
  185.0 24.0 %collective-permute-start.29 = (bf16[4,256,512]{2,1,0:T(8,128)(2,1)S(1)}, bf16[4,256,512]{2,1,0:T(8,128)(2,1)S(1)}, u32[]{:S(2)}, u32[]{:S(2)}) collective-permute-start(bf16[4,256,512]{2,1,0:T(8,128)(2,1)S(1)} %collective-permute-done.26.refs_6_.refs_28_.refs_31_.refs_17_.refs_15_.refs_8_), channel_id=1, source_target_pairs={{0,1},{1,0},{2,3},{3,2},{4,5},{5,4},{6,7},{7,6},{8,9},{9,8},{10,11... | collective-permute-start | bytes 3145736 | tf_op jit(solution)/shard_map/ppermute | solution.py:681
  221.4 15.2 %collective-permute-start.33 = (bf16[256,1024]{1,0:T(8,128)(2,1)}, bf16[256,1024]{1,0:T(8,128)(2,1)}, u32[]{:S(2)}, u32[]{:S(2)}) collective-permute-start(bf16[256,1024]{1,0:T(8,128)(2,1)} %get-tuple-element.354.refs_11_), channel_id=1, source_target_pairs={{0,16},{1,17},{2,18},{3,19},{4,20},{5,21},{6,22},{7,23},{8,24},{9,... | collective-permute-start | bytes 1572872 | tf_op jit(solution)/shard_map/ppermute | solution.py:33
  234.6 28.3 %collective-permute-start.34 = (bf16[256,1024]{1,0:T(8,128)(2,1)}, bf16[256,1024]{1,0:T(8,128)(2,1)S(1)}, u32[]{:S(2)}, u32[]{:S(2)}) collective-permute-start(bf16[256,1024]{1,0:T(8,128)(2,1)} %get-tuple-element.357.refs_12_), channel_id=1, source_target_pairs={{0,16},{1,17},{2,18},{3,19},{4,20},{5,21},{6,22},{7,23},{8,24},{9,... | collective-permute-start | bytes 1572872 | tf_op jit(solution)/shard_map/ppermute | solution.py:33
  258.9 27.0 %all-to-all-start = ((bf16[16,64,128]{2,1,0:T(8,128)(2,1)}), bf16[16,64,128]{2,1,0:T(8,128)(2,1)S(1)}, u32[]{:S(2)}, u32[]{:S(2)}) async-start(bf16[16,64,128]{2,1,0:T(8,128)(2,1)} %broadcast_in_dim.157), calls=%async_computation | async-start | bytes 524288 | tf_op jit(solution)/shard_map/all_to_all | solution.py:1164
  286.6 16.1 %all-to-all-start.1 = ((bf16[16,64,128]{2,1,0:T(8,128)(2,1)}), bf16[16,64,128]{2,1,0:T(8,128)(2,1)S(1)}, u32[]{:S(2)}, u32[]{:S(2)}) async-start(bf16[16,64,128]{2,1,0:T(8,128)(2,1)} %broadcast_in_dim.158), calls=%async_computation.1 | async-start | bytes 524288 | tf_op jit(solution)/shard_map/all_to_all | solution.py:1164
  306.4 11.7 %all-to-all-start.2 = ((f32[16,2,1,3,3,128]{5,1,4,3,2,0:T(2,128)}), f32[16,2,1,3,3,128]{5,1,4,3,2,0:T(2,128)S(1)}, u32[]{:S(2)}, u32[]{:S(2)}) async-start(f32[16,2,1,3,3,128]{5,1,4,3,2,0:T(2,128)} %broadcast_in_dim.160), calls=%async_computation.2 | async-start | bytes 294912 | tf_op jit(solution)/shard_map/all_to_all | solution.py:1164
  322.7 14.2 %all-to-all-start.4 = ((bf16[16,64,128]{2,1,0:T(8,128)(2,1)}), bf16[16,64,128]{2,1,0:T(8,128)(2,1)S(1)}, u32[]{:S(2)}, u32[]{:S(2)}) async-start(bf16[16,64,128]{2,1,0:T(8,128)(2,1)} %get-tuple-element.360), calls=%async_computation.4 | async-start | bytes 524288 | tf_op jit(solution)/shard_map/all_to_all | solution.py:1555
  337.0 36.8 %all-to-all-start.3 = ((bf16[16,64,128]{2,1,0:T(8,128)(2,1)}), bf16[16,64,128]{2,1,0:T(8,128)(2,1)S(1)}, u32[]{:S(2)}, u32[]{:S(2)}) async-start(bf16[16,64,128]{2,1,0:T(8,128)(2,1)} %get-tuple-element.367), calls=%async_computation.3 | async-start | bytes 524288 | tf_op jit(solution)/shard_map/all_to_all | solution.py:1555
  372.5 32.5 %collective-permute-start.37 = (bf16[256,1024]{1,0:T(8,128)(2,1)}, bf16[256,1024]{1,0:T(8,128)(2,1)S(1)}, u32[]{:S(2)}, u32[]{:S(2)}) collective-permute-start(bf16[256,1024]{1,0:T(8,128)(2,1)} %get-tuple-element.382), channel_id=1, source_target_pairs={{16,0},{17,1},{18,2},{19,3},{20,4},{21,5},{22,6},{23,7},{24,8},{25... | collective-permute-start | bytes 1572872 | tf_op jit(solution)/shard_map/ppermute | solution.py:33
  403.7 31.3 %collective-permute-start.36 = (bf16[256,1024]{1,0:T(8,128)(2,1)}, bf16[256,1024]{1,0:T(8,128)(2,1)S(1)}, u32[]{:S(2)}, u32[]{:S(2)}) collective-permute-start(bf16[256,1024]{1,0:T(8,128)(2,1)} %get-tuple-element.374), channel_id=1, source_target_pairs={{16,0},{17,1},{18,2},{19,3},{20,4},{21,5},{22,6},{23,7},{24,8},{25... | collective-permute-start | bytes 1572872 | tf_op jit(solution)/shard_map/ppermute | solution.py:33
  450.9 32.0 %collective-permute-start.40 = (bf16[2048,512]{1,0:T(8,128)(2,1)S(1)}, bf16[2048,512]{1,0:T(8,128)(2,1)S(1)}, u32[]{:S(2)}, u32[]{:S(2)}) collective-permute-start(bf16[2048,512]{1,0:T(8,128)(2,1)S(1)} %down_send.3), channel_id=1, source_target_pairs={{0,1},{1,0},{2,3},{3,2},{4,5},{5,4},{6,7},{7,6},{8,9},{9,8},{10,11... | collective-permute-start | bytes 6291464 | tf_op jit(solution)/shard_map/ppermute | solution.py:681
  458.8 31.9 %collective-permute-start.39 = (bf16[4,256,512]{2,1,0:T(8,128)(2,1)S(1)}, bf16[4,256,512]{2,1,0:T(8,128)(2,1)S(1)}, u32[]{:S(2)}, u32[]{:S(2)}) collective-permute-start(bf16[4,256,512]{2,1,0:T(8,128)(2,1)S(1)} %get-tuple-element.401), channel_id=1, source_target_pairs={{0,2},{1,3},{2,0},{3,1},{4,6},{5,7},{6,4},{7,5},{8,10},{9,11},{10,... | collective-permute-start | bytes 3145736 | tf_op jit(solution)/shard_map/ppermute | solution.py:681
  490.7 21.9 %collective-permute-start.41 = (bf16[512,4096]{1,0:T(8,128)(2,1)S(1)}, bf16[512,4096]{1,0:T(8,128)(2,1)}, u32[]{:S(2)}, u32[]{:S(2)}) collective-permute-start(bf16[512,4096]{1,0:T(8,128)(2,1)S(1)} %up_send.1), channel_id=1, source_target_pairs={{0,1},{1,0},{2,3},{3,2},{4,5},{5,4},{6,7},{7,6},{8,9},{9,8},{10,11... | collective-permute-start | bytes 12582920 | tf_op jit(solution)/shard_map/ppermute | solution.py:681
  491.0 27.0 %collective-permute-start.43 = (bf16[2,256,512]{2,1,0:T(8,128)(2,1)S(1)}, bf16[2,256,512]{2,1,0:T(8,128)(2,1)S(1)}, u32[]{:S(2)}, u32[]{:S(2)}) collective-permute-start(bf16[2,256,512]{2,1,0:T(8,128)(2,1)S(1)} %get-tuple-element.432), channel_id=1, source_target_pairs={{0,4},{1,5},{2,6},{3,7},{4,0},{5,1},{6,2},{7,3},{8,12},{9,13},{10,... | collective-permute-start | bytes 1572872 | tf_op jit(solution)/shard_map/ppermute | solution.py:681
  492.5 25.4 %collective-permute-start.42 = (bf16[4,256,512]{2,1,0:T(8,128)(2,1)S(1)}, bf16[4,256,512]{2,1,0:T(8,128)(2,1)S(1)}, u32[]{:S(2)}, u32[]{:S(2)}) collective-permute-start(bf16[4,256,512]{2,1,0:T(8,128)(2,1)S(1)} %get-tuple-element.430), channel_id=1, source_target_pairs={{0,2},{1,3},{2,0},{3,1},{4,6},{5,7},{6,4},{7,5},{8,10},{9,11},{10,... | collective-permute-start | bytes 3145736 | tf_op jit(solution)/shard_map/ppermute | solution.py:681
  520.2 19.5 %collective-permute-start.46 = (bf16[1,256,512]{2,1,0:T(8,128)(2,1)S(1)}, bf16[1,256,512]{2,1,0:T(8,128)(2,1)S(1)}, u32[]{:S(2)}, u32[]{:S(2)}) collective-permute-start(bf16[1,256,512]{2,1,0:T(8,128)(2,1)S(1)} %get-tuple-element.441), channel_id=1, source_target_pairs={{0,8},{1,9},{2,10},{3,11},{4,12},{5,13},{6,14},{7,15},{8,0},{9,1},... | collective-permute-start | bytes 786440 | tf_op jit(solution)/shard_map/ppermute | solution.py:681
  522.5 19.0 %collective-permute-start.45 = (bf16[2,256,512]{2,1,0:T(8,128)(2,1)S(1)}, bf16[2,256,512]{2,1,0:T(8,128)(2,1)S(1)}, u32[]{:S(2)}, u32[]{:S(2)}) collective-permute-start(bf16[2,256,512]{2,1,0:T(8,128)(2,1)S(1)} %get-tuple-element.438), channel_id=1, source_target_pairs={{0,4},{1,5},{2,6},{3,7},{4,0},{5,1},{6,2},{7,3},{8,12},{9,13},{10,... | collective-permute-start | bytes 1572872 | tf_op jit(solution)/shard_map/ppermute | solution.py:681
  523.1 24.4 %collective-permute-start.44 = (bf16[4,64,2048]{2,1,0:T(8,128)(2,1)S(1)}, bf16[4,64,2048]{2,1,0:T(8,128)(2,1)S(1)}, u32[]{:S(2)}, u32[]{:S(2)}) collective-permute-start(bf16[4,64,2048]{2,1,0:T(8,128)(2,1)S(1)} %get-tuple-element.436), channel_id=1, source_target_pairs={{0,2},{1,3},{2,0},{3,1},{4,6},{5,7},{6,4},{7,5},{8,10},{9,11},{10,... | collective-permute-start | bytes 3145736 | tf_op jit(solution)/shard_map/ppermute | solution.py:681
  550.7 15.4 %collective-permute-start.50 = (bf16[1,256,512]{2,1,0:T(8,128)(2,1)S(1)}, bf16[1,256,512]{2,1,0:T(8,128)(2,1)S(1)}, u32[]{:S(2)}, u32[]{:S(2)}) collective-permute-start(bf16[1,256,512]{2,1,0:T(8,128)(2,1)S(1)} %get-tuple-element.468), channel_id=1, source_target_pairs={{0,8},{1,9},{2,10},{3,11},{4,12},{5,13},{6,14},{7,15},{8,0},{9,1},... | collective-permute-start | bytes 786440 | tf_op jit(solution)/shard_map/ppermute | solution.py:681
  551.1 19.7 %collective-permute-start.49 = (bf16[2,64,2048]{2,1,0:T(8,128)(2,1)S(1)}, bf16[2,64,2048]{2,1,0:T(8,128)(2,1)S(1)}, u32[]{:S(2)}, u32[]{:S(2)}) collective-permute-start(bf16[2,64,2048]{2,1,0:T(8,128)(2,1)S(1)} %get-tuple-element.465), channel_id=1, source_target_pairs={{0,4},{1,5},{2,6},{3,7},{4,0},{5,1},{6,2},{7,3},{8,12},{9,13},{10,... | collective-permute-start | bytes 1572872 | tf_op jit(solution)/shard_map/ppermute | solution.py:681
  552.8 25.0 %collective-permute-start.48 = (bf16[4,64,2048]{2,1,0:T(8,128)(2,1)S(1)}, bf16[4,64,2048]{2,1,0:T(8,128)(2,1)S(1)}, u32[]{:S(2)}, u32[]{:S(2)}) collective-permute-start(bf16[4,64,2048]{2,1,0:T(8,128)(2,1)S(1)} %copy-done.13), channel_id=1, source_target_pairs={{0,2},{1,3},{2,0},{3,1},{4,6},{5,7},{6,4},{7,5},{8,10},{9,11},{10,... | collective-permute-start | bytes 3145736 | tf_op jit(solution)/shard_map/ppermute | solution.py:681
  554.3 23.6 %collective-permute-start.51 = (bf16[512,1024]{1,0:T(8,128)(2,1)S(1)}, bf16[512,1024]{1,0:T(8,128)(2,1)S(1)}, u32[]{:S(2)}, u32[]{:S(2)}) collective-permute-start(bf16[512,1024]{1,0:T(8,128)(2,1)S(1)} %copy-done.11), channel_id=1, source_target_pairs={{0,1},{1,0},{2,3},{3,2},{4,5},{5,4},{6,7},{7,6},{8,9},{9,8},{10,11... | collective-permute-start | bytes 3145736 | tf_op jit(solution)/shard_map/ppermute | solution.py:681
  578.2 10.9 %collective-permute-start.56 = (f32[16,1024]{1,0:T(8,128)S(1)}, f32[16,1024]{1,0:T(8,128)S(1)}, u32[]{:S(2)}, u32[]{:S(2)}) collective-permute-start(f32[16,1024]{1,0:T(8,128)S(1)} %add_add_fusion), channel_id=1, source_target_pairs={{0,1},{1,0},{2,3},{3,2},{4,5},{5,4},{6,7},{7,6},{8,9},{9,8},{10,11... | collective-permute-start | bytes 196616 | tf_op jit(solution)/shard_map/ppermute | solution.py:681
  578.3 10.9 %collective-permute-start.55 = (f32[8,2,32,128]{3,2,1,0:T(8,128)S(1)}, f32[8,2,32,128]{3,2,1,0:T(8,128)S(1)}, u32[]{:S(2)}, u32[]{:S(2)}) collective-permute-start(f32[8,2,32,128]{3,2,1,0:T(8,128)S(1)} %bitcast.145), channel_id=1, source_target_pairs={{0,1},{1,0},{2,3},{3,2},{4,5},{5,4},{6,7},{7,6},{8,9},{9,8},{10,11... | collective-permute-start | bytes 786440 | tf_op jit(solution)/shard_map/ppermute | solution.py:681
  578.8 14.7 %collective-permute-start.54 = (bf16[1,64,2048]{2,1,0:T(8,128)(2,1)S(1)}, bf16[1,64,2048]{2,1,0:T(8,128)(2,1)S(1)}, u32[]{:S(2)}, u32[]{:S(2)}) collective-permute-start(bf16[1,64,2048]{2,1,0:T(8,128)(2,1)S(1)} %get-tuple-element.481), channel_id=1, source_target_pairs={{0,8},{1,9},{2,10},{3,11},{4,12},{5,13},{6,14},{7,15},{8,0},{9,1},... | collective-permute-start | bytes 786440 | tf_op jit(solution)/shard_map/ppermute | solution.py:681
  581.1 19.1 %collective-permute-start.53 = (bf16[2,64,2048]{2,1,0:T(8,128)(2,1)S(1)}, bf16[2,64,2048]{2,1,0:T(8,128)(2,1)S(1)}, u32[]{:S(2)}, u32[]{:S(2)}) collective-permute-start(bf16[2,64,2048]{2,1,0:T(8,128)(2,1)S(1)} %get-tuple-element.478), channel_id=1, source_target_pairs={{0,4},{1,5},{2,6},{3,7},{4,0},{5,1},{6,2},{7,3},{8,12},{9,13},{10,... | collective-permute-start | bytes 1572872 | tf_op jit(solution)/shard_map/ppermute | solution.py:681
  581.7 24.6 %collective-permute-start.52 = (bf16[4,64,2048]{2,1,0:T(8,128)(2,1)S(1)}, bf16[4,64,2048]{2,1,0:T(8,128)(2,1)S(1)}, u32[]{:S(2)}, u32[]{:S(2)}) collective-permute-start(bf16[4,64,2048]{2,1,0:T(8,128)(2,1)S(1)} %get-tuple-element.476), channel_id=1, source_target_pairs={{0,2},{1,3},{2,0},{3,1},{4,6},{5,7},{6,4},{7,5},{8,10},{9,11},{10,... | collective-permute-start | bytes 3145736 | tf_op jit(solution)/shard_map/ppermute | solution.py:681
  608.2 17.8 %collective-permute-start.58 = (bf16[2,64,2048]{2,1,0:T(8,128)(2,1)S(1)}, bf16[2,64,2048]{2,1,0:T(8,128)(2,1)S(1)}, u32[]{:S(2)}, u32[]{:S(2)}) collective-permute-start(bf16[2,64,2048]{2,1,0:T(8,128)(2,1)S(1)} %get-tuple-element.502), channel_id=1, source_target_pairs={{0,4},{1,5},{2,6},{3,7},{4,0},{5,1},{6,2},{7,3},{8,12},{9,13},{10,... | collective-permute-start | bytes 1572872 | tf_op jit(solution)/shard_map/ppermute | solution.py:681
  609.6 16.3 %collective-permute-start.57 = (bf16[4,64,1024]{2,1,0:T(8,128)(2,1)S(1)}, bf16[4,64,1024]{2,1,0:T(8,128)(2,1)S(1)}, u32[]{:S(2)}, u32[]{:S(2)}) collective-permute-start(bf16[4,64,1024]{2,1,0:T(8,128)(2,1)S(1)} %get-tuple-element.500), channel_id=1, source_target_pairs={{0,2},{1,3},{2,0},{3,1},{4,6},{5,7},{6,4},{7,5},{8,10},{9,11},{10,... | collective-permute-start | bytes 1572872 | tf_op jit(solution)/shard_map/ppermute | solution.py:681
  610.2 14.7 %collective-permute-start.60 = (f32[4,2,32,128]{3,2,1,0:T(8,128)S(1)}, f32[4,2,32,128]{3,2,1,0:T(8,128)S(1)}, u32[]{:S(2)}, u32[]{:S(2)}) collective-permute-start(f32[4,2,32,128]{3,2,1,0:T(8,128)S(1)} %dynamic-slice_bitcast_fusion), channel_id=1, source_target_pairs={{0,2},{1,3},{2,0},{3,1},{4,6},{5,7},{6,4},{7,5},{8,10},{9,11},{10,... | collective-permute-start | bytes 393224 | tf_op jit(solution)/shard_map/ppermute | solution.py:681
  611.8 13.4 %collective-permute-start.59 = (bf16[1,64,2048]{2,1,0:T(8,128)(2,1)S(1)}, bf16[1,64,2048]{2,1,0:T(8,128)(2,1)S(1)}, u32[]{:S(2)}, u32[]{:S(2)}) collective-permute-start(bf16[1,64,2048]{2,1,0:T(8,128)(2,1)S(1)} %get-tuple-element.505), channel_id=1, source_target_pairs={{0,8},{1,9},{2,10},{3,11},{4,12},{5,13},{6,14},{7,15},{8,0},{9,1},... | collective-permute-start | bytes 786440 | tf_op jit(solution)/shard_map/ppermute | solution.py:681
  626.0 14.8 %collective-permute-start.62 = (bf16[4,64,1024]{2,1,0:T(8,128)(2,1)S(1)}, bf16[4,64,1024]{2,1,0:T(8,128)(2,1)S(1)}, u32[]{:S(2)}, u32[]{:S(2)}) collective-permute-start(bf16[4,64,1024]{2,1,0:T(8,128)(2,1)S(1)} %get-tuple-element.514), channel_id=1, source_target_pairs={{0,2},{1,3},{2,0},{3,1},{4,6},{5,7},{6,4},{7,5},{8,10},{9,11},{10,... | collective-permute-start | bytes 1572872 | tf_op jit(solution)/shard_map/ppermute | solution.py:681
  629.0 11.8 %collective-permute-start.63 = (bf16[2,64,1024]{2,1,0:T(8,128)(2,1)S(1)}, bf16[2,64,1024]{2,1,0:T(8,128)(2,1)S(1)}, u32[]{:S(2)}, u32[]{:S(2)}) collective-permute-start(bf16[2,64,1024]{2,1,0:T(8,128)(2,1)S(1)} %get-tuple-element.516), channel_id=1, source_target_pairs={{0,4},{1,5},{2,6},{3,7},{4,0},{5,1},{6,2},{7,3},{8,12},{9,13},{10,... | collective-permute-start | bytes 786440 | tf_op jit(solution)/shard_map/ppermute | solution.py:681
  629.3 11.4 %collective-permute-start.64 = (bf16[1,64,2048]{2,1,0:T(8,128)(2,1)S(1)}, bf16[1,64,2048]{2,1,0:T(8,128)(2,1)S(1)}, u32[]{:S(2)}, u32[]{:S(2)}) collective-permute-start(bf16[1,64,2048]{2,1,0:T(8,128)(2,1)S(1)} %get-tuple-element.518), channel_id=1, source_target_pairs={{0,8},{1,9},{2,10},{3,11},{4,12},{5,13},{6,14},{7,15},{8,0},{9,1},... | collective-permute-start | bytes 786440 | tf_op jit(solution)/shard_map/ppermute | solution.py:681
  (64 other events, 555.8 us)

commit v4 on v3

--- a/solution.py
+++ b/solution.py
@@ -132,7 +132,6 @@
 
 BLOCK = 512
 NO_COST = pl.CostEstimate(flops=1, bytes_accessed=1, transcendentals=0)
-SOME_COST = pl.CostEstimate(flops=10**8, bytes_accessed=2 * 10**6, transcendentals=0)
 FULL_COST = pl.CostEstimate(flops=40 * 10**9, bytes_accessed=10**8, transcendentals=0)
 
 
@@ -641,7 +640,6 @@
             [feed_back_part],
             [(loads, weights, outs, {}), ({"total": total, "sum_one": state["sum_one"]}, {}, {}, {})],
             pick,
-            cost=FULL_COST,
         )
 
     def attend_back(self, state, attended, grad_one, earlier, pick):
@@ -651,7 +649,6 @@
             [self.attend_back_set(state, earlier)],
             pick,
             {"attended": attended, "grad_one": grad_one},
-            cost=FULL_COST,
         )
 
 
@@ -750,7 +747,7 @@
             self.advance()
         return self.held[number]
 
-    def advance(self, *needed):
+    def advance(self, beside=None):
         sends, takers = [], []
         for number, (value, order, start) in enumerate(self.chunks):
             if start <= self.step < start + len(order):
@@ -759,7 +756,7 @@
                     for group in self.held[number]:
                         sends.append((group, step_along(self.dims, dim, steps)))
                         takers.append(number)
-        self.arrived = stage(sends, [*self.arrived, *needed])
+        self.arrived = stage(sends, self.arrived, beside)
         for number in sorted(set(takers)):
             value, order, start = self.chunks[number]
             got = [one for one, taker in zip(self.arrived, takers) if taker == number]
@@ -1499,14 +1496,26 @@
             layer, block[:, 0], block[:, 1 : 1 + proj_lines.shape[0]]
         )
         layer.qkv = whole(1, 1)
-        states = [layer.attend(rows, pick) for rows, pick in zip(own_rows, picks)]
+        states = []
+
+        def attend_beside(micro_step):
+            def beside(earlier, arriving):
+                rows = after(own_rows[micro_step], *earlier)
+                states.append(layer.attend(rows, picks[micro_step]))
+                return [states[-1]["norm"]]
+
+            return beside
+
+        def up_beside(earlier, arriving):
+            for state, pick in zip(states, picks):
+                state |= layer.rise(after(state["norm"], *earlier), pick)
+            return [state["active"] for state in states]
+
+        gather.advance(attend_beside(0))
+        gather.advance(attend_beside(1))
+        layer.up = whole(2, 3)
+        gather.advance(up_beside)
         gather.advance()
-        gather.advance(states[0]["norm"])
-        layer.up = whole(2, 3)
-        for state, pick in zip(states, picks):
-            state |= layer.rise(state["norm"], pick)
-        gather.advance(states[1]["norm"])
-        gather.advance(*(state["active"] for state in states))
         layer.down = whole(3, 5)
     else:
         layer = Layer(jnp.zeros((1,), jnp.int32), layout)
@@ -1616,29 +1625,29 @@
         def first_stage(earlier):
             feed_back(*pieces[0])
             vectors_of.append(grads["vectors"])
-            sent = weight_of("up", 1, "gate").make(SOME_COST)
-            pieces[1] = downs[1].keep(half, half, SOME_COST, [sent])
+            sent = weight_of("up", 1, "gate").make(NO_COST)
+            pieces[1] = downs[1].keep(half, half, NO_COST, [sent])
             return pieces[1]
 
         def second_stage(earlier):
             attend_back(*earlier)
             vectors_of.append(grads["vectors"])
-            pieces[2] = weights["up"].keep(0, hidden // 2, SOME_COST, [grads["mixed"]])
+            pieces[2] = weights["up"].keep(0, hidden // 2, NO_COST, [grads["mixed"]])
             return pieces[2]
 
         def third_stage(earlier):
-            sent = weight_of("qkv", 3, "mixed").make(FULL_COST, earlier)
-            sent = weight_of("out", 2, "attended").make(FULL_COST, [sent])
-            pieces[3] = weights["up"].keep(hidden // 2, hidden // 2, FULL_COST, [sent])
+            sent = weight_of("qkv", 3, "mixed").make(NO_COST, earlier)
+            sent = weight_of("out", 2, "attended").make(NO_COST, [sent])
+            pieces[3] = weights["up"].keep(hidden // 2, hidden // 2, NO_COST, [sent])
             return pieces[3]
 
         def fourth_stage(earlier):
-            pieces[4] = weights["qkv"].keep(0, 2 * width, FULL_COST, earlier)
-            pieces[5] = weights["qkv"].keep(2 * width, width, FULL_COST, pieces[4])
+            pieces[4] = weights["qkv"].keep(0, 2 * width, NO_COST, earlier)
+            pieces[5] = weights["qkv"].keep(2 * width, width, NO_COST, pieces[4])
             return pieces[5]
 
         def fifth_stage(earlier):
-            pieces[6] = weights["out"].keep(0, width, FULL_COST, earlier)
+            pieces[6] = weights["out"].keep(0, width, NO_COST, earlier)
             return pieces[6]
 
         def projection_grad():

time: 673 us -> 658 us (0.978)
  waiting for transfers between devices: 180 us -> 168 us
    ppermute x67, waiting for transfers between devices: 160 us -> 148 us  [shifted(): return lax.ppermute(value, 'dp', pairs)]
    unnamed x106 -> x116, local copies, waits for them, and re-layouts: 13.7 us -> 14.1 us
  transfers between devices with their start and end apart: 78 -> 78, of which waited for: 41 -> 43; matrix products, arithmetic and copies ran while one was open for 4% -> 5% of each run, Pallas kernels for 43% -> 45%
where the time goes in v4:
time: 658 us; the launch traced here: 651 us
  Pallas kernels  315 us (48%)
  waiting for transfers between devices  168 us (26%)
  starting transfers between devices  103 us (16%)
  local copies, waits for them, and re-layouts  32 us (5%)
  other arithmetic  31 us (5%)
    pallas_call x14, Pallas kernels, run_parts(): pl.pallas_call(kernel, in_specs=[pl.BlockSpec(memory_space=pltpu.SMEM)] *...  227 us
    ppermute x67, waiting for transfers between devices, shifted(): return lax.ppermute(value, 'dp', pairs)  148 us
    ppermute x67, starting transfers between devices, shifted(): return lax.ppermute(value, 'dp', pairs)  70.1 us
    pallas_call x12, Pallas kernels, product(): pl.pallas_call(partial(grad_kernel, rows=rows, slots=slots, outer=outer,...  64.9 us
    concatenate x16, other arithmetic, advance(): held = [jnp.concatenate(held)]  18.7 us
    unnamed x116, local copies, waits for them, and re-layouts  14.1 us
    all_to_all x3, waiting for transfers between devices, spread(): lax.all_to_all(jnp.broadcast_to(value[None], (count, *value.shape)), 'dp'...  14 us
    all_to_all x3, starting transfers between devices, spread(): lax.all_to_all(jnp.broadcast_to(value[None], (count, *value.shape)), 'dp'...  13.7 us
  transfers between devices with their start and end apart: 78, of which 43 were waited for; matrix products, arithmetic and copies ran while one was open for 5% of the time, Pallas kernels for 45%

profile of v4, /device:TPU:0, one launch (start us, length us, event | category | flops | bytes accessed | tf_op | source)
XLA Modules:
  0.0 651.4 jit_solution(4599545797437636875)
XLA Ops:
  3.4 4.1 collective-permute-start
  9.3 5.8 collective-permute-done
  16.9 3.4 collective-permute-start.2
  20.7 5.3 collective-permute-done.2
  28.4 3.4 collective-permute-start.4
  33.7 8.0 %collective-permute-done.4 = bf16[2,64,1024]{2,1,0:T(8,128)(2,1)} collective-permute-done((bf16[2,64,1024]{2,1,0:T(8,128)(2,1)S(1)}, bf16[2,64,1024]{2,1,0:T(8,128)(2,1)}, u32[]{:S(2)}, u32[]{:S(2)}) %collective-permute-start.4) | collective-permute-done | bytes 262176 | tf_op jit(solution)/shard_map/ppermute | solution.py:678
  41.8 3.9 collective-permute-done.5
  56.7 15.5 %collective-permute-done.9 = bf16[1,64,2048]{2,1,0:T(8,128)(2,1)} collective-permute-done((bf16[1,64,2048]{2,1,0:T(8,128)(2,1)}, bf16[1,64,2048]{2,1,0:T(8,128)(2,1)}, u32[]{:S(2)}, u32[]{:S(2)}) %collective-permute-start.9) | collective-permute-done | bytes 262176 | tf_op jit(solution)/shard_map/ppermute | solution.py:678
  72.9 2.7 pad_maximum_fusion.1.refs_11_.refs_13_.refs_16_.refs_36_.refs_34_.refs_18_
  84.0 14.2 %collective-permute-done.13 = bf16[1,64,2048]{2,1,0:T(8,128)(2,1)S(1)} collective-permute-done((bf16[1,64,2048]{2,1,0:T(8,128)(2,1)S(1)}, bf16[1,64,2048]{2,1,0:T(8,128)(2,1)S(1)}, u32[]{:S(2)}, u32[]{:S(2)}) %collective-permute-start.13) | collective-permute-done | bytes 262176 | tf_op jit(solution)/shard_map/ppermute | solution.py:678
  101.2 2.5 collective-permute-done.11.refs_12_.refs_14_.refs_17_.refs_37_.refs_35_.refs_19_
  111.9 13.5 %collective-permute-done.18 = bf16[1,256,512]{2,1,0:T(8,128)(2,1)S(1)} collective-permute-done((bf16[1,256,512]{2,1,0:T(8,128)(2,1)S(1)}, bf16[1,256,512]{2,1,0:T(8,128)(2,1)S(1)}, u32[]{:S(2)}, u32[]{:S(2)}) %collective-permute-start.18) | collective-permute-done | bytes 262176 | tf_op jit(solution)/shard_map/ppermute | solution.py:678
  129.8 2.6 pad_maximum_fusion.4.refs_8_.refs_23_.refs_26_.refs_28_.refs_19_
  137.1 2.6 place.1
  143.4 10.5 %attend.2 = (bf16[256,1024]{1,0:T(8,128)(2,1)}, bf16[256,1024]{1,0:T(8,128)(2,1)}, bf16[256,1024]{1,0:T(8,128)(2,1)}, bf16[256,1024]{1,0:T(8,128)(2,1)}, f32[256,1024]{1,0:T(8,128)}, /*index=5*/bf16[256,1024]{1,0:T(8,128)(2,1)}) custom-call(s32[2]{0:T(128)S(1)} %get-tuple-element.601.refs_0_, s32[16]{0:T(128)S(1)} %copy-done.11, ...), custom_call_target="tpu_custom_call" | custom-call | flops 1 | bytes 1 | tf_op jit(solution)/shard_map/attend/pallas_call | solution.py:260
  161.3 10.7 %attend.3 = (bf16[256,1024]{1,0:T(8,128)(2,1)}, bf16[256,1024]{1,0:T(8,128)(2,1)}, bf16[256,1024]{1,0:T(8,128)(2,1)}, bf16[256,1024]{1,0:T(8,128)(2,1)}, f32[256,1024]{1,0:T(8,128)}, /*index=5*/bf16[256,1024]{1,0:T(8,128)(2,1)}) custom-call(s32[2]{0:T(128)S(1)} %get-tuple-element.602.refs_0_, s32[16]{0:T(128)S(1)} %copy-done.11, ...), custom_call_target="tpu_custom_call" | custom-call | flops 1 | bytes 1 | tf_op jit(solution)/shard_map/attend/pallas_call | solution.py:260
  173.8 8.0 %collective-permute-done.26.refs_6_.refs_28_.refs_31_.refs_17_.refs_15_.refs_8_ = bf16[4,256,512]{2,1,0:T(8,128)(2,1)S(1)} collective-permute-done((bf16[4,256,512]{2,1,0:T(8,128)(2,1)S(1)}, bf16[4,256,512]{2,1,0:T(8,128)(2,1)S(1)}, u32[]{:S(2)}, u32[]{:S(2)}) %collective-permute-start.26) | collective-permute-done | bytes 1048608 | tf_op jit(solution)/shard_map/ppermute | solution.py:678
  184.1 11.1 %up.2 = (bf16[256,4096]{1,0:T(8,128)(2,1)}, bf16[256,4096]{1,0:T(8,128)(2,1)}) custom-call(s32[2]{0:T(128)S(1)} %get-tuple-element.601.refs_0_, s32[16]{0:T(128)S(1)} %copy-done.11, bf16[256,1024]{1,0:T(8,128)(2,1)} %get-tuple-element.348.refs_2_.refs_3_, f32[1,4096]{1,0:T(1,128)S(1)} %bitcast.130, bf16[4,64,2048]{2,1,0:T(8,128)(2,1)} %copy-done.14, ...), custom_call_target="tpu_custom_call" | custom-call | flops 1 | bytes 1 | tf_op jit(solution)/shard_map/up/pallas_call | solution.py:260
  195.2 11.1 %up.3 = (bf16[256,4096]{1,0:T(8,128)(2,1)}, bf16[256,4096]{1,0:T(8,128)(2,1)}) custom-call(s32[2]{0:T(128)S(1)} %get-tuple-element.602.refs_0_, s32[16]{0:T(128)S(1)} %copy-done.11, bf16[256,1024]{1,0:T(8,128)(2,1)} %get-tuple-element.353.refs_2_.refs_3_.refs_0_, f32[1,4096]{1,0:T(1,128)S(1)} %bitcast.131, bf16[4,64,2048]{2,1,0:T(8,128)(2,1)} %copy-done.14, ...), custom_call_target="tpu_custom_call" | custom-call | flops 1 | bytes 1 | tf_op jit(solution)/shard_map/up/pallas_call | solution.py:260
  210.9 7.7 %down.2 = (f32[256,1024]{1,0:T(8,128)}, bf16[256,1024]{1,0:T(8,128)(2,1)}) custom-call(s32[2]{0:T(128)S(1)} %get-tuple-element.601.refs_0_, s32[16]{0:T(128)S(1)} %copy-done.11, bf16[256,4096]{1,0:T(8,128)(2,1)} %get-tuple-element.349.refs_2_, bf16[256,1024]{1,0:T(8,128)(2,1)} %get-tuple-element.348.refs_2_.refs_3_, ...), custom_call_target="tpu_custom_call" | custom-call | flops 1 | bytes 1 | tf_op jit(solution)/shard_map/down/pallas_call | solution.py:260
  218.7 3.4 collective-permute-start.33
  224.3 7.7 %down.3 = (f32[256,1024]{1,0:T(8,128)}, bf16[256,1024]{1,0:T(8,128)(2,1)}) custom-call(s32[2]{0:T(128)S(1)} %get-tuple-element.602.refs_0_, s32[16]{0:T(128)S(1)} %copy-done.11, bf16[256,4096]{1,0:T(8,128)(2,1)} %get-tuple-element.364.refs_2_.refs_0_, bf16[256,1024]{1,0:T(8,128)(2,1)} %get-tuple-element.353.refs_2_.refs_3_.refs_0_, ...), custom_call_target="tpu_custom_call" | custom-call | flops 1 | bytes 1 | tf_op jit(solution)/shard_map/down/pallas_call | solution.py:260
  234.7 20.7 %forward.2 = (bf16[256,1024]{1,0:T(8,128)(2,1)}, bf16[256,1024]{1,0:T(8,128)(2,1)}, bf16[256,1024]{1,0:T(8,128)(2,1)}, bf16[256,1024]{1,0:T(8,128)(2,1)}, f32[25...) custom-call(s32[2]{0:T(128)S(1)} %get-tuple-element.601.refs_0_, ...), custom_call_target="tpu_custom_call" | custom-call | flops 40000000000 | bytes 100000000 | tf_op jit(solution)/shard_map/forward/pallas_call | solution.py:260
  256.8 4.2 all-to-all-start
  261.8 21.3 %forward.3 = (bf16[256,1024]{1,0:T(8,128)(2,1)}, bf16[256,1024]{1,0:T(8,128)(2,1)}, bf16[256,1024]{1,0:T(8,128)(2,1)}, bf16[256,1024]{1,0:T(8,128)(2,1)}, f32[25...) custom-call(s32[2]{0:T(128)S(1)} %get-tuple-element.602.refs_0_, ...), custom_call_target="tpu_custom_call" | custom-call | flops 40000000000 | bytes 100000000 | tf_op jit(solution)/shard_map/forward/pallas_call | solution.py:260
  284.7 6.0 all-to-all-start.1
  294.0 6.8 %all-to-all-done.1.queries_ref = bf16[16,64,128]{2,1,0:T(8,128)(2,1)S(1)} async-done(((bf16[16,64,128]{2,1,0:T(8,128)(2,1)}), bf16[16,64,128]{2,1,0:T(8,128)(2,1)S(1)}, u32[]{:S(2)}, u32[]{:S(2)}) %all-to-all-start.1) | async-done | bytes 262176 | tf_op jit(solution)/shard_map/all_to_all | solution.py:1161
  304.5 3.5 all-to-all-start.2
  309.0 7.2 %all-to-all-done.2 = f32[16,2,1,3,3,128]{5,1,4,3,2,0:T(2,128)S(1)} async-done(((f32[16,2,1,3,3,128]{5,1,4,3,2,0:T(2,128)}), f32[16,2,1,3,3,128]{5,1,4,3,2,0:T(2,128)S(1)}, u32[]{:S(2)}, u32[]{:S(2)}) %all-to-all-start.2) | async-done | bytes 147488 | tf_op jit(solution)/shard_map/all_to_all | solution.py:1161
  316.3 4.4 losses.2
  320.8 3.5 all-to-all-start.4
  324.4 4.5 losses.3
  330.3 4.1 collective-permute-done.35
  335.0 6.0 all-to-all-start.3
  341.0 29.5 %backward.4 = (bf16[256,1024]{1,0:T(8,128)(2,1)}, f32[16,1024]{1,0:T(8,128)}, bf16[256,128]{1,0:T(8,128)(2,1)}, bf16[256,4096]{1,0:T(8,128)(2,1)}, bf16[256,1024...) custom-call(s32[2]{0:T(128)S(1)} %get-tuple-element.602.refs_0_, ...), custom_call_target="tpu_custom_call" | custom-call | flops 40000000000 | bytes 100000000 | tf_op jit(solution)/shard_map/backward/pallas_call | solution.py:260
  372.5 29.2 %backward.3 = (bf16[256,1024]{1,0:T(8,128)(2,1)}, f32[16,1024]{1,0:T(8,128)}, bf16[256,128]{1,0:T(8,128)(2,1)}, bf16[256,4096]{1,0:T(8,128)(2,1)}, bf16[256,1024...) custom-call(s32[2]{0:T(128)S(1)} %get-tuple-element.601.refs_0_, ...), custom_call_target="tpu_custom_call" | custom-call | flops 40000000000 | bytes 100000000 | tf_op jit(solution)/shard_map/backward/pallas_call | solution.py:260
  403.8 29.3 %backward.5 = (bf16[256,1024]{1,0:T(8,128)(2,1)}, f32[16,1024]{1,0:T(8,128)}, bf16[256,4096]{1,0:T(8,128)(2,1)}, bf16[256,1024]{1,0:T(8,128)(2,1)}, bf16[3,256,1...) custom-call(s32[2]{0:T(128)S(1)} %get-tuple-element.602.refs_0_, s32[16]{0:T(128)S(1)} %copy-done.11, ...), custom_call_target="tpu_custom_call" | custom-call | flops 40000000000 | bytes 100000000 | tf_op jit(solution)/shard_map/backward/pallas_call | solution.py:260
  433.9 3.9 norm_back.1
  437.8 5.3 down_send.2
  443.6 5.3 down_send.3
  450.5 6.4 down_keep.2
  458.9 15.3 %feed_back.1 = (bf16[256,4096]{1,0:T(8,128)(2,1)}, bf16[256,1024]{1,0:T(8,128)(2,1)}, f32[16,1024]{1,0:T(8,128)}, f32[256,1024]{1,0:T(8,128)}) custom-call(s32[2]{0:T(128)S(1)} %get-tuple-element.601.refs_0_, s32[16]{0:T(128)S(1)} %copy-done.11, bf16[256,1024]{1,0:T(8,128)(2,1)} %get-tuple-element.410.refs_6_.refs_2_, ...), custom_call_target="tpu_custom_call" | custom-call | flops 1 | bytes 1 | tf_op jit(solution)/shard_map/feed_back/pallas_call | solution.py:260
  474.2 6.8 %up_send.1 = bf16[512,4096]{1,0:T(8,128)(2,1)S(1)} custom-call(s32[3]{0:T(128)S(1)} %pad_add_fusion.3.pick_ref, bf16[256,1024]{1,0:T(8,128)(2,1)} %get-tuple-element.353.refs_2_.refs_3_.refs_0_, bf16[256,1024]{1,0:T(8,128)(2,1)} %get-tuple-element.415.refs_1_, bf16[256,1024]{1,0:T(8,128)(2,1)} %get-tuple-element.348.refs_2_.refs_3_, ...), custom_call_target="tpu_custom_call" | custom-call | flops 1 | bytes 1 | tf_op jit(solution)/shard_map/up_send/pallas_call | solution.py:996
  482.4 6.4 down_keep.3
  491.2 19.5 %attend_back.1 = (bf16[3,256,1024]{2,1,0:T(8,128)(2,1)}, f32[16,1024]{1,0:T(8,128)}, f32[512,1024]{1,0:T(8,128)}) custom-call(s32[2]{0:T(128)S(1)} %get-tuple-element.601.refs_0_, s32[16]{0:T(128)S(1)} %copy-done.11, bf16[256,1024]{1,0:T(8,128)(2,1)} %get-tuple-element.425.refs_2_.refs_6_, f32[256,1024]{1,0:T(8,128)} %get-tuple-element.426.refs_3_, ...), custom_call_target="tpu_custom_call" | custom-call | flops 1 | bytes 1 | tf_op jit(solution)/shard_map/attend_back/pallas_call | solution.py:260
  510.7 5.3 up_keep.2
  519.3 2.4 collective-permute-start.46
  521.7 5.5 qkv_send.1
  527.2 4.0 out_send.1
  531.2 5.5 up_keep.3
  537.8 3.3 collective-permute-done.44.other_ref
  546.2 2.4 collective-permute-start.50
  548.6 4.9 qkv_keep.2
  553.6 4.6 qkv_keep.3
  558.3 4.5 collective-permute-done.50
  573.2 2.4 collective-permute-start.54
  577.9 4.8 out_keep.1
  582.8 5.5 collective-permute-done.54
  598.8 11.0 %collective-permute-done.60 = f32[4,2,32,128]{3,2,1,0:T(8,128)S(1)} collective-permute-done((f32[4,2,32,128]{3,2,1,0:T(8,128)S(1)}, f32[4,2,32,128]{3,2,1,0:T(8,128)S(1)}, u32[]{:S(2)}, u32[]{:S(2)}) %collective-permute-start.60) | collective-permute-done | bytes 131104 | tf_op jit(solution)/shard_map/ppermute | solution.py:678
  612.6 2.4 collective-permute-start.65
  623.0 4.4 collective-permute-done.63.other_ref
  627.4 3.0 collective-permute-done.64
  630.7 2.9 collective-permute-start.70
  639.6 3.1 collective-permute-done.67.other_ref
  (377 shorter events, 160.2 us)
Async XLA Ops:
  3.4 11.8 %collective-permute-start = (bf16[1,80,1024]{2,1,0:T(8,128)(2,1)S(1)}, bf16[1,80,1024]{2,1,0:T(8,128)(2,1)S(1)}, u32[]{:S(2)}, u32[]{:S(2)}) collective-permute-start(bf16[1,80,1024]{2,1,0:T(8,128)(2,1)S(1)} %maximum_bitcast_fusion.3), channel_id=1, source_target_pairs={{0,8},{1,9},{2,10},{3,11},{4,12},{5,13},{6,14},{7,15},{8,0},{9,1},... | collective-permute-start | bytes 491528 | tf_op jit(solution)/shard_map/ppermute | solution.py:678
  15.2 11.8 %collective-permute-start.1 = (bf16[2,80,1024]{2,1,0:T(8,128)(2,1)S(1)}, bf16[2,80,1024]{2,1,0:T(8,128)(2,1)S(1)}, u32[]{:S(2)}, u32[]{:S(2)}) collective-permute-start(bf16[2,80,1024]{2,1,0:T(8,128)(2,1)S(1)} %pad_maximum_fusion.14), channel_id=1, source_target_pairs={{0,4},{1,5},{2,6},{3,7},{4,0},{5,1},{6,2},{7,3},{8,12},{9,13},{10,... | collective-permute-start | bytes 983048 | tf_op jit(solution)/shard_map/ppermute | solution.py:678
  16.9 9.0 %collective-permute-start.2 = (bf16[1,64,1024]{2,1,0:T(8,128)(2,1)S(1)}, bf16[1,64,1024]{2,1,0:T(8,128)(2,1)S(1)}, u32[]{:S(2)}, u32[]{:S(2)}) collective-permute-start(bf16[1,64,1024]{2,1,0:T(8,128)(2,1)S(1)} %slice_bitcast_fusion.5), channel_id=1, source_target_pairs={{0,8},{1,9},{2,10},{3,11},{4,12},{5,13},{6,14},{7,15},{8,0},{9,1},... | collective-permute-start | bytes 393224 | tf_op jit(solution)/shard_map/ppermute | solution.py:678
  27.0 18.6 %collective-permute-start.3 = (bf16[4,80,1024]{2,1,0:T(8,128)(2,1)S(1)}, bf16[4,80,1024]{2,1,0:T(8,128)(2,1)}, u32[]{:S(2)}, u32[]{:S(2)}) collective-permute-start(bf16[4,80,1024]{2,1,0:T(8,128)(2,1)S(1)} %pad_maximum_fusion.7), channel_id=1, source_target_pairs={{0,2},{1,3},{2,0},{3,1},{4,6},{5,7},{6,4},{7,5},{8,10},{9,11},{10,... | collective-permute-start | bytes 1966088 | tf_op jit(solution)/shard_map/ppermute | solution.py:678
  28.4 13.4 %collective-permute-start.4 = (bf16[2,64,1024]{2,1,0:T(8,128)(2,1)S(1)}, bf16[2,64,1024]{2,1,0:T(8,128)(2,1)}, u32[]{:S(2)}, u32[]{:S(2)}) collective-permute-start(bf16[2,64,1024]{2,1,0:T(8,128)(2,1)S(1)} %pad_maximum_fusion.15), channel_id=1, source_target_pairs={{0,4},{1,5},{2,6},{3,7},{4,0},{5,1},{6,2},{7,3},{8,12},{9,13},{10,... | collective-permute-start | bytes 786440 | tf_op jit(solution)/shard_map/ppermute | solution.py:678
  31.8 13.8 %collective-permute-start.5 = (bf16[1,64,2048]{2,1,0:T(8,128)(2,1)S(1)}, bf16[1,64,2048]{2,1,0:T(8,128)(2,1)}, u32[]{:S(2)}, u32[]{:S(2)}) collective-permute-start(bf16[1,64,2048]{2,1,0:T(8,128)(2,1)S(1)} %slice_bitcast_fusion.4), channel_id=1, source_target_pairs={{0,8},{1,9},{2,10},{3,11},{4,12},{5,13},{6,14},{7,15},{8,0},{9,1},... | collective-permute-start | bytes 786440 | tf_op jit(solution)/shard_map/ppermute | solution.py:678
  46.9 26.0 %collective-permute-start.6 = (bf16[8,80,1024]{2,1,0:T(8,128)(2,1)S(1)}, bf16[8,80,1024]{2,1,0:T(8,128)(2,1)S(1)}, u32[]{:S(2)}, u32[]{:S(2)}) collective-permute-start(bf16[8,80,1024]{2,1,0:T(8,128)(2,1)S(1)} %pad_maximum_fusion.refs_0_.refs_15_.refs_17_.refs_20_.refs_32_.refs_30_.refs_14_), channel_id=1, source_target_pairs={{0,1},{1,0},{2,3},{3,2},{4,5},{5,4},{6,7},{7,6},{8,9},{9,8},{10,11... | collective-permute-start | bytes 3932168 | tf_op jit(solution)/shard_map/ppermute | solution.py:678
  52.8 19.4 %collective-permute-start.7 = (bf16[4,64,1024]{2,1,0:T(8,128)(2,1)}, bf16[4,64,1024]{2,1,0:T(8,128)(2,1)}, u32[]{:S(2)}, u32[]{:S(2)}) collective-permute-start(bf16[4,64,1024]{2,1,0:T(8,128)(2,1)} %pad_maximum_fusion.8), channel_id=1, source_target_pairs={{0,2},{1,3},{2,0},{3,1},{4,6},{5,7},{6,4},{7,5},{8,10},{9,11},{10,... | collective-permute-start | bytes 1572872 | tf_op jit(solution)/shard_map/ppermute | solution.py:678
  53.3 19.6 %collective-permute-start.8 = (bf16[2,64,2048]{2,1,0:T(8,128)(2,1)}, bf16[2,64,2048]{2,1,0:T(8,128)(2,1)}, u32[]{:S(2)}, u32[]{:S(2)}) collective-permute-start(bf16[2,64,2048]{2,1,0:T(8,128)(2,1)} %pad_maximum_fusion.9), channel_id=1, source_target_pairs={{0,4},{1,5},{2,6},{3,7},{4,0},{5,1},{6,2},{7,3},{8,12},{9,13},{10,... | collective-permute-start | bytes 1572872 | tf_op jit(solution)/shard_map/ppermute | solution.py:678
  55.1 17.0 %collective-permute-start.9 = (bf16[1,64,2048]{2,1,0:T(8,128)(2,1)}, bf16[1,64,2048]{2,1,0:T(8,128)(2,1)}, u32[]{:S(2)}, u32[]{:S(2)}) collective-permute-start(bf16[1,64,2048]{2,1,0:T(8,128)(2,1)} %get-tuple-element.303), channel_id=1, source_target_pairs={{0,8},{1,9},{2,10},{3,11},{4,12},{5,13},{6,14},{7,15},{8,0},{9,1},... | collective-permute-start | bytes 786440 | tf_op jit(solution)/shard_map/ppermute | solution.py:678
  77.8 22.4 %collective-permute-start.10 = (bf16[8,64,1024]{2,1,0:T(8,128)(2,1)}, bf16[8,64,1024]{2,1,0:T(8,128)(2,1)S(1)}, u32[]{:S(2)}, u32[]{:S(2)}) collective-permute-start(bf16[8,64,1024]{2,1,0:T(8,128)(2,1)} %pad_maximum_fusion.2.refs_9_.refs_11_.refs_14_.refs_34_.refs_32_.refs_16_), channel_id=1, source_target_pairs={{0,1},{1,0},{2,3},{3,2},{4,5},{5,4},{6,7},{7,6},{8,9},{9,8},{10,11... | collective-permute-start | bytes 3145736 | tf_op jit(solution)/shard_map/ppermute | solution.py:678
  77.8 25.9 %collective-permute-start.11 = (bf16[4,64,2048]{2,1,0:T(8,128)(2,1)}, bf16[4,64,2048]{2,1,0:T(8,128)(2,1)}, u32[]{:S(2)}, u32[]{:S(2)}) collective-permute-start(bf16[4,64,2048]{2,1,0:T(8,128)(2,1)} %pad_maximum_fusion.1.refs_11_.refs_13_.refs_16_.refs_36_.refs_34_.refs_18_), channel_id=1, source_target_pairs={{0,2},{1,3},{2,0},{3,1},{4,6},{5,7},{6,4},{7,5},{8,10},{9,11},{10,... | collective-permute-start | bytes 3145736 | tf_op jit(solution)/shard_map/ppermute | solution.py:678
  80.4 19.7 %collective-permute-start.12 = (bf16[2,64,2048]{2,1,0:T(8,128)(2,1)S(1)}, bf16[2,64,2048]{2,1,0:T(8,128)(2,1)S(1)}, u32[]{:S(2)}, u32[]{:S(2)}) collective-permute-start(bf16[2,64,2048]{2,1,0:T(8,128)(2,1)S(1)} %pad_maximum_fusion.10), channel_id=1, source_target_pairs={{0,4},{1,5},{2,6},{3,7},{4,0},{5,1},{6,2},{7,3},{8,12},{9,13},{10,... | collective-permute-start | bytes 1572872 | tf_op jit(solution)/shard_map/ppermute | solution.py:678
  81.1 17.1 %collective-permute-start.13 = (bf16[1,64,2048]{2,1,0:T(8,128)(2,1)S(1)}, bf16[1,64,2048]{2,1,0:T(8,128)(2,1)S(1)}, u32[]{:S(2)}, u32[]{:S(2)}) collective-permute-start(bf16[1,64,2048]{2,1,0:T(8,128)(2,1)S(1)} %get-tuple-element.311), channel_id=1, source_target_pairs={{0,8},{1,9},{2,10},{3,11},{4,12},{5,13},{6,14},{7,15},{8,0},{9,1},... | collective-permute-start | bytes 786440 | tf_op jit(solution)/shard_map/ppermute | solution.py:678
  104.8 25.0 %collective-permute-start.16 = (bf16[4,64,2048]{2,1,0:T(8,128)(2,1)S(1)}, bf16[4,64,2048]{2,1,0:T(8,128)(2,1)}, u32[]{:S(2)}, u32[]{:S(2)}) collective-permute-start(bf16[4,64,2048]{2,1,0:T(8,128)(2,1)S(1)} %pad_maximum_fusion.3.refs_4_.refs_19_.refs_22_.refs_24_.refs_15_), channel_id=1, source_target_pairs={{0,2},{1,3},{2,0},{3,1},{4,6},{5,7},{6,4},{7,5},{8,10},{9,11},{10,... | collective-permute-start | bytes 3145736 | tf_op jit(solution)/shard_map/ppermute | solution.py:678
  106.3 23.4 %collective-permute-start.14 = (bf16[4,64,2048]{2,1,0:T(8,128)(2,1)}, bf16[4,64,2048]{2,1,0:T(8,128)(2,1)S(1)}, u32[]{:S(2)}, u32[]{:S(2)}) collective-permute-start(bf16[4,64,2048]{2,1,0:T(8,128)(2,1)} %pad_maximum_fusion.1.refs_11_.refs_13_.refs_16_.refs_36_.refs_34_.refs_18_), channel_id=1, source_target_pairs={{0,1},{1,0},{2,3},{3,2},{4,5},{5,4},{6,7},{7,6},{8,9},{9,8},{10,11... | collective-permute-start | bytes 3145736 | tf_op jit(solution)/shard_map/ppermute | solution.py:678
  106.3 23.4 %collective-permute-start.15 = (bf16[4,64,2048]{2,1,0:T(8,128)(2,1)}, bf16[4,64,2048]{2,1,0:T(8,128)(2,1)}, u32[]{:S(2)}, u32[]{:S(2)}) collective-permute-start(bf16[4,64,2048]{2,1,0:T(8,128)(2,1)} %collective-permute-done.11.refs_12_.refs_14_.refs_17_.refs_37_.refs_35_.refs_19_), channel_id=1, source_target_pairs={{0,1},{1,0},{2,3},{3,2},{4,5},{5,4},{6,7},{7,6},{8,9},{9,8},{10,11... | collective-permute-start | bytes 3145736 | tf_op jit(solution)/shard_map/ppermute | solution.py:678
  107.8 19.8 %collective-permute-start.17 = (bf16[2,64,2048]{2,1,0:T(8,128)(2,1)}, bf16[2,64,2048]{2,1,0:T(8,128)(2,1)}, u32[]{:S(2)}, u32[]{:S(2)}) collective-permute-start(bf16[2,64,2048]{2,1,0:T(8,128)(2,1)} %pad_maximum_fusion.11), channel_id=1, source_target_pairs={{0,4},{1,5},{2,6},{3,7},{4,0},{5,1},{6,2},{7,3},{8,12},{9,13},{10,... | collective-permute-start | bytes 1572872 | tf_op jit(solution)/shard_map/ppermute | solution.py:678
  108.9 16.6 %collective-permute-start.18 = (bf16[1,256,512]{2,1,0:T(8,128)(2,1)S(1)}, bf16[1,256,512]{2,1,0:T(8,128)(2,1)S(1)}, u32[]{:S(2)}, u32[]{:S(2)}) collective-permute-start(bf16[1,256,512]{2,1,0:T(8,128)(2,1)S(1)} %get-tuple-element.320), channel_id=1, source_target_pairs={{0,8},{1,9},{2,10},{3,11},{4,12},{5,13},{6,14},{7,15},{8,0},{9,1},... | collective-permute-start | bytes 786440 | tf_op jit(solution)/shard_map/ppermute | solution.py:678
  132.4 24.2 %collective-permute-start.21 = (bf16[4,64,2048]{2,1,0:T(8,128)(2,1)}, bf16[4,64,2048]{2,1,0:T(8,128)(2,1)}, u32[]{:S(2)}, u32[]{:S(2)}) collective-permute-start(bf16[4,64,2048]{2,1,0:T(8,128)(2,1)} %pad_maximum_fusion.4.refs_8_.refs_23_.refs_26_.refs_28_.refs_19_), channel_id=1, source_target_pairs={{0,2},{1,3},{2,0},{3,1},{4,6},{5,7},{6,4},{7,5},{8,10},{9,11},{10,... | collective-permute-start | bytes 3145736 | tf_op jit(solution)/shard_map/ppermute | solution.py:678
  133.8 22.8 %collective-permute-start.19 = (bf16[4,64,2048]{2,1,0:T(8,128)(2,1)S(1)}, bf16[4,64,2048]{2,1,0:T(8,128)(2,1)}, u32[]{:S(2)}, u32[]{:S(2)}) collective-permute-start(bf16[4,64,2048]{2,1,0:T(8,128)(2,1)S(1)} %pad_maximum_fusion.3.refs_4_.refs_19_.refs_22_.refs_24_.refs_15_), channel_id=1, source_target_pairs={{0,1},{1,0},{2,3},{3,2},{4,5},{5,4},{6,7},{7,6},{8,9},{9,8},{10,11... | collective-permute-start | bytes 3145736 | tf_op jit(solution)/shard_map/ppermute | solution.py:678
  133.8 22.8 %collective-permute-start.20 = (bf16[4,64,2048]{2,1,0:T(8,128)(2,1)}, bf16[4,64,2048]{2,1,0:T(8,128)(2,1)}, u32[]{:S(2)}, u32[]{:S(2)}) collective-permute-start(bf16[4,64,2048]{2,1,0:T(8,128)(2,1)} %collective-permute-done.16.refs_5_.refs_20_.refs_23_.refs_25_.refs_16_), channel_id=1, source_target_pairs={{0,1},{1,0},{2,3},{3,2},{4,5},{5,4},{6,7},{7,6},{8,9},{9,8},{10,11... | collective-permute-start | bytes 3145736 | tf_op jit(solution)/shard_map/ppermute | solution.py:678
  136.5 19.8 %collective-permute-start.22 = (bf16[2,256,512]{2,1,0:T(8,128)(2,1)}, bf16[2,256,512]{2,1,0:T(8,128)(2,1)}, u32[]{:S(2)}, u32[]{:S(2)}) collective-permute-start(bf16[2,256,512]{2,1,0:T(8,128)(2,1)} %pad_maximum_fusion.12), channel_id=1, source_target_pairs={{0,4},{1,5},{2,6},{3,7},{4,0},{5,1},{6,2},{7,3},{8,12},{9,13},{10,... | collective-permute-start | bytes 1572872 | tf_op jit(solution)/shard_map/ppermute | solution.py:678
  140.7 13.5 %collective-permute-start.23 = (bf16[1,256,512]{2,1,0:T(8,128)(2,1)S(1)}, bf16[1,256,512]{2,1,0:T(8,128)(2,1)S(1)}, u32[]{:S(2)}, u32[]{:S(2)}) collective-permute-start(bf16[1,256,512]{2,1,0:T(8,128)(2,1)S(1)} %get-tuple-element.332), channel_id=1, source_target_pairs={{0,8},{1,9},{2,10},{3,11},{4,12},{5,13},{6,14},{7,15},{8,0},{9,1},... | collective-permute-start | bytes 786440 | tf_op jit(solution)/shard_map/ppermute | solution.py:678
  157.8 24.0 %collective-permute-start.26 = (bf16[4,256,512]{2,1,0:T(8,128)(2,1)S(1)}, bf16[4,256,512]{2,1,0:T(8,128)(2,1)S(1)}, u32[]{:S(2)}, u32[]{:S(2)}) collective-permute-start(bf16[4,256,512]{2,1,0:T(8,128)(2,1)S(1)} %pad_maximum_fusion.5.refs_5_.refs_27_.refs_30_.refs_16_.refs_14_.refs_7_), channel_id=1, source_target_pairs={{0,2},{1,3},{2,0},{3,1},{4,6},{5,7},{6,4},{7,5},{8,10},{9,11},{10,... | collective-permute-start | bytes 3145736 | tf_op jit(solution)/shard_map/ppermute | solution.py:678
  159.3 22.5 %collective-permute-start.24 = (bf16[4,64,2048]{2,1,0:T(8,128)(2,1)}, bf16[4,64,2048]{2,1,0:T(8,128)(2,1)S(1)}, u32[]{:S(2)}, u32[]{:S(2)}) collective-permute-start(bf16[4,64,2048]{2,1,0:T(8,128)(2,1)} %pad_maximum_fusion.4.refs_8_.refs_23_.refs_26_.refs_28_.refs_19_), channel_id=1, source_target_pairs={{0,1},{1,0},{2,3},{3,2},{4,5},{5,4},{6,7},{7,6},{8,9},{9,8},{10,11... | collective-permute-start | bytes 3145736 | tf_op jit(solution)/shard_map/ppermute | solution.py:678
  159.3 22.5 %collective-permute-start.25 = (bf16[4,64,2048]{2,1,0:T(8,128)(2,1)}, bf16[4,64,2048]{2,1,0:T(8,128)(2,1)S(1)}, u32[]{:S(2)}, u32[]{:S(2)}) collective-permute-start(bf16[4,64,2048]{2,1,0:T(8,128)(2,1)} %collective-permute-done.21.refs_9_.refs_24_.refs_27_.refs_29_.refs_20_), channel_id=1, source_target_pairs={{0,1},{1,0},{2,3},{3,2},{4,5},{5,4},{6,7},{7,6},{8,9},{9,8},{10,11... | collective-permute-start | bytes 3145736 | tf_op jit(solution)/shard_map/ppermute | solution.py:678
  159.9 13.9 %collective-permute-start.27 = (bf16[2,256,512]{2,1,0:T(8,128)(2,1)S(1)}, bf16[2,256,512]{2,1,0:T(8,128)(2,1)S(1)}, u32[]{:S(2)}, u32[]{:S(2)}) collective-permute-start(bf16[2,256,512]{2,1,0:T(8,128)(2,1)S(1)} %pad_maximum_fusion.13), channel_id=1, source_target_pairs={{0,4},{1,5},{2,6},{3,7},{4,0},{5,1},{6,2},{7,3},{8,12},{9,13},{10,... | collective-permute-start | bytes 1572872 | tf_op jit(solution)/shard_map/ppermute | solution.py:678
  183.0 23.3 %collective-permute-start.30 = (bf16[4,256,512]{2,1,0:T(8,128)(2,1)}, bf16[4,256,512]{2,1,0:T(8,128)(2,1)}, u32[]{:S(2)}, u32[]{:S(2)}) collective-permute-start(bf16[4,256,512]{2,1,0:T(8,128)(2,1)} %pad_maximum_fusion.6.refs_9_.refs_31_.refs_34_.refs_20_.refs_18_.refs_11_), channel_id=1, source_target_pairs={{0,2},{1,3},{2,0},{3,1},{4,6},{5,7},{6,4},{7,5},{8,10},{9,11},{10,... | collective-permute-start | bytes 3145736 | tf_op jit(solution)/shard_map/ppermute | solution.py:678
  183.5 22.8 %collective-permute-start.28 = (bf16[4,256,512]{2,1,0:T(8,128)(2,1)S(1)}, bf16[4,256,512]{2,1,0:T(8,128)(2,1)S(1)}, u32[]{:S(2)}, u32[]{:S(2)}) collective-permute-start(bf16[4,256,512]{2,1,0:T(8,128)(2,1)S(1)} %pad_maximum_fusion.5.refs_5_.refs_27_.refs_30_.refs_16_.refs_14_.refs_7_), channel_id=1, source_target_pairs={{0,1},{1,0},{2,3},{3,2},{4,5},{5,4},{6,7},{7,6},{8,9},{9,8},{10,11... | collective-permute-start | bytes 3145736 | tf_op jit(solution)/shard_map/ppermute | solution.py:678
  183.5 22.8 %collective-permute-start.29 = (bf16[4,256,512]{2,1,0:T(8,128)(2,1)S(1)}, bf16[4,256,512]{2,1,0:T(8,128)(2,1)S(1)}, u32[]{:S(2)}, u32[]{:S(2)}) collective-permute-start(bf16[4,256,512]{2,1,0:T(8,128)(2,1)S(1)} %collective-permute-done.26.refs_6_.refs_28_.refs_31_.refs_17_.refs_15_.refs_8_), channel_id=1, source_target_pairs={{0,1},{1,0},{2,3},{3,2},{4,5},{5,4},{6,7},{7,6},{8,9},{9,8},{10,11... | collective-permute-start | bytes 3145736 | tf_op jit(solution)/shard_map/ppermute | solution.py:678
  218.7 15.2 %collective-permute-start.33 = (bf16[256,1024]{1,0:T(8,128)(2,1)}, bf16[256,1024]{1,0:T(8,128)(2,1)S(1)}, u32[]{:S(2)}, u32[]{:S(2)}) collective-permute-start(bf16[256,1024]{1,0:T(8,128)(2,1)} %get-tuple-element.362.refs_11_), channel_id=1, source_target_pairs={{0,16},{1,17},{2,18},{3,19},{4,20},{5,21},{6,22},{7,23},{8,24},{9,... | collective-permute-start | bytes 1572872 | tf_op jit(solution)/shard_map/ppermute | solution.py:33
  232.0 29.0 %collective-permute-start.34 = (bf16[256,1024]{1,0:T(8,128)(2,1)}, bf16[256,1024]{1,0:T(8,128)(2,1)S(1)}, u32[]{:S(2)}, u32[]{:S(2)}) collective-permute-start(bf16[256,1024]{1,0:T(8,128)(2,1)} %get-tuple-element.365.refs_12_), channel_id=1, source_target_pairs={{0,16},{1,17},{2,18},{3,19},{4,20},{5,21},{6,22},{7,23},{8,24},{9,... | collective-permute-start | bytes 1572872 | tf_op jit(solution)/shard_map/ppermute | solution.py:33
  256.8 27.1 %all-to-all-start = ((bf16[16,64,128]{2,1,0:T(8,128)(2,1)}), bf16[16,64,128]{2,1,0:T(8,128)(2,1)S(1)}, u32[]{:S(2)}, u32[]{:S(2)}) async-start(bf16[16,64,128]{2,1,0:T(8,128)(2,1)} %broadcast_in_dim.157), calls=%async_computation | async-start | bytes 524288 | tf_op jit(solution)/shard_map/all_to_all | solution.py:1161
  284.7 16.0 %all-to-all-start.1 = ((bf16[16,64,128]{2,1,0:T(8,128)(2,1)}), bf16[16,64,128]{2,1,0:T(8,128)(2,1)S(1)}, u32[]{:S(2)}, u32[]{:S(2)}) async-start(bf16[16,64,128]{2,1,0:T(8,128)(2,1)} %broadcast_in_dim.158), calls=%async_computation.1 | async-start | bytes 524288 | tf_op jit(solution)/shard_map/all_to_all | solution.py:1161
  304.5 11.7 %all-to-all-start.2 = ((f32[16,2,1,3,3,128]{5,1,4,3,2,0:T(2,128)}), f32[16,2,1,3,3,128]{5,1,4,3,2,0:T(2,128)S(1)}, u32[]{:S(2)}, u32[]{:S(2)}) async-start(f32[16,2,1,3,3,128]{5,1,4,3,2,0:T(2,128)} %broadcast_in_dim.160), calls=%async_computation.2 | async-start | bytes 294912 | tf_op jit(solution)/shard_map/all_to_all | solution.py:1161
  320.8 14.3 %all-to-all-start.4 = ((bf16[16,64,128]{2,1,0:T(8,128)(2,1)}), bf16[16,64,128]{2,1,0:T(8,128)(2,1)S(1)}, u32[]{:S(2)}, u32[]{:S(2)}) async-start(bf16[16,64,128]{2,1,0:T(8,128)(2,1)} %get-tuple-element.368), calls=%async_computation.4 | async-start | bytes 524288 | tf_op jit(solution)/shard_map/all_to_all | solution.py:1564
  335.0 36.7 %all-to-all-start.3 = ((bf16[16,64,128]{2,1,0:T(8,128)(2,1)}), bf16[16,64,128]{2,1,0:T(8,128)(2,1)S(1)}, u32[]{:S(2)}, u32[]{:S(2)}) async-start(bf16[16,64,128]{2,1,0:T(8,128)(2,1)} %get-tuple-element.375), calls=%async_computation.3 | async-start | bytes 524288 | tf_op jit(solution)/shard_map/all_to_all | solution.py:1564
  370.5 32.5 %collective-permute-start.37 = (bf16[256,1024]{1,0:T(8,128)(2,1)}, bf16[256,1024]{1,0:T(8,128)(2,1)S(1)}, u32[]{:S(2)}, u32[]{:S(2)}) collective-permute-start(bf16[256,1024]{1,0:T(8,128)(2,1)} %get-tuple-element.390), channel_id=1, source_target_pairs={{16,0},{17,1},{18,2},{19,3},{20,4},{21,5},{22,6},{23,7},{24,8},{25... | collective-permute-start | bytes 1572872 | tf_op jit(solution)/shard_map/ppermute | solution.py:33
  401.7 31.4 %collective-permute-start.36 = (bf16[256,1024]{1,0:T(8,128)(2,1)}, bf16[256,1024]{1,0:T(8,128)(2,1)S(1)}, u32[]{:S(2)}, u32[]{:S(2)}) collective-permute-start(bf16[256,1024]{1,0:T(8,128)(2,1)} %get-tuple-element.382), channel_id=1, source_target_pairs={{16,0},{17,1},{18,2},{19,3},{20,4},{21,5},{22,6},{23,7},{24,8},{25... | collective-permute-start | bytes 1572872 | tf_op jit(solution)/shard_map/ppermute | solution.py:33
  449.0 32.0 %collective-permute-start.40 = (bf16[2048,512]{1,0:T(8,128)(2,1)S(1)}, bf16[2048,512]{1,0:T(8,128)(2,1)S(1)}, u32[]{:S(2)}, u32[]{:S(2)}) collective-permute-start(bf16[2048,512]{1,0:T(8,128)(2,1)S(1)} %down_send.3), channel_id=1, source_target_pairs={{0,1},{1,0},{2,3},{3,2},{4,5},{5,4},{6,7},{7,6},{8,9},{9,8},{10,11... | collective-permute-start | bytes 6291464 | tf_op jit(solution)/shard_map/ppermute | solution.py:678
  456.9 31.9 %collective-permute-start.39 = (bf16[4,256,512]{2,1,0:T(8,128)(2,1)S(1)}, bf16[4,256,512]{2,1,0:T(8,128)(2,1)S(1)}, u32[]{:S(2)}, u32[]{:S(2)}) collective-permute-start(bf16[4,256,512]{2,1,0:T(8,128)(2,1)S(1)} %get-tuple-element.409), channel_id=1, source_target_pairs={{0,2},{1,3},{2,0},{3,1},{4,6},{5,7},{6,4},{7,5},{8,10},{9,11},{10,... | collective-permute-start | bytes 3145736 | tf_op jit(solution)/shard_map/ppermute | solution.py:678
  488.7 21.9 %collective-permute-start.41 = (bf16[512,4096]{1,0:T(8,128)(2,1)S(1)}, bf16[512,4096]{1,0:T(8,128)(2,1)}, u32[]{:S(2)}, u32[]{:S(2)}) collective-permute-start(bf16[512,4096]{1,0:T(8,128)(2,1)S(1)} %up_send.1), channel_id=1, source_target_pairs={{0,1},{1,0},{2,3},{3,2},{4,5},{5,4},{6,7},{7,6},{8,9},{9,8},{10,11... | collective-permute-start | bytes 12582920 | tf_op jit(solution)/shard_map/ppermute | solution.py:678
  488.8 27.2 %collective-permute-start.42 = (bf16[4,256,512]{2,1,0:T(8,128)(2,1)S(1)}, bf16[4,256,512]{2,1,0:T(8,128)(2,1)S(1)}, u32[]{:S(2)}, u32[]{:S(2)}) collective-permute-start(bf16[4,256,512]{2,1,0:T(8,128)(2,1)S(1)} %get-tuple-element.438), channel_id=1, source_target_pairs={{0,2},{1,3},{2,0},{3,1},{4,6},{5,7},{6,4},{7,5},{8,10},{9,11},{10,... | collective-permute-start | bytes 3145736 | tf_op jit(solution)/shard_map/ppermute | solution.py:678
  489.3 26.8 %collective-permute-start.43 = (bf16[2,256,512]{2,1,0:T(8,128)(2,1)S(1)}, bf16[2,256,512]{2,1,0:T(8,128)(2,1)S(1)}, u32[]{:S(2)}, u32[]{:S(2)}) collective-permute-start(bf16[2,256,512]{2,1,0:T(8,128)(2,1)S(1)} %get-tuple-element.440), channel_id=1, source_target_pairs={{0,4},{1,5},{2,6},{3,7},{4,0},{5,1},{6,2},{7,3},{8,12},{9,13},{10,... | collective-permute-start | bytes 1572872 | tf_op jit(solution)/shard_map/ppermute | solution.py:678
  516.1 25.0 %collective-permute-start.44 = (bf16[4,64,2048]{2,1,0:T(8,128)(2,1)S(1)}, bf16[4,64,2048]{2,1,0:T(8,128)(2,1)S(1)}, u32[]{:S(2)}, u32[]{:S(2)}) collective-permute-start(bf16[4,64,2048]{2,1,0:T(8,128)(2,1)S(1)} %get-tuple-element.444), channel_id=1, source_target_pairs={{0,2},{1,3},{2,0},{3,1},{4,6},{5,7},{6,4},{7,5},{8,10},{9,11},{10,... | collective-permute-start | bytes 3145736 | tf_op jit(solution)/shard_map/ppermute | solution.py:678
  517.8 19.9 %collective-permute-start.45 = (bf16[2,256,512]{2,1,0:T(8,128)(2,1)S(1)}, bf16[2,256,512]{2,1,0:T(8,128)(2,1)S(1)}, u32[]{:S(2)}, u32[]{:S(2)}) collective-permute-start(bf16[2,256,512]{2,1,0:T(8,128)(2,1)S(1)} %get-tuple-element.446), channel_id=1, source_target_pairs={{0,4},{1,5},{2,6},{3,7},{4,0},{5,1},{6,2},{7,3},{8,12},{9,13},{10,... | collective-permute-start | bytes 1572872 | tf_op jit(solution)/shard_map/ppermute | solution.py:678
  519.3 18.4 %collective-permute-start.46 = (bf16[1,256,512]{2,1,0:T(8,128)(2,1)S(1)}, bf16[1,256,512]{2,1,0:T(8,128)(2,1)S(1)}, u32[]{:S(2)}, u32[]{:S(2)}) collective-permute-start(bf16[1,256,512]{2,1,0:T(8,128)(2,1)S(1)} %get-tuple-element.449), channel_id=1, source_target_pairs={{0,8},{1,9},{2,10},{3,11},{4,12},{5,13},{6,14},{7,15},{8,0},{9,1},... | collective-permute-start | bytes 786440 | tf_op jit(solution)/shard_map/ppermute | solution.py:678
  541.1 25.9 %collective-permute-start.48 = (bf16[4,64,2048]{2,1,0:T(8,128)(2,1)}, bf16[4,64,2048]{2,1,0:T(8,128)(2,1)}, u32[]{:S(2)}, u32[]{:S(2)}) collective-permute-start(bf16[4,64,2048]{2,1,0:T(8,128)(2,1)} %get-tuple-element.471), channel_id=1, source_target_pairs={{0,2},{1,3},{2,0},{3,1},{4,6},{5,7},{6,4},{7,5},{8,10},{9,11},{10,... | collective-permute-start | bytes 3145736 | tf_op jit(solution)/shard_map/ppermute | solution.py:678
  542.6 24.4 %collective-permute-start.51 = (bf16[512,1024]{1,0:T(8,128)(2,1)}, bf16[512,1024]{1,0:T(8,128)(2,1)}, u32[]{:S(2)}, u32[]{:S(2)}) collective-permute-start(bf16[512,1024]{1,0:T(8,128)(2,1)} %out_send.1), channel_id=1, source_target_pairs={{0,1},{1,0},{2,3},{3,2},{4,5},{5,4},{6,7},{7,6},{8,9},{9,8},{10,11... | collective-permute-start | bytes 3145736 | tf_op jit(solution)/shard_map/ppermute | solution.py:678
  544.7 20.0 %collective-permute-start.49 = (bf16[2,64,2048]{2,1,0:T(8,128)(2,1)}, bf16[2,64,2048]{2,1,0:T(8,128)(2,1)}, u32[]{:S(2)}, u32[]{:S(2)}) collective-permute-start(bf16[2,64,2048]{2,1,0:T(8,128)(2,1)} %get-tuple-element.473), channel_id=1, source_target_pairs={{0,4},{1,5},{2,6},{3,7},{4,0},{5,1},{6,2},{7,3},{8,12},{9,13},{10,... | collective-permute-start | bytes 1572872 | tf_op jit(solution)/shard_map/ppermute | solution.py:678
  546.2 16.5 %collective-permute-start.50 = (bf16[1,256,512]{2,1,0:T(8,128)(2,1)S(1)}, bf16[1,256,512]{2,1,0:T(8,128)(2,1)}, u32[]{:S(2)}, u32[]{:S(2)}) collective-permute-start(bf16[1,256,512]{2,1,0:T(8,128)(2,1)S(1)} %get-tuple-element.476), channel_id=1, source_target_pairs={{0,8},{1,9},{2,10},{3,11},{4,12},{5,13},{6,14},{7,15},{8,0},{9,1},... | collective-permute-start | bytes 786440 | tf_op jit(solution)/shard_map/ppermute | solution.py:678
  567.0 24.8 %collective-permute-start.52 = (bf16[4,64,2048]{2,1,0:T(8,128)(2,1)S(1)}, bf16[4,64,2048]{2,1,0:T(8,128)(2,1)S(1)}, u32[]{:S(2)}, u32[]{:S(2)}) collective-permute-start(bf16[4,64,2048]{2,1,0:T(8,128)(2,1)S(1)} %get-tuple-element.484), channel_id=1, source_target_pairs={{0,2},{1,3},{2,0},{3,1},{4,6},{5,7},{6,4},{7,5},{8,10},{9,11},{10,... | collective-permute-start | bytes 3145736 | tf_op jit(solution)/shard_map/ppermute | solution.py:678
  571.2 19.0 %collective-permute-start.53 = (bf16[2,64,2048]{2,1,0:T(8,128)(2,1)S(1)}, bf16[2,64,2048]{2,1,0:T(8,128)(2,1)S(1)}, u32[]{:S(2)}, u32[]{:S(2)}) collective-permute-start(bf16[2,64,2048]{2,1,0:T(8,128)(2,1)S(1)} %get-tuple-element.486), channel_id=1, source_target_pairs={{0,4},{1,5},{2,6},{3,7},{4,0},{5,1},{6,2},{7,3},{8,12},{9,13},{10,... | collective-permute-start | bytes 1572872 | tf_op jit(solution)/shard_map/ppermute | solution.py:678
  573.1 9.7 %collective-permute-start.55 = (f32[8,2,32,128]{3,2,1,0:T(8,128)S(1)}, f32[8,2,32,128]{3,2,1,0:T(8,128)S(1)}, u32[]{:S(2)}, u32[]{:S(2)}) collective-permute-start(f32[8,2,32,128]{3,2,1,0:T(8,128)S(1)} %bitcast.145), channel_id=1, source_target_pairs={{0,1},{1,0},{2,3},{3,2},{4,5},{5,4},{6,7},{7,6},{8,9},{9,8},{10,11... | collective-permute-start | bytes 786440 | tf_op jit(solution)/shard_map/ppermute | solution.py:678
  573.2 15.1 %collective-permute-start.54 = (bf16[1,64,2048]{2,1,0:T(8,128)(2,1)S(1)}, bf16[1,64,2048]{2,1,0:T(8,128)(2,1)S(1)}, u32[]{:S(2)}, u32[]{:S(2)}) collective-permute-start(bf16[1,64,2048]{2,1,0:T(8,128)(2,1)S(1)} %get-tuple-element.489), channel_id=1, source_target_pairs={{0,8},{1,9},{2,10},{3,11},{4,12},{5,13},{6,14},{7,15},{8,0},{9,1},... | collective-permute-start | bytes 786440 | tf_op jit(solution)/shard_map/ppermute | solution.py:678
  593.7 18.0 %collective-permute-start.58 = (bf16[2,64,2048]{2,1,0:T(8,128)(2,1)S(1)}, bf16[2,64,2048]{2,1,0:T(8,128)(2,1)S(1)}, u32[]{:S(2)}, u32[]{:S(2)}) collective-permute-start(bf16[2,64,2048]{2,1,0:T(8,128)(2,1)S(1)} %get-tuple-element.510), channel_id=1, source_target_pairs={{0,4},{1,5},{2,6},{3,7},{4,0},{5,1},{6,2},{7,3},{8,12},{9,13},{10,... | collective-permute-start | bytes 1572872 | tf_op jit(solution)/shard_map/ppermute | solution.py:678
  594.2 17.4 %collective-permute-start.57 = (bf16[4,64,1024]{2,1,0:T(8,128)(2,1)S(1)}, bf16[4,64,1024]{2,1,0:T(8,128)(2,1)S(1)}, u32[]{:S(2)}, u32[]{:S(2)}) collective-permute-start(bf16[4,64,1024]{2,1,0:T(8,128)(2,1)S(1)} %get-tuple-element.508), channel_id=1, source_target_pairs={{0,2},{1,3},{2,0},{3,1},{4,6},{5,7},{6,4},{7,5},{8,10},{9,11},{10,... | collective-permute-start | bytes 1572872 | tf_op jit(solution)/shard_map/ppermute | solution.py:678
  595.0 14.8 %collective-permute-start.60 = (f32[4,2,32,128]{3,2,1,0:T(8,128)S(1)}, f32[4,2,32,128]{3,2,1,0:T(8,128)S(1)}, u32[]{:S(2)}, u32[]{:S(2)}) collective-permute-start(f32[4,2,32,128]{3,2,1,0:T(8,128)S(1)} %dynamic-slice_bitcast_fusion), channel_id=1, source_target_pairs={{0,2},{1,3},{2,0},{3,1},{4,6},{5,7},{6,4},{7,5},{8,10},{9,11},{10,... | collective-permute-start | bytes 393224 | tf_op jit(solution)/shard_map/ppermute | solution.py:678
  596.4 13.5 %collective-permute-start.59 = (bf16[1,64,2048]{2,1,0:T(8,128)(2,1)S(1)}, bf16[1,64,2048]{2,1,0:T(8,128)(2,1)S(1)}, u32[]{:S(2)}, u32[]{:S(2)}) collective-permute-start(bf16[1,64,2048]{2,1,0:T(8,128)(2,1)S(1)} %get-tuple-element.513), channel_id=1, source_target_pairs={{0,8},{1,9},{2,10},{3,11},{4,12},{5,13},{6,14},{7,15},{8,0},{9,1},... | collective-permute-start | bytes 786440 | tf_op jit(solution)/shard_map/ppermute | solution.py:678
  611.7 18.7 %collective-permute-start.62 = (bf16[4,64,1024]{2,1,0:T(8,128)(2,1)S(1)}, bf16[4,64,1024]{2,1,0:T(8,128)(2,1)S(1)}, u32[]{:S(2)}, u32[]{:S(2)}) collective-permute-start(bf16[4,64,1024]{2,1,0:T(8,128)(2,1)S(1)} %get-tuple-element.522), channel_id=1, source_target_pairs={{0,2},{1,3},{2,0},{3,1},{4,6},{5,7},{6,4},{7,5},{8,10},{9,11},{10,... | collective-permute-start | bytes 1572872 | tf_op jit(solution)/shard_map/ppermute | solution.py:678
  615.1 12.3 %collective-permute-start.63 = (bf16[2,64,1024]{2,1,0:T(8,128)(2,1)S(1)}, bf16[2,64,1024]{2,1,0:T(8,128)(2,1)S(1)}, u32[]{:S(2)}, u32[]{:S(2)}) collective-permute-start(bf16[2,64,1024]{2,1,0:T(8,128)(2,1)S(1)} %get-tuple-element.524), channel_id=1, source_target_pairs={{0,4},{1,5},{2,6},{3,7},{4,0},{5,1},{6,2},{7,3},{8,12},{9,13},{10,... | collective-permute-start | bytes 786440 | tf_op jit(solution)/shard_map/ppermute | solution.py:678
  617.1 13.3 %collective-permute-start.64 = (bf16[1,64,2048]{2,1,0:T(8,128)(2,1)S(1)}, bf16[1,64,2048]{2,1,0:T(8,128)(2,1)S(1)}, u32[]{:S(2)}, u32[]{:S(2)}) collective-permute-start(bf16[1,64,2048]{2,1,0:T(8,128)(2,1)S(1)} %get-tuple-element.526), channel_id=1, source_target_pairs={{0,8},{1,9},{2,10},{3,11},{4,12},{5,13},{6,14},{7,15},{8,0},{9,1},... | collective-permute-start | bytes 786440 | tf_op jit(solution)/shard_map/ppermute | solution.py:678
  633.7 9.0 %collective-permute-start.67 = (bf16[2,64,1024]{2,1,0:T(8,128)(2,1)S(1)}, bf16[2,64,1024]{2,1,0:T(8,128)(2,1)S(1)}, u32[]{:S(2)}, u32[]{:S(2)}) collective-permute-start(bf16[2,64,1024]{2,1,0:T(8,128)(2,1)S(1)} %get-tuple-element.537), channel_id=1, source_target_pairs={{0,4},{1,5},{2,6},{3,7},{4,0},{5,1},{6,2},{7,3},{8,12},{9,13},{10,... | collective-permute-start | bytes 786440 | tf_op jit(solution)/shard_map/ppermute | solution.py:678
  (69 other events, 643.9 us)

commit v5 on v4

--- a/solution.py
+++ b/solution.py
@@ -1622,32 +1622,39 @@
             weight.other = shifted(weight.sent, dims, len(dims) - 1, 1)
         pieces = {0: downs[0].keep(0, half, NO_COST, [downs[1].sent])}
 
+        def exchanged(weight, earlier):
+            weight.make(NO_COST, earlier)
+            weight.other = shifted(weight.sent, dims, len(dims) - 1, 1)
+            return weight.sent
+
         def first_stage(earlier):
             feed_back(*pieces[0])
             vectors_of.append(grads["vectors"])
-            sent = weight_of("up", 1, "gate").make(NO_COST)
-            pieces[1] = downs[1].keep(half, half, NO_COST, [sent])
+            pieces[1] = downs[1].keep(half, half, NO_COST, [grads["gate"]])
             return pieces[1]
 
         def second_stage(earlier):
+            exchanged(weight_of("up", 1, "gate"), earlier)
+            pieces[2] = weights["up"].keep(0, hidden // 2, NO_COST)
+            return pieces[2]
+
+        def third_stage(earlier):
             attend_back(*earlier)
             vectors_of.append(grads["vectors"])
-            pieces[2] = weights["up"].keep(0, hidden // 2, NO_COST, [grads["mixed"]])
-            return pieces[2]
-
-        def third_stage(earlier):
-            sent = weight_of("qkv", 3, "mixed").make(NO_COST, earlier)
+            pieces[3] = weights["up"].keep(
+                hidden // 2, hidden // 2, NO_COST, [grads["mixed"]]
+            )
+            return pieces[3]
+
+        def fourth_stage(earlier):
+            sent = exchanged(weight_of("qkv", 3, "mixed"), earlier)
             sent = weight_of("out", 2, "attended").make(NO_COST, [sent])
-            pieces[3] = weights["up"].keep(hidden // 2, hidden // 2, NO_COST, [sent])
-            return pieces[3]
-
-        def fourth_stage(earlier):
-            pieces[4] = weights["qkv"].keep(0, 2 * width, NO_COST, earlier)
-            pieces[5] = weights["qkv"].keep(2 * width, width, NO_COST, pieces[4])
-            return pieces[5]
+            pieces[4] = weights["qkv"].keep(0, 2 * width, NO_COST, [sent])
+            return pieces[4]
 
         def fifth_stage(earlier):
-            pieces[6] = weights["out"].keep(0, width, NO_COST, earlier)
+            pieces[5] = weights["qkv"].keep(2 * width, width, NO_COST, earlier)
+            pieces[6] = weights["out"].keep(0, width, NO_COST, pieces[5])
             return pieces[6]
 
         def projection_grad():
@@ -1670,10 +1677,7 @@
             list(reversed(range(last_dim + 1))),
             dims,
             at,
-            {
-                1: lambda: [weights["up"]],
-                3: lambda: [weights["qkv"], weights["out"]],
-            },
+            {4: lambda: [weights["out"]]},
             {4: lambda: [projection_grad(), vector_grads()]},
             [first_stage, second_stage, third_stage, fourth_stage, fifth_stage],
         )

time: 658 us -> 670 us (1.018)
  waiting for transfers between devices: 168 us -> 186 us
  starting transfers between devices: 103 us -> 96.3 us
    ppermute x67, waiting for transfers between devices: 148 us -> 167 us  [shifted(): return lax.ppermute(value, 'dp', pairs)]
  transfers between devices with their start and end apart: 78 -> 78, of which waited for: 43 -> 46; matrix products, arithmetic and copies ran while one was open for 5% -> 5% of each run, Pallas kernels for 45% -> 41%
where the time goes in v5:
time: 670 us; the launch traced here: 663 us
  Pallas kernels  311 us (46%)
  waiting for transfers between devices  186 us (28%)
  starting transfers between devices  96.3 us (14%)
  local copies, waits for them, and re-layouts  36.1 us (5%)
  other arithmetic  30 us (4%)
    pallas_call x14, Pallas kernels, run_parts(): pl.pallas_call(kernel, in_specs=[pl.BlockSpec(memory_space=pltpu.SMEM)] *...  227 us
    ppermute x67, waiting for transfers between devices, shifted(): return lax.ppermute(value, 'dp', pairs)  167 us
    pallas_call x12, Pallas kernels, product(): pl.pallas_call(partial(grad_kernel, rows=rows, slots=slots, outer=outer,...  64.2 us
    ppermute x67, starting transfers between devices, shifted(): return lax.ppermute(value, 'dp', pairs)  63.9 us
    concatenate x16, other arithmetic, advance(): held = [jnp.concatenate(held)]  18.7 us
    unnamed x116, local copies, waits for them, and re-layouts  18.2 us
    all_to_all x3, waiting for transfers between devices, spread(): lax.all_to_all(jnp.broadcast_to(value[None], (count, *value.shape)), 'dp'...  14 us
  transfers between devices with their start and end apart: 78, of which 46 were waited for; matrix products, arithmetic and copies ran while one was open for 5% of the time, Pallas kernels for 41%

profile of v5, /device:TPU:0, one launch (start us, length us, event | category | flops | bytes accessed | tf_op | source)
XLA Modules:
  0.0 663.2 jit_solution(8760538698868273406)
XLA Ops:
  3.4 4.1 collective-permute-start
  9.3 5.8 collective-permute-done
  16.9 3.4 collective-permute-start.2
  20.7 5.3 collective-permute-done.2
  28.4 3.4 collective-permute-start.4
  33.7 8.0 %collective-permute-done.4 = bf16[2,64,1024]{2,1,0:T(8,128)(2,1)} collective-permute-done((bf16[2,64,1024]{2,1,0:T(8,128)(2,1)S(1)}, bf16[2,64,1024]{2,1,0:T(8,128)(2,1)}, u32[]{:S(2)}, u32[]{:S(2)}) %collective-permute-start.4) | collective-permute-done | bytes 262176 | tf_op jit(solution)/shard_map/ppermute | solution.py:678
  41.8 3.7 collective-permute-done.5
  56.7 15.5 %collective-permute-done.9 = bf16[1,64,2048]{2,1,0:T(8,128)(2,1)} collective-permute-done((bf16[1,64,2048]{2,1,0:T(8,128)(2,1)}, bf16[1,64,2048]{2,1,0:T(8,128)(2,1)}, u32[]{:S(2)}, u32[]{:S(2)}) %collective-permute-start.9) | collective-permute-done | bytes 262176 | tf_op jit(solution)/shard_map/ppermute | solution.py:678
  73.4 2.7 pad_maximum_fusion.1.refs_11_.refs_13_.refs_16_.refs_36_.refs_34_.refs_18_
  84.0 14.7 %collective-permute-done.13 = bf16[1,64,2048]{2,1,0:T(8,128)(2,1)S(1)} collective-permute-done((bf16[1,64,2048]{2,1,0:T(8,128)(2,1)S(1)}, bf16[1,64,2048]{2,1,0:T(8,128)(2,1)S(1)}, u32[]{:S(2)}, u32[]{:S(2)}) %collective-permute-start.13) | collective-permute-done | bytes 262176 | tf_op jit(solution)/shard_map/ppermute | solution.py:678
  101.7 2.5 collective-permute-done.11.refs_12_.refs_14_.refs_17_.refs_37_.refs_35_.refs_19_
  111.9 13.9 %collective-permute-done.18 = bf16[1,256,512]{2,1,0:T(8,128)(2,1)S(1)} collective-permute-done((bf16[1,256,512]{2,1,0:T(8,128)(2,1)S(1)}, bf16[1,256,512]{2,1,0:T(8,128)(2,1)S(1)}, u32[]{:S(2)}, u32[]{:S(2)}) %collective-permute-start.18) | collective-permute-done | bytes 262176 | tf_op jit(solution)/shard_map/ppermute | solution.py:678
  130.3 2.6 pad_maximum_fusion.4.refs_8_.refs_23_.refs_26_.refs_28_.refs_19_
  137.5 2.6 place.1
  143.4 10.4 %attend.2 = (bf16[256,1024]{1,0:T(8,128)(2,1)}, bf16[256,1024]{1,0:T(8,128)(2,1)}, bf16[256,1024]{1,0:T(8,128)(2,1)}, bf16[256,1024]{1,0:T(8,128)(2,1)}, f32[256,1024]{1,0:T(8,128)}, /*index=5*/bf16[256,1024]{1,0:T(8,128)(2,1)}) custom-call(s32[2]{0:T(128)S(1)} %get-tuple-element.597.refs_0_, s32[16]{0:T(128)S(1)} %copy-done.11, ...), custom_call_target="tpu_custom_call" | custom-call | flops 1 | bytes 1 | tf_op jit(solution)/shard_map/attend/pallas_call | solution.py:260
  161.3 10.4 %attend.3 = (bf16[256,1024]{1,0:T(8,128)(2,1)}, bf16[256,1024]{1,0:T(8,128)(2,1)}, bf16[256,1024]{1,0:T(8,128)(2,1)}, bf16[256,1024]{1,0:T(8,128)(2,1)}, f32[256,1024]{1,0:T(8,128)}, /*index=5*/bf16[256,1024]{1,0:T(8,128)(2,1)}) custom-call(s32[2]{0:T(128)S(1)} %get-tuple-element.598.refs_0_, s32[16]{0:T(128)S(1)} %copy-done.11, ...), custom_call_target="tpu_custom_call" | custom-call | flops 1 | bytes 1 | tf_op jit(solution)/shard_map/attend/pallas_call | solution.py:260
  171.7 2.6 collective-permute-done.27
  174.3 8.0 %collective-permute-done.26.refs_6_.refs_28_.refs_31_.refs_17_.refs_15_.refs_8_ = bf16[4,256,512]{2,1,0:T(8,128)(2,1)S(1)} collective-permute-done((bf16[4,256,512]{2,1,0:T(8,128)(2,1)S(1)}, bf16[4,256,512]{2,1,0:T(8,128)(2,1)S(1)}, u32[]{:S(2)}, u32[]{:S(2)}) %collective-permute-start.26) | collective-permute-done | bytes 1048608 | tf_op jit(solution)/shard_map/ppermute | solution.py:678
  184.6 11.0 %up.2 = (bf16[256,4096]{1,0:T(8,128)(2,1)}, bf16[256,4096]{1,0:T(8,128)(2,1)}) custom-call(s32[2]{0:T(128)S(1)} %get-tuple-element.597.refs_0_, s32[16]{0:T(128)S(1)} %copy-done.11, bf16[256,1024]{1,0:T(8,128)(2,1)} %get-tuple-element.346.refs_2_.refs_3_, f32[1,4096]{1,0:T(1,128)S(1)} %bitcast.130, bf16[4,64,2048]{2,1,0:T(8,128)(2,1)} %copy-done.16, ...), custom_call_target="tpu_custom_call" | custom-call | flops 1 | bytes 1 | tf_op jit(solution)/shard_map/up/pallas_call | solution.py:260
  195.7 11.3 %up.3 = (bf16[256,4096]{1,0:T(8,128)(2,1)}, bf16[256,4096]{1,0:T(8,128)(2,1)}) custom-call(s32[2]{0:T(128)S(1)} %get-tuple-element.598.refs_0_, s32[16]{0:T(128)S(1)} %copy-done.11, bf16[256,1024]{1,0:T(8,128)(2,1)} %get-tuple-element.351.refs_2_.refs_3_.refs_0_, f32[1,4096]{1,0:T(1,128)S(1)} %bitcast.131, bf16[4,64,2048]{2,1,0:T(8,128)(2,1)} %copy-done.16, ...), custom_call_target="tpu_custom_call" | custom-call | flops 1 | bytes 1 | tf_op jit(solution)/shard_map/up/pallas_call | solution.py:260
  211.6 7.7 %down.2 = (f32[256,1024]{1,0:T(8,128)}, bf16[256,1024]{1,0:T(8,128)(2,1)}) custom-call(s32[2]{0:T(128)S(1)} %get-tuple-element.597.refs_0_, s32[16]{0:T(128)S(1)} %copy-done.11, bf16[256,4096]{1,0:T(8,128)(2,1)} %get-tuple-element.347.refs_2_, bf16[256,1024]{1,0:T(8,128)(2,1)} %get-tuple-element.346.refs_2_.refs_3_, ...), custom_call_target="tpu_custom_call" | custom-call | flops 1 | bytes 1 | tf_op jit(solution)/shard_map/down/pallas_call | solution.py:260
  219.4 3.4 collective-permute-start.33
  225.0 7.7 %down.3 = (f32[256,1024]{1,0:T(8,128)}, bf16[256,1024]{1,0:T(8,128)(2,1)}) custom-call(s32[2]{0:T(128)S(1)} %get-tuple-element.598.refs_0_, s32[16]{0:T(128)S(1)} %copy-done.11, bf16[256,4096]{1,0:T(8,128)(2,1)} %get-tuple-element.362.refs_2_.refs_0_, bf16[256,1024]{1,0:T(8,128)(2,1)} %get-tuple-element.351.refs_2_.refs_3_.refs_0_, ...), custom_call_target="tpu_custom_call" | custom-call | flops 1 | bytes 1 | tf_op jit(solution)/shard_map/down/pallas_call | solution.py:260
  235.4 20.9 %forward.2 = (bf16[256,1024]{1,0:T(8,128)(2,1)}, bf16[256,1024]{1,0:T(8,128)(2,1)}, bf16[256,1024]{1,0:T(8,128)(2,1)}, bf16[256,1024]{1,0:T(8,128)(2,1)}, f32[25...) custom-call(s32[2]{0:T(128)S(1)} %get-tuple-element.597.refs_0_, ...), custom_call_target="tpu_custom_call" | custom-call | flops 40000000000 | bytes 100000000 | tf_op jit(solution)/shard_map/forward/pallas_call | solution.py:260
  257.8 3.5 all-to-all-start
  262.1 21.1 %forward.3 = (bf16[256,1024]{1,0:T(8,128)(2,1)}, bf16[256,1024]{1,0:T(8,128)(2,1)}, bf16[256,1024]{1,0:T(8,128)(2,1)}, bf16[256,1024]{1,0:T(8,128)(2,1)}, f32[25...) custom-call(s32[2]{0:T(128)S(1)} %get-tuple-element.598.refs_0_, ...), custom_call_target="tpu_custom_call" | custom-call | flops 40000000000 | bytes 100000000 | tf_op jit(solution)/shard_map/forward/pallas_call | solution.py:260
  284.8 6.0 all-to-all-start.1
  294.0 6.8 %all-to-all-done.1.queries_ref = bf16[16,64,128]{2,1,0:T(8,128)(2,1)S(1)} async-done(((bf16[16,64,128]{2,1,0:T(8,128)(2,1)}), bf16[16,64,128]{2,1,0:T(8,128)(2,1)S(1)}, u32[]{:S(2)}, u32[]{:S(2)}) %all-to-all-start.1) | async-done | bytes 262176 | tf_op jit(solution)/shard_map/all_to_all | solution.py:1161
  304.5 3.5 all-to-all-start.2
  309.1 7.2 %all-to-all-done.2 = f32[16,2,1,3,3,128]{5,1,4,3,2,0:T(2,128)S(1)} async-done(((f32[16,2,1,3,3,128]{5,1,4,3,2,0:T(2,128)}), f32[16,2,1,3,3,128]{5,1,4,3,2,0:T(2,128)S(1)}, u32[]{:S(2)}, u32[]{:S(2)}) %all-to-all-start.2) | async-done | bytes 147488 | tf_op jit(solution)/shard_map/all_to_all | solution.py:1161
  316.4 4.4 losses.2
  320.8 3.5 all-to-all-start.4
  324.5 4.5 losses.3
  330.4 4.1 collective-permute-done.35
  335.1 6.0 all-to-all-start.3
  341.1 29.2 %backward.4 = (bf16[256,1024]{1,0:T(8,128)(2,1)}, f32[16,1024]{1,0:T(8,128)}, bf16[256,128]{1,0:T(8,128)(2,1)}, bf16[256,4096]{1,0:T(8,128)(2,1)}, bf16[256,1024...) custom-call(s32[2]{0:T(128)S(1)} %get-tuple-element.598.refs_0_, ...), custom_call_target="tpu_custom_call" | custom-call | flops 40000000000 | bytes 100000000 | tf_op jit(solution)/shard_map/backward/pallas_call | solution.py:260
  372.3 29.4 %backward.3 = (bf16[256,1024]{1,0:T(8,128)(2,1)}, f32[16,1024]{1,0:T(8,128)}, bf16[256,128]{1,0:T(8,128)(2,1)}, bf16[256,4096]{1,0:T(8,128)(2,1)}, bf16[256,1024...) custom-call(s32[2]{0:T(128)S(1)} %get-tuple-element.597.refs_0_, ...), custom_call_target="tpu_custom_call" | custom-call | flops 40000000000 | bytes 100000000 | tf_op jit(solution)/shard_map/backward/pallas_call | solution.py:260
  403.8 29.0 %backward.5 = (bf16[256,1024]{1,0:T(8,128)(2,1)}, f32[16,1024]{1,0:T(8,128)}, bf16[256,4096]{1,0:T(8,128)(2,1)}, bf16[256,1024]{1,0:T(8,128)(2,1)}, bf16[3,256,1...) custom-call(s32[2]{0:T(128)S(1)} %get-tuple-element.598.refs_0_, s32[16]{0:T(128)S(1)} %copy-done.11, ...), custom_call_target="tpu_custom_call" | custom-call | flops 40000000000 | bytes 100000000 | tf_op jit(solution)/shard_map/backward/pallas_call | solution.py:260
  433.7 3.9 norm_back.1
  437.6 5.3 down_send.2
  443.4 5.3 down_send.3
  450.3 6.4 down_keep.2
  458.7 15.4 %feed_back.1 = (bf16[256,4096]{1,0:T(8,128)(2,1)}, bf16[256,1024]{1,0:T(8,128)(2,1)}, f32[16,1024]{1,0:T(8,128)}, f32[256,1024]{1,0:T(8,128)}) custom-call(s32[2]{0:T(128)S(1)} %get-tuple-element.597.refs_0_, s32[16]{0:T(128)S(1)} %copy-done.11, bf16[256,1024]{1,0:T(8,128)(2,1)} %get-tuple-element.408.refs_6_.refs_2_, ...), custom_call_target="tpu_custom_call" | custom-call | flops 1 | bytes 1 | tf_op jit(solution)/shard_map/feed_back/pallas_call | solution.py:260
  475.5 6.4 down_keep.3
  482.2 6.8 %up_send.1 = bf16[512,4096]{1,0:T(8,128)(2,1)S(1)} custom-call(s32[3]{0:T(128)S(1)} %pad_add_fusion.3.pick_ref, bf16[256,1024]{1,0:T(8,128)(2,1)} %get-tuple-element.351.refs_2_.refs_3_.refs_0_, bf16[256,1024]{1,0:T(8,128)(2,1)} %get-tuple-element.421.refs_1_, bf16[256,1024]{1,0:T(8,128)(2,1)} %get-tuple-element.346.refs_2_.refs_3_, ...), custom_call_target="tpu_custom_call" | custom-call | flops 1 | bytes 1 | tf_op jit(solution)/shard_map/up_send/pallas_call | solution.py:996
  492.6 3.7 collective-permute-done.43.refs_8_
  498.2 5.1 up_keep.2
  505.1 9.6 %collective-permute-done.41.other_ref = bf16[4,256,512]{2,1,0:T(8,128)(2,1)S(1)} collective-permute-done((bf16[4,256,512]{2,1,0:T(8,128)(2,1)S(1)}, bf16[4,256,512]{2,1,0:T(8,128)(2,1)S(1)}, u32[]{:S(2)}, u32[]{:S(2)}) %collective-permute-start.41) | collective-permute-done | bytes 1048608 | tf_op jit(solution)/shard_map/ppermute | solution.py:678
  521.3 19.4 %attend_back.1 = (bf16[3,256,1024]{2,1,0:T(8,128)(2,1)}, f32[16,1024]{1,0:T(8,128)}, f32[512,1024]{1,0:T(8,128)}) custom-call(s32[2]{0:T(128)S(1)} %get-tuple-element.597.refs_0_, s32[16]{0:T(128)S(1)} %copy-done.11, bf16[256,1024]{1,0:T(8,128)(2,1)} %get-tuple-element.431.refs_2_.refs_6_, f32[256,1024]{1,0:T(8,128)} %get-tuple-element.432.refs_3_, ...), custom_call_target="tpu_custom_call" | custom-call | flops 1 | bytes 1 | tf_op jit(solution)/shard_map/attend_back/pallas_call | solution.py:260
  540.8 5.2 up_keep.3
  546.0 5.5 qkv_send.1
  555.4 4.0 out_send.1
  561.0 4.9 qkv_keep.2
  566.0 5.2 collective-permute-done.50
  573.9 3.3 collective-permute-done.48.other_ref
  583.3 4.6 qkv_keep.3
  587.9 4.6 out_keep.1
  592.6 5.2 collective-permute-done.53
  599.7 3.3 collective-permute-done.51.other_ref
  608.5 12.7 %collective-permute-done.60 = f32[4,2,32,128]{3,2,1,0:T(8,128)S(1)} collective-permute-done((f32[4,2,32,128]{3,2,1,0:T(8,128)S(1)}, f32[4,2,32,128]{3,2,1,0:T(8,128)S(1)}, u32[]{:S(2)}, u32[]{:S(2)}) %collective-permute-start.60) | collective-permute-done | bytes 131104 | tf_op jit(solution)/shard_map/ppermute | solution.py:678
  629.5 4.1 collective-permute-done.65
  633.6 2.8 collective-permute-done.66
  636.4 3.3 collective-permute-done.63.other_ref
  648.7 3.4 collective-permute-done.68
  (377 shorter events, 161.4 us)
Async XLA Ops:
  3.4 11.8 %collective-permute-start = (bf16[1,80,1024]{2,1,0:T(8,128)(2,1)S(1)}, bf16[1,80,1024]{2,1,0:T(8,128)(2,1)S(1)}, u32[]{:S(2)}, u32[]{:S(2)}) collective-permute-start(bf16[1,80,1024]{2,1,0:T(8,128)(2,1)S(1)} %maximum_bitcast_fusion.3), channel_id=1, source_target_pairs={{0,8},{1,9},{2,10},{3,11},{4,12},{5,13},{6,14},{7,15},{8,0},{9,1},... | collective-permute-start | bytes 491528 | tf_op jit(solution)/shard_map/ppermute | solution.py:678
  15.2 11.8 %collective-permute-start.1 = (bf16[2,80,1024]{2,1,0:T(8,128)(2,1)S(1)}, bf16[2,80,1024]{2,1,0:T(8,128)(2,1)S(1)}, u32[]{:S(2)}, u32[]{:S(2)}) collective-permute-start(bf16[2,80,1024]{2,1,0:T(8,128)(2,1)S(1)} %pad_maximum_fusion.14), channel_id=1, source_target_pairs={{0,4},{1,5},{2,6},{3,7},{4,0},{5,1},{6,2},{7,3},{8,12},{9,13},{10,... | collective-permute-start | bytes 983048 | tf_op jit(solution)/shard_map/ppermute | solution.py:678
  16.9 9.0 %collective-permute-start.2 = (bf16[1,64,1024]{2,1,0:T(8,128)(2,1)S(1)}, bf16[1,64,1024]{2,1,0:T(8,128)(2,1)S(1)}, u32[]{:S(2)}, u32[]{:S(2)}) collective-permute-start(bf16[1,64,1024]{2,1,0:T(8,128)(2,1)S(1)} %slice_bitcast_fusion.5), channel_id=1, source_target_pairs={{0,8},{1,9},{2,10},{3,11},{4,12},{5,13},{6,14},{7,15},{8,0},{9,1},... | collective-permute-start | bytes 393224 | tf_op jit(solution)/shard_map/ppermute | solution.py:678
  27.0 18.5 %collective-permute-start.3 = (bf16[4,80,1024]{2,1,0:T(8,128)(2,1)S(1)}, bf16[4,80,1024]{2,1,0:T(8,128)(2,1)}, u32[]{:S(2)}, u32[]{:S(2)}) collective-permute-start(bf16[4,80,1024]{2,1,0:T(8,128)(2,1)S(1)} %pad_maximum_fusion.7), channel_id=1, source_target_pairs={{0,2},{1,3},{2,0},{3,1},{4,6},{5,7},{6,4},{7,5},{8,10},{9,11},{10,... | collective-permute-start | bytes 1966088 | tf_op jit(solution)/shard_map/ppermute | solution.py:678
  28.4 13.4 %collective-permute-start.4 = (bf16[2,64,1024]{2,1,0:T(8,128)(2,1)S(1)}, bf16[2,64,1024]{2,1,0:T(8,128)(2,1)}, u32[]{:S(2)}, u32[]{:S(2)}) collective-permute-start(bf16[2,64,1024]{2,1,0:T(8,128)(2,1)S(1)} %pad_maximum_fusion.15), channel_id=1, source_target_pairs={{0,4},{1,5},{2,6},{3,7},{4,0},{5,1},{6,2},{7,3},{8,12},{9,13},{10,... | collective-permute-start | bytes 786440 | tf_op jit(solution)/shard_map/ppermute | solution.py:678
  31.8 13.7 %collective-permute-start.5 = (bf16[1,64,2048]{2,1,0:T(8,128)(2,1)S(1)}, bf16[1,64,2048]{2,1,0:T(8,128)(2,1)S(1)}, u32[]{:S(2)}, u32[]{:S(2)}) collective-permute-start(bf16[1,64,2048]{2,1,0:T(8,128)(2,1)S(1)} %slice_bitcast_fusion.4), channel_id=1, source_target_pairs={{0,8},{1,9},{2,10},{3,11},{4,12},{5,13},{6,14},{7,15},{8,0},{9,1},... | collective-permute-start | bytes 786440 | tf_op jit(solution)/shard_map/ppermute | solution.py:678
  47.5 25.9 %collective-permute-start.6 = (bf16[8,80,1024]{2,1,0:T(8,128)(2,1)S(1)}, bf16[8,80,1024]{2,1,0:T(8,128)(2,1)S(1)}, u32[]{:S(2)}, u32[]{:S(2)}) collective-permute-start(bf16[8,80,1024]{2,1,0:T(8,128)(2,1)S(1)} %pad_maximum_fusion.refs_0_.refs_15_.refs_17_.refs_20_.refs_32_.refs_30_.refs_14_), channel_id=1, source_target_pairs={{0,1},{1,0},{2,3},{3,2},{4,5},{5,4},{6,7},{7,6},{8,9},{9,8},{10,11... | collective-permute-start | bytes 3932168 | tf_op jit(solution)/shard_map/ppermute | solution.py:678
  53.4 18.8 %collective-permute-start.7 = (bf16[4,64,1024]{2,1,0:T(8,128)(2,1)}, bf16[4,64,1024]{2,1,0:T(8,128)(2,1)}, u32[]{:S(2)}, u32[]{:S(2)}) collective-permute-start(bf16[4,64,1024]{2,1,0:T(8,128)(2,1)} %pad_maximum_fusion.8), channel_id=1, source_target_pairs={{0,2},{1,3},{2,0},{3,1},{4,6},{5,7},{6,4},{7,5},{8,10},{9,11},{10,... | collective-permute-start | bytes 1572872 | tf_op jit(solution)/shard_map/ppermute | solution.py:678
  53.9 19.5 %collective-permute-start.8 = (bf16[2,64,2048]{2,1,0:T(8,128)(2,1)}, bf16[2,64,2048]{2,1,0:T(8,128)(2,1)}, u32[]{:S(2)}, u32[]{:S(2)}) collective-permute-start(bf16[2,64,2048]{2,1,0:T(8,128)(2,1)} %pad_maximum_fusion.9), channel_id=1, source_target_pairs={{0,4},{1,5},{2,6},{3,7},{4,0},{5,1},{6,2},{7,3},{8,12},{9,13},{10,... | collective-permute-start | bytes 1572872 | tf_op jit(solution)/shard_map/ppermute | solution.py:678
  55.1 17.0 %collective-permute-start.9 = (bf16[1,64,2048]{2,1,0:T(8,128)(2,1)}, bf16[1,64,2048]{2,1,0:T(8,128)(2,1)}, u32[]{:S(2)}, u32[]{:S(2)}) collective-permute-start(bf16[1,64,2048]{2,1,0:T(8,128)(2,1)} %get-tuple-element.301), channel_id=1, source_target_pairs={{0,8},{1,9},{2,10},{3,11},{4,12},{5,13},{6,14},{7,15},{8,0},{9,1},... | collective-permute-start | bytes 786440 | tf_op jit(solution)/shard_map/ppermute | solution.py:678
  78.3 22.5 %collective-permute-start.10 = (bf16[8,64,1024]{2,1,0:T(8,128)(2,1)}, bf16[8,64,1024]{2,1,0:T(8,128)(2,1)S(1)}, u32[]{:S(2)}, u32[]{:S(2)}) collective-permute-start(bf16[8,64,1024]{2,1,0:T(8,128)(2,1)} %pad_maximum_fusion.2.refs_9_.refs_11_.refs_14_.refs_34_.refs_32_.refs_16_), channel_id=1, source_target_pairs={{0,1},{1,0},{2,3},{3,2},{4,5},{5,4},{6,7},{7,6},{8,9},{9,8},{10,11... | collective-permute-start | bytes 3145736 | tf_op jit(solution)/shard_map/ppermute | solution.py:678
  78.3 25.9 %collective-permute-start.11 = (bf16[4,64,2048]{2,1,0:T(8,128)(2,1)}, bf16[4,64,2048]{2,1,0:T(8,128)(2,1)}, u32[]{:S(2)}, u32[]{:S(2)}) collective-permute-start(bf16[4,64,2048]{2,1,0:T(8,128)(2,1)} %pad_maximum_fusion.1.refs_11_.refs_13_.refs_16_.refs_36_.refs_34_.refs_18_), channel_id=1, source_target_pairs={{0,2},{1,3},{2,0},{3,1},{4,6},{5,7},{6,4},{7,5},{8,10},{9,11},{10,... | collective-permute-start | bytes 3145736 | tf_op jit(solution)/shard_map/ppermute | solution.py:678
  81.0 19.7 %collective-permute-start.12 = (bf16[2,64,2048]{2,1,0:T(8,128)(2,1)S(1)}, bf16[2,64,2048]{2,1,0:T(8,128)(2,1)S(1)}, u32[]{:S(2)}, u32[]{:S(2)}) collective-permute-start(bf16[2,64,2048]{2,1,0:T(8,128)(2,1)S(1)} %pad_maximum_fusion.10), channel_id=1, source_target_pairs={{0,4},{1,5},{2,6},{3,7},{4,0},{5,1},{6,2},{7,3},{8,12},{9,13},{10,... | collective-permute-start | bytes 1572872 | tf_op jit(solution)/shard_map/ppermute | solution.py:678
  81.5 17.1 %collective-permute-start.13 = (bf16[1,64,2048]{2,1,0:T(8,128)(2,1)S(1)}, bf16[1,64,2048]{2,1,0:T(8,128)(2,1)S(1)}, u32[]{:S(2)}, u32[]{:S(2)}) collective-permute-start(bf16[1,64,2048]{2,1,0:T(8,128)(2,1)S(1)} %get-tuple-element.309), channel_id=1, source_target_pairs={{0,8},{1,9},{2,10},{3,11},{4,12},{5,13},{6,14},{7,15},{8,0},{9,1},... | collective-permute-start | bytes 786440 | tf_op jit(solution)/shard_map/ppermute | solution.py:678
  105.3 25.0 %collective-permute-start.16 = (bf16[4,64,2048]{2,1,0:T(8,128)(2,1)S(1)}, bf16[4,64,2048]{2,1,0:T(8,128)(2,1)}, u32[]{:S(2)}, u32[]{:S(2)}) collective-permute-start(bf16[4,64,2048]{2,1,0:T(8,128)(2,1)S(1)} %pad_maximum_fusion.3.refs_4_.refs_19_.refs_22_.refs_24_.refs_15_), channel_id=1, source_target_pairs={{0,2},{1,3},{2,0},{3,1},{4,6},{5,7},{6,4},{7,5},{8,10},{9,11},{10,... | collective-permute-start | bytes 3145736 | tf_op jit(solution)/shard_map/ppermute | solution.py:678
  106.9 23.4 %collective-permute-start.14 = (bf16[4,64,2048]{2,1,0:T(8,128)(2,1)}, bf16[4,64,2048]{2,1,0:T(8,128)(2,1)S(1)}, u32[]{:S(2)}, u32[]{:S(2)}) collective-permute-start(bf16[4,64,2048]{2,1,0:T(8,128)(2,1)} %pad_maximum_fusion.1.refs_11_.refs_13_.refs_16_.refs_36_.refs_34_.refs_18_), channel_id=1, source_target_pairs={{0,1},{1,0},{2,3},{3,2},{4,5},{5,4},{6,7},{7,6},{8,9},{9,8},{10,11... | collective-permute-start | bytes 3145736 | tf_op jit(solution)/shard_map/ppermute | solution.py:678
  106.9 23.4 %collective-permute-start.15 = (bf16[4,64,2048]{2,1,0:T(8,128)(2,1)}, bf16[4,64,2048]{2,1,0:T(8,128)(2,1)}, u32[]{:S(2)}, u32[]{:S(2)}) collective-permute-start(bf16[4,64,2048]{2,1,0:T(8,128)(2,1)} %collective-permute-done.11.refs_12_.refs_14_.refs_17_.refs_37_.refs_35_.refs_19_), channel_id=1, source_target_pairs={{0,1},{1,0},{2,3},{3,2},{4,5},{5,4},{6,7},{7,6},{8,9},{9,8},{10,11... | collective-permute-start | bytes 3145736 | tf_op jit(solution)/shard_map/ppermute | solution.py:678
  108.3 19.8 %collective-permute-start.17 = (bf16[2,64,2048]{2,1,0:T(8,128)(2,1)}, bf16[2,64,2048]{2,1,0:T(8,128)(2,1)}, u32[]{:S(2)}, u32[]{:S(2)}) collective-permute-start(bf16[2,64,2048]{2,1,0:T(8,128)(2,1)} %pad_maximum_fusion.11), channel_id=1, source_target_pairs={{0,4},{1,5},{2,6},{3,7},{4,0},{5,1},{6,2},{7,3},{8,12},{9,13},{10,... | collective-permute-start | bytes 1572872 | tf_op jit(solution)/shard_map/ppermute | solution.py:678
  109.3 16.6 %collective-permute-start.18 = (bf16[1,256,512]{2,1,0:T(8,128)(2,1)S(1)}, bf16[1,256,512]{2,1,0:T(8,128)(2,1)S(1)}, u32[]{:S(2)}, u32[]{:S(2)}) collective-permute-start(bf16[1,256,512]{2,1,0:T(8,128)(2,1)S(1)} %get-tuple-element.318), channel_id=1, source_target_pairs={{0,8},{1,9},{2,10},{3,11},{4,12},{5,13},{6,14},{7,15},{8,0},{9,1},... | collective-permute-start | bytes 786440 | tf_op jit(solution)/shard_map/ppermute | solution.py:678
  132.9 24.2 %collective-permute-start.21 = (bf16[4,64,2048]{2,1,0:T(8,128)(2,1)}, bf16[4,64,2048]{2,1,0:T(8,128)(2,1)}, u32[]{:S(2)}, u32[]{:S(2)}) collective-permute-start(bf16[4,64,2048]{2,1,0:T(8,128)(2,1)} %pad_maximum_fusion.4.refs_8_.refs_23_.refs_26_.refs_28_.refs_19_), channel_id=1, source_target_pairs={{0,2},{1,3},{2,0},{3,1},{4,6},{5,7},{6,4},{7,5},{8,10},{9,11},{10,... | collective-permute-start | bytes 3145736 | tf_op jit(solution)/shard_map/ppermute | solution.py:678
  134.4 22.7 %collective-permute-start.19 = (bf16[4,64,2048]{2,1,0:T(8,128)(2,1)S(1)}, bf16[4,64,2048]{2,1,0:T(8,128)(2,1)}, u32[]{:S(2)}, u32[]{:S(2)}) collective-permute-start(bf16[4,64,2048]{2,1,0:T(8,128)(2,1)S(1)} %pad_maximum_fusion.3.refs_4_.refs_19_.refs_22_.refs_24_.refs_15_), channel_id=1, source_target_pairs={{0,1},{1,0},{2,3},{3,2},{4,5},{5,4},{6,7},{7,6},{8,9},{9,8},{10,11... | collective-permute-start | bytes 3145736 | tf_op jit(solution)/shard_map/ppermute | solution.py:678
  134.4 22.7 %collective-permute-start.20 = (bf16[4,64,2048]{2,1,0:T(8,128)(2,1)}, bf16[4,64,2048]{2,1,0:T(8,128)(2,1)}, u32[]{:S(2)}, u32[]{:S(2)}) collective-permute-start(bf16[4,64,2048]{2,1,0:T(8,128)(2,1)} %collective-permute-done.16.refs_5_.refs_20_.refs_23_.refs_25_.refs_16_), channel_id=1, source_target_pairs={{0,1},{1,0},{2,3},{3,2},{4,5},{5,4},{6,7},{7,6},{8,9},{9,8},{10,11... | collective-permute-start | bytes 3145736 | tf_op jit(solution)/shard_map/ppermute | solution.py:678
  137.1 19.8 %collective-permute-start.22 = (bf16[2,256,512]{2,1,0:T(8,128)(2,1)}, bf16[2,256,512]{2,1,0:T(8,128)(2,1)}, u32[]{:S(2)}, u32[]{:S(2)}) collective-permute-start(bf16[2,256,512]{2,1,0:T(8,128)(2,1)} %pad_maximum_fusion.12), channel_id=1, source_target_pairs={{0,4},{1,5},{2,6},{3,7},{4,0},{5,1},{6,2},{7,3},{8,12},{9,13},{10,... | collective-permute-start | bytes 1572872 | tf_op jit(solution)/shard_map/ppermute | solution.py:678
  141.2 13.5 %collective-permute-start.23 = (bf16[1,256,512]{2,1,0:T(8,128)(2,1)S(1)}, bf16[1,256,512]{2,1,0:T(8,128)(2,1)S(1)}, u32[]{:S(2)}, u32[]{:S(2)}) collective-permute-start(bf16[1,256,512]{2,1,0:T(8,128)(2,1)S(1)} %get-tuple-element.330), channel_id=1, source_target_pairs={{0,8},{1,9},{2,10},{3,11},{4,12},{5,13},{6,14},{7,15},{8,0},{9,1},... | collective-permute-start | bytes 786440 | tf_op jit(solution)/shard_map/ppermute | solution.py:678
  158.3 24.0 %collective-permute-start.26 = (bf16[4,256,512]{2,1,0:T(8,128)(2,1)S(1)}, bf16[4,256,512]{2,1,0:T(8,128)(2,1)S(1)}, u32[]{:S(2)}, u32[]{:S(2)}) collective-permute-start(bf16[4,256,512]{2,1,0:T(8,128)(2,1)S(1)} %pad_maximum_fusion.5.refs_5_.refs_27_.refs_30_.refs_16_.refs_14_.refs_7_), channel_id=1, source_target_pairs={{0,2},{1,3},{2,0},{3,1},{4,6},{5,7},{6,4},{7,5},{8,10},{9,11},{10,... | collective-permute-start | bytes 3145736 | tf_op jit(solution)/shard_map/ppermute | solution.py:678
  159.9 22.5 %collective-permute-start.24 = (bf16[4,64,2048]{2,1,0:T(8,128)(2,1)}, bf16[4,64,2048]{2,1,0:T(8,128)(2,1)S(1)}, u32[]{:S(2)}, u32[]{:S(2)}) collective-permute-start(bf16[4,64,2048]{2,1,0:T(8,128)(2,1)} %pad_maximum_fusion.4.refs_8_.refs_23_.refs_26_.refs_28_.refs_19_), channel_id=1, source_target_pairs={{0,1},{1,0},{2,3},{3,2},{4,5},{5,4},{6,7},{7,6},{8,9},{9,8},{10,11... | collective-permute-start | bytes 3145736 | tf_op jit(solution)/shard_map/ppermute | solution.py:678
  159.9 22.5 %collective-permute-start.25 = (bf16[4,64,2048]{2,1,0:T(8,128)(2,1)}, bf16[4,64,2048]{2,1,0:T(8,128)(2,1)S(1)}, u32[]{:S(2)}, u32[]{:S(2)}) collective-permute-start(bf16[4,64,2048]{2,1,0:T(8,128)(2,1)} %collective-permute-done.21.refs_9_.refs_24_.refs_27_.refs_29_.refs_20_), channel_id=1, source_target_pairs={{0,1},{1,0},{2,3},{3,2},{4,5},{5,4},{6,7},{7,6},{8,9},{9,8},{10,11... | collective-permute-start | bytes 3145736 | tf_op jit(solution)/shard_map/ppermute | solution.py:678
  160.4 13.9 %collective-permute-start.27 = (bf16[2,256,512]{2,1,0:T(8,128)(2,1)S(1)}, bf16[2,256,512]{2,1,0:T(8,128)(2,1)S(1)}, u32[]{:S(2)}, u32[]{:S(2)}) collective-permute-start(bf16[2,256,512]{2,1,0:T(8,128)(2,1)S(1)} %pad_maximum_fusion.13), channel_id=1, source_target_pairs={{0,4},{1,5},{2,6},{3,7},{4,0},{5,1},{6,2},{7,3},{8,12},{9,13},{10,... | collective-permute-start | bytes 1572872 | tf_op jit(solution)/shard_map/ppermute | solution.py:678
  183.5 23.5 %collective-permute-start.30 = (bf16[4,256,512]{2,1,0:T(8,128)(2,1)}, bf16[4,256,512]{2,1,0:T(8,128)(2,1)}, u32[]{:S(2)}, u32[]{:S(2)}) collective-permute-start(bf16[4,256,512]{2,1,0:T(8,128)(2,1)} %pad_maximum_fusion.6.refs_9_.refs_31_.refs_34_.refs_20_.refs_18_.refs_11_), channel_id=1, source_target_pairs={{0,2},{1,3},{2,0},{3,1},{4,6},{5,7},{6,4},{7,5},{8,10},{9,11},{10,... | collective-permute-start | bytes 3145736 | tf_op jit(solution)/shard_map/ppermute | solution.py:678
  184.1 23.0 %collective-permute-start.28 = (bf16[4,256,512]{2,1,0:T(8,128)(2,1)S(1)}, bf16[4,256,512]{2,1,0:T(8,128)(2,1)S(1)}, u32[]{:S(2)}, u32[]{:S(2)}) collective-permute-start(bf16[4,256,512]{2,1,0:T(8,128)(2,1)S(1)} %pad_maximum_fusion.5.refs_5_.refs_27_.refs_30_.refs_16_.refs_14_.refs_7_), channel_id=1, source_target_pairs={{0,1},{1,0},{2,3},{3,2},{4,5},{5,4},{6,7},{7,6},{8,9},{9,8},{10,11... | collective-permute-start | bytes 3145736 | tf_op jit(solution)/shard_map/ppermute | solution.py:678
  184.1 23.0 %collective-permute-start.29 = (bf16[4,256,512]{2,1,0:T(8,128)(2,1)S(1)}, bf16[4,256,512]{2,1,0:T(8,128)(2,1)S(1)}, u32[]{:S(2)}, u32[]{:S(2)}) collective-permute-start(bf16[4,256,512]{2,1,0:T(8,128)(2,1)S(1)} %collective-permute-done.26.refs_6_.refs_28_.refs_31_.refs_17_.refs_15_.refs_8_), channel_id=1, source_target_pairs={{0,1},{1,0},{2,3},{3,2},{4,5},{5,4},{6,7},{7,6},{8,9},{9,8},{10,11... | collective-permute-start | bytes 3145736 | tf_op jit(solution)/shard_map/ppermute | solution.py:678
  219.4 15.2 %collective-permute-start.33 = (bf16[256,1024]{1,0:T(8,128)(2,1)}, bf16[256,1024]{1,0:T(8,128)(2,1)S(1)}, u32[]{:S(2)}, u32[]{:S(2)}) collective-permute-start(bf16[256,1024]{1,0:T(8,128)(2,1)} %get-tuple-element.360.refs_11_), channel_id=1, source_target_pairs={{0,16},{1,17},{2,18},{3,19},{4,20},{5,21},{6,22},{7,23},{8,24},{9,... | collective-permute-start | bytes 1572872 | tf_op jit(solution)/shard_map/ppermute | solution.py:33
  232.8 28.5 %collective-permute-start.34 = (bf16[256,1024]{1,0:T(8,128)(2,1)}, bf16[256,1024]{1,0:T(8,128)(2,1)S(1)}, u32[]{:S(2)}, u32[]{:S(2)}) collective-permute-start(bf16[256,1024]{1,0:T(8,128)(2,1)} %get-tuple-element.363.refs_12_), channel_id=1, source_target_pairs={{0,16},{1,17},{2,18},{3,19},{4,20},{5,21},{6,22},{7,23},{8,24},{9,... | collective-permute-start | bytes 1572872 | tf_op jit(solution)/shard_map/ppermute | solution.py:33
  257.8 26.2 %all-to-all-start = ((bf16[16,64,128]{2,1,0:T(8,128)(2,1)}), bf16[16,64,128]{2,1,0:T(8,128)(2,1)S(1)}, u32[]{:S(2)}, u32[]{:S(2)}) async-start(bf16[16,64,128]{2,1,0:T(8,128)(2,1)} %broadcast_in_dim.157), calls=%async_computation | async-start | bytes 524288 | tf_op jit(solution)/shard_map/all_to_all | solution.py:1161
  284.8 16.0 %all-to-all-start.1 = ((bf16[16,64,128]{2,1,0:T(8,128)(2,1)}), bf16[16,64,128]{2,1,0:T(8,128)(2,1)S(1)}, u32[]{:S(2)}, u32[]{:S(2)}) async-start(bf16[16,64,128]{2,1,0:T(8,128)(2,1)} %broadcast_in_dim.158), calls=%async_computation.1 | async-start | bytes 524288 | tf_op jit(solution)/shard_map/all_to_all | solution.py:1161
  304.5 11.7 %all-to-all-start.2 = ((f32[16,2,1,3,3,128]{5,1,4,3,2,0:T(2,128)}), f32[16,2,1,3,3,128]{5,1,4,3,2,0:T(2,128)S(1)}, u32[]{:S(2)}, u32[]{:S(2)}) async-start(f32[16,2,1,3,3,128]{5,1,4,3,2,0:T(2,128)} %broadcast_in_dim.160), calls=%async_computation.2 | async-start | bytes 294912 | tf_op jit(solution)/shard_map/all_to_all | solution.py:1161
  320.8 14.3 %all-to-all-start.4 = ((bf16[16,64,128]{2,1,0:T(8,128)(2,1)}), bf16[16,64,128]{2,1,0:T(8,128)(2,1)S(1)}, u32[]{:S(2)}, u32[]{:S(2)}) async-start(bf16[16,64,128]{2,1,0:T(8,128)(2,1)} %get-tuple-element.366), calls=%async_computation.4 | async-start | bytes 524288 | tf_op jit(solution)/shard_map/all_to_all | solution.py:1564
  335.1 36.5 %all-to-all-start.3 = ((bf16[16,64,128]{2,1,0:T(8,128)(2,1)}), bf16[16,64,128]{2,1,0:T(8,128)(2,1)S(1)}, u32[]{:S(2)}, u32[]{:S(2)}) async-start(bf16[16,64,128]{2,1,0:T(8,128)(2,1)} %get-tuple-element.373), calls=%async_computation.3 | async-start | bytes 524288 | tf_op jit(solution)/shard_map/all_to_all | solution.py:1564
  370.3 32.7 %collective-permute-start.37 = (bf16[256,1024]{1,0:T(8,128)(2,1)}, bf16[256,1024]{1,0:T(8,128)(2,1)S(1)}, u32[]{:S(2)}, u32[]{:S(2)}) collective-permute-start(bf16[256,1024]{1,0:T(8,128)(2,1)} %get-tuple-element.388), channel_id=1, source_target_pairs={{16,0},{17,1},{18,2},{19,3},{20,4},{21,5},{22,6},{23,7},{24,8},{25... | collective-permute-start | bytes 1572872 | tf_op jit(solution)/shard_map/ppermute | solution.py:33
  401.7 31.2 %collective-permute-start.36 = (bf16[256,1024]{1,0:T(8,128)(2,1)}, bf16[256,1024]{1,0:T(8,128)(2,1)S(1)}, u32[]{:S(2)}, u32[]{:S(2)}) collective-permute-start(bf16[256,1024]{1,0:T(8,128)(2,1)} %get-tuple-element.380), channel_id=1, source_target_pairs={{16,0},{17,1},{18,2},{19,3},{20,4},{21,5},{22,6},{23,7},{24,8},{25... | collective-permute-start | bytes 1572872 | tf_op jit(solution)/shard_map/ppermute | solution.py:33
  448.8 25.3 %collective-permute-start.39 = (bf16[2048,512]{1,0:T(8,128)(2,1)S(1)}, bf16[2048,512]{1,0:T(8,128)(2,1)S(1)}, u32[]{:S(2)}, u32[]{:S(2)}) collective-permute-start(bf16[2048,512]{1,0:T(8,128)(2,1)S(1)} %down_send.3), channel_id=1, source_target_pairs={{0,1},{1,0},{2,3},{3,2},{4,5},{5,4},{6,7},{7,6},{8,9},{9,8},{10,11... | collective-permute-start | bytes 6291464 | tf_op jit(solution)/shard_map/ppermute | solution.py:678
  456.7 25.6 %collective-permute-start.40 = (bf16[4,256,512]{2,1,0:T(8,128)(2,1)S(1)}, bf16[4,256,512]{2,1,0:T(8,128)(2,1)S(1)}, u32[]{:S(2)}, u32[]{:S(2)}) collective-permute-start(bf16[4,256,512]{2,1,0:T(8,128)(2,1)S(1)} %get-tuple-element.407), channel_id=1, source_target_pairs={{0,2},{1,3},{2,0},{3,1},{4,6},{5,7},{6,4},{7,5},{8,10},{9,11},{10,... | collective-permute-start | bytes 3145736 | tf_op jit(solution)/shard_map/ppermute | solution.py:678
  489.1 25.6 %collective-permute-start.41 = (bf16[4,256,512]{2,1,0:T(8,128)(2,1)S(1)}, bf16[4,256,512]{2,1,0:T(8,128)(2,1)S(1)}, u32[]{:S(2)}, u32[]{:S(2)}) collective-permute-start(bf16[4,256,512]{2,1,0:T(8,128)(2,1)S(1)} %get-tuple-element.418), channel_id=1, source_target_pairs={{0,2},{1,3},{2,0},{3,1},{4,6},{5,7},{6,4},{7,5},{8,10},{9,11},{10,... | collective-permute-start | bytes 3145736 | tf_op jit(solution)/shard_map/ppermute | solution.py:678
  491.0 14.1 %collective-permute-start.42 = (bf16[2,256,512]{2,1,0:T(8,128)(2,1)S(1)}, bf16[2,256,512]{2,1,0:T(8,128)(2,1)S(1)}, u32[]{:S(2)}, u32[]{:S(2)}) collective-permute-start(bf16[2,256,512]{2,1,0:T(8,128)(2,1)S(1)} %get-tuple-element.420), channel_id=1, source_target_pairs={{0,4},{1,5},{2,6},{3,7},{4,0},{5,1},{6,2},{7,3},{8,12},{9,13},{10,... | collective-permute-start | bytes 1572872 | tf_op jit(solution)/shard_map/ppermute | solution.py:678
  514.7 31.3 %collective-permute-start.44 = (bf16[4,64,2048]{2,1,0:T(8,128)(2,1)S(1)}, bf16[4,64,2048]{2,1,0:T(8,128)(2,1)S(1)}, u32[]{:S(2)}, u32[]{:S(2)}) collective-permute-start(bf16[4,64,2048]{2,1,0:T(8,128)(2,1)S(1)} %get-tuple-element.440), channel_id=1, source_target_pairs={{0,2},{1,3},{2,0},{3,1},{4,6},{5,7},{6,4},{7,5},{8,10},{9,11},{10,... | collective-permute-start | bytes 3145736 | tf_op jit(solution)/shard_map/ppermute | solution.py:678
  516.5 29.4 %collective-permute-start.45 = (bf16[2,256,512]{2,1,0:T(8,128)(2,1)S(1)}, bf16[2,256,512]{2,1,0:T(8,128)(2,1)S(1)}, u32[]{:S(2)}, u32[]{:S(2)}) collective-permute-start(bf16[2,256,512]{2,1,0:T(8,128)(2,1)S(1)} %get-tuple-element.442), channel_id=1, source_target_pairs={{0,4},{1,5},{2,6},{3,7},{4,0},{5,1},{6,2},{7,3},{8,12},{9,13},{10,... | collective-permute-start | bytes 1572872 | tf_op jit(solution)/shard_map/ppermute | solution.py:678
  519.0 27.0 %collective-permute-start.46 = (bf16[1,256,512]{2,1,0:T(8,128)(2,1)S(1)}, bf16[1,256,512]{2,1,0:T(8,128)(2,1)S(1)}, u32[]{:S(2)}, u32[]{:S(2)}) collective-permute-start(bf16[1,256,512]{2,1,0:T(8,128)(2,1)S(1)} %get-tuple-element.445), channel_id=1, source_target_pairs={{0,8},{1,9},{2,10},{3,11},{4,12},{5,13},{6,14},{7,15},{8,0},{9,1},... | collective-permute-start | bytes 786440 | tf_op jit(solution)/shard_map/ppermute | solution.py:678
  551.6 25.6 %collective-permute-start.48 = (bf16[4,64,2048]{2,1,0:T(8,128)(2,1)S(1)}, bf16[4,64,2048]{2,1,0:T(8,128)(2,1)S(1)}, u32[]{:S(2)}, u32[]{:S(2)}) collective-permute-start(bf16[4,64,2048]{2,1,0:T(8,128)(2,1)S(1)} %get-tuple-element.467), channel_id=1, source_target_pairs={{0,2},{1,3},{2,0},{3,1},{4,6},{5,7},{6,4},{7,5},{8,10},{9,11},{10,... | collective-permute-start | bytes 3145736 | tf_op jit(solution)/shard_map/ppermute | solution.py:678
  553.5 19.6 %collective-permute-start.49 = (bf16[2,64,2048]{2,1,0:T(8,128)(2,1)S(1)}, bf16[2,64,2048]{2,1,0:T(8,128)(2,1)S(1)}, u32[]{:S(2)}, u32[]{:S(2)}) collective-permute-start(bf16[2,64,2048]{2,1,0:T(8,128)(2,1)S(1)} %get-tuple-element.469), channel_id=1, source_target_pairs={{0,4},{1,5},{2,6},{3,7},{4,0},{5,1},{6,2},{7,3},{8,12},{9,13},{10,... | collective-permute-start | bytes 1572872 | tf_op jit(solution)/shard_map/ppermute | solution.py:678
  555.0 16.2 %collective-permute-start.50 = (bf16[1,256,512]{2,1,0:T(8,128)(2,1)S(1)}, bf16[1,256,512]{2,1,0:T(8,128)(2,1)S(1)}, u32[]{:S(2)}, u32[]{:S(2)}) collective-permute-start(bf16[1,256,512]{2,1,0:T(8,128)(2,1)S(1)} %get-tuple-element.472), channel_id=1, source_target_pairs={{0,8},{1,9},{2,10},{3,11},{4,12},{5,13},{6,14},{7,15},{8,0},{9,1},... | collective-permute-start | bytes 786440 | tf_op jit(solution)/shard_map/ppermute | solution.py:678
  577.3 25.8 %collective-permute-start.51 = (bf16[4,64,2048]{2,1,0:T(8,128)(2,1)}, bf16[4,64,2048]{2,1,0:T(8,128)(2,1)S(1)}, u32[]{:S(2)}, u32[]{:S(2)}) collective-permute-start(bf16[4,64,2048]{2,1,0:T(8,128)(2,1)} %copy-done.12), channel_id=1, source_target_pairs={{0,2},{1,3},{2,0},{3,1},{4,6},{5,7},{6,4},{7,5},{8,10},{9,11},{10,... | collective-permute-start | bytes 3145736 | tf_op jit(solution)/shard_map/ppermute | solution.py:678
  580.1 19.7 %collective-permute-start.52 = (bf16[2,64,2048]{2,1,0:T(8,128)(2,1)S(1)}, bf16[2,64,2048]{2,1,0:T(8,128)(2,1)S(1)}, u32[]{:S(2)}, u32[]{:S(2)}) collective-permute-start(bf16[2,64,2048]{2,1,0:T(8,128)(2,1)S(1)} %get-tuple-element.478), channel_id=1, source_target_pairs={{0,4},{1,5},{2,6},{3,7},{4,0},{5,1},{6,2},{7,3},{8,12},{9,13},{10,... | collective-permute-start | bytes 1572872 | tf_op jit(solution)/shard_map/ppermute | solution.py:678
  581.2 11.4 %collective-permute-start.55 = (f32[8,2,32,128]{3,2,1,0:T(8,128)S(1)}, f32[8,2,32,128]{3,2,1,0:T(8,128)S(1)}, u32[]{:S(2)}, u32[]{:S(2)}) collective-permute-start(f32[8,2,32,128]{3,2,1,0:T(8,128)S(1)} %bitcast.145), channel_id=1, source_target_pairs={{0,1},{1,0},{2,3},{3,2},{4,5},{5,4},{6,7},{7,6},{8,9},{9,8},{10,11... | collective-permute-start | bytes 786440 | tf_op jit(solution)/shard_map/ppermute | solution.py:678
  581.4 16.4 %collective-permute-start.53 = (bf16[1,64,2048]{2,1,0:T(8,128)(2,1)S(1)}, bf16[1,64,2048]{2,1,0:T(8,128)(2,1)S(1)}, u32[]{:S(2)}, u32[]{:S(2)}) collective-permute-start(bf16[1,64,2048]{2,1,0:T(8,128)(2,1)S(1)} %get-tuple-element.481), channel_id=1, source_target_pairs={{0,8},{1,9},{2,10},{3,11},{4,12},{5,13},{6,14},{7,15},{8,0},{9,1},... | collective-permute-start | bytes 786440 | tf_op jit(solution)/shard_map/ppermute | solution.py:678
  582.1 10.5 %collective-permute-start.56 = (f32[16,1024]{1,0:T(8,128)S(1)}, f32[16,1024]{1,0:T(8,128)S(1)}, u32[]{:S(2)}, u32[]{:S(2)}) collective-permute-start(f32[16,1024]{1,0:T(8,128)S(1)} %add_add_fusion), channel_id=1, source_target_pairs={{0,1},{1,0},{2,3},{3,2},{4,5},{5,4},{6,7},{7,6},{8,9},{9,8},{10,11... | collective-permute-start | bytes 196616 | tf_op jit(solution)/shard_map/ppermute | solution.py:678
  604.1 18.8 %collective-permute-start.58 = (bf16[2,64,2048]{2,1,0:T(8,128)(2,1)S(1)}, bf16[2,64,2048]{2,1,0:T(8,128)(2,1)S(1)}, u32[]{:S(2)}, u32[]{:S(2)}) collective-permute-start(bf16[2,64,2048]{2,1,0:T(8,128)(2,1)S(1)} %get-tuple-element.506), channel_id=1, source_target_pairs={{0,4},{1,5},{2,6},{3,7},{4,0},{5,1},{6,2},{7,3},{8,12},{9,13},{10,... | collective-permute-start | bytes 1572872 | tf_op jit(solution)/shard_map/ppermute | solution.py:678
  604.6 18.3 %collective-permute-start.57 = (bf16[4,64,1024]{2,1,0:T(8,128)(2,1)S(1)}, bf16[4,64,1024]{2,1,0:T(8,128)(2,1)S(1)}, u32[]{:S(2)}, u32[]{:S(2)}) collective-permute-start(bf16[4,64,1024]{2,1,0:T(8,128)(2,1)S(1)} %get-tuple-element.504), channel_id=1, source_target_pairs={{0,2},{1,3},{2,0},{3,1},{4,6},{5,7},{6,4},{7,5},{8,10},{9,11},{10,... | collective-permute-start | bytes 1572872 | tf_op jit(solution)/shard_map/ppermute | solution.py:678
  606.2 15.0 %collective-permute-start.60 = (f32[4,2,32,128]{3,2,1,0:T(8,128)S(1)}, f32[4,2,32,128]{3,2,1,0:T(8,128)S(1)}, u32[]{:S(2)}, u32[]{:S(2)}) collective-permute-start(f32[4,2,32,128]{3,2,1,0:T(8,128)S(1)} %dynamic-slice_bitcast_fusion), channel_id=1, source_target_pairs={{0,2},{1,3},{2,0},{3,1},{4,6},{5,7},{6,4},{7,5},{8,10},{9,11},{10,... | collective-permute-start | bytes 393224 | tf_op jit(solution)/shard_map/ppermute | solution.py:678
  606.8 14.4 %collective-permute-start.59 = (bf16[1,64,2048]{2,1,0:T(8,128)(2,1)S(1)}, bf16[1,64,2048]{2,1,0:T(8,128)(2,1)S(1)}, u32[]{:S(2)}, u32[]{:S(2)}) collective-permute-start(bf16[1,64,2048]{2,1,0:T(8,128)(2,1)S(1)} %get-tuple-element.509), channel_id=1, source_target_pairs={{0,8},{1,9},{2,10},{3,11},{4,12},{5,13},{6,14},{7,15},{8,0},{9,1},... | collective-permute-start | bytes 786440 | tf_op jit(solution)/shard_map/ppermute | solution.py:678
  623.0 16.7 %collective-permute-start.62 = (bf16[4,64,1024]{2,1,0:T(8,128)(2,1)S(1)}, bf16[4,64,1024]{2,1,0:T(8,128)(2,1)S(1)}, u32[]{:S(2)}, u32[]{:S(2)}) collective-permute-start(bf16[4,64,1024]{2,1,0:T(8,128)(2,1)S(1)} %get-tuple-element.518), channel_id=1, source_target_pairs={{0,2},{1,3},{2,0},{3,1},{4,6},{5,7},{6,4},{7,5},{8,10},{9,11},{10,... | collective-permute-start | bytes 1572872 | tf_op jit(solution)/shard_map/ppermute | solution.py:678
  625.4 11.0 %collective-permute-start.66 = (f32[16,1024]{1,0:T(8,128)S(1)}, f32[16,1024]{1,0:T(8,128)S(1)}, u32[]{:S(2)}, u32[]{:S(2)}) collective-permute-start(f32[16,1024]{1,0:T(8,128)S(1)} %add.360), channel_id=1, source_target_pairs={{0,4},{1,5},{2,6},{3,7},{4,0},{5,1},{6,2},{7,3},{8,12},{9,13},{10,... | collective-permute-start | bytes 196616 | tf_op jit(solution)/shard_map/ppermute | solution.py:678
  626.9 12.8 %collective-permute-start.63 = (bf16[2,64,1024]{2,1,0:T(8,128)(2,1)S(1)}, bf16[2,64,1024]{2,1,0:T(8,128)(2,1)S(1)}, u32[]{:S(2)}, u32[]{:S(2)}) collective-permute-start(bf16[2,64,1024]{2,1,0:T(8,128)(2,1)S(1)} %get-tuple-element.520), channel_id=1, source_target_pairs={{0,4},{1,5},{2,6},{3,7},{4,0},{5,1},{6,2},{7,3},{8,12},{9,13},{10,... | collective-permute-start | bytes 786440 | tf_op jit(solution)/shard_map/ppermute | solution.py:678
  627.4 12.3 %collective-permute-start.64 = (bf16[1,64,2048]{2,1,0:T(8,128)(2,1)S(1)}, bf16[1,64,2048]{2,1,0:T(8,128)(2,1)S(1)}, u32[]{:S(2)}, u32[]{:S(2)}) collective-permute-start(bf16[1,64,2048]{2,1,0:T(8,128)(2,1)S(1)} %get-tuple-element.522), channel_id=1, source_target_pairs={{0,8},{1,9},{2,10},{3,11},{4,12},{5,13},{6,14},{7,15},{8,0},{9,1},... | collective-permute-start | bytes 786440 | tf_op jit(solution)/shard_map/ppermute | solution.py:678
  643.0 9.1 %collective-permute-start.68 = (bf16[1,64,1024]{2,1,0:T(8,128)(2,1)S(1)}, bf16[1,64,1024]{2,1,0:T(8,128)(2,1)S(1)}, u32[]{:S(2)}, u32[]{:S(2)}) collective-permute-start(bf16[1,64,1024]{2,1,0:T(8,128)(2,1)S(1)} %get-tuple-element.535), channel_id=1, source_target_pairs={{0,8},{1,9},{2,10},{3,11},{4,12},{5,13},{6,14},{7,15},{8,0},{9,1},... | collective-permute-start | bytes 393224 | tf_op jit(solution)/shard_map/ppermute | solution.py:678
  (69 other events, 565.2 us)
